TPU v7x, 32 devices: a whole 2x2x4 slice. The times are simulated.
32 devices in a mesh: rep: 2 (over y), dev: 4 (over z), sub: 4 (over x, core).
Axes of the slice: x: 2, y: 2, z: 4, core: 2. Of those that a mesh axis runs over, the one named last changes fastest.
Arguments:
- tokens: bfloat16 [256, 3072], P(('rep', 'dev', 'sub')), parts along dimension 0, may hold values from -6 to 6
- queries: bfloat16 [256, 3072], P(('rep', 'dev', 'sub')), parts along dimension 0, may hold values from -12 to 12
- request_key_cache: bfloat16 [256, 128, 512], P(('rep', 'dev', 'sub')), parts along dimension 0, may hold values from -12 to 12
- request_value_cache: bfloat16 [256, 128, 512], P(('rep', 'dev', 'sub')), parts along dimension 0, may hold values from -6 to 6
- lengths: int32 [256], P(('rep', 'dev', 'sub')), parts along dimension 0, may hold values from 2 to 128, as said below
- norm_gain: bfloat16 [3072], replicated, may hold values from 0.5 to 1.5
- router_weight: bfloat16 [3072, 4], replicated, may hold values from -0.109375 to 0.109375
- routes: int32 [256, 2], P(('rep', 'dev')), parts along dimension 0, may hold values from 0 to 3, all different within a row; in each aligned block of 32 rows (0 to 31, 32 to 63, ...) at most 26 rows name the same one
- gate_weight: bfloat16 [3072, 32768], P(None, ('dev', 'sub')), may hold values from -0.109375 to 0.109375
- up_weight: bfloat16 [3072, 32768], P(None, ('dev', 'sub')), may hold values from -0.109375 to 0.109375
- down_weight: bfloat16 [32768, 3072], P('dev', 'sub'), may hold values from -0.0625 to 0.0625
Outputs:
- layer_output: bfloat16 [256, 3072], P(('rep', 'dev', 'sub')), parts along dimension 0
There are 2 independent parts, one for each index of `rep`. A program takes and returns all parts, laid end to end along the dimension named above; an argument that names none is the same for every part. Nothing has to cross between parts.
Inputs may be any that keep to these rules, and one draw needn't show every extreme that they name: `routes`: in each aligned block of 32 rows no expert is named by more than 26 rows, and some block reaches 26. `lengths`: some request's length is 128.
All inputs are finite; a program needn't handle non-finite values.
Results may differ from a plain program's by a relative error of at most 0.0059.
Values may be sent and summed in bfloat16 or wider, within the bound.
No kernel may reach another device: no remote copies, remote signals or barrier semaphores. Data moves between devices by JAX's collectives and lax.ppermute only.
A program may use at most 128 MiB of HBM per device.

v0:
```python
import math

import jax
import jax.numpy as jnp
from jax import lax
from jax.sharding import PartitionSpec as P

HEAD_SIZE = 128
QUERY_HEADS = 24
KEY_VALUE_HEADS = 4
EXPERTS = 4


def per_device(
    tokens,
    queries,
    request_key_cache,
    request_value_cache,
    lengths,
    norm_gain,
    router_weight,
    routes,
    gate_weight,
    up_weight,
    down_weight,
):
    token_count = tokens.shape[0]
    feat_width = tokens.shape[1]
    cache_length = request_key_cache.shape[1]
    device_group = QUERY_HEADS // KEY_VALUE_HEADS
    query_tensor_four = queries.reshape(token_count, KEY_VALUE_HEADS, device_group, HEAD_SIZE)
    key_tensor_four = request_key_cache.reshape(
        token_count, cache_length, KEY_VALUE_HEADS, HEAD_SIZE
    )
    value_tensor_four = request_value_cache.reshape(
        token_count, cache_length, KEY_VALUE_HEADS, HEAD_SIZE
    )
    scores = jnp.einsum(
        "thgd,tchd->thgc", query_tensor_four, key_tensor_four, preferred_element_type=jnp.float32
    ) * (1.0 / math.sqrt(HEAD_SIZE))
    in_cache = (jnp.arange(cache_length)[None, :] < lengths[:, None])[:, None, None, :]
    scores = jnp.where(in_cache, scores, -jnp.inf)
    peak_score = jnp.max(scores, axis=-1, keepdims=True)
    exp_scores = jnp.exp(scores - peak_score)
    weights_bf = (exp_scores / jnp.sum(exp_scores, axis=-1, keepdims=True)).astype(jnp.bfloat16)
    attended = jnp.einsum(
        "thgc,tchd->thgd", weights_bf, value_tensor_four, preferred_element_type=jnp.float32
    ).reshape(token_count, feat_width)
    resid = (tokens.astype(jnp.float32) + attended).astype(jnp.bfloat16)
    resid_f = resid.astype(jnp.float32)
    stats = jnp.mean(resid_f * resid_f, axis=-1, keepdims=True)
    normed = (resid_f * lax.rsqrt(stats + 1e-05) * norm_gain.astype(jnp.float32)).astype(
        jnp.bfloat16
    )
    logits = jnp.dot(normed, router_weight, preferred_element_type=jnp.float32)
    sub_index = lax.axis_index("sub")
    sub_count = lax.axis_size("sub")
    dev_count = lax.axis_size("dev")
    expert_ids = jnp.arange(EXPERTS)
    own_routes = lax.dynamic_slice_in_dim(routes, sub_index * token_count, token_count, 0)
    first_logit = jnp.sum(jnp.where(own_routes[:, 0:1] == expert_ids[None, :], logits, 0.0), axis=1)
    second_logit = jnp.sum(
        jnp.where(own_routes[:, 1:2] == expert_ids[None, :], logits, 0.0), axis=1
    )
    first_share = jax.nn.sigmoid(first_logit - second_logit)
    second_share = jax.nn.sigmoid(second_logit - first_logit)
    block_rows = lax.all_gather(normed, "sub", axis=0, tiled=True)
    block_len = token_count * sub_count
    capacity = 5 * block_len // 6
    group_size = dev_count // EXPERTS
    flat_ids = routes.reshape(-1)
    route_hot = (flat_ids[:, None] == expert_ids[None, :]).astype(jnp.int32)
    earlier = jnp.cumsum(route_hot, axis=0) - route_hot
    slot_number = jnp.sum(earlier * route_hot, axis=1)
    slot_index = (flat_ids * capacity + slot_number).reshape(block_len, 2)
    slot_range = jnp.arange(EXPERTS * capacity)
    place_matrix = jnp.any(slot_index[None, :, :] == slot_range[:, None, None], axis=-1).astype(
        jnp.bfloat16
    )
    slot_total = dev_count * capacity
    packed = jnp.dot(place_matrix, block_rows, preferred_element_type=jnp.float32).astype(
        jnp.bfloat16
    )
    outgoing = jnp.repeat(packed.reshape(EXPERTS, capacity, feat_width), group_size, axis=0)
    arrived = lax.all_to_all(outgoing, "dev", split_axis=0, concat_axis=0, tiled=True).reshape(
        slot_total, feat_width
    )
    gate_part = jnp.dot(arrived, gate_weight, preferred_element_type=jnp.float32)
    up_part = jnp.dot(arrived, up_weight, preferred_element_type=jnp.float32)
    hidden = (jax.nn.silu(gate_part) * up_part).astype(jnp.bfloat16)
    out_width = down_weight.shape[1]
    partial_out = jnp.dot(
        lax.all_gather(hidden, "sub", axis=1, tiled=True),
        down_weight,
        preferred_element_type=jnp.float32,
    )
    returned = lax.all_to_all(
        partial_out.reshape(dev_count, capacity, out_width),
        "dev",
        split_axis=0,
        concat_axis=0,
        tiled=True,
    )
    expert_out = jnp.sum(
        returned.reshape(EXPERTS, group_size, capacity, out_width), axis=1
    ).reshape(EXPERTS * capacity, out_width)
    pick_matrix = (slot_index.reshape(-1)[:, None] == slot_range[None, :]).astype(jnp.float32)
    per_route = jnp.dot(pick_matrix, expert_out, precision=lax.Precision.HIGHEST).reshape(
        block_len, 2, out_width
    )
    own_outputs = lax.all_to_all(per_route, "sub", split_axis=0, concat_axis=2, tiled=True)
    mixture = (
        first_share[:, None] * own_outputs[:, 0, :] + second_share[:, None] * own_outputs[:, 1, :]
    )
    return (resid_f + mixture).astype(jnp.bfloat16)


def solution(mesh):
    in_specs = (
        P(("rep", "dev", "sub"), None),
        P(("rep", "dev", "sub"), None),
        P(("rep", "dev", "sub"), None, None),
        P(("rep", "dev", "sub"), None, None),
        P(("rep", "dev", "sub")),
        P(),
        P(),
        P(("rep", "dev"), None),
        P(None, ("dev", "sub")),
        P(None, ("dev", "sub")),
        P("dev", "sub"),
    )
    out_specs = P(("rep", "dev", "sub"), None)
    return jax.shard_map(
        per_device, mesh=mesh, in_specs=in_specs, out_specs=out_specs, check_vma=False
    )
```

profile of v0, /device:TPU:0, one launch (start us, length us, event | category | flops | bytes accessed | tf_op | source)
XLA Modules:
  0.0 123.5 jit_solution(17499251519798478400)
XLA Ops:
  6.5 0.0 copy-start
  6.5 0.0 all-gather.2.cloned.1.call-start
  6.5 0.8 iota_compare_fusion.3
  7.4 0.7 convert_element_type.36
  8.0 0.8 copy.48
  8.8 0.1 eq.95
  8.9 0.1 fusion.19
  9.0 0.1 reduce_window_sum.11
  9.1 0.2 select_reduce_fusion
  9.3 0.1 reduce_sum.56
  9.4 0.1 copy.49
  9.5 0.7 multiply_add_fusion
  10.2 0.1 fusion.23
  10.2 0.0 copy-done
  10.3 1.4 %fusion.4 = f32[8,4,6,128]{3,2,1,0:T(8,128)S(1)} fusion(bf16[8,4,6,128]{3,0,2,1:T(8,128)(2,1)} %bitcast.55, pred[8,128]{1,0:T(8,128)(4,1)S(1)} %iota_compare_fusion.3, bf16[8,128,512]{2,1,0:T(8,128)(2,1)S(1)} %copy-done), kind=kOutput, calls=%fused_computation.7 | convolution fusion | flops 6340608 | bytes 1197056 | tf_op jit(solution)/shard_map/thgd,tchd->thgc/dot_general | solution.py:38
  11.7 0.2 fusion.25
  11.9 1.8 %fusion.5 = f32[8,4,6,128]{3,2,1,0:T(8,128)S(1)} fusion(f32[8,4,6]{2,1,0:T(4,128)S(1)} %fusion.25, f32[8,4,6,128]{3,2,1,0:T(8,128)S(1)} %fusion.4, bf16[8,128,512]{2,1,0:T(8,128)(2,1)} %param.14), kind=kOutput, calls=%fused_computation.8 | convolution fusion | flops 6365503 | bytes 1245952 | tf_op jit(solution)/shard_map/thgc,tchd->thgd/dot_general | solution.py:46
  13.8 0.9 fusion.10
  14.7 0.1 fusion.12
  14.8 6.8 %all_gather.6 = bf16[32,3072]{1,0:T(8,128)(2,1)S(1)} all-gather(bf16[8,3072]{1,0:T(8,128)(2,1)S(1)} %fusion.12), channel_id=1, replica_groups=mesh['rep'=2,'dev'=4,'sub'=4] {'sub'}, dimensions={0}, use_global_device_ids=true | all-gather | bytes 245760 | tf_op jit(solution)/shard_map/all_gather | solution.py:67
  21.7 0.4 convolution_convert_fusion
  22.0 0.2 reshape_broadcast_in_dim_reshape.3
  22.2 25.5 %all_to_all.28 = bf16[4,26,3072]{2,1,0:T(8,128)(2,1)S(1)} all-to-all(bf16[4,26,3072]{2,1,0:T(8,128)(2,1)S(1)} %reshape_broadcast_in_dim_reshape.3), channel_id=1, replica_groups=mesh['rep'=2,'dev'=4,'sub'=4] {'dev'}, dimensions={0} | all-to-all | bytes 1277952 | tf_op jit(solution)/shard_map/all_to_all | solution.py:85
  47.7 0.2 reshape.115
  47.9 6.5 %fusion.26 = f32[104,2048]{1,0:T(8,128)S(1)} fusion(bf16[104,3072]{1,0:T(8,128)(2,1)S(1)} %reshape.115, bf16[3072,2048]{1,0:T(8,128)(2,1)} %param.19), kind=kOutput, calls=%fused_computation.51 | convolution fusion | flops 1308622848 | bytes 14073856 | tf_op jit(solution)/shard_map/dot_general | solution.py:88
  54.5 7.4 %fusion.1 = bf16[104,2048]{1,0:T(8,128)(2,1)} fusion(bf16[104,3072]{1,0:T(8,128)(2,1)S(1)} %reshape.115, bf16[3072,2048]{1,0:T(8,128)(2,1)} %param.20, f32[104,2048]{1,0:T(8,128)S(1)} %fusion.26), kind=kOutput, calls=%fused_computation.3 | convolution fusion | flops 1309900800 | bytes 14499840 | tf_op jit(solution)/shard_map/dot_general | solution.py:89
  61.9 0.0 copy-start.1
  61.9 0.0 copy-start.2
  61.9 0.0 all-gather.2.cloned.1.call-update
  61.9 19.6 %all-gather.2.cloned.1.call-done = bf16[104,8192]{1,0:T(8,128)(2,1)} async-done(((bf16[104,2048]{1,0:T(8,128)(2,1)}), bf16[104,8192]{1,0:T(8,128)(2,1)}) %all-gather.2.cloned.1.call-update) | async-done | bytes 1703952 | tf_op jit(solution)/shard_map/all_gather | solution.py:93
  81.5 7.1 %fusion.27 = f32[104,768]{1,0:T(8,128)S(1)} fusion(bf16[104,8192]{1,0:T(8,128)(2,1)} %all-gather.2.cloned.1.call-done, bf16[8192,768]{1,0:T(8,128)(2,1)} %param.21), kind=kOutput, calls=%fused_computation.52 | convolution fusion | flops 1308622848 | bytes 14606336 | tf_op jit(solution)/shard_map/dot_general | solution.py:92
  88.6 0.8 reshape.116
  89.4 4.6 %all-to-all-start.1 = ((f32[4,26,768]{2,1,0:T(8,128)}), f32[4,26,768]{2,1,0:T(8,128)S(1)}, u32[]{:S(2)}, u32[]{:S(2)}) async-start(f32[4,26,768]{2,1,0:T(8,128)} %reshape.116), calls=%async_computation.1 | async-start | bytes 786432 | tf_op jit(solution)/shard_map/all_to_all | solution.py:97
  94.0 0.0 copy-done.1
  94.0 0.1 constant_dynamic-slice_fusion
  94.1 0.0 copy-done.2
  94.1 0.2 select_reduce_fusion.2
  94.2 11.9 %all-to-all-done.1 = f32[4,26,768]{2,1,0:T(8,128)S(1)} async-done(((f32[4,26,768]{2,1,0:T(8,128)}), f32[4,26,768]{2,1,0:T(8,128)S(1)}, u32[]{:S(2)}, u32[]{:S(2)}) %all-to-all-start.1) | async-done | bytes 319520 | tf_op jit(solution)/shard_map/all_to_all | solution.py:97
  106.1 0.3 fusion.21
  106.4 0.8 copy.50
  107.3 3.4 %all-to-all-start.2 = ((f32[32,2,768]{2,1,0:T(2,128)}), f32[32,2,768]{2,1,0:T(2,128)S(1)}, u32[]{:S(2)}, u32[]{:S(2)}) async-start(f32[32,2,768]{2,1,0:T(2,128)} %copy.50), calls=%async_computation.2 | async-start | bytes 393216 | tf_op jit(solution)/shard_map/all_to_all | solution.py:111
  110.6 5.3 %all-to-all-done.2 = f32[32,2,768]{2,1,0:T(2,128)S(1)} async-done(((f32[32,2,768]{2,1,0:T(2,128)}), f32[32,2,768]{2,1,0:T(2,128)S(1)}, u32[]{:S(2)}, u32[]{:S(2)}) %all-to-all-start.2) | async-done | bytes 196640 | tf_op jit(solution)/shard_map/all_to_all | solution.py:111
  115.9 0.7 fusion.13
  (6 shorter events, 0.1 us)
Async XLA Ops:
  6.5 3.7 %copy-start = (bf16[8,128,512]{2,1,0:T(8,128)(2,1)S(1)}, bf16[8,128,512]{2,1,0:T(8,128)(2,1)}, u32[]{:S(2)}) copy-start(bf16[8,128,512]{2,1,0:T(8,128)(2,1)} %param.13) | copy-start | bytes 3145732
  6.5 75.0 %all-gather.2.cloned.1.call-start = ((), (), s32[]{:S(2)}) async-start(), calls=%async_computation.3 | async-start | bytes 2129920 | tf_op jit(solution)/shard_map/all_gather | solution.py:93
  61.9 32.1 %copy-start.1 = (s32[32,2]{0,1:T(2,128)S(1)}, s32[32,2]{0,1:T(2,128)}, u32[]{:S(2)}) copy-start(s32[32,2]{0,1:T(2,128)} %param.18) | copy-start | bytes 772
  61.9 32.2 %copy-start.2 = (bf16[3072,4]{0,1:T(4,128)(2,1)S(1)}, bf16[3072,4]{0,1:T(4,128)(2,1)}, u32[]{:S(2)}) copy-start(bf16[3072,4]{0,1:T(4,128)(2,1)} %param.17) | copy-start | bytes 73732
  89.4 16.7 %all-to-all-start.1 = ((f32[4,26,768]{2,1,0:T(8,128)}), f32[4,26,768]{2,1,0:T(8,128)S(1)}, u32[]{:S(2)}, u32[]{:S(2)}) async-start(f32[4,26,768]{2,1,0:T(8,128)} %reshape.116), calls=%async_computation.1 | async-start | bytes 786432 | tf_op jit(solution)/shard_map/all_to_all | solution.py:97
  107.3 8.7 %all-to-all-start.2 = ((f32[32,2,768]{2,1,0:T(2,128)}), f32[32,2,768]{2,1,0:T(2,128)S(1)}, u32[]{:S(2)}, u32[]{:S(2)}) async-start(f32[32,2,768]{2,1,0:T(2,128)} %copy.50), calls=%async_computation.2 | async-start | bytes 393216 | tf_op jit(solution)/shard_map/all_to_all | solution.py:111
Sparse Core Ops, SparseCore 0:
  62.0 19.4 all-gather.1
where the time goes:
time: 124 us
  waiting for transfers between devices  36.8 us (30%)
  blocking collectives  32.3 us (26%)
  matrix products  25.1 us (20%)
  between operations  13.5 us (11%)
  starting transfers between devices  7.96 us (6%)
  other arithmetic  4.62 us (4%)
  local copies, waits for them, and re-layouts  3.21 us (3%)
    all_to_all x1, blocking collectives, per_device(): lax.all_to_all(outgoing, 'dev', split_axis=0, concat_axis=0, tiled=True)  25.5 us
    all_gather x1, waiting for transfers between devices, per_device(): lax.all_gather(hidden, 'sub', axis=1, tiled=True)  19.6 us
    all_to_all x1, waiting for transfers between devices, per_device(): lax.all_to_all(partial_out.reshape(dev_count, capacity, out_width), 'dev'...  11.9 us
    dot_general x1, matrix products, per_device(): up_part = jnp.dot(arrived, up_weight, preferred_element_type=jnp.float32)  7.39 us
    dot_general x1, matrix products, per_device(): jnp.dot(lax.all_gather(hidden, 'sub', axis=1, tiled=True), down_weight, p...  7.08 us
    all_gather x1, blocking collectives, per_device(): block_rows = lax.all_gather(normed, 'sub', axis=0, tiled=True)  6.84 us
    dot_general x1, matrix products, per_device(): jnp.dot(arrived, gate_weight, preferred_element_type=jnp.float32)  6.54 us
    all_to_all x1, waiting for transfers between devices, per_device(): lax.all_to_all(per_route, 'sub', split_axis=0, concat_axis=2, tiled=True)  5.28 us
  transfers between devices with their start and end apart: 3, of which 3 were waited for; matrix products, arithmetic and copies ran while one was open for 0% of the time, Pallas kernels for 0%

commit v1 on v0

--- a/solution.py
+++ b/solution.py
@@ -3,6 +3,8 @@
 import jax
 import jax.numpy as jnp
 from jax import lax
+from jax.experimental import pallas as pl
+from jax.experimental.pallas import tpu as pltpu
 from jax.sharding import PartitionSpec as P
 
 HEAD_SIZE = 128
@@ -11,7 +13,7 @@
 EXPERTS = 4
 
 
-def per_device(
+def general_plan(
     tokens,
     queries,
     request_key_cache,
@@ -115,6 +117,331 @@
     return (resid_f + mixture).astype(jnp.bfloat16)
 
 
+VMEM_SPEC = pl.BlockSpec(memory_space=pltpu.VMEM)
+SMEM_SPEC = pl.BlockSpec(memory_space=pltpu.SMEM)
+MIB = 1024 * 1024
+EXTRA = 128
+
+
+def call(body, out_shapes, operands, specs, flops, vmem, scratch=(), bytes_accessed=0):
+    return pl.pallas_call(
+        body,
+        out_shape=out_shapes,
+        in_specs=specs,
+        out_specs=jax.tree.map(lambda _: VMEM_SPEC, out_shapes),
+        scratch_shapes=list(scratch),
+        compiler_params=pltpu.CompilerParams(vmem_limit_bytes=vmem),
+        cost_estimate=pl.CostEstimate(
+            flops=flops, bytes_accessed=bytes_accessed, transcendentals=0
+        ),
+    )(*operands)
+
+
+def dot(a, b):
+    return jnp.dot(a, b, preferred_element_type=jnp.float32)
+
+
+def dot_nt(a, b):
+    return lax.dot_general(a, b, (((1,), (1,)), ((), ())), preferred_element_type=jnp.float32)
+
+
+def attention_kernel(
+    lengths_ref,
+    routes_ref,
+    tokens_ref,
+    queries_ref,
+    keys_ref,
+    values_ref,
+    gain_ref,
+    router_ref,
+    payload_ref,
+    resid_ref,
+    att_ref,
+):
+    rows, width = tokens_ref.shape
+    cache = keys_ref.shape[1]
+    group = QUERY_HEADS // KEY_VALUE_HEADS
+    row = lax.broadcasted_iota(jnp.int32, (rows, 1), 0)
+    live = jnp.zeros((rows, 1), jnp.int32)
+    first = jnp.zeros((rows, 1), jnp.int32)
+    second = jnp.zeros((rows, 1), jnp.int32)
+    base = lax.axis_index("sub") * rows
+    for t in range(rows):
+        live = jnp.where(row == t, lengths_ref[t], live)
+        first = jnp.where(row == t, routes_ref[0, base + t], first)
+        second = jnp.where(row == t, routes_ref[1, base + t], second)
+    column = lax.broadcasted_iota(jnp.int32, (rows, rows * cache), 1)
+    start = row * cache
+    in_cache = (column >= start) & (column < start + live)
+    in_cache = jnp.concatenate([in_cache.astype(jnp.int32)] * group, axis=0) > 0
+    scale = 1.0 / math.sqrt(HEAD_SIZE)
+    for kv in range(KEY_VALUE_HEADS):
+        heads = [queries_ref[:, h * HEAD_SIZE : (h + 1) * HEAD_SIZE].astype(jnp.float32)
+                 for h in range(kv * group, (kv + 1) * group)]
+        query = jnp.concatenate(heads, axis=0).astype(jnp.bfloat16)
+        lanes = slice(kv * HEAD_SIZE, (kv + 1) * HEAD_SIZE)
+        key = keys_ref[:, :, lanes].reshape(rows * cache, HEAD_SIZE)
+        value = values_ref[:, :, lanes].reshape(rows * cache, HEAD_SIZE)
+        scores = jnp.where(in_cache, dot_nt(query, key) * scale, -jnp.inf)
+        exp_scores = jnp.exp(scores - jnp.max(scores, axis=1, keepdims=True))
+        total = jnp.sum(exp_scores, axis=1, keepdims=True)
+        probs = (exp_scores * (1.0 / total)).astype(jnp.bfloat16)
+        attended = dot(probs, value)
+        for g in range(group):
+            h = kv * group + g
+            att_ref[:, h * HEAD_SIZE : (h + 1) * HEAD_SIZE] = attended[g * rows : (g + 1) * rows]
+    resid = (tokens_ref[...].astype(jnp.float32) + att_ref[...]).astype(jnp.bfloat16)
+    resid_ref[...] = resid
+    resid_f = resid.astype(jnp.float32)
+    stats = jnp.sum(resid_f * resid_f, axis=1, keepdims=True) * (1.0 / width)
+    gain = gain_ref[...].astype(jnp.float32).reshape(1, width)
+    normed = (resid_f * lax.rsqrt(stats + 1e-05) * gain).astype(jnp.bfloat16)
+    payload_ref[:, :width] = normed
+    logits = dot_nt(normed, router_ref[...])
+    expert = lax.broadcasted_iota(jnp.int32, (rows, EXPERTS), 1)
+    first_logit = jnp.sum(jnp.where(first == expert, logits, 0.0), axis=1, keepdims=True)
+    second_logit = jnp.sum(jnp.where(second == expert, logits, 0.0), axis=1, keepdims=True)
+    first_share = 1.0 / (1.0 + jnp.exp(second_logit - first_logit))
+    second_share = 1.0 / (1.0 + jnp.exp(first_logit - second_logit))
+    lane = lax.broadcasted_iota(jnp.int32, (rows, EXTRA), 1)
+    place = lane % EXPERTS
+    routed = ((first == place) | (second == place)).astype(jnp.float32)
+    share = jnp.where(first == place, first_share, 0.0) + jnp.where(second == place, second_share, 0.0)
+    high = share.astype(jnp.bfloat16).astype(jnp.float32)
+    low = share - high
+    extra = jnp.where(
+        lane < EXPERTS,
+        routed,
+        jnp.where(lane < 2 * EXPERTS, high, jnp.where(lane < 3 * EXPERTS, low, 0.0)),
+    )
+    payload_ref[:, width:] = extra.astype(jnp.bfloat16)
+
+
+def own_offset(rows):
+    return (lax.axis_index("dev") * lax.axis_size("sub") + lax.axis_index("sub")) * rows
+
+
+def slot_matrix(extra, offset):
+    count = extra.shape[0]
+    here = lax.broadcasted_iota(jnp.int32, (count, count), 0) ^ offset
+    there = lax.broadcasted_iota(jnp.int32, (count, count), 1) ^ offset
+    earlier = dot((there < here).astype(jnp.bfloat16), extra)
+    lane = lax.broadcasted_iota(jnp.int32, (count, EXTRA), 1)
+    mine = lane == lax.axis_index("dev")
+    rank = jnp.sum(jnp.where(mine, earlier, 0.0), axis=1, keepdims=True)
+    routed = jnp.sum(jnp.where(mine, extra.astype(jnp.float32), 0.0), axis=1, keepdims=True)
+    slot = jnp.where(routed > 0.5, rank, -1.0).astype(jnp.int32)
+    return (slot == lax.broadcasted_iota(jnp.int32, (count, count), 1)).astype(jnp.float32)
+
+
+def hidden_columns(x, gate_ref, up_ref, out_ref, begin):
+    step = 256
+    for j in range(0, out_ref.shape[1], step):
+        gate = dot(x, gate_ref[:, begin + j : begin + j + step])
+        up = dot(x, up_ref[:, begin + j : begin + j + step])
+        out_ref[:, j : j + step] = (gate / (1.0 + jnp.exp(-gate)) * up).astype(jnp.bfloat16)
+
+
+def first_hidden_kernel(pieces, slots, *refs):
+    piece_refs = refs[:pieces]
+    gate_ref, up_ref, x_ref, extra_ref, hidden_ref, rows_ref = refs[pieces:]
+    width = x_ref.shape[1]
+    at = 0
+    for first, second in zip(piece_refs[0::2], piece_refs[1::2], strict=True):
+        both = [first[...].astype(jnp.float32), second[...].astype(jnp.float32)]
+        size = first.shape[0] + second.shape[0]
+        rows_ref[at : at + size, :] = jnp.concatenate(both, axis=0).astype(jnp.bfloat16)
+        at += size
+    extra = rows_ref[:, width:]
+    extra_ref[...] = extra
+    rows = piece_refs[0].shape[0]
+    place = slot_matrix(extra, own_offset(rows)).T[:slots].astype(jnp.bfloat16)
+    x_ref[...] = dot(place, rows_ref[:, :width]).astype(jnp.bfloat16)
+    hidden_columns(x_ref[...], gate_ref, up_ref, hidden_ref, 0)
+
+
+def next_hidden_kernel(begin, x_ref, gate_ref, up_ref, hidden_ref):
+    hidden_columns(x_ref[...], gate_ref, up_ref, hidden_ref, begin)
+
+
+def down_part(sources, down_ref, own_width):
+    sub = lax.axis_index("sub")
+    total = None
+    for hidden_ref, flip, begin in sources:
+        height = hidden_ref.shape[1]
+        at = pl.multiple_of((sub ^ flip) * own_width + begin, 256)
+        part = dot(hidden_ref[...], down_ref[pl.ds(at, height), :])
+        total = part if total is None else total + part
+    return total
+
+
+def down_kernel(flips, own_width, has_total, *refs):
+    count = len(flips)
+    hidden_refs = refs[:count]
+    rest = refs[count:]
+    sources = [(r, f, b) for r, (f, b) in zip(hidden_refs, flips, strict=True)]
+    total = down_part(sources, rest[0], own_width)
+    if has_total:
+        total = total + rest[1][...]
+    rest[-1][...] = total
+
+
+def last_down_kernel(flips, own_width, rows, *refs):
+    count = len(flips)
+    hidden_refs = refs[:count]
+    down_ref, total_ref, extra_ref, out_ref = refs[count:]
+    sources = [(r, f, b) for r, (f, b) in zip(hidden_refs, flips, strict=True)]
+    slots = total_ref.shape[0]
+    offset = own_offset(rows)
+    extra = extra_ref[...]
+    tokens = extra.shape[0]
+    here = slot_matrix(extra, offset)
+    lane = lax.broadcasted_iota(jnp.int32, (tokens, EXTRA), 1)
+    dev = lax.axis_index("dev")
+    mine = (lane == EXPERTS + dev) | (lane == 2 * EXPERTS + dev)
+    shares = jnp.where(mine, extra.astype(jnp.float32), 0.0).astype(jnp.bfloat16)
+    by_slot = dot(here.T[:slots].astype(jnp.bfloat16), shares)
+    share = jnp.sum(by_slot, axis=1, keepdims=True)
+    token = lax.broadcasted_iota(jnp.int32, (tokens, tokens), 0)
+    moved = (token ^ offset) == lax.broadcasted_iota(jnp.int32, (tokens, tokens), 1)
+    spread = dot(moved.astype(jnp.bfloat16), here.astype(jnp.bfloat16)).astype(jnp.bfloat16)
+    total = total_ref[...] + down_part(sources, down_ref, own_width)
+    out_ref[...] = dot(spread[:, :slots], (total * share).astype(jnp.bfloat16)).astype(jnp.bfloat16)
+
+
+def finish_kernel(resid_ref, arrived_ref, out_ref):
+    subs, devs = lax.axis_size("sub"), lax.axis_size("dev")
+    width = arrived_ref.shape[2]
+    for s in range(subs):
+        lanes = slice(s * width, (s + 1) * width)
+        mixture = arrived_ref[s].astype(jnp.float32)
+        for d in range(1, devs):
+            mixture = mixture + arrived_ref[d * subs + s].astype(jnp.float32)
+        out_ref[:, lanes] = (resid_ref[:, lanes].astype(jnp.float32) + mixture).astype(jnp.bfloat16)
+
+
+def flip(x, axis, bits):
+    return lax.ppermute(x, axis, [(i, i ^ bits) for i in range(lax.axis_size(axis))])
+
+
+def per_device(
+    tokens,
+    queries,
+    request_key_cache,
+    request_value_cache,
+    lengths,
+    norm_gain,
+    router_weight,
+    routes,
+    gate_weight,
+    up_weight,
+    down_weight,
+):
+    rows, width = tokens.shape
+    devs, subs = lax.axis_size("dev"), lax.axis_size("sub")
+    all_rows = rows * devs * subs
+    slots = devs * (5 * rows * subs // 6)
+    own_hidden = gate_weight.shape[1]
+    out_width = down_weight.shape[1]
+    bf16 = jnp.bfloat16
+    payload, resid = call(
+        attention_kernel,
+        (
+            jax.ShapeDtypeStruct((rows, width + EXTRA), bf16),
+            jax.ShapeDtypeStruct((rows, width), bf16),
+        ),
+        (
+            lengths,
+            routes.T,
+            tokens,
+            queries,
+            request_key_cache,
+            request_value_cache,
+            norm_gain,
+            router_weight.T,
+        ),
+        [SMEM_SPEC, SMEM_SPEC] + [VMEM_SPEC] * 6,
+        flops=30 * 10**9,
+        bytes_accessed=100 * MIB,
+        vmem=8 * MIB,
+        scratch=[pltpu.VMEM((rows, width), jnp.float32)],
+    )
+    over_z = [payload] + [flip(payload, "dev", k) for k in (1, 2, 3)]
+    over_x = [flip(p, "sub", 2) for p in over_z]
+    over_core = [[flip(p, "sub", 1) for p in group] for group in (over_z, over_x)]
+    pieces = []
+    for k in range(devs):
+        pieces += [over_z[k], over_core[0][k], over_x[k], over_core[1][k]]
+    half = own_hidden // 2
+    x, extra, hidden_a = call(
+        lambda *refs: first_hidden_kernel(len(pieces), slots, *refs),
+        (
+            jax.ShapeDtypeStruct((slots, width), bf16),
+            jax.ShapeDtypeStruct((all_rows, EXTRA), bf16),
+            jax.ShapeDtypeStruct((slots, half), bf16),
+        ),
+        (*pieces, gate_weight, up_weight),
+        [VMEM_SPEC] * (len(pieces) + 2),
+        flops=2 * 10**9,
+        vmem=6 * MIB,
+        scratch=[pltpu.VMEM((all_rows, width + EXTRA), bf16)],
+    )
+    hidden_b = call(
+        lambda *refs: next_hidden_kernel(half, *refs),
+        jax.ShapeDtypeStruct((slots, own_hidden - half), bf16),
+        (x, gate_weight, up_weight),
+        [VMEM_SPEC] * 3,
+        flops=2 * 10**9,
+        vmem=4 * MIB,
+    )
+    far_a, near_a = flip(hidden_a, "sub", 2), flip(hidden_a, "sub", 1)
+    far_b, near_b = flip(hidden_b, "sub", 2), flip(hidden_b, "sub", 1)
+    across_a, across_b = flip(far_a, "sub", 1), flip(far_b, "sub", 1)
+    total_shape = jax.ShapeDtypeStruct((slots, out_width), jnp.float32)
+    flips = ((0, 0), (0, half), (1, 0), (1, half))
+    total = call(
+        lambda *refs: down_kernel(flips, own_hidden, False, *refs),
+        total_shape,
+        (hidden_a, hidden_b, near_a, near_b, down_weight),
+        [VMEM_SPEC] * 5,
+        flops=10**9,
+        vmem=4 * MIB,
+    )
+    flips_a = ((2, 0), (3, 0))
+    total = call(
+        lambda *refs: down_kernel(flips_a, own_hidden, True, *refs),
+        total_shape,
+        (far_a, across_a, down_weight, total),
+        [VMEM_SPEC] * 4,
+        flops=10**9,
+        vmem=4 * MIB,
+    )
+    flips_b = ((2, half), (3, half))
+    weighted = call(
+        lambda *refs: last_down_kernel(flips_b, own_hidden, rows, *refs),
+        jax.ShapeDtypeStruct((all_rows, out_width), bf16),
+        (far_b, across_b, down_weight, total, extra),
+        [VMEM_SPEC] * 5,
+        flops=10**9,
+        vmem=4 * MIB,
+    )
+    arrived = lax.all_to_all(
+        weighted.reshape(devs * subs, rows, out_width),
+        ("dev", "sub"),
+        split_axis=0,
+        concat_axis=0,
+        tiled=True,
+    )
+    return call(
+        finish_kernel,
+        jax.ShapeDtypeStruct((rows, width), bf16),
+        (resid, arrived),
+        [VMEM_SPEC] * 2,
+        flops=10**6,
+        vmem=4 * MIB,
+    )
+
+
 def solution(mesh):
     in_specs = (
         P(("rep", "dev", "sub"), None),
@@ -130,6 +457,11 @@
         P("dev", "sub"),
     )
     out_specs = P(("rep", "dev", "sub"), None)
+    one_expert_each = mesh.shape["dev"] == EXPERTS and mesh.shape["sub"] == 4
     return jax.shard_map(
-        per_device, mesh=mesh, in_specs=in_specs, out_specs=out_specs, check_vma=False
-    )
+        per_device if one_expert_each else general_plan,
+        mesh=mesh,
+        in_specs=in_specs,
+        out_specs=out_specs,
+        check_vma=False,
+    )

time: 124 us -> 58.8 us (0.47)
  matrix products: 25.1 us -> 0 us
  waiting for transfers between devices: 36.8 us -> 11.9 us
  blocking collectives: 32.3 us -> 13.5 us
  between operations: 13.5 us -> 0.15 us
  Pallas kernels: 0 us -> 10.8 us
  starting transfers between devices: 7.96 us -> 15.2 us
  other arithmetic: 4.62 us -> 0.01 us
  local copies, waits for them, and re-layouts: 3.21 us -> 6.82 us
    dot_general x8 -> x0, matrix products: 25.1 us -> none  [the longest x1 7.39 us: per_device(): up_part = jnp.dot(arrived, up_weight, preferred_element_type=jnp.float32)]
    all_gather x1 -> x0, waiting for transfers between devices: 19.6 us -> none  [per_device(): lax.all_gather(hidden, 'sub', axis=1, tiled=True)]
    all_to_all x2 -> x0, waiting for transfers between devices: 17.1 us -> none  [the longest x1 11.9 us: per_device(): lax.all_to_all(partial_out.reshape(dev_count, capacity, out_width), 'dev'...]
    ppermute x0 -> x21, starting transfers between devices: none -> 15.2 us  [flip(): lax.ppermute(x, axis, [(i, i ^ bits) for i in range(lax.axis_size(axis))])]
    all_to_all x1, blocking collectives: 25.5 us -> 13.5 us  [per_device(): lax.all_to_all(weighted.reshape(devs * subs, rows, out_width), ('dev', 's...]
    ppermute x0 -> x21, waiting for transfers between devices: none -> 11.9 us  [flip(): lax.ppermute(x, axis, [(i, i ^ bits) for i in range(lax.axis_size(axis))])]
    pallas_call x0 -> x7, Pallas kernels: none -> 10.8 us  [call(): pl.pallas_call(body, out_shape=out_shapes, in_specs=specs, out_specs=jax....]
    all_to_all x2 -> x0, starting transfers between devices: 7.96 us -> none  [the longest x1 4.6 us: per_device(): lax.all_to_all(partial_out.reshape(dev_count, capacity, out_width), 'dev'...]
  transfers between devices with their start and end apart: 3 -> 21, of which waited for: 3 -> 6; matrix products, arithmetic and copies ran while one was open for 0% -> 0% of each run, Pallas kernels for 0% -> 7%
where the time goes in v1:
time: 58.8 us; the launch traced here: 58.3 us
  starting transfers between devices  15.2 us (26%)
  blocking collectives  13.5 us (23%)
  waiting for transfers between devices  11.9 us (20%)
  Pallas kernels  10.8 us (18%)
  local copies, waits for them, and re-layouts  6.82 us (12%)
    ppermute x21, starting transfers between devices, flip(): lax.ppermute(x, axis, [(i, i ^ bits) for i in range(lax.axis_size(axis))])  15.2 us
    all_to_all x1, blocking collectives, per_device(): lax.all_to_all(weighted.reshape(devs * subs, rows, out_width), ('dev', 's...  13.5 us
    ppermute x21, waiting for transfers between devices, flip(): lax.ppermute(x, axis, [(i, i ^ bits) for i in range(lax.axis_size(axis))])  11.9 us
    pallas_call x7, Pallas kernels, call(): pl.pallas_call(body, out_shape=out_shapes, in_specs=specs, out_specs=jax....  10.8 us
    unnamed x26, local copies, waits for them, and re-layouts  6.82 us
  transfers between devices with their start and end apart: 21, of which 6 were waited for; matrix products, arithmetic and copies ran while one was open for 0% of the time, Pallas kernels for 7%

profile of v1, /device:TPU:0, one launch (start us, length us, event | category | flops | bytes accessed | tf_op | source)
XLA Modules:
  0.0 58.3 jit_solution(17548916571213814555)
XLA Ops:
  0.0 1.2 %copy-done.2 = bf16[8,128,512]{2,1,0:T(8,128)(2,1)S(1)} copy-done((bf16[8,128,512]{2,1,0:T(8,128)(2,1)S(1)}, bf16[8,128,512]{2,1,0:T(8,128)(2,1)}, u32[]{:S(2)}) %copy-start.2) | copy-done | bytes 1048600
  1.2 1.2 %copy-done.3 = bf16[8,128,512]{2,1,0:T(8,128)(2,1)S(1)} copy-done((bf16[8,128,512]{2,1,0:T(8,128)(2,1)S(1)}, bf16[8,128,512]{2,1,0:T(8,128)(2,1)}, u32[]{:S(2)}) %copy-start.3) | copy-done | bytes 1048600
  2.5 0.8 %copy-done.4 = bf16[8,3072]{1,0:T(8,128)(2,1)S(1)} copy-done((bf16[8,3072]{1,0:T(8,128)(2,1)S(1)}, bf16[8,3072]{1,0:T(8,128)(2,1)}, u32[]{:S(2)}) %copy-start.4) | copy-done | bytes 49176
  3.3 0.8 %copy-done.5 = bf16[8,3072]{1,0:T(8,128)(2,1)S(1)} copy-done((bf16[8,3072]{1,0:T(8,128)(2,1)S(1)}, bf16[8,3072]{1,0:T(8,128)(2,1)}, u32[]{:S(2)}) %copy-start.5) | copy-done | bytes 49176
  4.1 0.7 %copy-done.6 = bf16[3072,4]{0,1:T(4,128)(2,1)S(1)} copy-done((bf16[3072,4]{0,1:T(4,128)(2,1)S(1)}, bf16[3072,4]{0,1:T(4,128)(2,1)}, u32[]{:S(2)}) %copy-start.6) | copy-done | bytes 24600
  4.8 0.7 %copy-done.7 = bf16[3072]{0:T(1024)(128)(2,1)S(1)} copy-done((bf16[3072]{0:T(1024)(128)(2,1)S(1)}, bf16[3072]{0:T(1024)(128)(2,1)}, u32[]{:S(2)}) %copy-start.7) | copy-done | bytes 6168
  5.5 0.7 %copy-done.8 = s32[32,2]{0,1:T(2,128)S(1)} copy-done((s32[32,2]{0,1:T(2,128)S(1)}, s32[32,2]{0,1:T(2,128)}, u32[]{:S(2)}) %copy-start.8) | copy-done | bytes 280
  6.2 0.7 %copy-done.9 = s32[8]{0:T(128)S(1)} copy-done((s32[8]{0:T(128)S(1)}, s32[8]{0:T(128)}, u32[]{:S(2)}) %copy-start.9) | copy-done | bytes 56
  6.8 2.7 %shard_map.109 = (bf16[8,3200]{1,0:T(8,128)(2,1)S(1)}, bf16[8,3072]{1,0:T(8,128)(2,1)S(1)}) custom-call(s32[8]{0:T(128)S(1)} %copy-done.9, s32[2,32]{1,0:T(2,128)S(1)} %bitcast.7, bf16[8,3072]{1,0:T(8,128)(2,1)S(1)} %copy-done.4, bf16[8,3072]{1,0:T(8,128)(2,1)S(1)} %copy-done.5, bf16[8,128,512]{2,1,0:T(8,128)(2,1)S(1)} %copy-done.2, ...), custom_call_target="tpu_custom_call" | custom-call | flops 30000001024 | bytes 104857600 | tf_op jit(solution)/shard_map/pallas_call | solution.py:127
  9.6 5.1 %collective-permute-start.11 = (bf16[8,3200]{1,0:T(8,128)(2,1)S(1)}, bf16[8,3200]{1,0:T(8,128)(2,1)S(1)}, u32[]{:S(2)}, u32[]{:S(2)}) collective-permute-start(bf16[8,3200]{1,0:T(8,128)(2,1)S(1)} %get-tuple-element.11.refs_0_), channel_id=1, source_target_pairs={{0,12},{4,8},{8,4},{12,0},{1,13},{5,9},{9,5},{13,1},{2,14},{6,10},... | collective-permute-start | bytes 153608 | tf_op jit(solution)/shard_map/ppermute | solution.py:324
  14.7 0.0 collective-permute-start.7
  14.7 0.6 %collective-permute-start.3 = (bf16[8,3200]{1,0:T(8,128)(2,1)S(1)}, bf16[8,3200]{1,0:T(8,128)(2,1)S(1)}, u32[]{:S(2)}, u32[]{:S(2)}) collective-permute-start(bf16[8,3200]{1,0:T(8,128)(2,1)S(1)} %get-tuple-element.11.refs_0_), channel_id=1, source_target_pairs={{0,4},{4,0},{8,12},{12,8},{1,5},{5,1},{9,13},{13,9},{2,6},{6,2},{1... | collective-permute-start | bytes 153608 | tf_op jit(solution)/shard_map/ppermute | solution.py:324
  15.3 1.6 %collective-permute-start.1 = (bf16[8,3200]{1,0:T(8,128)(2,1)S(1)}, bf16[8,3200]{1,0:T(8,128)(2,1)S(1)}, u32[]{:S(2)}, u32[]{:S(2)}) collective-permute-start(bf16[8,3200]{1,0:T(8,128)(2,1)S(1)} %get-tuple-element.11.refs_0_), channel_id=1, source_target_pairs={{0,2},{1,3},{2,0},{3,1},{4,6},{5,7},{6,4},{7,5},{8,10},{9,11},{10,... | collective-permute-start | bytes 153608 | tf_op jit(solution)/shard_map/ppermute | solution.py:324
  17.0 0.0 collective-permute-start
  17.0 0.0 collective-permute-done.11.refs_12_
  17.0 1.8 %collective-permute-start.13 = (bf16[8,3200]{1,0:T(8,128)(2,1)S(1)}, bf16[8,3200]{1,0:T(8,128)(2,1)S(1)}, u32[]{:S(2)}, u32[]{:S(2)}) collective-permute-start(bf16[8,3200]{1,0:T(8,128)(2,1)S(1)} %collective-permute-done.11.refs_12_), channel_id=1, source_target_pairs={{0,2},{1,3},{2,0},{3,1},{4,6},{5,7},{6,4},{7,5},{8,10},{9,11},{10,... | collective-permute-start | bytes 153608 | tf_op jit(solution)/shard_map/ppermute | solution.py:324
  18.8 0.9 %collective-permute-done.7.refs_8_ = bf16[8,3200]{1,0:T(8,128)(2,1)S(1)} collective-permute-done((bf16[8,3200]{1,0:T(8,128)(2,1)S(1)}, bf16[8,3200]{1,0:T(8,128)(2,1)S(1)}, u32[]{:S(2)}, u32[]{:S(2)}) %collective-permute-start.7) | collective-permute-done | bytes 51232 | tf_op jit(solution)/shard_map/ppermute | solution.py:324
  19.7 0.0 collective-permute-start.12
  19.7 1.5 %collective-permute-start.9 = (bf16[8,3200]{1,0:T(8,128)(2,1)S(1)}, bf16[8,3200]{1,0:T(8,128)(2,1)S(1)}, u32[]{:S(2)}, u32[]{:S(2)}) collective-permute-start(bf16[8,3200]{1,0:T(8,128)(2,1)S(1)} %collective-permute-done.7.refs_8_), channel_id=1, source_target_pairs={{0,2},{1,3},{2,0},{3,1},{4,6},{5,7},{6,4},{7,5},{8,10},{9,11},{10,... | collective-permute-start | bytes 153608 | tf_op jit(solution)/shard_map/ppermute | solution.py:324
  21.2 0.2 collective-permute-start.8
  21.4 0.0 collective-permute-done.refs_1_
  21.4 0.5 collective-permute-start.5
  22.0 0.0 collective-permute-done.13.refs_14_
  22.0 0.0 collective-permute-start.4
  22.0 0.0 collective-permute-done.12.refs_13_
  22.0 0.5 collective-permute-start.2
  22.5 1.4 %collective-permute-done.9.refs_10_ = bf16[8,3200]{1,0:T(8,128)(2,1)S(1)} collective-permute-done((bf16[8,3200]{1,0:T(8,128)(2,1)S(1)}, bf16[8,3200]{1,0:T(8,128)(2,1)S(1)}, u32[]{:S(2)}, u32[]{:S(2)}) %collective-permute-start.9) | collective-permute-done | bytes 51232 | tf_op jit(solution)/shard_map/ppermute | solution.py:324
  23.9 0.0 collective-permute-start.14
  23.9 0.0 collective-permute-done.8.refs_9_
  23.9 0.5 collective-permute-start.10
  24.4 1.1 %collective-permute-done.5.refs_6_ = bf16[8,3200]{1,0:T(8,128)(2,1)S(1)} collective-permute-done((bf16[8,3200]{1,0:T(8,128)(2,1)S(1)}, bf16[8,3200]{1,0:T(8,128)(2,1)S(1)}, u32[]{:S(2)}, u32[]{:S(2)}) %collective-permute-start.5) | collective-permute-done | bytes 51232 | tf_op jit(solution)/shard_map/ppermute | solution.py:324
  25.6 0.0 collective-permute-done.14.refs_15_
  25.6 1.2 %collective-permute-done.6.refs_7_ = bf16[8,3200]{1,0:T(8,128)(2,1)S(1)} collective-permute-done((bf16[8,3200]{1,0:T(8,128)(2,1)S(1)}, bf16[8,3200]{1,0:T(8,128)(2,1)S(1)}, u32[]{:S(2)}, u32[]{:S(2)}) %collective-permute-start.6) | collective-permute-done | bytes 51232 | tf_op jit(solution)/shard_map/ppermute | solution.py:324
  26.8 2.5 %shard_map.110 = (bf16[104,3072]{1,0:T(8,128)(2,1)S(1)}, bf16[128,128]{1,0:T(8,128)(2,1)S(1)}, bf16[104,1024]{1,0:T(8,128)(2,1)S(1)}) custom-call(bf16[8,3200]{1,0:T(8,128)(2,1)S(1)} %get-tuple-element.11.refs_0_, bf16[8,3200]{1,0:T(8,128)(2,1)S(1)} %collective-permute-done.refs_1_, bf16[8,3200]{1,0:T(8,128)(2,1)S(1)} %collective-permute-done.1.refs_2_, ...), custom_call_target="tpu_custom_call" | custom-call | flops 2000000000 | tf_op jit(solution)/shard_map/pallas_call | solution.py:127
  29.3 1.0 %collective-permute-start.17 = (bf16[104,1024]{1,0:T(8,128)(2,1)S(1)}, bf16[104,1024]{1,0:T(8,128)(2,1)S(1)}, u32[]{:S(2)}, u32[]{:S(2)}) collective-permute-start(bf16[104,1024]{1,0:T(8,128)(2,1)S(1)} %get-tuple-element.13.refs_0_), channel_id=1, source_target_pairs={{0,2},{1,3},{2,0},{3,1},{4,6},{5,7},{6,4},{7,5},{8,10},{9,11},{10,... | collective-permute-start | bytes 638984 | tf_op jit(solution)/shard_map/ppermute | solution.py:324
  30.3 2.1 %shard_map.111.refs_1_ = bf16[104,1024]{1,0:T(8,128)(2,1)S(1)} custom-call(bf16[104,3072]{1,0:T(8,128)(2,1)S(1)} %get-tuple-element.12.refs_0_, bf16[3072,2048]{1,0:T(8,128)(2,1)S(1)} %copy-done, bf16[3072,2048]{1,0:T(8,128)(2,1)S(1)} %copy-done.1), custom_call_target="tpu_custom_call" | custom-call | flops 2000000000 | tf_op jit(solution)/shard_map/pallas_call | solution.py:127
  32.4 1.2 %collective-permute-start.15 = (bf16[104,1024]{1,0:T(8,128)(2,1)S(1)}, bf16[104,1024]{1,0:T(8,128)(2,1)S(1)}, u32[]{:S(2)}, u32[]{:S(2)}) collective-permute-start(bf16[104,1024]{1,0:T(8,128)(2,1)S(1)} %shard_map.111.refs_1_), channel_id=1, source_target_pairs={{0,2},{1,3},{2,0},{3,1},{4,6},{5,7},{6,4},{7,5},{8,10},{9,11},{10,... | collective-permute-start | bytes 638984 | tf_op jit(solution)/shard_map/ppermute | solution.py:324
  33.6 0.0 collective-permute-start.20
  33.6 0.5 collective-permute-start.19
  34.1 3.4 %collective-permute-done.17.refs_0_ = bf16[104,1024]{1,0:T(8,128)(2,1)S(1)} collective-permute-done((bf16[104,1024]{1,0:T(8,128)(2,1)S(1)}, bf16[104,1024]{1,0:T(8,128)(2,1)S(1)}, u32[]{:S(2)}, u32[]{:S(2)}) %collective-permute-start.17) | collective-permute-done | bytes 213024 | tf_op jit(solution)/shard_map/ppermute | solution.py:324
  37.5 0.0 collective-permute-start.18
  37.5 3.8 %collective-permute-done.15.refs_0_ = bf16[104,1024]{1,0:T(8,128)(2,1)S(1)} collective-permute-done((bf16[104,1024]{1,0:T(8,128)(2,1)S(1)}, bf16[104,1024]{1,0:T(8,128)(2,1)S(1)}, u32[]{:S(2)}, u32[]{:S(2)}) %collective-permute-start.15) | collective-permute-done | bytes 213024 | tf_op jit(solution)/shard_map/ppermute | solution.py:324
  41.3 0.0 collective-permute-start.16
  41.3 1.1 %shard_map.112.refs_3_ = f32[104,768]{1,0:T(8,128)S(1)} custom-call(bf16[104,1024]{1,0:T(8,128)(2,1)S(1)} %get-tuple-element.13.refs_0_, bf16[104,1024]{1,0:T(8,128)(2,1)S(1)} %shard_map.111.refs_1_, bf16[104,1024]{1,0:T(8,128)(2,1)S(1)} %collective-permute-done.19.refs_2_, bf16[104,1024]{1,0:T(8,128)(2,1)S(1)} %collective-permute-done.20.refs_3_, ...), custom_call_target="tpu_custom_call" | custom-call | flops 1000000000 | tf_op jit(solution)/shard_map/pallas_call | solution.py:127
  42.4 0.6 %shard_map.113.refs_3_ = f32[104,768]{1,0:T(8,128)S(1)} custom-call(bf16[104,1024]{1,0:T(8,128)(2,1)S(1)} %collective-permute-done.17.refs_0_, bf16[104,1024]{1,0:T(8,128)(2,1)S(1)} %collective-permute-done.18.refs_1_, bf16[8192,768]{1,0:T(8,128)(2,1)S(1)} %bitcast.4, f32[104,768]{1,0:T(8,128)S(1)} %shard_map.112.refs_3_), custom_call_target="tpu_custom_call" | custom-call | flops 1000000000 | tf_op jit(solution)/shard_map/pallas_call | solution.py:127
  43.1 1.1 %shard_map.114 = bf16[128,768]{1,0:T(8,128)(2,1)S(1)} custom-call(bf16[104,1024]{1,0:T(8,128)(2,1)S(1)} %collective-permute-done.15.refs_0_, bf16[104,1024]{1,0:T(8,128)(2,1)S(1)} %collective-permute-done.16.refs_1_, bf16[8192,768]{1,0:T(8,128)(2,1)S(1)} %bitcast.4, f32[104,768]{1,0:T(8,128)S(1)} %shard_map.113.refs_3_, ...), custom_call_target="tpu_custom_call" | custom-call | flops 1000000000 | tf_op jit(solution)/shard_map/pallas_call | solution.py:127
  44.1 13.5 %all_to_all.5.arrived_ref = bf16[16,8,768]{2,1,0:T(8,128)(2,1)S(1)} all-to-all(bf16[16,8,768]{2,1,0:T(8,128)(2,1)S(1)} %bitcast.5), channel_id=1, replica_groups=mesh['rep'=2,'dev'=4,'sub'=4] {'dev','sub'}, dimensions={0} | all-to-all | bytes 393216 | tf_op jit(solution)/shard_map/all_to_all | solution.py:428
  57.7 0.7 %shard_map.115 = bf16[8,3072]{1,0:T(8,128)(2,1)} custom-call(bf16[8,3072]{1,0:T(8,128)(2,1)S(1)} %get-tuple-element.10.resid_ref, bf16[16,8,768]{2,1,0:T(8,128)(2,1)S(1)} %all_to_all.5.arrived_ref), custom_call_target="tpu_custom_call" | custom-call | flops 1000000 | tf_op jit(solution)/shard_map/pallas_call | solution.py:127
  (29 shorter events, 0.1 us)
Async XLA Ops:
  0.0 1.2 %copy-start.2 = (bf16[8,128,512]{2,1,0:T(8,128)(2,1)S(1)}, bf16[8,128,512]{2,1,0:T(8,128)(2,1)}, u32[]{:S(2)}) copy-start(bf16[8,128,512]{2,1,0:T(8,128)(2,1)} %keys_ref.1) | copy-start | bytes 3145732
  1.2 1.2 %copy-start.3 = (bf16[8,128,512]{2,1,0:T(8,128)(2,1)S(1)}, bf16[8,128,512]{2,1,0:T(8,128)(2,1)}, u32[]{:S(2)}) copy-start(bf16[8,128,512]{2,1,0:T(8,128)(2,1)} %values_ref.1) | copy-start | bytes 3145732
  2.5 0.8 %copy-start.4 = (bf16[8,3072]{1,0:T(8,128)(2,1)S(1)}, bf16[8,3072]{1,0:T(8,128)(2,1)}, u32[]{:S(2)}) copy-start(bf16[8,3072]{1,0:T(8,128)(2,1)} %tokens_ref.1) | copy-start | bytes 147460
  3.2 0.8 %copy-start.5 = (bf16[8,3072]{1,0:T(8,128)(2,1)S(1)}, bf16[8,3072]{1,0:T(8,128)(2,1)}, u32[]{:S(2)}) copy-start(bf16[8,3072]{1,0:T(8,128)(2,1)} %queries_ref.1) | copy-start | bytes 147460
  4.0 0.7 %copy-start.6 = (bf16[3072,4]{0,1:T(4,128)(2,1)S(1)}, bf16[3072,4]{0,1:T(4,128)(2,1)}, u32[]{:S(2)}) copy-start(bf16[3072,4]{0,1:T(4,128)(2,1)} %param.17) | copy-start | bytes 73732
  4.8 0.7 %copy-start.7 = (bf16[3072]{0:T(1024)(128)(2,1)S(1)}, bf16[3072]{0:T(1024)(128)(2,1)}, u32[]{:S(2)}) copy-start(bf16[3072]{0:T(1024)(128)(2,1)} %gain_ref.1) | copy-start | bytes 18436
  5.5 0.7 %copy-start.8 = (s32[32,2]{0,1:T(2,128)S(1)}, s32[32,2]{0,1:T(2,128)}, u32[]{:S(2)}) copy-start(s32[32,2]{0,1:T(2,128)} %param.18) | copy-start | bytes 772
  6.2 0.7 %copy-start.9 = (s32[8]{0:T(128)S(1)}, s32[8]{0:T(128)}, u32[]{:S(2)}) copy-start(s32[8]{0:T(128)} %lengths_ref.1) | copy-start | bytes 100
  6.8 20.0 %copy-start = (bf16[3072,2048]{1,0:T(8,128)(2,1)S(1)}, bf16[3072,2048]{1,0:T(8,128)(2,1)}, u32[]{:S(2)}) copy-start(bf16[3072,2048]{1,0:T(8,128)(2,1)} %refs_1_.1) | copy-start | bytes 37748740
  6.8 20.0 %copy-start.1 = (bf16[3072,2048]{1,0:T(8,128)(2,1)S(1)}, bf16[3072,2048]{1,0:T(8,128)(2,1)}, u32[]{:S(2)}) copy-start(bf16[3072,2048]{1,0:T(8,128)(2,1)} %refs_2_.3) | copy-start | bytes 37748740
  9.6 7.4 %collective-permute-start.11 = (bf16[8,3200]{1,0:T(8,128)(2,1)S(1)}, bf16[8,3200]{1,0:T(8,128)(2,1)S(1)}, u32[]{:S(2)}, u32[]{:S(2)}) collective-permute-start(bf16[8,3200]{1,0:T(8,128)(2,1)S(1)} %get-tuple-element.11.refs_0_), channel_id=1, source_target_pairs={{0,12},{4,8},{8,4},{12,0},{1,13},{5,9},{9,5},{13,1},{2,14},{6,10},... | collective-permute-start | bytes 153608 | tf_op jit(solution)/shard_map/ppermute | solution.py:324
  14.7 5.0 %collective-permute-start.7 = (bf16[8,3200]{1,0:T(8,128)(2,1)S(1)}, bf16[8,3200]{1,0:T(8,128)(2,1)S(1)}, u32[]{:S(2)}, u32[]{:S(2)}) collective-permute-start(bf16[8,3200]{1,0:T(8,128)(2,1)S(1)} %get-tuple-element.11.refs_0_), channel_id=1, source_target_pairs={{0,8},{4,12},{8,0},{12,4},{1,9},{5,13},{9,1},{13,5},{2,10},{6,14},... | collective-permute-start | bytes 153608 | tf_op jit(solution)/shard_map/ppermute | solution.py:324
  14.7 5.0 %collective-permute-start.3 = (bf16[8,3200]{1,0:T(8,128)(2,1)S(1)}, bf16[8,3200]{1,0:T(8,128)(2,1)S(1)}, u32[]{:S(2)}, u32[]{:S(2)}) collective-permute-start(bf16[8,3200]{1,0:T(8,128)(2,1)S(1)} %get-tuple-element.11.refs_0_), channel_id=1, source_target_pairs={{0,4},{4,0},{8,12},{12,8},{1,5},{5,1},{9,13},{13,9},{2,6},{6,2},{1... | collective-permute-start | bytes 153608 | tf_op jit(solution)/shard_map/ppermute | solution.py:324
  15.3 5.9 %collective-permute-start.1 = (bf16[8,3200]{1,0:T(8,128)(2,1)S(1)}, bf16[8,3200]{1,0:T(8,128)(2,1)S(1)}, u32[]{:S(2)}, u32[]{:S(2)}) collective-permute-start(bf16[8,3200]{1,0:T(8,128)(2,1)S(1)} %get-tuple-element.11.refs_0_), channel_id=1, source_target_pairs={{0,2},{1,3},{2,0},{3,1},{4,6},{5,7},{6,4},{7,5},{8,10},{9,11},{10,... | collective-permute-start | bytes 153608 | tf_op jit(solution)/shard_map/ppermute | solution.py:324
  17.0 4.5 %collective-permute-start = (bf16[8,3200]{1,0:T(8,128)(2,1)S(1)}, bf16[8,3200]{1,0:T(8,128)(2,1)S(1)}, u32[]{:S(2)}, u32[]{:S(2)}) collective-permute-start(bf16[8,3200]{1,0:T(8,128)(2,1)S(1)} %get-tuple-element.11.refs_0_), channel_id=1, source_target_pairs={{0,1},{1,0},{2,3},{3,2},{4,5},{5,4},{6,7},{7,6},{8,9},{9,8},{10,11... | collective-permute-start | bytes 153608 | tf_op jit(solution)/shard_map/ppermute | solution.py:324
  17.0 5.0 %collective-permute-start.13 = (bf16[8,3200]{1,0:T(8,128)(2,1)S(1)}, bf16[8,3200]{1,0:T(8,128)(2,1)S(1)}, u32[]{:S(2)}, u32[]{:S(2)}) collective-permute-start(bf16[8,3200]{1,0:T(8,128)(2,1)S(1)} %collective-permute-done.11.refs_12_), channel_id=1, source_target_pairs={{0,2},{1,3},{2,0},{3,1},{4,6},{5,7},{6,4},{7,5},{8,10},{9,11},{10,... | collective-permute-start | bytes 153608 | tf_op jit(solution)/shard_map/ppermute | solution.py:324
  19.7 2.3 %collective-permute-start.12 = (bf16[8,3200]{1,0:T(8,128)(2,1)S(1)}, bf16[8,3200]{1,0:T(8,128)(2,1)S(1)}, u32[]{:S(2)}, u32[]{:S(2)}) collective-permute-start(bf16[8,3200]{1,0:T(8,128)(2,1)S(1)} %collective-permute-done.11.refs_12_), channel_id=1, source_target_pairs={{0,1},{1,0},{2,3},{3,2},{4,5},{5,4},{6,7},{7,6},{8,9},{9,8},{10,11... | collective-permute-start | bytes 153608 | tf_op jit(solution)/shard_map/ppermute | solution.py:324
  19.7 4.2 %collective-permute-start.9 = (bf16[8,3200]{1,0:T(8,128)(2,1)S(1)}, bf16[8,3200]{1,0:T(8,128)(2,1)S(1)}, u32[]{:S(2)}, u32[]{:S(2)}) collective-permute-start(bf16[8,3200]{1,0:T(8,128)(2,1)S(1)} %collective-permute-done.7.refs_8_), channel_id=1, source_target_pairs={{0,2},{1,3},{2,0},{3,1},{4,6},{5,7},{6,4},{7,5},{8,10},{9,11},{10,... | collective-permute-start | bytes 153608 | tf_op jit(solution)/shard_map/ppermute | solution.py:324
  21.2 2.7 %collective-permute-start.8 = (bf16[8,3200]{1,0:T(8,128)(2,1)S(1)}, bf16[8,3200]{1,0:T(8,128)(2,1)S(1)}, u32[]{:S(2)}, u32[]{:S(2)}) collective-permute-start(bf16[8,3200]{1,0:T(8,128)(2,1)S(1)} %collective-permute-done.7.refs_8_), channel_id=1, source_target_pairs={{0,1},{1,0},{2,3},{3,2},{4,5},{5,4},{6,7},{7,6},{8,9},{9,8},{10,11... | collective-permute-start | bytes 153608 | tf_op jit(solution)/shard_map/ppermute | solution.py:324
  21.4 4.1 %collective-permute-start.5 = (bf16[8,3200]{1,0:T(8,128)(2,1)S(1)}, bf16[8,3200]{1,0:T(8,128)(2,1)S(1)}, u32[]{:S(2)}, u32[]{:S(2)}) collective-permute-start(bf16[8,3200]{1,0:T(8,128)(2,1)S(1)} %collective-permute-done.3.refs_4_), channel_id=1, source_target_pairs={{0,2},{1,3},{2,0},{3,1},{4,6},{5,7},{6,4},{7,5},{8,10},{9,11},{10,... | collective-permute-start | bytes 153608 | tf_op jit(solution)/shard_map/ppermute | solution.py:324
  22.0 3.6 %collective-permute-start.4 = (bf16[8,3200]{1,0:T(8,128)(2,1)S(1)}, bf16[8,3200]{1,0:T(8,128)(2,1)S(1)}, u32[]{:S(2)}, u32[]{:S(2)}) collective-permute-start(bf16[8,3200]{1,0:T(8,128)(2,1)S(1)} %collective-permute-done.3.refs_4_), channel_id=1, source_target_pairs={{0,1},{1,0},{2,3},{3,2},{4,5},{5,4},{6,7},{7,6},{8,9},{9,8},{10,11... | collective-permute-start | bytes 153608 | tf_op jit(solution)/shard_map/ppermute | solution.py:324
  22.0 3.6 %collective-permute-start.2 = (bf16[8,3200]{1,0:T(8,128)(2,1)S(1)}, bf16[8,3200]{1,0:T(8,128)(2,1)S(1)}, u32[]{:S(2)}, u32[]{:S(2)}) collective-permute-start(bf16[8,3200]{1,0:T(8,128)(2,1)S(1)} %collective-permute-done.1.refs_2_), channel_id=1, source_target_pairs={{0,1},{1,0},{2,3},{3,2},{4,5},{5,4},{6,7},{7,6},{8,9},{9,8},{10,11... | collective-permute-start | bytes 153608 | tf_op jit(solution)/shard_map/ppermute | solution.py:324
  23.9 1.7 %collective-permute-start.14 = (bf16[8,3200]{1,0:T(8,128)(2,1)S(1)}, bf16[8,3200]{1,0:T(8,128)(2,1)S(1)}, u32[]{:S(2)}, u32[]{:S(2)}) collective-permute-start(bf16[8,3200]{1,0:T(8,128)(2,1)S(1)} %collective-permute-done.13.refs_14_), channel_id=1, source_target_pairs={{0,1},{1,0},{2,3},{3,2},{4,5},{5,4},{6,7},{7,6},{8,9},{9,8},{10,11... | collective-permute-start | bytes 153608 | tf_op jit(solution)/shard_map/ppermute | solution.py:324
  23.9 1.7 %collective-permute-start.10 = (bf16[8,3200]{1,0:T(8,128)(2,1)S(1)}, bf16[8,3200]{1,0:T(8,128)(2,1)S(1)}, u32[]{:S(2)}, u32[]{:S(2)}) collective-permute-start(bf16[8,3200]{1,0:T(8,128)(2,1)S(1)} %collective-permute-done.9.refs_10_), channel_id=1, source_target_pairs={{0,1},{1,0},{2,3},{3,2},{4,5},{5,4},{6,7},{7,6},{8,9},{9,8},{10,11... | collective-permute-start | bytes 153608 | tf_op jit(solution)/shard_map/ppermute | solution.py:324
  25.5 1.2 %collective-permute-start.6 = (bf16[8,3200]{1,0:T(8,128)(2,1)S(1)}, bf16[8,3200]{1,0:T(8,128)(2,1)S(1)}, u32[]{:S(2)}, u32[]{:S(2)}) collective-permute-start(bf16[8,3200]{1,0:T(8,128)(2,1)S(1)} %collective-permute-done.5.refs_6_), channel_id=1, source_target_pairs={{0,1},{1,0},{2,3},{3,2},{4,5},{5,4},{6,7},{7,6},{8,9},{9,8},{10,11... | collective-permute-start | bytes 153608 | tf_op jit(solution)/shard_map/ppermute | solution.py:324
  26.8 14.5 %slice-start = ((s8[12582912]{0:T(1024)(128)(4,1)}), s8[4194304]{0:T(1024)(128)(4,1)S(1)}, s32[]{:S(2)}) async-start(s8[12582912]{0:T(1024)(128)(4,1)} %bitcast.3), calls=%async_computation.1 | async-start | bytes 8388608
  26.8 14.5 %slice-start.1 = ((s8[12582912]{0:T(1024)(128)(4,1)}), s8[4194304]{0:T(1024)(128)(4,1)S(1)}, s32[]{:S(2)}) async-start(s8[12582912]{0:T(1024)(128)(4,1)} %bitcast.3), calls=%async_computation.2 | async-start | bytes 8388608
  29.3 8.2 %collective-permute-start.17 = (bf16[104,1024]{1,0:T(8,128)(2,1)S(1)}, bf16[104,1024]{1,0:T(8,128)(2,1)S(1)}, u32[]{:S(2)}, u32[]{:S(2)}) collective-permute-start(bf16[104,1024]{1,0:T(8,128)(2,1)S(1)} %get-tuple-element.13.refs_0_), channel_id=1, source_target_pairs={{0,2},{1,3},{2,0},{3,1},{4,6},{5,7},{6,4},{7,5},{8,10},{9,11},{10,... | collective-permute-start | bytes 638984 | tf_op jit(solution)/shard_map/ppermute | solution.py:324
  30.3 11.0 %slice-start.2 = ((s8[12582912]{0:T(1024)(128)(4,1)}), s8[4194304]{0:T(1024)(128)(4,1)S(1)}, s32[]{:S(2)}) async-start(s8[12582912]{0:T(1024)(128)(4,1)} %bitcast.3), calls=%async_computation.3 | async-start | bytes 8388608
  32.4 8.8 %collective-permute-start.15 = (bf16[104,1024]{1,0:T(8,128)(2,1)S(1)}, bf16[104,1024]{1,0:T(8,128)(2,1)S(1)}, u32[]{:S(2)}, u32[]{:S(2)}) collective-permute-start(bf16[104,1024]{1,0:T(8,128)(2,1)S(1)} %shard_map.111.refs_1_), channel_id=1, source_target_pairs={{0,2},{1,3},{2,0},{3,1},{4,6},{5,7},{6,4},{7,5},{8,10},{9,11},{10,... | collective-permute-start | bytes 638984 | tf_op jit(solution)/shard_map/ppermute | solution.py:324
  33.6 7.7 %collective-permute-start.20 = (bf16[104,1024]{1,0:T(8,128)(2,1)S(1)}, bf16[104,1024]{1,0:T(8,128)(2,1)S(1)}, u32[]{:S(2)}, u32[]{:S(2)}) collective-permute-start(bf16[104,1024]{1,0:T(8,128)(2,1)S(1)} %shard_map.111.refs_1_), channel_id=1, source_target_pairs={{0,1},{1,0},{2,3},{3,2},{4,5},{5,4},{6,7},{7,6},{8,9},{9,8},{10,11... | collective-permute-start | bytes 638984 | tf_op jit(solution)/shard_map/ppermute | solution.py:324
  33.6 7.7 %collective-permute-start.19 = (bf16[104,1024]{1,0:T(8,128)(2,1)S(1)}, bf16[104,1024]{1,0:T(8,128)(2,1)S(1)}, u32[]{:S(2)}, u32[]{:S(2)}) collective-permute-start(bf16[104,1024]{1,0:T(8,128)(2,1)S(1)} %get-tuple-element.13.refs_0_), channel_id=1, source_target_pairs={{0,1},{1,0},{2,3},{3,2},{4,5},{5,4},{6,7},{7,6},{8,9},{9,8},{10,11... | collective-permute-start | bytes 638984 | tf_op jit(solution)/shard_map/ppermute | solution.py:324
  37.5 4.9 %collective-permute-start.18 = (bf16[104,1024]{1,0:T(8,128)(2,1)S(1)}, bf16[104,1024]{1,0:T(8,128)(2,1)S(1)}, u32[]{:S(2)}, u32[]{:S(2)}) collective-permute-start(bf16[104,1024]{1,0:T(8,128)(2,1)S(1)} %collective-permute-done.17.refs_0_), channel_id=1, source_target_pairs={{0,1},{1,0},{2,3},{3,2},{4,5},{5,4},{6,7},{7,6},{8,9},{9,8},{10,11... | collective-permute-start | bytes 638984 | tf_op jit(solution)/shard_map/ppermute | solution.py:324
  41.3 1.8 %collective-permute-start.16 = (bf16[104,1024]{1,0:T(8,128)(2,1)S(1)}, bf16[104,1024]{1,0:T(8,128)(2,1)S(1)}, u32[]{:S(2)}, u32[]{:S(2)}) collective-permute-start(bf16[104,1024]{1,0:T(8,128)(2,1)S(1)} %collective-permute-done.15.refs_0_), channel_id=1, source_target_pairs={{0,1},{1,0},{2,3},{3,2},{4,5},{5,4},{6,7},{7,6},{8,9},{9,8},{10,11... | collective-permute-start | bytes 638984 | tf_op jit(solution)/shard_map/ppermute | solution.py:324

commit v2 on v1

--- a/solution.py
+++ b/solution.py
@@ -120,6 +120,7 @@
 VMEM_SPEC = pl.BlockSpec(memory_space=pltpu.VMEM)
 SMEM_SPEC = pl.BlockSpec(memory_space=pltpu.SMEM)
 MIB = 1024 * 1024
+OPENING_FLOPS = 4 * 10**9
 EXTRA = 128
 
 
@@ -145,13 +146,18 @@
     return lax.dot_general(a, b, (((1,), (1,)), ((), ())), preferred_element_type=jnp.float32)
 
 
+def opening_kernel(out_ref):
+    out_ref[...] = jnp.zeros_like(out_ref)
+
+
 def attention_kernel(
+    _,
     lengths_ref,
     routes_ref,
-    tokens_ref,
     queries_ref,
     keys_ref,
     values_ref,
+    tokens_ref,
     gain_ref,
     router_ref,
     payload_ref,
@@ -344,23 +350,33 @@
     own_hidden = gate_weight.shape[1]
     out_width = down_weight.shape[1]
     bf16 = jnp.bfloat16
+    opening = call(
+        opening_kernel,
+        jax.ShapeDtypeStruct((8, 128), jnp.float32),
+        (),
+        [],
+        flops=OPENING_FLOPS,
+        vmem=MIB,
+    )
+    operands = (
+        opening,
+        lengths,
+        routes.T,
+        queries,
+        request_key_cache,
+        request_value_cache,
+        tokens,
+        norm_gain,
+        router_weight.T,
+    )
     payload, resid = call(
         attention_kernel,
         (
             jax.ShapeDtypeStruct((rows, width + EXTRA), bf16),
             jax.ShapeDtypeStruct((rows, width), bf16),
         ),
-        (
-            lengths,
-            routes.T,
-            tokens,
-            queries,
-            request_key_cache,
-            request_value_cache,
-            norm_gain,
-            router_weight.T,
-        ),
-        [SMEM_SPEC, SMEM_SPEC] + [VMEM_SPEC] * 6,
+        operands,
+        [VMEM_SPEC, SMEM_SPEC, SMEM_SPEC] + [VMEM_SPEC] * 6,
         flops=30 * 10**9,
         bytes_accessed=100 * MIB,
         vmem=8 * MIB,

time: 58.8 us -> 53.4 us (0.908)
  local copies, waits for them, and re-layouts: 6.82 us -> 1.59 us
    unnamed x26 -> x34, local copies, waits for them, and re-layouts: 6.82 us -> 1.59 us
    pallas_call x7 -> x8, Pallas kernels: 10.8 us -> 10.9 us  [call(): pl.pallas_call(body, out_shape=out_shapes, in_specs=specs, out_specs=jax....]
where the time goes in v2:
time: 53.4 us; the launch traced here: 53.3 us
  starting transfers between devices  15.1 us (28%)
  blocking collectives  13.5 us (25%)
  waiting for transfers between devices  11.9 us (22%)
  Pallas kernels  10.9 us (20%)
  local copies, waits for them, and re-layouts  1.59 us (3%)
    ppermute x21, starting transfers between devices, flip(): lax.ppermute(x, axis, [(i, i ^ bits) for i in range(lax.axis_size(axis))])  15.1 us
    all_to_all x1, blocking collectives, per_device(): lax.all_to_all(weighted.reshape(devs * subs, rows, out_width), ('dev', 's...  13.5 us
    ppermute x21, waiting for transfers between devices, flip(): lax.ppermute(x, axis, [(i, i ^ bits) for i in range(lax.axis_size(axis))])  11.9 us
    pallas_call x8, Pallas kernels, call(): pl.pallas_call(body, out_shape=out_shapes, in_specs=specs, out_specs=jax....  10.9 us
    unnamed x34, local copies, waits for them, and re-layouts  1.59 us
  transfers between devices with their start and end apart: 21, of which 6 were waited for; matrix products, arithmetic and copies ran while one was open for 0% of the time, Pallas kernels for 7%

profile of v2, /device:TPU:0, one launch (start us, length us, event | category | flops | bytes accessed | tf_op | source)
XLA Modules:
  0.0 53.3 jit_solution(16551437763768959063)
XLA Ops:
  0.0 0.0 slice-start.3
  0.1 0.0 slice-start.6
  0.1 0.6 %copy-done.6 = s32[32,2]{0,1:T(2,128)S(1)} copy-done((s32[32,2]{0,1:T(2,128)S(1)}, s32[32,2]{0,1:T(2,128)}, u32[]{:S(2)}) %copy-start.6) | copy-done | bytes 280
  0.7 0.1 copy-done.4
  0.8 0.5 copy-done.1
  1.3 0.3 copy-done
  1.6 0.0 slice-start.7
  1.6 0.0 slice-start.8
  1.6 2.7 %shard_map.110 = (bf16[8,3200]{1,0:T(8,128)(2,1)S(1)}, bf16[8,3072]{1,0:T(8,128)(2,1)S(1)}) custom-call(f32[8,128]{1,0:T(8,128)S(1)} %shard_map.109._, s32[8]{0:T(128)S(1)} %copy-done.7, s32[2,32]{1,0:T(2,128)S(1)} %bitcast.11, bf16[8,3072]{1,0:T(8,128)(2,1)S(1)} %copy-done.2, bf16[8,128,512]{2,1,0:T(8,128)(2,1)S(1)} %copy-done, ...), custom_call_target="tpu_custom_call" | custom-call | flops 30000001024 | bytes 104857600 | tf_op jit(solution)/shard_map/pallas_call | solution.py:128
  4.4 5.1 %collective-permute-start.11 = (bf16[8,3200]{1,0:T(8,128)(2,1)S(1)}, bf16[8,3200]{1,0:T(8,128)(2,1)S(1)}, u32[]{:S(2)}, u32[]{:S(2)}) collective-permute-start(bf16[8,3200]{1,0:T(8,128)(2,1)S(1)} %get-tuple-element.11.refs_0_), channel_id=1, source_target_pairs={{0,12},{4,8},{8,4},{12,0},{1,13},{5,9},{9,5},{13,1},{2,14},{6,10},... | collective-permute-start | bytes 153608 | tf_op jit(solution)/shard_map/ppermute | solution.py:330
  9.5 0.0 collective-permute-start.7
  9.5 0.6 %collective-permute-start.3 = (bf16[8,3200]{1,0:T(8,128)(2,1)S(1)}, bf16[8,3200]{1,0:T(8,128)(2,1)S(1)}, u32[]{:S(2)}, u32[]{:S(2)}) collective-permute-start(bf16[8,3200]{1,0:T(8,128)(2,1)S(1)} %get-tuple-element.11.refs_0_), channel_id=1, source_target_pairs={{0,4},{4,0},{8,12},{12,8},{1,5},{5,1},{9,13},{13,9},{2,6},{6,2},{1... | collective-permute-start | bytes 153608 | tf_op jit(solution)/shard_map/ppermute | solution.py:330
  10.2 1.6 %collective-permute-start.1 = (bf16[8,3200]{1,0:T(8,128)(2,1)S(1)}, bf16[8,3200]{1,0:T(8,128)(2,1)S(1)}, u32[]{:S(2)}, u32[]{:S(2)}) collective-permute-start(bf16[8,3200]{1,0:T(8,128)(2,1)S(1)} %get-tuple-element.11.refs_0_), channel_id=1, source_target_pairs={{0,2},{1,3},{2,0},{3,1},{4,6},{5,7},{6,4},{7,5},{8,10},{9,11},{10,... | collective-permute-start | bytes 153608 | tf_op jit(solution)/shard_map/ppermute | solution.py:330
  11.8 0.0 collective-permute-start
  11.8 0.0 collective-permute-done.11.refs_12_
  11.8 1.8 %collective-permute-start.13 = (bf16[8,3200]{1,0:T(8,128)(2,1)S(1)}, bf16[8,3200]{1,0:T(8,128)(2,1)S(1)}, u32[]{:S(2)}, u32[]{:S(2)}) collective-permute-start(bf16[8,3200]{1,0:T(8,128)(2,1)S(1)} %collective-permute-done.11.refs_12_), channel_id=1, source_target_pairs={{0,2},{1,3},{2,0},{3,1},{4,6},{5,7},{6,4},{7,5},{8,10},{9,11},{10,... | collective-permute-start | bytes 153608 | tf_op jit(solution)/shard_map/ppermute | solution.py:330
  13.6 0.9 %collective-permute-done.7.refs_8_ = bf16[8,3200]{1,0:T(8,128)(2,1)S(1)} collective-permute-done((bf16[8,3200]{1,0:T(8,128)(2,1)S(1)}, bf16[8,3200]{1,0:T(8,128)(2,1)S(1)}, u32[]{:S(2)}, u32[]{:S(2)}) %collective-permute-start.7) | collective-permute-done | bytes 51232 | tf_op jit(solution)/shard_map/ppermute | solution.py:330
  14.5 0.0 collective-permute-start.12
  14.5 1.5 %collective-permute-start.9 = (bf16[8,3200]{1,0:T(8,128)(2,1)S(1)}, bf16[8,3200]{1,0:T(8,128)(2,1)S(1)}, u32[]{:S(2)}, u32[]{:S(2)}) collective-permute-start(bf16[8,3200]{1,0:T(8,128)(2,1)S(1)} %collective-permute-done.7.refs_8_), channel_id=1, source_target_pairs={{0,2},{1,3},{2,0},{3,1},{4,6},{5,7},{6,4},{7,5},{8,10},{9,11},{10,... | collective-permute-start | bytes 153608 | tf_op jit(solution)/shard_map/ppermute | solution.py:330
  16.0 0.2 collective-permute-start.8
  16.3 0.5 collective-permute-start.5
  16.8 0.0 collective-permute-done.13.refs_14_
  16.8 0.0 collective-permute-start.4
  16.8 0.5 collective-permute-start.2
  17.3 1.4 %collective-permute-done.9.refs_10_ = bf16[8,3200]{1,0:T(8,128)(2,1)S(1)} collective-permute-done((bf16[8,3200]{1,0:T(8,128)(2,1)S(1)}, bf16[8,3200]{1,0:T(8,128)(2,1)S(1)}, u32[]{:S(2)}, u32[]{:S(2)}) %collective-permute-start.9) | collective-permute-done | bytes 51232 | tf_op jit(solution)/shard_map/ppermute | solution.py:330
  18.7 0.5 collective-permute-start.10
  19.2 1.1 %collective-permute-done.5.refs_6_ = bf16[8,3200]{1,0:T(8,128)(2,1)S(1)} collective-permute-done((bf16[8,3200]{1,0:T(8,128)(2,1)S(1)}, bf16[8,3200]{1,0:T(8,128)(2,1)S(1)}, u32[]{:S(2)}, u32[]{:S(2)}) %collective-permute-start.5) | collective-permute-done | bytes 51232 | tf_op jit(solution)/shard_map/ppermute | solution.py:330
  20.4 0.0 collective-permute-done.2.refs_3_
  20.4 0.0 collective-permute-done.14.refs_15_
  20.4 1.2 %collective-permute-done.6.refs_7_ = bf16[8,3200]{1,0:T(8,128)(2,1)S(1)} collective-permute-done((bf16[8,3200]{1,0:T(8,128)(2,1)S(1)}, bf16[8,3200]{1,0:T(8,128)(2,1)S(1)}, u32[]{:S(2)}, u32[]{:S(2)}) %collective-permute-start.6) | collective-permute-done | bytes 51232 | tf_op jit(solution)/shard_map/ppermute | solution.py:330
  21.7 0.0 slice-start
  21.7 0.0 slice-start.1
  21.7 2.6 %shard_map.111 = (bf16[104,3072]{1,0:T(8,128)(2,1)S(1)}, bf16[128,128]{1,0:T(8,128)(2,1)S(1)}, bf16[104,1024]{1,0:T(8,128)(2,1)S(1)}) custom-call(bf16[8,3200]{1,0:T(8,128)(2,1)S(1)} %get-tuple-element.11.refs_0_, bf16[8,3200]{1,0:T(8,128)(2,1)S(1)} %collective-permute-done.refs_1_, bf16[8,3200]{1,0:T(8,128)(2,1)S(1)} %collective-permute-done.1.refs_2_, ...), custom_call_target="tpu_custom_call" | custom-call | flops 2000000000 | tf_op jit(solution)/shard_map/pallas_call | solution.py:128
  24.3 1.0 %collective-permute-start.17 = (bf16[104,1024]{1,0:T(8,128)(2,1)S(1)}, bf16[104,1024]{1,0:T(8,128)(2,1)S(1)}, u32[]{:S(2)}, u32[]{:S(2)}) collective-permute-start(bf16[104,1024]{1,0:T(8,128)(2,1)S(1)} %get-tuple-element.13.refs_0_), channel_id=1, source_target_pairs={{0,2},{1,3},{2,0},{3,1},{4,6},{5,7},{6,4},{7,5},{8,10},{9,11},{10,... | collective-permute-start | bytes 638984 | tf_op jit(solution)/shard_map/ppermute | solution.py:330
  25.3 2.1 %shard_map.112.refs_1_ = bf16[104,1024]{1,0:T(8,128)(2,1)S(1)} custom-call(bf16[104,3072]{1,0:T(8,128)(2,1)S(1)} %get-tuple-element.12.refs_0_, bf16[3072,2048]{1,0:T(8,128)(2,1)S(1)} %bitcast.6, bf16[3072,2048]{1,0:T(8,128)(2,1)S(1)} %bitcast.8), custom_call_target="tpu_custom_call" | custom-call | flops 2000000000 | tf_op jit(solution)/shard_map/pallas_call | solution.py:128
  27.4 1.1 %collective-permute-start.15 = (bf16[104,1024]{1,0:T(8,128)(2,1)S(1)}, bf16[104,1024]{1,0:T(8,128)(2,1)S(1)}, u32[]{:S(2)}, u32[]{:S(2)}) collective-permute-start(bf16[104,1024]{1,0:T(8,128)(2,1)S(1)} %shard_map.112.refs_1_), channel_id=1, source_target_pairs={{0,2},{1,3},{2,0},{3,1},{4,6},{5,7},{6,4},{7,5},{8,10},{9,11},{10,... | collective-permute-start | bytes 638984 | tf_op jit(solution)/shard_map/ppermute | solution.py:330
  28.5 0.5 collective-permute-start.19
  29.1 3.4 %collective-permute-done.17.refs_0_ = bf16[104,1024]{1,0:T(8,128)(2,1)S(1)} collective-permute-done((bf16[104,1024]{1,0:T(8,128)(2,1)S(1)}, bf16[104,1024]{1,0:T(8,128)(2,1)S(1)}, u32[]{:S(2)}, u32[]{:S(2)}) %collective-permute-start.17) | collective-permute-done | bytes 213024 | tf_op jit(solution)/shard_map/ppermute | solution.py:330
  32.4 3.8 %collective-permute-done.15.refs_0_ = bf16[104,1024]{1,0:T(8,128)(2,1)S(1)} collective-permute-done((bf16[104,1024]{1,0:T(8,128)(2,1)S(1)}, bf16[104,1024]{1,0:T(8,128)(2,1)S(1)}, u32[]{:S(2)}, u32[]{:S(2)}) %collective-permute-start.15) | collective-permute-done | bytes 213024 | tf_op jit(solution)/shard_map/ppermute | solution.py:330
  36.2 0.0 collective-permute-start.16
  36.2 0.0 collective-permute-done.20.refs_3_
  36.2 0.0 collective-permute-done.19.refs_2_
  36.3 1.1 %shard_map.113.refs_3_ = f32[104,768]{1,0:T(8,128)S(1)} custom-call(bf16[104,1024]{1,0:T(8,128)(2,1)S(1)} %get-tuple-element.13.refs_0_, bf16[104,1024]{1,0:T(8,128)(2,1)S(1)} %shard_map.112.refs_1_, bf16[104,1024]{1,0:T(8,128)(2,1)S(1)} %collective-permute-done.19.refs_2_, bf16[104,1024]{1,0:T(8,128)(2,1)S(1)} %collective-permute-done.20.refs_3_, ...), custom_call_target="tpu_custom_call" | custom-call | flops 1000000000 | tf_op jit(solution)/shard_map/pallas_call | solution.py:128
  37.3 0.6 %shard_map.114.refs_3_ = f32[104,768]{1,0:T(8,128)S(1)} custom-call(bf16[104,1024]{1,0:T(8,128)(2,1)S(1)} %collective-permute-done.17.refs_0_, bf16[104,1024]{1,0:T(8,128)(2,1)S(1)} %collective-permute-done.18.refs_1_, bf16[8192,768]{1,0:T(8,128)(2,1)S(1)} %bitcast.4, f32[104,768]{1,0:T(8,128)S(1)} %shard_map.113.refs_3_), custom_call_target="tpu_custom_call" | custom-call | flops 1000000000 | tf_op jit(solution)/shard_map/pallas_call | solution.py:128
  38.0 0.0 collective-permute-done.16.refs_1_
  38.0 1.1 %shard_map.115 = bf16[128,768]{1,0:T(8,128)(2,1)S(1)} custom-call(bf16[104,1024]{1,0:T(8,128)(2,1)S(1)} %collective-permute-done.15.refs_0_, bf16[104,1024]{1,0:T(8,128)(2,1)S(1)} %collective-permute-done.16.refs_1_, bf16[8192,768]{1,0:T(8,128)(2,1)S(1)} %bitcast.4, f32[104,768]{1,0:T(8,128)S(1)} %shard_map.114.refs_3_, ...), custom_call_target="tpu_custom_call" | custom-call | flops 1000000000 | tf_op jit(solution)/shard_map/pallas_call | solution.py:128
  39.1 13.5 %all_to_all.5.arrived_ref = bf16[16,8,768]{2,1,0:T(8,128)(2,1)S(1)} all-to-all(bf16[16,8,768]{2,1,0:T(8,128)(2,1)S(1)} %bitcast.9), channel_id=1, replica_groups=mesh['rep'=2,'dev'=4,'sub'=4] {'dev','sub'}, dimensions={0} | all-to-all | bytes 393216 | tf_op jit(solution)/shard_map/all_to_all | solution.py:444
  52.6 0.7 %shard_map.116 = bf16[8,3072]{1,0:T(8,128)(2,1)} custom-call(bf16[8,3072]{1,0:T(8,128)(2,1)S(1)} %get-tuple-element.10.resid_ref, bf16[16,8,768]{2,1,0:T(8,128)(2,1)S(1)} %all_to_all.5.arrived_ref), custom_call_target="tpu_custom_call" | custom-call | flops 1000000 | tf_op jit(solution)/shard_map/pallas_call | solution.py:128
  (40 shorter events, 0.1 us)
Async XLA Ops:
  0.0 0.7 %copy-start.6 = (s32[32,2]{0,1:T(2,128)S(1)}, s32[32,2]{0,1:T(2,128)}, u32[]{:S(2)}) copy-start(s32[32,2]{0,1:T(2,128)} %param.18) | copy-start | bytes 772
  0.0 0.8 %copy-start.4 = (bf16[3072,4]{0,1:T(4,128)(2,1)S(1)}, bf16[3072,4]{0,1:T(4,128)(2,1)}, u32[]{:S(2)}) copy-start(bf16[3072,4]{0,1:T(4,128)(2,1)} %param.17) | copy-start | bytes 73732
  0.0 0.8 %copy-start.5 = (bf16[3072]{0:T(1024)(128)(2,1)S(1)}, bf16[3072]{0:T(1024)(128)(2,1)}, u32[]{:S(2)}) copy-start(bf16[3072]{0:T(1024)(128)(2,1)} %gain_ref.1) | copy-start | bytes 18436
  0.0 0.8 %copy-start.7 = (s32[8]{0:T(128)S(1)}, s32[8]{0:T(128)}, u32[]{:S(2)}) copy-start(s32[8]{0:T(128)} %lengths_ref.1) | copy-start | bytes 100
  0.0 1.3 %copy-start.1 = (bf16[8,128,512]{2,1,0:T(8,128)(2,1)S(1)}, bf16[8,128,512]{2,1,0:T(8,128)(2,1)}, u32[]{:S(2)}) copy-start(bf16[8,128,512]{2,1,0:T(8,128)(2,1)} %values_ref.1) | copy-start | bytes 3145732
  0.0 1.6 %copy-start = (bf16[8,128,512]{2,1,0:T(8,128)(2,1)S(1)}, bf16[8,128,512]{2,1,0:T(8,128)(2,1)}, u32[]{:S(2)}) copy-start(bf16[8,128,512]{2,1,0:T(8,128)(2,1)} %keys_ref.1) | copy-start | bytes 3145732
  0.0 1.6 %copy-start.2 = (bf16[8,3072]{1,0:T(8,128)(2,1)S(1)}, bf16[8,3072]{1,0:T(8,128)(2,1)}, u32[]{:S(2)}) copy-start(bf16[8,3072]{1,0:T(8,128)(2,1)} %queries_ref.1) | copy-start | bytes 147460
  0.0 1.6 %copy-start.3 = (bf16[8,3072]{1,0:T(8,128)(2,1)S(1)}, bf16[8,3072]{1,0:T(8,128)(2,1)}, u32[]{:S(2)}) copy-start(bf16[8,3072]{1,0:T(8,128)(2,1)} %tokens_ref.1) | copy-start | bytes 147460
  0.0 21.6 %slice-start.3 = ((s8[12582912]{0:T(1024)(128)(4,1)}), s8[4194304]{0:T(1024)(128)(4,1)S(1)}, s32[]{:S(2)}) async-start(s8[12582912]{0:T(1024)(128)(4,1)} %bitcast.5), calls=%async_computation.4 | async-start | bytes 8388608
  0.1 21.6 %slice-start.6 = ((s8[12582912]{0:T(1024)(128)(4,1)}), s8[4194304]{0:T(1024)(128)(4,1)S(1)}, s32[]{:S(2)}) async-start(s8[12582912]{0:T(1024)(128)(4,1)} %bitcast.7), calls=%async_computation.7 | async-start | bytes 8388608
  1.6 20.0 %slice-start.4 = ((s8[12582912]{0:T(1024)(128)(4,1)}), s8[4194304]{0:T(1024)(128)(4,1)S(1)}, s32[]{:S(2)}) async-start(s8[12582912]{0:T(1024)(128)(4,1)} %bitcast.5), calls=%async_computation.5 | async-start | bytes 8388608
  1.6 20.0 %slice-start.5 = ((s8[12582912]{0:T(1024)(128)(4,1)}), s8[4194304]{0:T(1024)(128)(4,1)S(1)}, s32[]{:S(2)}) async-start(s8[12582912]{0:T(1024)(128)(4,1)} %bitcast.5), calls=%async_computation.6 | async-start | bytes 8388608
  1.6 20.0 %slice-start.7 = ((s8[12582912]{0:T(1024)(128)(4,1)}), s8[4194304]{0:T(1024)(128)(4,1)S(1)}, s32[]{:S(2)}) async-start(s8[12582912]{0:T(1024)(128)(4,1)} %bitcast.7), calls=%async_computation.8 | async-start | bytes 8388608
  1.6 20.0 %slice-start.8 = ((s8[12582912]{0:T(1024)(128)(4,1)}), s8[4194304]{0:T(1024)(128)(4,1)S(1)}, s32[]{:S(2)}) async-start(s8[12582912]{0:T(1024)(128)(4,1)} %bitcast.7), calls=%async_computation.9 | async-start | bytes 8388608
  4.4 7.4 %collective-permute-start.11 = (bf16[8,3200]{1,0:T(8,128)(2,1)S(1)}, bf16[8,3200]{1,0:T(8,128)(2,1)S(1)}, u32[]{:S(2)}, u32[]{:S(2)}) collective-permute-start(bf16[8,3200]{1,0:T(8,128)(2,1)S(1)} %get-tuple-element.11.refs_0_), channel_id=1, source_target_pairs={{0,12},{4,8},{8,4},{12,0},{1,13},{5,9},{9,5},{13,1},{2,14},{6,10},... | collective-permute-start | bytes 153608 | tf_op jit(solution)/shard_map/ppermute | solution.py:330
  9.5 5.0 %collective-permute-start.7 = (bf16[8,3200]{1,0:T(8,128)(2,1)S(1)}, bf16[8,3200]{1,0:T(8,128)(2,1)S(1)}, u32[]{:S(2)}, u32[]{:S(2)}) collective-permute-start(bf16[8,3200]{1,0:T(8,128)(2,1)S(1)} %get-tuple-element.11.refs_0_), channel_id=1, source_target_pairs={{0,8},{4,12},{8,0},{12,4},{1,9},{5,13},{9,1},{13,5},{2,10},{6,14},... | collective-permute-start | bytes 153608 | tf_op jit(solution)/shard_map/ppermute | solution.py:330
  9.5 5.0 %collective-permute-start.3 = (bf16[8,3200]{1,0:T(8,128)(2,1)S(1)}, bf16[8,3200]{1,0:T(8,128)(2,1)S(1)}, u32[]{:S(2)}, u32[]{:S(2)}) collective-permute-start(bf16[8,3200]{1,0:T(8,128)(2,1)S(1)} %get-tuple-element.11.refs_0_), channel_id=1, source_target_pairs={{0,4},{4,0},{8,12},{12,8},{1,5},{5,1},{9,13},{13,9},{2,6},{6,2},{1... | collective-permute-start | bytes 153608 | tf_op jit(solution)/shard_map/ppermute | solution.py:330
  10.2 5.9 %collective-permute-start.1 = (bf16[8,3200]{1,0:T(8,128)(2,1)S(1)}, bf16[8,3200]{1,0:T(8,128)(2,1)S(1)}, u32[]{:S(2)}, u32[]{:S(2)}) collective-permute-start(bf16[8,3200]{1,0:T(8,128)(2,1)S(1)} %get-tuple-element.11.refs_0_), channel_id=1, source_target_pairs={{0,2},{1,3},{2,0},{3,1},{4,6},{5,7},{6,4},{7,5},{8,10},{9,11},{10,... | collective-permute-start | bytes 153608 | tf_op jit(solution)/shard_map/ppermute | solution.py:330
  11.8 4.5 %collective-permute-start = (bf16[8,3200]{1,0:T(8,128)(2,1)S(1)}, bf16[8,3200]{1,0:T(8,128)(2,1)S(1)}, u32[]{:S(2)}, u32[]{:S(2)}) collective-permute-start(bf16[8,3200]{1,0:T(8,128)(2,1)S(1)} %get-tuple-element.11.refs_0_), channel_id=1, source_target_pairs={{0,1},{1,0},{2,3},{3,2},{4,5},{5,4},{6,7},{7,6},{8,9},{9,8},{10,11... | collective-permute-start | bytes 153608 | tf_op jit(solution)/shard_map/ppermute | solution.py:330
  11.8 5.0 %collective-permute-start.13 = (bf16[8,3200]{1,0:T(8,128)(2,1)S(1)}, bf16[8,3200]{1,0:T(8,128)(2,1)S(1)}, u32[]{:S(2)}, u32[]{:S(2)}) collective-permute-start(bf16[8,3200]{1,0:T(8,128)(2,1)S(1)} %collective-permute-done.11.refs_12_), channel_id=1, source_target_pairs={{0,2},{1,3},{2,0},{3,1},{4,6},{5,7},{6,4},{7,5},{8,10},{9,11},{10,... | collective-permute-start | bytes 153608 | tf_op jit(solution)/shard_map/ppermute | solution.py:330
  14.5 2.3 %collective-permute-start.12 = (bf16[8,3200]{1,0:T(8,128)(2,1)S(1)}, bf16[8,3200]{1,0:T(8,128)(2,1)S(1)}, u32[]{:S(2)}, u32[]{:S(2)}) collective-permute-start(bf16[8,3200]{1,0:T(8,128)(2,1)S(1)} %collective-permute-done.11.refs_12_), channel_id=1, source_target_pairs={{0,1},{1,0},{2,3},{3,2},{4,5},{5,4},{6,7},{7,6},{8,9},{9,8},{10,11... | collective-permute-start | bytes 153608 | tf_op jit(solution)/shard_map/ppermute | solution.py:330
  14.5 4.2 %collective-permute-start.9 = (bf16[8,3200]{1,0:T(8,128)(2,1)S(1)}, bf16[8,3200]{1,0:T(8,128)(2,1)S(1)}, u32[]{:S(2)}, u32[]{:S(2)}) collective-permute-start(bf16[8,3200]{1,0:T(8,128)(2,1)S(1)} %collective-permute-done.7.refs_8_), channel_id=1, source_target_pairs={{0,2},{1,3},{2,0},{3,1},{4,6},{5,7},{6,4},{7,5},{8,10},{9,11},{10,... | collective-permute-start | bytes 153608 | tf_op jit(solution)/shard_map/ppermute | solution.py:330
  16.0 2.7 %collective-permute-start.8 = (bf16[8,3200]{1,0:T(8,128)(2,1)S(1)}, bf16[8,3200]{1,0:T(8,128)(2,1)S(1)}, u32[]{:S(2)}, u32[]{:S(2)}) collective-permute-start(bf16[8,3200]{1,0:T(8,128)(2,1)S(1)} %collective-permute-done.7.refs_8_), channel_id=1, source_target_pairs={{0,1},{1,0},{2,3},{3,2},{4,5},{5,4},{6,7},{7,6},{8,9},{9,8},{10,11... | collective-permute-start | bytes 153608 | tf_op jit(solution)/shard_map/ppermute | solution.py:330
  16.3 4.1 %collective-permute-start.5 = (bf16[8,3200]{1,0:T(8,128)(2,1)S(1)}, bf16[8,3200]{1,0:T(8,128)(2,1)S(1)}, u32[]{:S(2)}, u32[]{:S(2)}) collective-permute-start(bf16[8,3200]{1,0:T(8,128)(2,1)S(1)} %collective-permute-done.3.refs_4_), channel_id=1, source_target_pairs={{0,2},{1,3},{2,0},{3,1},{4,6},{5,7},{6,4},{7,5},{8,10},{9,11},{10,... | collective-permute-start | bytes 153608 | tf_op jit(solution)/shard_map/ppermute | solution.py:330
  16.8 3.6 %collective-permute-start.4 = (bf16[8,3200]{1,0:T(8,128)(2,1)S(1)}, bf16[8,3200]{1,0:T(8,128)(2,1)S(1)}, u32[]{:S(2)}, u32[]{:S(2)}) collective-permute-start(bf16[8,3200]{1,0:T(8,128)(2,1)S(1)} %collective-permute-done.3.refs_4_), channel_id=1, source_target_pairs={{0,1},{1,0},{2,3},{3,2},{4,5},{5,4},{6,7},{7,6},{8,9},{9,8},{10,11... | collective-permute-start | bytes 153608 | tf_op jit(solution)/shard_map/ppermute | solution.py:330
  16.8 3.6 %collective-permute-start.2 = (bf16[8,3200]{1,0:T(8,128)(2,1)S(1)}, bf16[8,3200]{1,0:T(8,128)(2,1)S(1)}, u32[]{:S(2)}, u32[]{:S(2)}) collective-permute-start(bf16[8,3200]{1,0:T(8,128)(2,1)S(1)} %collective-permute-done.1.refs_2_), channel_id=1, source_target_pairs={{0,1},{1,0},{2,3},{3,2},{4,5},{5,4},{6,7},{7,6},{8,9},{9,8},{10,11... | collective-permute-start | bytes 153608 | tf_op jit(solution)/shard_map/ppermute | solution.py:330
  18.7 1.7 %collective-permute-start.14 = (bf16[8,3200]{1,0:T(8,128)(2,1)S(1)}, bf16[8,3200]{1,0:T(8,128)(2,1)S(1)}, u32[]{:S(2)}, u32[]{:S(2)}) collective-permute-start(bf16[8,3200]{1,0:T(8,128)(2,1)S(1)} %collective-permute-done.13.refs_14_), channel_id=1, source_target_pairs={{0,1},{1,0},{2,3},{3,2},{4,5},{5,4},{6,7},{7,6},{8,9},{9,8},{10,11... | collective-permute-start | bytes 153608 | tf_op jit(solution)/shard_map/ppermute | solution.py:330
  18.7 1.7 %collective-permute-start.10 = (bf16[8,3200]{1,0:T(8,128)(2,1)S(1)}, bf16[8,3200]{1,0:T(8,128)(2,1)S(1)}, u32[]{:S(2)}, u32[]{:S(2)}) collective-permute-start(bf16[8,3200]{1,0:T(8,128)(2,1)S(1)} %collective-permute-done.9.refs_10_), channel_id=1, source_target_pairs={{0,1},{1,0},{2,3},{3,2},{4,5},{5,4},{6,7},{7,6},{8,9},{9,8},{10,11... | collective-permute-start | bytes 153608 | tf_op jit(solution)/shard_map/ppermute | solution.py:330
  20.4 1.2 %collective-permute-start.6 = (bf16[8,3200]{1,0:T(8,128)(2,1)S(1)}, bf16[8,3200]{1,0:T(8,128)(2,1)S(1)}, u32[]{:S(2)}, u32[]{:S(2)}) collective-permute-start(bf16[8,3200]{1,0:T(8,128)(2,1)S(1)} %collective-permute-done.5.refs_6_), channel_id=1, source_target_pairs={{0,1},{1,0},{2,3},{3,2},{4,5},{5,4},{6,7},{7,6},{8,9},{9,8},{10,11... | collective-permute-start | bytes 153608 | tf_op jit(solution)/shard_map/ppermute | solution.py:330
  21.7 14.6 %slice-start = ((s8[12582912]{0:T(1024)(128)(4,1)}), s8[4194304]{0:T(1024)(128)(4,1)S(1)}, s32[]{:S(2)}) async-start(s8[12582912]{0:T(1024)(128)(4,1)} %bitcast.3), calls=%async_computation.1 | async-start | bytes 8388608
  21.7 14.6 %slice-start.1 = ((s8[12582912]{0:T(1024)(128)(4,1)}), s8[4194304]{0:T(1024)(128)(4,1)S(1)}, s32[]{:S(2)}) async-start(s8[12582912]{0:T(1024)(128)(4,1)} %bitcast.3), calls=%async_computation.2 | async-start | bytes 8388608
  24.3 8.2 %collective-permute-start.17 = (bf16[104,1024]{1,0:T(8,128)(2,1)S(1)}, bf16[104,1024]{1,0:T(8,128)(2,1)S(1)}, u32[]{:S(2)}, u32[]{:S(2)}) collective-permute-start(bf16[104,1024]{1,0:T(8,128)(2,1)S(1)} %get-tuple-element.13.refs_0_), channel_id=1, source_target_pairs={{0,2},{1,3},{2,0},{3,1},{4,6},{5,7},{6,4},{7,5},{8,10},{9,11},{10,... | collective-permute-start | bytes 638984 | tf_op jit(solution)/shard_map/ppermute | solution.py:330
  25.3 11.0 %slice-start.2 = ((s8[12582912]{0:T(1024)(128)(4,1)}), s8[4194304]{0:T(1024)(128)(4,1)S(1)}, s32[]{:S(2)}) async-start(s8[12582912]{0:T(1024)(128)(4,1)} %bitcast.3), calls=%async_computation.3 | async-start | bytes 8388608
  27.4 8.8 %collective-permute-start.15 = (bf16[104,1024]{1,0:T(8,128)(2,1)S(1)}, bf16[104,1024]{1,0:T(8,128)(2,1)S(1)}, u32[]{:S(2)}, u32[]{:S(2)}) collective-permute-start(bf16[104,1024]{1,0:T(8,128)(2,1)S(1)} %shard_map.112.refs_1_), channel_id=1, source_target_pairs={{0,2},{1,3},{2,0},{3,1},{4,6},{5,7},{6,4},{7,5},{8,10},{9,11},{10,... | collective-permute-start | bytes 638984 | tf_op jit(solution)/shard_map/ppermute | solution.py:330
  28.5 7.7 %collective-permute-start.20 = (bf16[104,1024]{1,0:T(8,128)(2,1)S(1)}, bf16[104,1024]{1,0:T(8,128)(2,1)S(1)}, u32[]{:S(2)}, u32[]{:S(2)}) collective-permute-start(bf16[104,1024]{1,0:T(8,128)(2,1)S(1)} %shard_map.112.refs_1_), channel_id=1, source_target_pairs={{0,1},{1,0},{2,3},{3,2},{4,5},{5,4},{6,7},{7,6},{8,9},{9,8},{10,11... | collective-permute-start | bytes 638984 | tf_op jit(solution)/shard_map/ppermute | solution.py:330
  28.5 7.7 %collective-permute-start.19 = (bf16[104,1024]{1,0:T(8,128)(2,1)S(1)}, bf16[104,1024]{1,0:T(8,128)(2,1)S(1)}, u32[]{:S(2)}, u32[]{:S(2)}) collective-permute-start(bf16[104,1024]{1,0:T(8,128)(2,1)S(1)} %get-tuple-element.13.refs_0_), channel_id=1, source_target_pairs={{0,1},{1,0},{2,3},{3,2},{4,5},{5,4},{6,7},{7,6},{8,9},{9,8},{10,11... | collective-permute-start | bytes 638984 | tf_op jit(solution)/shard_map/ppermute | solution.py:330
  32.4 4.9 %collective-permute-start.18 = (bf16[104,1024]{1,0:T(8,128)(2,1)S(1)}, bf16[104,1024]{1,0:T(8,128)(2,1)S(1)}, u32[]{:S(2)}, u32[]{:S(2)}) collective-permute-start(bf16[104,1024]{1,0:T(8,128)(2,1)S(1)} %collective-permute-done.17.refs_0_), channel_id=1, source_target_pairs={{0,1},{1,0},{2,3},{3,2},{4,5},{5,4},{6,7},{7,6},{8,9},{9,8},{10,11... | collective-permute-start | bytes 638984 | tf_op jit(solution)/shard_map/ppermute | solution.py:330
  36.2 1.8 %collective-permute-start.16 = (bf16[104,1024]{1,0:T(8,128)(2,1)S(1)}, bf16[104,1024]{1,0:T(8,128)(2,1)S(1)}, u32[]{:S(2)}, u32[]{:S(2)}) collective-permute-start(bf16[104,1024]{1,0:T(8,128)(2,1)S(1)} %collective-permute-done.15.refs_0_), channel_id=1, source_target_pairs={{0,1},{1,0},{2,3},{3,2},{4,5},{5,4},{6,7},{7,6},{8,9},{9,8},{10,11... | collective-permute-start | bytes 638984 | tf_op jit(solution)/shard_map/ppermute | solution.py:330

commit v3 on v2

--- a/solution.py
+++ b/solution.py
@@ -1,3 +1,4 @@
+import functools
 import math
 
 import jax
@@ -120,7 +121,14 @@
 VMEM_SPEC = pl.BlockSpec(memory_space=pltpu.VMEM)
 SMEM_SPEC = pl.BlockSpec(memory_space=pltpu.SMEM)
 MIB = 1024 * 1024
+CHUNKS = (4, 4, 4, 4)
+Z_ORDER = (3, 2, 1)
+EARLY, LATE = (1, 3), (0, 2)
+PACK_FLOPS = 10**8
 OPENING_FLOPS = 4 * 10**9
+ATTENTION_FLOPS = 30 * 10**9
+GATE_FLOPS = 10**9
+DOWN_FLOPS = 10**9
 EXTRA = 128
 
 
@@ -159,7 +167,6 @@
     values_ref,
     tokens_ref,
     gain_ref,
-    router_ref,
     payload_ref,
     resid_ref,
     att_ref,
@@ -203,66 +210,73 @@
     gain = gain_ref[...].astype(jnp.float32).reshape(1, width)
     normed = (resid_f * lax.rsqrt(stats + 1e-05) * gain).astype(jnp.bfloat16)
     payload_ref[:, :width] = normed
-    logits = dot_nt(normed, router_ref[...])
-    expert = lax.broadcasted_iota(jnp.int32, (rows, EXPERTS), 1)
-    first_logit = jnp.sum(jnp.where(first == expert, logits, 0.0), axis=1, keepdims=True)
-    second_logit = jnp.sum(jnp.where(second == expert, logits, 0.0), axis=1, keepdims=True)
-    first_share = 1.0 / (1.0 + jnp.exp(second_logit - first_logit))
-    second_share = 1.0 / (1.0 + jnp.exp(first_logit - second_logit))
     lane = lax.broadcasted_iota(jnp.int32, (rows, EXTRA), 1)
-    place = lane % EXPERTS
-    routed = ((first == place) | (second == place)).astype(jnp.float32)
-    share = jnp.where(first == place, first_share, 0.0) + jnp.where(second == place, second_share, 0.0)
-    high = share.astype(jnp.bfloat16).astype(jnp.float32)
-    low = share - high
-    extra = jnp.where(
-        lane < EXPERTS,
-        routed,
-        jnp.where(lane < 2 * EXPERTS, high, jnp.where(lane < 3 * EXPERTS, low, 0.0)),
-    )
-    payload_ref[:, width:] = extra.astype(jnp.bfloat16)
+    routed = ((first == lane) | (second == lane)).astype(jnp.float32)
+    payload_ref[:, width:] = routed.astype(jnp.bfloat16)
 
 
 def own_offset(rows):
-    return (lax.axis_index("dev") * lax.axis_size("sub") + lax.axis_index("sub")) * rows
-
-
-def slot_matrix(extra, offset):
+    return lax.axis_index("sub") * rows
+
+
+def slot_matrix(extra, offset, block_rows, blocks, cap):
     count = extra.shape[0]
-    here = lax.broadcasted_iota(jnp.int32, (count, count), 0) ^ offset
-    there = lax.broadcasted_iota(jnp.int32, (count, count), 1) ^ offset
-    earlier = dot((there < here).astype(jnp.bfloat16), extra)
+    here = lax.broadcasted_iota(jnp.int32, (count, count), 0)
+    there = lax.broadcasted_iota(jnp.int32, (count, count), 1)
+    before = (there // block_rows == here // block_rows) & ((there ^ offset) < (here ^ offset))
+    earlier = dot(before.astype(jnp.bfloat16), extra)
     lane = lax.broadcasted_iota(jnp.int32, (count, EXTRA), 1)
     mine = lane == lax.axis_index("dev")
     rank = jnp.sum(jnp.where(mine, earlier, 0.0), axis=1, keepdims=True)
     routed = jnp.sum(jnp.where(mine, extra.astype(jnp.float32), 0.0), axis=1, keepdims=True)
-    slot = jnp.where(routed > 0.5, rank, -1.0).astype(jnp.int32)
-    return (slot == lax.broadcasted_iota(jnp.int32, (count, count), 1)).astype(jnp.float32)
+    block = lax.broadcasted_iota(jnp.int32, (count, 1), 0) // block_rows
+    base = jnp.zeros((count, 1), jnp.int32)
+    for i, k in enumerate(blocks):
+        base = jnp.where(block == i, k * cap, base)
+    slot = jnp.where(routed > 0.5, rank.astype(jnp.int32) + base, -1)
+    return (slot == lax.broadcasted_iota(jnp.int32, (count, EXTRA), 1)).astype(jnp.float32)
 
 
 def hidden_columns(x, gate_ref, up_ref, out_ref, begin):
-    step = 256
-    for j in range(0, out_ref.shape[1], step):
-        gate = dot(x, gate_ref[:, begin + j : begin + j + step])
-        up = dot(x, up_ref[:, begin + j : begin + j + step])
-        out_ref[:, j : j + step] = (gate / (1.0 + jnp.exp(-gate)) * up).astype(jnp.bfloat16)
-
-
-def first_hidden_kernel(pieces, slots, *refs):
-    piece_refs = refs[:pieces]
-    gate_ref, up_ref, x_ref, extra_ref, hidden_ref, rows_ref = refs[pieces:]
-    width = x_ref.shape[1]
+    step = min(256, out_ref.shape[1])
+    end = out_ref.shape[1]
+    for j in range(0, end, step):
+        columns = slice(begin + j, begin + min(j + step, end))
+        gate = dot(x, gate_ref[:, columns])
+        up = dot(x, up_ref[:, columns])
+        out_ref[:, j : min(j + step, end)] = (gate / (1.0 + jnp.exp(-gate)) * up).astype(jnp.bfloat16)
+
+
+def join(piece_refs, rows_ref):
     at = 0
     for first, second in zip(piece_refs[0::2], piece_refs[1::2], strict=True):
         both = [first[...].astype(jnp.float32), second[...].astype(jnp.float32)]
         size = first.shape[0] + second.shape[0]
         rows_ref[at : at + size, :] = jnp.concatenate(both, axis=0).astype(jnp.bfloat16)
         at += size
-    extra = rows_ref[:, width:]
-    extra_ref[...] = extra
-    rows = piece_refs[0].shape[0]
-    place = slot_matrix(extra, own_offset(rows)).T[:slots].astype(jnp.bfloat16)
-    x_ref[...] = dot(place, rows_ref[:, :width]).astype(jnp.bfloat16)
+
+
+def placed(rows_ref, width, piece_rows, blocks, cap, slots):
+    block_rows = rows_ref.shape[0] // len(blocks)
+    place = slot_matrix(rows_ref[:, width:], own_offset(piece_rows), block_rows, blocks, cap)
+    return dot(place.T[:slots].astype(jnp.bfloat16), rows_ref[:, :width])
+
+
+def pack_kernel(pieces, blocks, cap, *refs):
+    x_ref, extra_ref, rows_ref = refs[pieces:]
+    slots, width = x_ref.shape
+    join(refs[:pieces], rows_ref)
+    extra_ref[...] = rows_ref[:, width:]
+    x_ref[...] = placed(rows_ref, width, refs[0].shape[0], blocks, cap, slots).astype(jnp.bfloat16)
+
+
+def first_hidden_kernel(pieces, blocks, cap, *refs):
+    packed_ref, gate_ref, up_ref, x_ref, extra_ref, hidden_ref, rows_ref = refs[pieces:]
+    slots, width = x_ref.shape
+    join(refs[:pieces], rows_ref)
+    extra_ref[...] = rows_ref[:, width:]
+    late = placed(rows_ref, width, refs[0].shape[0], blocks, cap, slots)
+    x_ref[...] = (packed_ref[...].astype(jnp.float32) + late).astype(jnp.bfloat16)
     hidden_columns(x_ref[...], gate_ref, up_ref, hidden_ref, 0)
 
 
@@ -275,7 +289,7 @@
     total = None
     for hidden_ref, flip, begin in sources:
         height = hidden_ref.shape[1]
-        at = pl.multiple_of((sub ^ flip) * own_width + begin, 256)
+        at = pl.multiple_of((sub ^ flip) * own_width + begin, 128)
         part = dot(hidden_ref[...], down_ref[pl.ds(at, height), :])
         total = part if total is None else total + part
     return total
@@ -292,37 +306,52 @@
     rest[-1][...] = total
 
 
-def last_down_kernel(flips, own_width, rows, *refs):
+def return_kernel(rows, order, cap, *refs):
+    *extra_refs, x_ref, router_ref, spread_ref, share_ref = refs
+    slots = share_ref.shape[0]
+    extra = jnp.concatenate([ref[...] for ref in extra_refs], axis=0)
+    here = slot_matrix(extra, own_offset(rows), extra.shape[0] // len(order), order, cap)
+    spread_ref[...] = here.astype(jnp.bfloat16)
+    routed = dot(here.T[:slots].astype(jnp.bfloat16), extra)[:, :EXPERTS] > 0.5
+    logits = dot_nt(x_ref[...], router_ref[...])
+    mine = lax.broadcasted_iota(jnp.int32, logits.shape, 1) == lax.axis_index("dev")
+    own_logit = jnp.sum(jnp.where(mine, logits, 0.0), axis=1, keepdims=True)
+    other_logit = jnp.sum(jnp.where(routed & ~mine, logits, 0.0), axis=1, keepdims=True)
+    share = 1.0 / (1.0 + jnp.exp(other_logit - own_logit))
+    share_ref[...] = jnp.broadcast_to(share, share_ref.shape)
+
+
+def last_down_kernel(flips, own_width, *refs):
     count = len(flips)
     hidden_refs = refs[:count]
-    down_ref, total_ref, extra_ref, out_ref = refs[count:]
+    down_ref, total_ref, spread_ref, share_ref, *out_refs = refs[count:]
     sources = [(r, f, b) for r, (f, b) in zip(hidden_refs, flips, strict=True)]
     slots = total_ref.shape[0]
-    offset = own_offset(rows)
-    extra = extra_ref[...]
-    tokens = extra.shape[0]
-    here = slot_matrix(extra, offset)
-    lane = lax.broadcasted_iota(jnp.int32, (tokens, EXTRA), 1)
-    dev = lax.axis_index("dev")
-    mine = (lane == EXPERTS + dev) | (lane == 2 * EXPERTS + dev)
-    shares = jnp.where(mine, extra.astype(jnp.float32), 0.0).astype(jnp.bfloat16)
-    by_slot = dot(here.T[:slots].astype(jnp.bfloat16), shares)
-    share = jnp.sum(by_slot, axis=1, keepdims=True)
-    token = lax.broadcasted_iota(jnp.int32, (tokens, tokens), 0)
-    moved = (token ^ offset) == lax.broadcasted_iota(jnp.int32, (tokens, tokens), 1)
-    spread = dot(moved.astype(jnp.bfloat16), here.astype(jnp.bfloat16)).astype(jnp.bfloat16)
     total = total_ref[...] + down_part(sources, down_ref, own_width)
-    out_ref[...] = dot(spread[:, :slots], (total * share).astype(jnp.bfloat16)).astype(jnp.bfloat16)
-
-
-def finish_kernel(resid_ref, arrived_ref, out_ref):
-    subs, devs = lax.axis_size("sub"), lax.axis_size("dev")
-    width = arrived_ref.shape[2]
-    for s in range(subs):
-        lanes = slice(s * width, (s + 1) * width)
-        mixture = arrived_ref[s].astype(jnp.float32)
-        for d in range(1, devs):
-            mixture = mixture + arrived_ref[d * subs + s].astype(jnp.float32)
+    weighted = (total * share_ref[:, :1]).astype(jnp.bfloat16)
+    result = dot(spread_ref[:, :slots], weighted).astype(jnp.bfloat16)
+    height = out_refs[0].shape[0]
+    for k, out_ref in enumerate(out_refs):
+        out_ref[...] = result[k * height : (k + 1) * height]
+
+
+def collect_kernel(rows, *refs):
+    parts, (own_ref, *out_refs) = refs[:-4], refs[-4:]
+    total = parts[0][...].astype(jnp.float32)
+    for part in parts[1:]:
+        total = total + part[...].astype(jnp.float32)
+    own_ref[...] = total[:rows]
+    for i, out_ref in enumerate(out_refs):
+        out_ref[...] = total[(i + 1) * rows : (i + 2) * rows].astype(jnp.bfloat16)
+
+
+def finish_kernel(resid_ref, *refs):
+    *mixture_refs, out_ref = refs
+    width = mixture_refs[0].shape[1]
+    sub = lax.axis_index("sub")
+    for bits, mixture_ref in enumerate(mixture_refs):
+        lanes = pl.ds(pl.multiple_of((sub ^ bits) * width, 128), width)
+        mixture = mixture_ref[...].astype(jnp.float32)
         out_ref[:, lanes] = (resid_ref[:, lanes].astype(jnp.float32) + mixture).astype(jnp.bfloat16)
 
 
@@ -346,7 +375,8 @@
     rows, width = tokens.shape
     devs, subs = lax.axis_size("dev"), lax.axis_size("sub")
     all_rows = rows * devs * subs
-    slots = devs * (5 * rows * subs // 6)
+    cap = 5 * rows * subs // 6
+    slots = devs * cap
     own_hidden = gate_weight.shape[1]
     out_width = down_weight.shape[1]
     bf16 = jnp.bfloat16
@@ -367,7 +397,6 @@
         request_value_cache,
         tokens,
         norm_gain,
-        router_weight.T,
     )
     payload, resid = call(
         attention_kernel,
@@ -376,83 +405,124 @@
             jax.ShapeDtypeStruct((rows, width), bf16),
         ),
         operands,
-        [VMEM_SPEC, SMEM_SPEC, SMEM_SPEC] + [VMEM_SPEC] * 6,
-        flops=30 * 10**9,
+        [VMEM_SPEC, SMEM_SPEC, SMEM_SPEC] + [VMEM_SPEC] * 5,
+        flops=ATTENTION_FLOPS,
         bytes_accessed=100 * MIB,
         vmem=8 * MIB,
         scratch=[pltpu.VMEM((rows, width), jnp.float32)],
     )
-    over_z = [payload] + [flip(payload, "dev", k) for k in (1, 2, 3)]
+    over_z = [payload] + [flip(payload, "dev", k) for k in range(1, devs)]
     over_x = [flip(p, "sub", 2) for p in over_z]
-    over_core = [[flip(p, "sub", 1) for p in group] for group in (over_z, over_x)]
-    pieces = []
-    for k in range(devs):
-        pieces += [over_z[k], over_core[0][k], over_x[k], over_core[1][k]]
-    half = own_hidden // 2
-    x, extra, hidden_a = call(
-        lambda *refs: first_hidden_kernel(len(pieces), slots, *refs),
+    pieces = [[z, flip(z, "sub", 1), x, flip(x, "sub", 1)] for z, x in zip(over_z, over_x, strict=True)]
+    unit = own_hidden // 16
+    widths = [unit * n for n in CHUNKS]
+    begins = [sum(widths[:i]) for i in range(len(widths))]
+    chunks = len(widths)
+    early = [p for k in EARLY for p in pieces[k]]
+    block_rows = all_rows // devs
+    early_rows = block_rows * len(EARLY)
+    packed, extra_early = call(
+        functools.partial(pack_kernel, len(early), EARLY, cap),
         (
             jax.ShapeDtypeStruct((slots, width), bf16),
+            jax.ShapeDtypeStruct((early_rows, EXTRA), bf16),
+        ),
+        early,
+        [VMEM_SPEC] * len(early),
+        flops=PACK_FLOPS,
+        vmem=6 * MIB,
+        scratch=[pltpu.VMEM((early_rows, width + EXTRA), bf16)],
+    )
+    late = [p for k in LATE for p in pieces[k]]
+    late_rows = block_rows * len(LATE)
+    x, extra_late, hidden = call(
+        functools.partial(first_hidden_kernel, len(late), LATE, cap),
+        (
+            jax.ShapeDtypeStruct((slots, width), bf16),
+            jax.ShapeDtypeStruct((late_rows, EXTRA), bf16),
+            jax.ShapeDtypeStruct((slots, widths[0]), bf16),
+        ),
+        (*late, packed, gate_weight, up_weight),
+        [VMEM_SPEC] * (len(late) + 3),
+        flops=GATE_FLOPS,
+        vmem=6 * MIB,
+        scratch=[pltpu.VMEM((late_rows, width + EXTRA), bf16)],
+    )
+    own = [hidden]
+    for i in range(1, chunks):
+        own.append(
+            call(
+                functools.partial(next_hidden_kernel, begins[i]),
+                jax.ShapeDtypeStruct((slots, widths[i]), bf16),
+                (x, gate_weight, up_weight),
+                [VMEM_SPEC] * 3,
+                flops=GATE_FLOPS,
+                vmem=4 * MIB,
+            )
+        )
+    far = [flip(h, "sub", 2) for h in own]
+    near = [flip(h, "sub", 1) for h in own]
+    across = [flip(h, "sub", 1) for h in far]
+    spread, share = call(
+        functools.partial(return_kernel, rows, (*EARLY, *LATE), cap),
+        (
             jax.ShapeDtypeStruct((all_rows, EXTRA), bf16),
-            jax.ShapeDtypeStruct((slots, half), bf16),
+            jax.ShapeDtypeStruct((slots, EXTRA), jnp.float32),
         ),
-        (*pieces, gate_weight, up_weight),
-        [VMEM_SPEC] * (len(pieces) + 2),
-        flops=2 * 10**9,
-        vmem=6 * MIB,
-        scratch=[pltpu.VMEM((all_rows, width + EXTRA), bf16)],
-    )
-    hidden_b = call(
-        lambda *refs: next_hidden_kernel(half, *refs),
-        jax.ShapeDtypeStruct((slots, own_hidden - half), bf16),
-        (x, gate_weight, up_weight),
-        [VMEM_SPEC] * 3,
-        flops=2 * 10**9,
+        (extra_early, extra_late, x, router_weight.T),
+        [VMEM_SPEC] * 4,
+        flops=DOWN_FLOPS,
         vmem=4 * MIB,
     )
-    far_a, near_a = flip(hidden_a, "sub", 2), flip(hidden_a, "sub", 1)
-    far_b, near_b = flip(hidden_b, "sub", 2), flip(hidden_b, "sub", 1)
-    across_a, across_b = flip(far_a, "sub", 1), flip(far_b, "sub", 1)
     total_shape = jax.ShapeDtypeStruct((slots, out_width), jnp.float32)
-    flips = ((0, 0), (0, half), (1, 0), (1, half))
-    total = call(
-        lambda *refs: down_kernel(flips, own_hidden, False, *refs),
-        total_shape,
-        (hidden_a, hidden_b, near_a, near_b, down_weight),
-        [VMEM_SPEC] * 5,
-        flops=10**9,
+    total = None
+    for i in range(chunks):
+        taken = [near[i], far[i], across[i]]
+        flips = [(1, begins[i]), (2, begins[i]), (3, begins[i])]
+        if i < chunks - 1:
+            taken.append(own[i])
+            flips.append((0, begins[i]))
+        if i == chunks - 2:
+            taken.append(own[i + 1])
+            flips.append((0, begins[i + 1]))
+        before = () if total is None else (total,)
+        if i < chunks - 1:
+            total = call(
+                functools.partial(down_kernel, flips, own_hidden, i > 0),
+                total_shape,
+                (*taken, down_weight, *before),
+                [VMEM_SPEC] * (len(taken) + 1 + len(before)),
+                flops=DOWN_FLOPS,
+                vmem=4 * MIB,
+            )
+        else:
+            weighted = call(
+                functools.partial(last_down_kernel, flips, own_hidden),
+                (jax.ShapeDtypeStruct((all_rows // devs, out_width), bf16),) * devs,
+                (*taken, down_weight, total, spread, share),
+                [VMEM_SPEC] * (len(taken) + 4),
+                flops=DOWN_FLOPS,
+                vmem=4 * MIB,
+            )
+    weighted = dict(zip((*EARLY, *LATE), weighted, strict=True))
+    arrived = [weighted[0]] + [flip(weighted[k], "dev", k) for k in Z_ORDER]
+    mixed, to_near, to_far, to_across = call(
+        functools.partial(collect_kernel, rows),
+        (jax.ShapeDtypeStruct((rows, out_width), jnp.float32),)
+        + (jax.ShapeDtypeStruct((rows, out_width), bf16),) * 3,
+        arrived,
+        [VMEM_SPEC] * devs,
+        flops=10**6,
         vmem=4 * MIB,
     )
-    flips_a = ((2, 0), (3, 0))
-    total = call(
-        lambda *refs: down_kernel(flips_a, own_hidden, True, *refs),
-        total_shape,
-        (far_a, across_a, down_weight, total),
-        [VMEM_SPEC] * 4,
-        flops=10**9,
-        vmem=4 * MIB,
-    )
-    flips_b = ((2, half), (3, half))
-    weighted = call(
-        lambda *refs: last_down_kernel(flips_b, own_hidden, rows, *refs),
-        jax.ShapeDtypeStruct((all_rows, out_width), bf16),
-        (far_b, across_b, down_weight, total, extra),
-        [VMEM_SPEC] * 5,
-        flops=10**9,
-        vmem=4 * MIB,
-    )
-    arrived = lax.all_to_all(
-        weighted.reshape(devs * subs, rows, out_width),
-        ("dev", "sub"),
-        split_axis=0,
-        concat_axis=0,
-        tiled=True,
-    )
+    from_across = flip(flip(to_across, "sub", 1), "sub", 2)
+    from_near = flip(to_near, "sub", 1)
+    from_far = flip(to_far, "sub", 2)
     return call(
         finish_kernel,
         jax.ShapeDtypeStruct((rows, width), bf16),
-        (resid, arrived),
-        [VMEM_SPEC] * 2,
+        (resid, mixed, from_near, from_far, from_across),
+        [VMEM_SPEC] * 5,
         flops=10**6,
         vmem=4 * MIB,
     )

time: 53.4 us -> 51.7 us (0.968)
  blocking collectives: 13.5 us -> 0 us
  starting transfers between devices: 15.1 us -> 24.5 us
  Pallas kernels: 10.9 us -> 12.1 us
  waiting for transfers between devices: 11.9 us -> 13.1 us
    all_to_all x1 -> x0, blocking collectives: 13.5 us -> none  [per_device(): lax.all_to_all(weighted.reshape(devs * subs, rows, out_width), ('dev', 's...]
    ppermute x21 -> x34, starting transfers between devices: 15.1 us -> 24.5 us  [flip(): lax.ppermute(x, axis, [(i, i ^ bits) for i in range(lax.axis_size(axis))])]
    ppermute x21 -> x34, waiting for transfers between devices: 11.9 us -> 13.1 us  [flip(): lax.ppermute(x, axis, [(i, i ^ bits) for i in range(lax.axis_size(axis))])]
    pallas_call x8 -> x14, Pallas kernels: 10.9 us -> 12.1 us  [call(): pl.pallas_call(body, out_shape=out_shapes, in_specs=specs, out_specs=jax....]
  transfers between devices with their start and end apart: 21 -> 34, of which waited for: 6 -> 11; matrix products, arithmetic and copies ran while one was open for 0% -> 0% of each run, Pallas kernels for 7% -> 13%
where the time goes in v3:
time: 51.7 us; the launch traced here: 51.6 us
  starting transfers between devices  24.5 us (47%)
  waiting for transfers between devices  13.1 us (25%)
  Pallas kernels  12.1 us (23%)
  local copies, waits for them, and re-layouts  1.61 us (3%)
    ppermute x34, starting transfers between devices, flip(): lax.ppermute(x, axis, [(i, i ^ bits) for i in range(lax.axis_size(axis))])  24.5 us
    ppermute x34, waiting for transfers between devices, flip(): lax.ppermute(x, axis, [(i, i ^ bits) for i in range(lax.axis_size(axis))])  13.1 us
    pallas_call x14, Pallas kernels, call(): pl.pallas_call(body, out_shape=out_shapes, in_specs=specs, out_specs=jax....  12.1 us
    unnamed x34, local copies, waits for them, and re-layouts  1.61 us
  transfers between devices with their start and end apart: 34, of which 11 were waited for; matrix products, arithmetic and copies ran while one was open for 0% of the time, Pallas kernels for 13%

profile of v3, /device:TPU:0, one launch (start us, length us, event | category | flops | bytes accessed | tf_op | source)
XLA Modules:
  0.0 51.6 jit_solution(9231213259396100390)
XLA Ops:
  0.1 0.6 %copy-done.6 = s32[32,2]{0,1:T(2,128)S(1)} copy-done((s32[32,2]{0,1:T(2,128)S(1)}, s32[32,2]{0,1:T(2,128)}, u32[]{:S(2)}) %copy-start.6) | copy-done | bytes 280
  0.7 0.1 copy-done.3
  0.8 0.5 copy-done
  1.3 0.3 copy-done.1
  1.7 2.4 %shard_map.110 = (bf16[8,3200]{1,0:T(8,128)(2,1)S(1)}, bf16[8,3072]{1,0:T(8,128)(2,1)S(1)}) custom-call(f32[8,128]{1,0:T(8,128)S(1)} %shard_map.109._, s32[8]{0:T(128)S(1)} %copy-done.7, s32[2,32]{1,0:T(2,128)S(1)} %bitcast.9, bf16[8,3072]{1,0:T(8,128)(2,1)S(1)} %copy-done.2, bf16[8,128,512]{2,1,0:T(8,128)(2,1)S(1)} %copy-done, ...), custom_call_target="tpu_custom_call" | custom-call | flops 30000001024 | bytes 104857600 | tf_op jit(solution)/shard_map/pallas_call | solution.py:136
  4.1 3.1 %collective-permute-start.7 = (bf16[8,3200]{1,0:T(8,128)(2,1)S(1)}, bf16[8,3200]{1,0:T(8,128)(2,1)S(1)}, u32[]{:S(2)}, u32[]{:S(2)}) collective-permute-start(bf16[8,3200]{1,0:T(8,128)(2,1)S(1)} %get-tuple-element.23.refs_0_), channel_id=1, source_target_pairs={{0,4},{4,0},{8,12},{12,8},{1,5},{5,1},{9,13},{13,9},{2,6},{6,2},{1... | collective-permute-start | bytes 153608 | tf_op jit(solution)/shard_map/ppermute | solution.py:359
  7.2 2.5 %collective-permute-start.11 = (bf16[8,3200]{1,0:T(8,128)(2,1)S(1)}, bf16[8,3200]{1,0:T(8,128)(2,1)S(1)}, u32[]{:S(2)}, u32[]{:S(2)}) collective-permute-start(bf16[8,3200]{1,0:T(8,128)(2,1)S(1)} %get-tuple-element.23.refs_0_), channel_id=1, source_target_pairs={{0,12},{4,8},{8,4},{12,0},{1,13},{5,9},{9,5},{13,1},{2,14},{6,10},... | collective-permute-start | bytes 153608 | tf_op jit(solution)/shard_map/ppermute | solution.py:359
  9.8 1.5 %collective-permute-start.1 = (bf16[8,3200]{1,0:T(8,128)(2,1)S(1)}, bf16[8,3200]{1,0:T(8,128)(2,1)S(1)}, u32[]{:S(2)}, u32[]{:S(2)}) collective-permute-start(bf16[8,3200]{1,0:T(8,128)(2,1)S(1)} %get-tuple-element.23.refs_0_), channel_id=1, source_target_pairs={{0,2},{1,3},{2,0},{3,1},{4,6},{5,7},{6,4},{7,5},{8,10},{9,11},{10,... | collective-permute-start | bytes 153608 | tf_op jit(solution)/shard_map/ppermute | solution.py:359
  11.3 0.5 %collective-permute-start.9 = (bf16[8,3200]{1,0:T(8,128)(2,1)S(1)}, bf16[8,3200]{1,0:T(8,128)(2,1)S(1)}, u32[]{:S(2)}, u32[]{:S(2)}) collective-permute-start(bf16[8,3200]{1,0:T(8,128)(2,1)S(1)} %collective-permute-done.7.refs_0_), channel_id=1, source_target_pairs={{0,2},{1,3},{2,0},{3,1},{4,6},{5,7},{6,4},{7,5},{8,10},{9,11},{10,... | collective-permute-start | bytes 153608 | tf_op jit(solution)/shard_map/ppermute | solution.py:359
  11.8 1.9 %collective-permute-done.11.refs_4_ = bf16[8,3200]{1,0:T(8,128)(2,1)S(1)} collective-permute-done((bf16[8,3200]{1,0:T(8,128)(2,1)S(1)}, bf16[8,3200]{1,0:T(8,128)(2,1)S(1)}, u32[]{:S(2)}, u32[]{:S(2)}) %collective-permute-start.11) | collective-permute-done | bytes 51232 | tf_op jit(solution)/shard_map/ppermute | solution.py:359
  13.7 1.5 %collective-permute-start.13 = (bf16[8,3200]{1,0:T(8,128)(2,1)S(1)}, bf16[8,3200]{1,0:T(8,128)(2,1)S(1)}, u32[]{:S(2)}, u32[]{:S(2)}) collective-permute-start(bf16[8,3200]{1,0:T(8,128)(2,1)S(1)} %collective-permute-done.11.refs_4_), channel_id=1, source_target_pairs={{0,2},{1,3},{2,0},{3,1},{4,6},{5,7},{6,4},{7,5},{8,10},{9,11},{10,... | collective-permute-start | bytes 153608 | tf_op jit(solution)/shard_map/ppermute | solution.py:359
  15.2 0.5 collective-permute-start.8
  15.8 1.0 %collective-permute-start.5 = (bf16[8,3200]{1,0:T(8,128)(2,1)S(1)}, bf16[8,3200]{1,0:T(8,128)(2,1)S(1)}, u32[]{:S(2)}, u32[]{:S(2)}) collective-permute-start(bf16[8,3200]{1,0:T(8,128)(2,1)S(1)} %collective-permute-done.3.refs_4_), channel_id=1, source_target_pairs={{0,2},{1,3},{2,0},{3,1},{4,6},{5,7},{6,4},{7,5},{8,10},{9,11},{10,... | collective-permute-start | bytes 153608 | tf_op jit(solution)/shard_map/ppermute | solution.py:359
  16.7 0.2 collective-permute-start.10
  16.9 0.9 %collective-permute-done.13.refs_6_ = bf16[8,3200]{1,0:T(8,128)(2,1)S(1)} collective-permute-done((bf16[8,3200]{1,0:T(8,128)(2,1)S(1)}, bf16[8,3200]{1,0:T(8,128)(2,1)S(1)}, u32[]{:S(2)}, u32[]{:S(2)}) %collective-permute-start.13) | collective-permute-done | bytes 51232 | tf_op jit(solution)/shard_map/ppermute | solution.py:359
  17.9 0.5 collective-permute-start
  18.4 1.4 %collective-permute-done.5.refs_6_ = bf16[8,3200]{1,0:T(8,128)(2,1)S(1)} collective-permute-done((bf16[8,3200]{1,0:T(8,128)(2,1)S(1)}, bf16[8,3200]{1,0:T(8,128)(2,1)S(1)}, u32[]{:S(2)}, u32[]{:S(2)}) %collective-permute-start.5) | collective-permute-done | bytes 51232 | tf_op jit(solution)/shard_map/ppermute | solution.py:359
  19.9 0.5 collective-permute-start.6
  20.4 0.6 %shard_map.111 = (bf16[104,3072]{1,0:T(8,128)(2,1)S(1)}, bf16[64,128]{1,0:T(8,128)(2,1)S(1)}) custom-call(bf16[8,3200]{1,0:T(8,128)(2,1)S(1)} %collective-permute-done.7.refs_0_, bf16[8,3200]{1,0:T(8,128)(2,1)S(1)} %collective-permute-done.8.refs_1_, bf16[8,3200]{1,0:T(8,128)(2,1)S(1)} %collective-permute-done.9.refs_2_, ...), custom_call_target="tpu_custom_call" | custom-call | flops 100000000 | tf_op jit(solution)/shard_map/pallas_call | solution.py:136
  21.1 0.2 collective-permute-done.6.refs_7_
  21.3 1.6 %shard_map.112 = (bf16[104,3072]{1,0:T(8,128)(2,1)S(1)}, bf16[64,128]{1,0:T(8,128)(2,1)S(1)}, bf16[104,512]{1,0:T(8,128)(2,1)S(1)}) custom-call(bf16[8,3200]{1,0:T(8,128)(2,1)S(1)} %get-tuple-element.23.refs_0_, bf16[8,3200]{1,0:T(8,128)(2,1)S(1)} %collective-permute-done.refs_1_, bf16[8,3200]{1,0:T(8,128)(2,1)S(1)} %collective-permute-done.1.refs_2_, ...), custom_call_target="tpu_custom_call" | custom-call | flops 1000000000 | tf_op jit(solution)/shard_map/pallas_call | solution.py:136
  22.9 1.1 %collective-permute-start.25 = (bf16[104,512]{1,0:T(8,128)(2,1)S(1)}, bf16[104,512]{1,0:T(8,128)(2,1)S(1)}, u32[]{:S(2)}, u32[]{:S(2)}) collective-permute-start(bf16[104,512]{1,0:T(8,128)(2,1)S(1)} %get-tuple-element.26.refs_3_), channel_id=1, source_target_pairs={{0,2},{1,3},{2,0},{3,1},{4,6},{5,7},{6,4},{7,5},{8,10},{9,11},{10,... | collective-permute-start | bytes 319496 | tf_op jit(solution)/shard_map/ppermute | solution.py:359
  24.1 1.2 %shard_map.115.refs_3_ = bf16[104,512]{1,0:T(8,128)(2,1)S(1)} custom-call(bf16[104,3072]{1,0:T(8,128)(2,1)S(1)} %get-tuple-element.25.x_ref.refs_2_, bf16[3072,2048]{1,0:T(8,128)(2,1)S(1)} %bitcast.5, bf16[3072,2048]{1,0:T(8,128)(2,1)S(1)} %bitcast.7), custom_call_target="tpu_custom_call" | custom-call | flops 1000000000 | tf_op jit(solution)/shard_map/pallas_call | solution.py:136
  25.3 1.0 %collective-permute-start.22 = (bf16[104,512]{1,0:T(8,128)(2,1)S(1)}, bf16[104,512]{1,0:T(8,128)(2,1)S(1)}, u32[]{:S(2)}, u32[]{:S(2)}) collective-permute-start(bf16[104,512]{1,0:T(8,128)(2,1)S(1)} %shard_map.115.refs_3_), channel_id=1, source_target_pairs={{0,2},{1,3},{2,0},{3,1},{4,6},{5,7},{6,4},{7,5},{8,10},{9,11},{10,... | collective-permute-start | bytes 319496 | tf_op jit(solution)/shard_map/ppermute | solution.py:359
  26.3 0.2 collective-permute-start.21
  26.5 1.2 %shard_map.114.refs_3_ = bf16[104,512]{1,0:T(8,128)(2,1)S(1)} custom-call(bf16[104,3072]{1,0:T(8,128)(2,1)S(1)} %get-tuple-element.25.x_ref.refs_2_, bf16[3072,2048]{1,0:T(8,128)(2,1)S(1)} %bitcast.5, bf16[3072,2048]{1,0:T(8,128)(2,1)S(1)} %bitcast.7), custom_call_target="tpu_custom_call" | custom-call | flops 1000000000 | tf_op jit(solution)/shard_map/pallas_call | solution.py:136
  27.6 1.1 %collective-permute-start.19 = (bf16[104,512]{1,0:T(8,128)(2,1)S(1)}, bf16[104,512]{1,0:T(8,128)(2,1)S(1)}, u32[]{:S(2)}, u32[]{:S(2)}) collective-permute-start(bf16[104,512]{1,0:T(8,128)(2,1)S(1)} %shard_map.114.refs_3_), channel_id=1, source_target_pairs={{0,2},{1,3},{2,0},{3,1},{4,6},{5,7},{6,4},{7,5},{8,10},{9,11},{10,... | collective-permute-start | bytes 319496 | tf_op jit(solution)/shard_map/ppermute | solution.py:359
  28.9 1.2 %shard_map.113.refs_4_ = bf16[104,512]{1,0:T(8,128)(2,1)S(1)} custom-call(bf16[104,3072]{1,0:T(8,128)(2,1)S(1)} %get-tuple-element.25.x_ref.refs_2_, bf16[3072,2048]{1,0:T(8,128)(2,1)S(1)} %bitcast.5, bf16[3072,2048]{1,0:T(8,128)(2,1)S(1)} %bitcast.7), custom_call_target="tpu_custom_call" | custom-call | flops 1000000000 | tf_op jit(solution)/shard_map/pallas_call | solution.py:136
  30.0 1.0 %collective-permute-start.16 = (bf16[104,512]{1,0:T(8,128)(2,1)S(1)}, bf16[104,512]{1,0:T(8,128)(2,1)S(1)}, u32[]{:S(2)}, u32[]{:S(2)}) collective-permute-start(bf16[104,512]{1,0:T(8,128)(2,1)S(1)} %shard_map.113.refs_4_), channel_id=1, source_target_pairs={{0,2},{1,3},{2,0},{3,1},{4,6},{5,7},{6,4},{7,5},{8,10},{9,11},{10,... | collective-permute-start | bytes 319496 | tf_op jit(solution)/shard_map/ppermute | solution.py:359
  31.1 0.2 collective-permute-start.23
  31.2 0.7 %shard_map.119 = (bf16[128,128]{1,0:T(8,128)(2,1)S(1)}, f32[104,128]{1,0:T(8,128)S(1)}) custom-call(bf16[64,128]{1,0:T(8,128)(2,1)S(1)} %get-tuple-element.27.refs_0_, bf16[64,128]{1,0:T(8,128)(2,1)S(1)} %get-tuple-element.28.refs_1_, bf16[104,3072]{1,0:T(8,128)(2,1)S(1)} %get-tuple-element.25.x_ref.refs_2_, bf16[4,3072]{1,0:T(4,128)(2,1)S(1)} %bitcast.8), custom_call_target="tpu_custom_call" | custom-call | flops 1000000000 | tf_op jit(solution)/shard_map/pallas_call | solution.py:136
  31.9 1.0 %collective-permute-done.19.refs_1_ = bf16[104,512]{1,0:T(8,128)(2,1)S(1)} collective-permute-done((bf16[104,512]{1,0:T(8,128)(2,1)S(1)}, bf16[104,512]{1,0:T(8,128)(2,1)S(1)}, u32[]{:S(2)}, u32[]{:S(2)}) %collective-permute-start.19) | collective-permute-done | bytes 106528 | tf_op jit(solution)/shard_map/ppermute | solution.py:359
  33.0 0.5 collective-permute-start.20
  33.5 0.6 %shard_map.116.refs_5_ = f32[104,768]{1,0:T(8,128)S(1)} custom-call(bf16[104,512]{1,0:T(8,128)(2,1)S(1)} %collective-permute-done.24.refs_0_, bf16[104,512]{1,0:T(8,128)(2,1)S(1)} %collective-permute-done.25.refs_1_, bf16[104,512]{1,0:T(8,128)(2,1)S(1)} %collective-permute-done.26.refs_2_, bf16[104,512]{1,0:T(8,128)(2,1)S(1)} %get-tuple-element.26.refs_3_, ...), custom_call_target="tpu_custom_call" | custom-call | flops 1000000000 | tf_op jit(solution)/shard_map/pallas_call | solution.py:136
  34.2 1.2 %collective-permute-done.16.refs_1_ = bf16[104,512]{1,0:T(8,128)(2,1)S(1)} collective-permute-done((bf16[104,512]{1,0:T(8,128)(2,1)S(1)}, bf16[104,512]{1,0:T(8,128)(2,1)S(1)}, u32[]{:S(2)}, u32[]{:S(2)}) %collective-permute-start.16) | collective-permute-done | bytes 106528 | tf_op jit(solution)/shard_map/ppermute | solution.py:359
  35.4 0.6 %shard_map.117.refs_6_ = f32[104,768]{1,0:T(8,128)S(1)} custom-call(bf16[104,512]{1,0:T(8,128)(2,1)S(1)} %collective-permute-done.21.refs_0_, bf16[104,512]{1,0:T(8,128)(2,1)S(1)} %collective-permute-done.22.refs_1_, bf16[104,512]{1,0:T(8,128)(2,1)S(1)} %collective-permute-done.23.refs_2_, bf16[104,512]{1,0:T(8,128)(2,1)S(1)} %shard_map.115.refs_3_, ...), custom_call_target="tpu_custom_call" | custom-call | flops 1000000000 | tf_op jit(solution)/shard_map/pallas_call | solution.py:136
  36.0 0.7 %shard_map.118.refs_4_ = f32[104,768]{1,0:T(8,128)S(1)} custom-call(bf16[104,512]{1,0:T(8,128)(2,1)S(1)} %collective-permute-done.18.refs_0_, bf16[104,512]{1,0:T(8,128)(2,1)S(1)} %collective-permute-done.19.refs_1_, bf16[104,512]{1,0:T(8,128)(2,1)S(1)} %collective-permute-done.20.refs_2_, bf16[104,512]{1,0:T(8,128)(2,1)S(1)} %shard_map.114.refs_3_, ...), custom_call_target="tpu_custom_call" | custom-call | flops 1000000000 | tf_op jit(solution)/shard_map/pallas_call | solution.py:136
  36.8 0.7 %shard_map.120 = (bf16[32,768]{1,0:T(8,128)(2,1)S(1)}, bf16[32,768]{1,0:T(8,128)(2,1)S(1)}, bf16[32,768]{1,0:T(8,128)(2,1)S(1)}, bf16[32,768]{1,0:T(8,128)(2,1)S(1)}) custom-call(bf16[104,512]{1,0:T(8,128)(2,1)S(1)} %collective-permute-done.15.refs_0_, bf16[104,512]{1,0:T(8,128)(2,1)S(1)} %collective-permute-done.16.refs_1_, ...), custom_call_target="tpu_custom_call" | custom-call | flops 1000000000 | tf_op jit(solution)/shard_map/pallas_call | solution.py:136
  37.5 2.3 %collective-permute-start.27 = (bf16[32,768]{1,0:T(8,128)(2,1)S(1)}, bf16[32,768]{1,0:T(8,128)(2,1)S(1)}, u32[]{:S(2)}, u32[]{:S(2)}) collective-permute-start(bf16[32,768]{1,0:T(8,128)(2,1)S(1)} %get-tuple-element.32), channel_id=1, source_target_pairs={{0,12},{4,8},{8,4},{12,0},{1,13},{5,9},{9,5},{13,1},{2,14},{6,10},... | collective-permute-start | bytes 147464 | tf_op jit(solution)/shard_map/ppermute | solution.py:359
  39.8 2.2 %collective-permute-start.29 = (bf16[32,768]{1,0:T(8,128)(2,1)S(1)}, bf16[32,768]{1,0:T(8,128)(2,1)S(1)}, u32[]{:S(2)}, u32[]{:S(2)}) collective-permute-start(bf16[32,768]{1,0:T(8,128)(2,1)S(1)} %get-tuple-element.34), channel_id=1, source_target_pairs={{0,4},{4,0},{8,12},{12,8},{1,5},{5,1},{9,13},{13,9},{2,6},{6,2},{1... | collective-permute-start | bytes 147464 | tf_op jit(solution)/shard_map/ppermute | solution.py:359
  42.0 1.8 %collective-permute-done.27.refs_1_ = bf16[32,768]{1,0:T(8,128)(2,1)S(1)} collective-permute-done((bf16[32,768]{1,0:T(8,128)(2,1)S(1)}, bf16[32,768]{1,0:T(8,128)(2,1)S(1)}, u32[]{:S(2)}, u32[]{:S(2)}) %collective-permute-start.27) | collective-permute-done | bytes 49184 | tf_op jit(solution)/shard_map/ppermute | solution.py:359
  43.8 1.8 %collective-permute-done.28.refs_2_ = bf16[32,768]{1,0:T(8,128)(2,1)S(1)} collective-permute-done((bf16[32,768]{1,0:T(8,128)(2,1)S(1)}, bf16[32,768]{1,0:T(8,128)(2,1)S(1)}, u32[]{:S(2)}, u32[]{:S(2)}) %collective-permute-start.28) | collective-permute-done | bytes 49184 | tf_op jit(solution)/shard_map/ppermute | solution.py:359
  45.8 0.5 collective-permute-start.30
  46.3 1.0 %collective-permute-start.31 = (bf16[8,768]{1,0:T(8,128)(2,1)S(1)}, bf16[8,768]{1,0:T(8,128)(2,1)S(1)}, u32[]{:S(2)}, u32[]{:S(2)}) collective-permute-start(bf16[8,768]{1,0:T(8,128)(2,1)S(1)} %get-tuple-element.37), channel_id=1, source_target_pairs={{0,2},{1,3},{2,0},{3,1},{4,6},{5,7},{6,4},{7,5},{8,10},{9,11},{10,... | collective-permute-start | bytes 36872 | tf_op jit(solution)/shard_map/ppermute | solution.py:359
  47.2 1.1 %collective-permute-start.33 = (bf16[8,768]{1,0:T(8,128)(2,1)S(1)}, bf16[8,768]{1,0:T(8,128)(2,1)S(1)}, u32[]{:S(2)}, u32[]{:S(2)}) collective-permute-start(bf16[8,768]{1,0:T(8,128)(2,1)S(1)} %collective-permute-done.32), channel_id=1, source_target_pairs={{0,2},{1,3},{2,0},{3,1},{4,6},{5,7},{6,4},{7,5},{8,10},{9,11},{10,... | collective-permute-start | bytes 36872 | tf_op jit(solution)/shard_map/ppermute | solution.py:359
  48.3 1.7 %collective-permute-done.31.refs_2_ = bf16[8,768]{1,0:T(8,128)(2,1)S(1)} collective-permute-done((bf16[8,768]{1,0:T(8,128)(2,1)S(1)}, bf16[8,768]{1,0:T(8,128)(2,1)S(1)}, u32[]{:S(2)}, u32[]{:S(2)}) %collective-permute-start.31) | collective-permute-done | bytes 12320 | tf_op jit(solution)/shard_map/ppermute | solution.py:359
  50.0 1.0 %collective-permute-done.33.refs_3_ = bf16[8,768]{1,0:T(8,128)(2,1)S(1)} collective-permute-done((bf16[8,768]{1,0:T(8,128)(2,1)S(1)}, bf16[8,768]{1,0:T(8,128)(2,1)S(1)}, u32[]{:S(2)}, u32[]{:S(2)}) %collective-permute-start.33) | collective-permute-done | bytes 12320 | tf_op jit(solution)/shard_map/ppermute | solution.py:359
  50.9 0.6 %shard_map.122 = bf16[8,3072]{1,0:T(8,128)(2,1)} custom-call(bf16[8,3072]{1,0:T(8,128)(2,1)S(1)} %get-tuple-element.22.resid_ref, f32[8,768]{1,0:T(8,128)S(1)} %get-tuple-element.35.refs_0_, bf16[8,768]{1,0:T(8,128)(2,1)S(1)} %collective-permute-done.30.refs_1_, bf16[8,768]{1,0:T(8,128)(2,1)S(1)} %collective-permute-done.31.refs_2_, ...), custom_call_target="tpu_custom_call" | custom-call | flops 1000000 | tf_op jit(solution)/shard_map/pallas_call | solution.py:136
  (71 shorter events, 0.8 us)
Async XLA Ops:
  0.0 1.3 %copy-start = (bf16[8,128,512]{2,1,0:T(8,128)(2,1)S(1)}, bf16[8,128,512]{2,1,0:T(8,128)(2,1)}, u32[]{:S(2)}) copy-start(bf16[8,128,512]{2,1,0:T(8,128)(2,1)} %keys_ref.1) | copy-start | bytes 3145732
  0.0 1.6 %copy-start.1 = (bf16[8,128,512]{2,1,0:T(8,128)(2,1)S(1)}, bf16[8,128,512]{2,1,0:T(8,128)(2,1)}, u32[]{:S(2)}) copy-start(bf16[8,128,512]{2,1,0:T(8,128)(2,1)} %values_ref.1) | copy-start | bytes 3145732
  0.0 1.6 %copy-start.7 = (s32[8]{0:T(128)S(1)}, s32[8]{0:T(128)}, u32[]{:S(2)}) copy-start(s32[8]{0:T(128)} %lengths_ref.1) | copy-start | bytes 100
  0.0 1.6 %copy-start.5 = (bf16[3072]{0:T(1024)(128)(2,1)S(1)}, bf16[3072]{0:T(1024)(128)(2,1)}, u32[]{:S(2)}) copy-start(bf16[3072]{0:T(1024)(128)(2,1)} %gain_ref.1) | copy-start | bytes 18436
  0.0 21.2 %slice-start.3 = ((s8[12582912]{0:T(1024)(128)(4,1)}), s8[4194304]{0:T(1024)(128)(4,1)S(1)}, s32[]{:S(2)}) async-start(s8[12582912]{0:T(1024)(128)(4,1)} %bitcast.4), calls=%async_computation.3 | async-start | bytes 8388608
  0.0 21.2 %slice-start.6 = ((s8[12582912]{0:T(1024)(128)(4,1)}), s8[4194304]{0:T(1024)(128)(4,1)S(1)}, s32[]{:S(2)}) async-start(s8[12582912]{0:T(1024)(128)(4,1)} %bitcast.6), calls=%async_computation.6 | async-start | bytes 8388608
  1.6 19.6 %slice-start.4 = ((s8[12582912]{0:T(1024)(128)(4,1)}), s8[4194304]{0:T(1024)(128)(4,1)S(1)}, s32[]{:S(2)}) async-start(s8[12582912]{0:T(1024)(128)(4,1)} %bitcast.4), calls=%async_computation.4 | async-start | bytes 8388608
  1.6 19.6 %slice-start.5 = ((s8[12582912]{0:T(1024)(128)(4,1)}), s8[4194304]{0:T(1024)(128)(4,1)S(1)}, s32[]{:S(2)}) async-start(s8[12582912]{0:T(1024)(128)(4,1)} %bitcast.4), calls=%async_computation.5 | async-start | bytes 8388608
  1.6 19.6 %slice-start.7 = ((s8[12582912]{0:T(1024)(128)(4,1)}), s8[4194304]{0:T(1024)(128)(4,1)S(1)}, s32[]{:S(2)}) async-start(s8[12582912]{0:T(1024)(128)(4,1)} %bitcast.6), calls=%async_computation.7 | async-start | bytes 8388608
  1.6 19.6 %slice-start.8 = ((s8[12582912]{0:T(1024)(128)(4,1)}), s8[4194304]{0:T(1024)(128)(4,1)S(1)}, s32[]{:S(2)}) async-start(s8[12582912]{0:T(1024)(128)(4,1)} %bitcast.6), calls=%async_computation.8 | async-start | bytes 8388608
  4.1 7.2 %collective-permute-start.7 = (bf16[8,3200]{1,0:T(8,128)(2,1)S(1)}, bf16[8,3200]{1,0:T(8,128)(2,1)S(1)}, u32[]{:S(2)}, u32[]{:S(2)}) collective-permute-start(bf16[8,3200]{1,0:T(8,128)(2,1)S(1)} %get-tuple-element.23.refs_0_), channel_id=1, source_target_pairs={{0,4},{4,0},{8,12},{12,8},{1,5},{5,1},{9,13},{13,9},{2,6},{6,2},{1... | collective-permute-start | bytes 153608 | tf_op jit(solution)/shard_map/ppermute | solution.py:359
  7.2 6.6 %collective-permute-start.11 = (bf16[8,3200]{1,0:T(8,128)(2,1)S(1)}, bf16[8,3200]{1,0:T(8,128)(2,1)S(1)}, u32[]{:S(2)}, u32[]{:S(2)}) collective-permute-start(bf16[8,3200]{1,0:T(8,128)(2,1)S(1)} %get-tuple-element.23.refs_0_), channel_id=1, source_target_pairs={{0,12},{4,8},{8,4},{12,0},{1,13},{5,9},{9,5},{13,1},{2,14},{6,10},... | collective-permute-start | bytes 153608 | tf_op jit(solution)/shard_map/ppermute | solution.py:359
  9.7 5.6 %collective-permute-start.3 = (bf16[8,3200]{1,0:T(8,128)(2,1)S(1)}, bf16[8,3200]{1,0:T(8,128)(2,1)S(1)}, u32[]{:S(2)}, u32[]{:S(2)}) collective-permute-start(bf16[8,3200]{1,0:T(8,128)(2,1)S(1)} %get-tuple-element.23.refs_0_), channel_id=1, source_target_pairs={{0,8},{4,12},{8,0},{12,4},{1,9},{5,13},{9,1},{13,5},{2,10},{6,14},... | collective-permute-start | bytes 153608 | tf_op jit(solution)/shard_map/ppermute | solution.py:359
  9.8 6.0 %collective-permute-start.1 = (bf16[8,3200]{1,0:T(8,128)(2,1)S(1)}, bf16[8,3200]{1,0:T(8,128)(2,1)S(1)}, u32[]{:S(2)}, u32[]{:S(2)}) collective-permute-start(bf16[8,3200]{1,0:T(8,128)(2,1)S(1)} %get-tuple-element.23.refs_0_), channel_id=1, source_target_pairs={{0,2},{1,3},{2,0},{3,1},{4,6},{5,7},{6,4},{7,5},{8,10},{9,11},{10,... | collective-permute-start | bytes 153608 | tf_op jit(solution)/shard_map/ppermute | solution.py:359
  11.3 5.5 %collective-permute-start.9 = (bf16[8,3200]{1,0:T(8,128)(2,1)S(1)}, bf16[8,3200]{1,0:T(8,128)(2,1)S(1)}, u32[]{:S(2)}, u32[]{:S(2)}) collective-permute-start(bf16[8,3200]{1,0:T(8,128)(2,1)S(1)} %collective-permute-done.7.refs_0_), channel_id=1, source_target_pairs={{0,2},{1,3},{2,0},{3,1},{4,6},{5,7},{6,4},{7,5},{8,10},{9,11},{10,... | collective-permute-start | bytes 153608 | tf_op jit(solution)/shard_map/ppermute | solution.py:359
  13.7 4.1 %collective-permute-start.13 = (bf16[8,3200]{1,0:T(8,128)(2,1)S(1)}, bf16[8,3200]{1,0:T(8,128)(2,1)S(1)}, u32[]{:S(2)}, u32[]{:S(2)}) collective-permute-start(bf16[8,3200]{1,0:T(8,128)(2,1)S(1)} %collective-permute-done.11.refs_4_), channel_id=1, source_target_pairs={{0,2},{1,3},{2,0},{3,1},{4,6},{5,7},{6,4},{7,5},{8,10},{9,11},{10,... | collective-permute-start | bytes 153608 | tf_op jit(solution)/shard_map/ppermute | solution.py:359
  15.2 2.6 %collective-permute-start.12 = (bf16[8,3200]{1,0:T(8,128)(2,1)S(1)}, bf16[8,3200]{1,0:T(8,128)(2,1)S(1)}, u32[]{:S(2)}, u32[]{:S(2)}) collective-permute-start(bf16[8,3200]{1,0:T(8,128)(2,1)S(1)} %collective-permute-done.11.refs_4_), channel_id=1, source_target_pairs={{0,1},{1,0},{2,3},{3,2},{4,5},{5,4},{6,7},{7,6},{8,9},{9,8},{10,11... | collective-permute-start | bytes 153608 | tf_op jit(solution)/shard_map/ppermute | solution.py:359
  15.2 3.1 %collective-permute-start.8 = (bf16[8,3200]{1,0:T(8,128)(2,1)S(1)}, bf16[8,3200]{1,0:T(8,128)(2,1)S(1)}, u32[]{:S(2)}, u32[]{:S(2)}) collective-permute-start(bf16[8,3200]{1,0:T(8,128)(2,1)S(1)} %collective-permute-done.7.refs_0_), channel_id=1, source_target_pairs={{0,1},{1,0},{2,3},{3,2},{4,5},{5,4},{6,7},{7,6},{8,9},{9,8},{10,11... | collective-permute-start | bytes 153608 | tf_op jit(solution)/shard_map/ppermute | solution.py:359
  15.8 4.1 %collective-permute-start.5 = (bf16[8,3200]{1,0:T(8,128)(2,1)S(1)}, bf16[8,3200]{1,0:T(8,128)(2,1)S(1)}, u32[]{:S(2)}, u32[]{:S(2)}) collective-permute-start(bf16[8,3200]{1,0:T(8,128)(2,1)S(1)} %collective-permute-done.3.refs_4_), channel_id=1, source_target_pairs={{0,2},{1,3},{2,0},{3,1},{4,6},{5,7},{6,4},{7,5},{8,10},{9,11},{10,... | collective-permute-start | bytes 153608 | tf_op jit(solution)/shard_map/ppermute | solution.py:359
  16.7 3.1 %collective-permute-start.10 = (bf16[8,3200]{1,0:T(8,128)(2,1)S(1)}, bf16[8,3200]{1,0:T(8,128)(2,1)S(1)}, u32[]{:S(2)}, u32[]{:S(2)}) collective-permute-start(bf16[8,3200]{1,0:T(8,128)(2,1)S(1)} %collective-permute-done.9.refs_2_), channel_id=1, source_target_pairs={{0,1},{1,0},{2,3},{3,2},{4,5},{5,4},{6,7},{7,6},{8,9},{9,8},{10,11... | collective-permute-start | bytes 153608 | tf_op jit(solution)/shard_map/ppermute | solution.py:359
  17.9 2.5 %collective-permute-start.14 = (bf16[8,3200]{1,0:T(8,128)(2,1)S(1)}, bf16[8,3200]{1,0:T(8,128)(2,1)S(1)}, u32[]{:S(2)}, u32[]{:S(2)}) collective-permute-start(bf16[8,3200]{1,0:T(8,128)(2,1)S(1)} %collective-permute-done.13.refs_6_), channel_id=1, source_target_pairs={{0,1},{1,0},{2,3},{3,2},{4,5},{5,4},{6,7},{7,6},{8,9},{9,8},{10,11... | collective-permute-start | bytes 153608 | tf_op jit(solution)/shard_map/ppermute | solution.py:359
  17.9 3.1 %collective-permute-start = (bf16[8,3200]{1,0:T(8,128)(2,1)S(1)}, bf16[8,3200]{1,0:T(8,128)(2,1)S(1)}, u32[]{:S(2)}, u32[]{:S(2)}) collective-permute-start(bf16[8,3200]{1,0:T(8,128)(2,1)S(1)} %get-tuple-element.23.refs_0_), channel_id=1, source_target_pairs={{0,1},{1,0},{2,3},{3,2},{4,5},{5,4},{6,7},{7,6},{8,9},{9,8},{10,11... | collective-permute-start | bytes 153608 | tf_op jit(solution)/shard_map/ppermute | solution.py:359
  18.4 2.6 %collective-permute-start.4 = (bf16[8,3200]{1,0:T(8,128)(2,1)S(1)}, bf16[8,3200]{1,0:T(8,128)(2,1)S(1)}, u32[]{:S(2)}, u32[]{:S(2)}) collective-permute-start(bf16[8,3200]{1,0:T(8,128)(2,1)S(1)} %collective-permute-done.3.refs_4_), channel_id=1, source_target_pairs={{0,1},{1,0},{2,3},{3,2},{4,5},{5,4},{6,7},{7,6},{8,9},{9,8},{10,11... | collective-permute-start | bytes 153608 | tf_op jit(solution)/shard_map/ppermute | solution.py:359
  19.9 1.2 %collective-permute-start.2 = (bf16[8,3200]{1,0:T(8,128)(2,1)S(1)}, bf16[8,3200]{1,0:T(8,128)(2,1)S(1)}, u32[]{:S(2)}, u32[]{:S(2)}) collective-permute-start(bf16[8,3200]{1,0:T(8,128)(2,1)S(1)} %collective-permute-done.1.refs_2_), channel_id=1, source_target_pairs={{0,1},{1,0},{2,3},{3,2},{4,5},{5,4},{6,7},{7,6},{8,9},{9,8},{10,11... | collective-permute-start | bytes 153608 | tf_op jit(solution)/shard_map/ppermute | solution.py:359
  19.9 1.4 %collective-permute-start.6 = (bf16[8,3200]{1,0:T(8,128)(2,1)S(1)}, bf16[8,3200]{1,0:T(8,128)(2,1)S(1)}, u32[]{:S(2)}, u32[]{:S(2)}) collective-permute-start(bf16[8,3200]{1,0:T(8,128)(2,1)S(1)} %collective-permute-done.5.refs_6_), channel_id=1, source_target_pairs={{0,1},{1,0},{2,3},{3,2},{4,5},{5,4},{6,7},{7,6},{8,9},{9,8},{10,11... | collective-permute-start | bytes 153608 | tf_op jit(solution)/shard_map/ppermute | solution.py:359
  22.9 5.9 %collective-permute-start.25 = (bf16[104,512]{1,0:T(8,128)(2,1)S(1)}, bf16[104,512]{1,0:T(8,128)(2,1)S(1)}, u32[]{:S(2)}, u32[]{:S(2)}) collective-permute-start(bf16[104,512]{1,0:T(8,128)(2,1)S(1)} %get-tuple-element.26.refs_3_), channel_id=1, source_target_pairs={{0,2},{1,3},{2,0},{3,1},{4,6},{5,7},{6,4},{7,5},{8,10},{9,11},{10,... | collective-permute-start | bytes 319496 | tf_op jit(solution)/shard_map/ppermute | solution.py:359
  24.0 6.0 %collective-permute-start.24 = (bf16[104,512]{1,0:T(8,128)(2,1)S(1)}, bf16[104,512]{1,0:T(8,128)(2,1)S(1)}, u32[]{:S(2)}, u32[]{:S(2)}) collective-permute-start(bf16[104,512]{1,0:T(8,128)(2,1)S(1)} %get-tuple-element.26.refs_3_), channel_id=1, source_target_pairs={{0,1},{1,0},{2,3},{3,2},{4,5},{5,4},{6,7},{7,6},{8,9},{9,8},{10,11... | collective-permute-start | bytes 319496 | tf_op jit(solution)/shard_map/ppermute | solution.py:359
  25.3 5.8 %collective-permute-start.22 = (bf16[104,512]{1,0:T(8,128)(2,1)S(1)}, bf16[104,512]{1,0:T(8,128)(2,1)S(1)}, u32[]{:S(2)}, u32[]{:S(2)}) collective-permute-start(bf16[104,512]{1,0:T(8,128)(2,1)S(1)} %shard_map.115.refs_3_), channel_id=1, source_target_pairs={{0,2},{1,3},{2,0},{3,1},{4,6},{5,7},{6,4},{7,5},{8,10},{9,11},{10,... | collective-permute-start | bytes 319496 | tf_op jit(solution)/shard_map/ppermute | solution.py:359
  26.3 7.8 %collective-permute-start.21 = (bf16[104,512]{1,0:T(8,128)(2,1)S(1)}, bf16[104,512]{1,0:T(8,128)(2,1)S(1)}, u32[]{:S(2)}, u32[]{:S(2)}) collective-permute-start(bf16[104,512]{1,0:T(8,128)(2,1)S(1)} %shard_map.115.refs_3_), channel_id=1, source_target_pairs={{0,1},{1,0},{2,3},{3,2},{4,5},{5,4},{6,7},{7,6},{8,9},{9,8},{10,11... | collective-permute-start | bytes 319496 | tf_op jit(solution)/shard_map/ppermute | solution.py:359
  26.5 7.0 %slice-start = ((s8[12582912]{0:T(1024)(128)(4,1)}), s8[4194304]{0:T(1024)(128)(4,1)S(1)}, s32[]{:S(2)}) async-start(s8[12582912]{0:T(1024)(128)(4,1)} %bitcast.2), calls=%async_computation | async-start | bytes 8388608
  26.5 7.0 %slice-start.1 = ((s8[12582912]{0:T(1024)(128)(4,1)}), s8[4194304]{0:T(1024)(128)(4,1)S(1)}, s32[]{:S(2)}) async-start(s8[12582912]{0:T(1024)(128)(4,1)} %bitcast.2), calls=%async_computation.1 | async-start | bytes 8388608
  27.6 3.6 %copy-start.4 = (bf16[3072,4]{0,1:T(4,128)(2,1)S(1)}, bf16[3072,4]{0,1:T(4,128)(2,1)}, u32[]{:S(2)}) copy-start(bf16[3072,4]{0,1:T(4,128)(2,1)} %param.17) | copy-start | bytes 73732
  27.6 5.8 %slice-start.2 = ((s8[12582912]{0:T(1024)(128)(4,1)}), s8[4194304]{0:T(1024)(128)(4,1)S(1)}, s32[]{:S(2)}) async-start(s8[12582912]{0:T(1024)(128)(4,1)} %bitcast.2), calls=%async_computation.2 | async-start | bytes 8388608
  27.6 5.3 %collective-permute-start.19 = (bf16[104,512]{1,0:T(8,128)(2,1)S(1)}, bf16[104,512]{1,0:T(8,128)(2,1)S(1)}, u32[]{:S(2)}, u32[]{:S(2)}) collective-permute-start(bf16[104,512]{1,0:T(8,128)(2,1)S(1)} %shard_map.114.refs_3_), channel_id=1, source_target_pairs={{0,2},{1,3},{2,0},{3,1},{4,6},{5,7},{6,4},{7,5},{8,10},{9,11},{10,... | collective-permute-start | bytes 319496 | tf_op jit(solution)/shard_map/ppermute | solution.py:359
  28.8 4.2 %collective-permute-start.26 = (bf16[104,512]{1,0:T(8,128)(2,1)S(1)}, bf16[104,512]{1,0:T(8,128)(2,1)S(1)}, u32[]{:S(2)}, u32[]{:S(2)}) collective-permute-start(bf16[104,512]{1,0:T(8,128)(2,1)S(1)} %collective-permute-done.25.refs_1_), channel_id=1, source_target_pairs={{0,1},{1,0},{2,3},{3,2},{4,5},{5,4},{6,7},{7,6},{8,9},{9,8},{10,11... | collective-permute-start | bytes 319496 | tf_op jit(solution)/shard_map/ppermute | solution.py:359
  30.0 5.4 %collective-permute-start.16 = (bf16[104,512]{1,0:T(8,128)(2,1)S(1)}, bf16[104,512]{1,0:T(8,128)(2,1)S(1)}, u32[]{:S(2)}, u32[]{:S(2)}) collective-permute-start(bf16[104,512]{1,0:T(8,128)(2,1)S(1)} %shard_map.113.refs_4_), channel_id=1, source_target_pairs={{0,2},{1,3},{2,0},{3,1},{4,6},{5,7},{6,4},{7,5},{8,10},{9,11},{10,... | collective-permute-start | bytes 319496 | tf_op jit(solution)/shard_map/ppermute | solution.py:359
  31.1 4.4 %collective-permute-start.23 = (bf16[104,512]{1,0:T(8,128)(2,1)S(1)}, bf16[104,512]{1,0:T(8,128)(2,1)S(1)}, u32[]{:S(2)}, u32[]{:S(2)}) collective-permute-start(bf16[104,512]{1,0:T(8,128)(2,1)S(1)} %collective-permute-done.22.refs_1_), channel_id=1, source_target_pairs={{0,1},{1,0},{2,3},{3,2},{4,5},{5,4},{6,7},{7,6},{8,9},{9,8},{10,11... | collective-permute-start | bytes 319496 | tf_op jit(solution)/shard_map/ppermute | solution.py:359
  32.9 3.1 %collective-permute-start.18 = (bf16[104,512]{1,0:T(8,128)(2,1)S(1)}, bf16[104,512]{1,0:T(8,128)(2,1)S(1)}, u32[]{:S(2)}, u32[]{:S(2)}) collective-permute-start(bf16[104,512]{1,0:T(8,128)(2,1)S(1)} %shard_map.114.refs_3_), channel_id=1, source_target_pairs={{0,1},{1,0},{2,3},{3,2},{4,5},{5,4},{6,7},{7,6},{8,9},{9,8},{10,11... | collective-permute-start | bytes 319496 | tf_op jit(solution)/shard_map/ppermute | solution.py:359
  33.0 3.1 %collective-permute-start.20 = (bf16[104,512]{1,0:T(8,128)(2,1)S(1)}, bf16[104,512]{1,0:T(8,128)(2,1)S(1)}, u32[]{:S(2)}, u32[]{:S(2)}) collective-permute-start(bf16[104,512]{1,0:T(8,128)(2,1)S(1)} %collective-permute-done.19.refs_1_), channel_id=1, source_target_pairs={{0,1},{1,0},{2,3},{3,2},{4,5},{5,4},{6,7},{7,6},{8,9},{9,8},{10,11... | collective-permute-start | bytes 319496 | tf_op jit(solution)/shard_map/ppermute | solution.py:359
  34.1 2.7 %collective-permute-start.15 = (bf16[104,512]{1,0:T(8,128)(2,1)S(1)}, bf16[104,512]{1,0:T(8,128)(2,1)S(1)}, u32[]{:S(2)}, u32[]{:S(2)}) collective-permute-start(bf16[104,512]{1,0:T(8,128)(2,1)S(1)} %shard_map.113.refs_4_), channel_id=1, source_target_pairs={{0,1},{1,0},{2,3},{3,2},{4,5},{5,4},{6,7},{7,6},{8,9},{9,8},{10,11... | collective-permute-start | bytes 319496 | tf_op jit(solution)/shard_map/ppermute | solution.py:359
  35.4 1.4 %collective-permute-start.17 = (bf16[104,512]{1,0:T(8,128)(2,1)S(1)}, bf16[104,512]{1,0:T(8,128)(2,1)S(1)}, u32[]{:S(2)}, u32[]{:S(2)}) collective-permute-start(bf16[104,512]{1,0:T(8,128)(2,1)S(1)} %collective-permute-done.16.refs_1_), channel_id=1, source_target_pairs={{0,1},{1,0},{2,3},{3,2},{4,5},{5,4},{6,7},{7,6},{8,9},{9,8},{10,11... | collective-permute-start | bytes 319496 | tf_op jit(solution)/shard_map/ppermute | solution.py:359
  37.5 6.3 %collective-permute-start.27 = (bf16[32,768]{1,0:T(8,128)(2,1)S(1)}, bf16[32,768]{1,0:T(8,128)(2,1)S(1)}, u32[]{:S(2)}, u32[]{:S(2)}) collective-permute-start(bf16[32,768]{1,0:T(8,128)(2,1)S(1)} %get-tuple-element.32), channel_id=1, source_target_pairs={{0,12},{4,8},{8,4},{12,0},{1,13},{5,9},{9,5},{13,1},{2,14},{6,10},... | collective-permute-start | bytes 147464 | tf_op jit(solution)/shard_map/ppermute | solution.py:359
  39.8 5.8 %collective-permute-start.28 = (bf16[32,768]{1,0:T(8,128)(2,1)S(1)}, bf16[32,768]{1,0:T(8,128)(2,1)S(1)}, u32[]{:S(2)}, u32[]{:S(2)}) collective-permute-start(bf16[32,768]{1,0:T(8,128)(2,1)S(1)} %get-tuple-element.33), channel_id=1, source_target_pairs={{0,8},{4,12},{8,0},{12,4},{1,9},{5,13},{9,1},{13,5},{2,10},{6,14},... | collective-permute-start | bytes 147464 | tf_op jit(solution)/shard_map/ppermute | solution.py:359
  39.8 5.8 %collective-permute-start.29 = (bf16[32,768]{1,0:T(8,128)(2,1)S(1)}, bf16[32,768]{1,0:T(8,128)(2,1)S(1)}, u32[]{:S(2)}, u32[]{:S(2)}) collective-permute-start(bf16[32,768]{1,0:T(8,128)(2,1)S(1)} %get-tuple-element.34), channel_id=1, source_target_pairs={{0,4},{4,0},{8,12},{12,8},{1,5},{5,1},{9,13},{13,9},{2,6},{6,2},{1... | collective-permute-start | bytes 147464 | tf_op jit(solution)/shard_map/ppermute | solution.py:359
  45.7 1.5 %collective-permute-start.32 = (bf16[8,768]{1,0:T(8,128)(2,1)S(1)}, bf16[8,768]{1,0:T(8,128)(2,1)S(1)}, u32[]{:S(2)}, u32[]{:S(2)}) collective-permute-start(bf16[8,768]{1,0:T(8,128)(2,1)S(1)} %get-tuple-element.38), channel_id=1, source_target_pairs={{0,1},{1,0},{2,3},{3,2},{4,5},{5,4},{6,7},{7,6},{8,9},{9,8},{10,11... | collective-permute-start | bytes 36872 | tf_op jit(solution)/shard_map/ppermute | solution.py:359
  45.8 2.5 %collective-permute-start.30 = (bf16[8,768]{1,0:T(8,128)(2,1)S(1)}, bf16[8,768]{1,0:T(8,128)(2,1)S(1)}, u32[]{:S(2)}, u32[]{:S(2)}) collective-permute-start(bf16[8,768]{1,0:T(8,128)(2,1)S(1)} %get-tuple-element.36), channel_id=1, source_target_pairs={{0,1},{1,0},{2,3},{3,2},{4,5},{5,4},{6,7},{7,6},{8,9},{9,8},{10,11... | collective-permute-start | bytes 36872 | tf_op jit(solution)/shard_map/ppermute | solution.py:359
  46.3 3.7 %collective-permute-start.31 = (bf16[8,768]{1,0:T(8,128)(2,1)S(1)}, bf16[8,768]{1,0:T(8,128)(2,1)S(1)}, u32[]{:S(2)}, u32[]{:S(2)}) collective-permute-start(bf16[8,768]{1,0:T(8,128)(2,1)S(1)} %get-tuple-element.37), channel_id=1, source_target_pairs={{0,2},{1,3},{2,0},{3,1},{4,6},{5,7},{6,4},{7,5},{8,10},{9,11},{10,... | collective-permute-start | bytes 36872 | tf_op jit(solution)/shard_map/ppermute | solution.py:359
  47.2 3.7 %collective-permute-start.33 = (bf16[8,768]{1,0:T(8,128)(2,1)S(1)}, bf16[8,768]{1,0:T(8,128)(2,1)S(1)}, u32[]{:S(2)}, u32[]{:S(2)}) collective-permute-start(bf16[8,768]{1,0:T(8,128)(2,1)S(1)} %collective-permute-done.32), channel_id=1, source_target_pairs={{0,2},{1,3},{2,0},{3,1},{4,6},{5,7},{6,4},{7,5},{8,10},{9,11},{10,... | collective-permute-start | bytes 36872 | tf_op jit(solution)/shard_map/ppermute | solution.py:359
  (3 other events, 2.3 us)

commit v4 on v3

--- a/solution.py
+++ b/solution.py
@@ -124,8 +124,10 @@
 CHUNKS = (4, 4, 4, 4)
 Z_ORDER = (3, 2, 1)
 EARLY, LATE = (1, 3), (0, 2)
+PAIRED = 0
+LAST_FLOPS = 10**9
 PACK_FLOPS = 10**8
-OPENING_FLOPS = 4 * 10**9
+OPENING_FLOPS = 6 * 10**9
 ATTENTION_FLOPS = 30 * 10**9
 GATE_FLOPS = 10**9
 DOWN_FLOPS = 10**9
@@ -186,23 +188,35 @@
     column = lax.broadcasted_iota(jnp.int32, (rows, rows * cache), 1)
     start = row * cache
     in_cache = (column >= start) & (column < start + live)
-    in_cache = jnp.concatenate([in_cache.astype(jnp.int32)] * group, axis=0) > 0
+    bias = jnp.where(in_cache, 0.0, -jnp.inf)[None]
     scale = 1.0 / math.sqrt(HEAD_SIZE)
-    for kv in range(KEY_VALUE_HEADS):
-        heads = [queries_ref[:, h * HEAD_SIZE : (h + 1) * HEAD_SIZE].astype(jnp.float32)
-                 for h in range(kv * group, (kv + 1) * group)]
-        query = jnp.concatenate(heads, axis=0).astype(jnp.bfloat16)
-        lanes = slice(kv * HEAD_SIZE, (kv + 1) * HEAD_SIZE)
-        key = keys_ref[:, :, lanes].reshape(rows * cache, HEAD_SIZE)
-        value = values_ref[:, :, lanes].reshape(rows * cache, HEAD_SIZE)
-        scores = jnp.where(in_cache, dot_nt(query, key) * scale, -jnp.inf)
-        exp_scores = jnp.exp(scores - jnp.max(scores, axis=1, keepdims=True))
-        total = jnp.sum(exp_scores, axis=1, keepdims=True)
-        probs = (exp_scores * (1.0 / total)).astype(jnp.bfloat16)
-        attended = dot(probs, value)
-        for g in range(group):
-            h = kv * group + g
-            att_ref[:, h * HEAD_SIZE : (h + 1) * HEAD_SIZE] = attended[g * rows : (g + 1) * rows]
+    pair = 4
+    for kv in range(0, KEY_VALUE_HEADS, pair):
+        lanes = slice(kv * HEAD_SIZE, (kv + pair) * HEAD_SIZE)
+        key = keys_ref[:, :, lanes].reshape(rows * cache, pair * HEAD_SIZE)
+        value = values_ref[:, :, lanes].reshape(rows * cache, pair * HEAD_SIZE)
+        queries = []
+        blank = jnp.zeros((group * rows, HEAD_SIZE), jnp.float32)
+        for one in range(pair):
+            heads = [
+                queries_ref[:, h * HEAD_SIZE : (h + 1) * HEAD_SIZE].astype(jnp.float32)
+                for h in range((kv + one) * group, (kv + one + 1) * group)
+            ]
+            blocks = [blank] * pair
+            blocks[one] = jnp.concatenate(heads, axis=0)
+            queries.append(jnp.concatenate(blocks, axis=1))
+        query = jnp.concatenate(queries, axis=0).astype(jnp.bfloat16)
+        scores = dot_nt(query, key).reshape(pair * group, rows, rows * cache) * scale + bias
+        exp_scores = jnp.exp(scores - jnp.max(scores, axis=2, keepdims=True))
+        total = jnp.sum(exp_scores, axis=2, keepdims=True)
+        probs = (exp_scores * (1.0 / total)).reshape(pair * group * rows, rows * cache)
+        attended = dot(probs.astype(jnp.bfloat16), value)
+        for n in range(pair * group):
+            h = kv * group + n
+            one = n // group
+            att_ref[:, h * HEAD_SIZE : (h + 1) * HEAD_SIZE] = attended[
+                n * rows : (n + 1) * rows, one * HEAD_SIZE : (one + 1) * HEAD_SIZE
+            ]
     resid = (tokens_ref[...].astype(jnp.float32) + att_ref[...]).astype(jnp.bfloat16)
     resid_ref[...] = resid
     resid_f = resid.astype(jnp.float32)
@@ -284,23 +298,25 @@
     hidden_columns(x_ref[...], gate_ref, up_ref, hidden_ref, begin)
 
 
-def down_part(sources, down_ref, own_width):
+def pair_kernel(first_ref, second_ref, out_ref):
+    width = first_ref.shape[1]
+    out_ref[:, :width] = first_ref[...]
+    out_ref[:, width:] = second_ref[...]
+
+
+def down_part(refs, sources, down_ref, own_width):
     sub = lax.axis_index("sub")
     total = None
-    for hidden_ref, flip, begin in sources:
-        height = hidden_ref.shape[1]
-        at = pl.multiple_of((sub ^ flip) * own_width + begin, 128)
-        part = dot(hidden_ref[...], down_ref[pl.ds(at, height), :])
+    for which, start, width, bits, begin in sources:
+        at = pl.multiple_of((sub ^ bits) * own_width + begin, 128)
+        part = dot(refs[which][:, start : start + width], down_ref[pl.ds(at, width), :])
         total = part if total is None else total + part
     return total
 
 
-def down_kernel(flips, own_width, has_total, *refs):
-    count = len(flips)
-    hidden_refs = refs[:count]
-    rest = refs[count:]
-    sources = [(r, f, b) for r, (f, b) in zip(hidden_refs, flips, strict=True)]
-    total = down_part(sources, rest[0], own_width)
+def down_kernel(sources, own_width, has_total, *refs):
+    rest = refs[-3:] if has_total else refs[-2:]
+    total = down_part(refs, sources, rest[0], own_width)
     if has_total:
         total = total + rest[1][...]
     rest[-1][...] = total
@@ -321,13 +337,10 @@
     share_ref[...] = jnp.broadcast_to(share, share_ref.shape)
 
 
-def last_down_kernel(flips, own_width, *refs):
-    count = len(flips)
-    hidden_refs = refs[:count]
-    down_ref, total_ref, spread_ref, share_ref, *out_refs = refs[count:]
-    sources = [(r, f, b) for r, (f, b) in zip(hidden_refs, flips, strict=True)]
+def last_down_kernel(sources, operands, own_width, *refs):
+    down_ref, total_ref, spread_ref, share_ref, *out_refs = refs[operands:]
     slots = total_ref.shape[0]
-    total = total_ref[...] + down_part(sources, down_ref, own_width)
+    total = total_ref[...] + down_part(refs, sources, down_ref, own_width)
     weighted = (total * share_ref[:, :1]).astype(jnp.bfloat16)
     result = dot(spread_ref[:, :slots], weighted).astype(jnp.bfloat16)
     height = out_refs[0].shape[0]
@@ -461,8 +474,6 @@
             )
         )
     far = [flip(h, "sub", 2) for h in own]
-    near = [flip(h, "sub", 1) for h in own]
-    across = [flip(h, "sub", 1) for h in far]
     spread, share = call(
         functools.partial(return_kernel, rows, (*EARLY, *LATE), cap),
         (
@@ -477,27 +488,39 @@
     total_shape = jax.ShapeDtypeStruct((slots, out_width), jnp.float32)
     total = None
     for i in range(chunks):
-        taken = [near[i], far[i], across[i]]
-        flips = [(1, begins[i]), (2, begins[i]), (3, begins[i])]
-        if i < chunks - 1:
-            taken.append(own[i])
-            flips.append((0, begins[i]))
-        if i == chunks - 2:
-            taken.append(own[i + 1])
-            flips.append((0, begins[i + 1]))
+        wide = widths[i]
+        if i < PAIRED:
+            both = call(
+                pair_kernel,
+                jax.ShapeDtypeStruct((slots, 2 * wide), bf16),
+                (own[i], far[i]),
+                [VMEM_SPEC] * 2,
+                flops=10**6,
+                vmem=4 * MIB,
+            )
+            taken = [both, flip(both, "sub", 1)]
+            sources = [(0, wide, wide, 2, begins[i]), (1, 0, wide, 1, begins[i]),
+                       (1, wide, wide, 3, begins[i])]
+        else:
+            taken = [far[i], flip(own[i], "sub", 1), flip(far[i], "sub", 1)]
+            sources = [(n, 0, wide, bits, begins[i]) for n, bits in enumerate((2, 1, 3))]
+        mine = [i] if i < chunks - 2 else [i, i + 1] if i == chunks - 2 else []
+        for n in mine:
+            sources.append((len(taken), 0, widths[n], 0, begins[n]))
+            taken.append(own[n])
         before = () if total is None else (total,)
         if i < chunks - 1:
             total = call(
-                functools.partial(down_kernel, flips, own_hidden, i > 0),
+                functools.partial(down_kernel, sources, own_hidden, i > 0),
                 total_shape,
                 (*taken, down_weight, *before),
                 [VMEM_SPEC] * (len(taken) + 1 + len(before)),
-                flops=DOWN_FLOPS,
+                flops=LAST_FLOPS if i == chunks - 2 else DOWN_FLOPS,
                 vmem=4 * MIB,
             )
         else:
             weighted = call(
-                functools.partial(last_down_kernel, flips, own_hidden),
+                functools.partial(last_down_kernel, sources, len(taken), own_hidden),
                 (jax.ShapeDtypeStruct((all_rows // devs, out_width), bf16),) * devs,
                 (*taken, down_weight, total, spread, share),
                 [VMEM_SPEC] * (len(taken) + 4),

time: 51.7 us -> 51 us (0.986)
  Pallas kernels: 12.1 us -> 11.3 us
    pallas_call x14, Pallas kernels: 12.1 us -> 11.3 us  [call(): pl.pallas_call(body, out_shape=out_shapes, in_specs=specs, out_specs=jax....]
where the time goes in v4:
time: 51 us; the launch traced here: 50.8 us
  starting transfers between devices  24.4 us (48%)
  waiting for transfers between devices  13.1 us (26%)
  Pallas kernels  11.3 us (22%)
  local copies, waits for them, and re-layouts  1.61 us (3%)
    ppermute x34, starting transfers between devices, flip(): lax.ppermute(x, axis, [(i, i ^ bits) for i in range(lax.axis_size(axis))])  24.4 us
    ppermute x34, waiting for transfers between devices, flip(): lax.ppermute(x, axis, [(i, i ^ bits) for i in range(lax.axis_size(axis))])  13.1 us
    pallas_call x14, Pallas kernels, call(): pl.pallas_call(body, out_shape=out_shapes, in_specs=specs, out_specs=jax....  11.3 us
    unnamed x34, local copies, waits for them, and re-layouts  1.61 us
  transfers between devices with their start and end apart: 34, of which 11 were waited for; matrix products, arithmetic and copies ran while one was open for 0% of the time, Pallas kernels for 13%

profile of v4, /device:TPU:0, one launch (start us, length us, event | category | flops | bytes accessed | tf_op | source)
XLA Modules:
  0.0 50.8 jit_solution(8410140632812569868)
XLA Ops:
  0.1 0.6 %copy-done.6 = s32[32,2]{0,1:T(2,128)S(1)} copy-done((s32[32,2]{0,1:T(2,128)S(1)}, s32[32,2]{0,1:T(2,128)}, u32[]{:S(2)}) %copy-start.6) | copy-done | bytes 280
  0.7 0.1 copy-done.3
  0.8 0.5 copy-done
  1.3 0.3 copy-done.1
  1.7 1.7 %shard_map.110 = (bf16[8,3200]{1,0:T(8,128)(2,1)S(1)}, bf16[8,3072]{1,0:T(8,128)(2,1)S(1)}) custom-call(f32[8,128]{1,0:T(8,128)S(1)} %shard_map.109._, s32[8]{0:T(128)S(1)} %copy-done.7, s32[2,32]{1,0:T(2,128)S(1)} %bitcast.9, bf16[8,3072]{1,0:T(8,128)(2,1)S(1)} %copy-done.2, bf16[8,128,512]{2,1,0:T(8,128)(2,1)S(1)} %copy-done, ...), custom_call_target="tpu_custom_call" | custom-call | flops 30000001024 | bytes 104857600 | tf_op jit(solution)/shard_map/pallas_call | solution.py:138
  3.3 3.1 %collective-permute-start.7 = (bf16[8,3200]{1,0:T(8,128)(2,1)S(1)}, bf16[8,3200]{1,0:T(8,128)(2,1)S(1)}, u32[]{:S(2)}, u32[]{:S(2)}) collective-permute-start(bf16[8,3200]{1,0:T(8,128)(2,1)S(1)} %get-tuple-element.23.refs_0_), channel_id=1, source_target_pairs={{0,4},{4,0},{8,12},{12,8},{1,5},{5,1},{9,13},{13,9},{2,6},{6,2},{1... | collective-permute-start | bytes 153608 | tf_op jit(solution)/shard_map/ppermute | solution.py:372
  6.4 2.5 %collective-permute-start.11 = (bf16[8,3200]{1,0:T(8,128)(2,1)S(1)}, bf16[8,3200]{1,0:T(8,128)(2,1)S(1)}, u32[]{:S(2)}, u32[]{:S(2)}) collective-permute-start(bf16[8,3200]{1,0:T(8,128)(2,1)S(1)} %get-tuple-element.23.refs_0_), channel_id=1, source_target_pairs={{0,12},{4,8},{8,4},{12,0},{1,13},{5,9},{9,5},{13,1},{2,14},{6,10},... | collective-permute-start | bytes 153608 | tf_op jit(solution)/shard_map/ppermute | solution.py:372
  9.0 1.5 %collective-permute-start.1 = (bf16[8,3200]{1,0:T(8,128)(2,1)S(1)}, bf16[8,3200]{1,0:T(8,128)(2,1)S(1)}, u32[]{:S(2)}, u32[]{:S(2)}) collective-permute-start(bf16[8,3200]{1,0:T(8,128)(2,1)S(1)} %get-tuple-element.23.refs_0_), channel_id=1, source_target_pairs={{0,2},{1,3},{2,0},{3,1},{4,6},{5,7},{6,4},{7,5},{8,10},{9,11},{10,... | collective-permute-start | bytes 153608 | tf_op jit(solution)/shard_map/ppermute | solution.py:372
  10.5 0.5 %collective-permute-start.9 = (bf16[8,3200]{1,0:T(8,128)(2,1)S(1)}, bf16[8,3200]{1,0:T(8,128)(2,1)S(1)}, u32[]{:S(2)}, u32[]{:S(2)}) collective-permute-start(bf16[8,3200]{1,0:T(8,128)(2,1)S(1)} %collective-permute-done.7.refs_0_), channel_id=1, source_target_pairs={{0,2},{1,3},{2,0},{3,1},{4,6},{5,7},{6,4},{7,5},{8,10},{9,11},{10,... | collective-permute-start | bytes 153608 | tf_op jit(solution)/shard_map/ppermute | solution.py:372
  11.1 1.9 %collective-permute-done.11.refs_4_ = bf16[8,3200]{1,0:T(8,128)(2,1)S(1)} collective-permute-done((bf16[8,3200]{1,0:T(8,128)(2,1)S(1)}, bf16[8,3200]{1,0:T(8,128)(2,1)S(1)}, u32[]{:S(2)}, u32[]{:S(2)}) %collective-permute-start.11) | collective-permute-done | bytes 51232 | tf_op jit(solution)/shard_map/ppermute | solution.py:372
  13.0 1.5 %collective-permute-start.13 = (bf16[8,3200]{1,0:T(8,128)(2,1)S(1)}, bf16[8,3200]{1,0:T(8,128)(2,1)S(1)}, u32[]{:S(2)}, u32[]{:S(2)}) collective-permute-start(bf16[8,3200]{1,0:T(8,128)(2,1)S(1)} %collective-permute-done.11.refs_4_), channel_id=1, source_target_pairs={{0,2},{1,3},{2,0},{3,1},{4,6},{5,7},{6,4},{7,5},{8,10},{9,11},{10,... | collective-permute-start | bytes 153608 | tf_op jit(solution)/shard_map/ppermute | solution.py:372
  14.5 0.5 collective-permute-start.8
  15.0 1.0 %collective-permute-start.5 = (bf16[8,3200]{1,0:T(8,128)(2,1)S(1)}, bf16[8,3200]{1,0:T(8,128)(2,1)S(1)}, u32[]{:S(2)}, u32[]{:S(2)}) collective-permute-start(bf16[8,3200]{1,0:T(8,128)(2,1)S(1)} %collective-permute-done.3.refs_4_), channel_id=1, source_target_pairs={{0,2},{1,3},{2,0},{3,1},{4,6},{5,7},{6,4},{7,5},{8,10},{9,11},{10,... | collective-permute-start | bytes 153608 | tf_op jit(solution)/shard_map/ppermute | solution.py:372
  16.0 0.2 collective-permute-start.10
  16.2 0.9 %collective-permute-done.13.refs_6_ = bf16[8,3200]{1,0:T(8,128)(2,1)S(1)} collective-permute-done((bf16[8,3200]{1,0:T(8,128)(2,1)S(1)}, bf16[8,3200]{1,0:T(8,128)(2,1)S(1)}, u32[]{:S(2)}, u32[]{:S(2)}) %collective-permute-start.13) | collective-permute-done | bytes 51232 | tf_op jit(solution)/shard_map/ppermute | solution.py:372
  17.1 0.5 collective-permute-start
  17.7 1.4 %collective-permute-done.5.refs_6_ = bf16[8,3200]{1,0:T(8,128)(2,1)S(1)} collective-permute-done((bf16[8,3200]{1,0:T(8,128)(2,1)S(1)}, bf16[8,3200]{1,0:T(8,128)(2,1)S(1)}, u32[]{:S(2)}, u32[]{:S(2)}) %collective-permute-start.5) | collective-permute-done | bytes 51232 | tf_op jit(solution)/shard_map/ppermute | solution.py:372
  19.1 0.5 collective-permute-start.6
  19.6 0.6 %shard_map.111 = (bf16[104,3072]{1,0:T(8,128)(2,1)S(1)}, bf16[64,128]{1,0:T(8,128)(2,1)S(1)}) custom-call(bf16[8,3200]{1,0:T(8,128)(2,1)S(1)} %collective-permute-done.7.refs_0_, bf16[8,3200]{1,0:T(8,128)(2,1)S(1)} %collective-permute-done.8.refs_1_, bf16[8,3200]{1,0:T(8,128)(2,1)S(1)} %collective-permute-done.9.refs_2_, ...), custom_call_target="tpu_custom_call" | custom-call | flops 100000000 | tf_op jit(solution)/shard_map/pallas_call | solution.py:138
  20.3 0.2 collective-permute-done.6.refs_7_
  20.6 1.6 %shard_map.112 = (bf16[104,3072]{1,0:T(8,128)(2,1)S(1)}, bf16[64,128]{1,0:T(8,128)(2,1)S(1)}, bf16[104,512]{1,0:T(8,128)(2,1)S(1)}) custom-call(bf16[8,3200]{1,0:T(8,128)(2,1)S(1)} %get-tuple-element.23.refs_0_, bf16[8,3200]{1,0:T(8,128)(2,1)S(1)} %collective-permute-done.refs_1_, bf16[8,3200]{1,0:T(8,128)(2,1)S(1)} %collective-permute-done.1.refs_2_, ...), custom_call_target="tpu_custom_call" | custom-call | flops 1000000000 | tf_op jit(solution)/shard_map/pallas_call | solution.py:138
  22.1 1.1 %collective-permute-start.24 = (bf16[104,512]{1,0:T(8,128)(2,1)S(1)}, bf16[104,512]{1,0:T(8,128)(2,1)S(1)}, u32[]{:S(2)}, u32[]{:S(2)}) collective-permute-start(bf16[104,512]{1,0:T(8,128)(2,1)S(1)} %get-tuple-element.26.refs_3_), channel_id=1, source_target_pairs={{0,2},{1,3},{2,0},{3,1},{4,6},{5,7},{6,4},{7,5},{8,10},{9,11},{10,... | collective-permute-start | bytes 319496 | tf_op jit(solution)/shard_map/ppermute | solution.py:372
  23.3 1.2 %shard_map.115.refs_3_ = bf16[104,512]{1,0:T(8,128)(2,1)S(1)} custom-call(bf16[104,3072]{1,0:T(8,128)(2,1)S(1)} %get-tuple-element.25.x_ref.refs_2_, bf16[3072,2048]{1,0:T(8,128)(2,1)S(1)} %bitcast.5, bf16[3072,2048]{1,0:T(8,128)(2,1)S(1)} %bitcast.7), custom_call_target="tpu_custom_call" | custom-call | flops 1000000000 | tf_op jit(solution)/shard_map/pallas_call | solution.py:138
  24.5 1.0 %collective-permute-start.21 = (bf16[104,512]{1,0:T(8,128)(2,1)S(1)}, bf16[104,512]{1,0:T(8,128)(2,1)S(1)}, u32[]{:S(2)}, u32[]{:S(2)}) collective-permute-start(bf16[104,512]{1,0:T(8,128)(2,1)S(1)} %shard_map.115.refs_3_), channel_id=1, source_target_pairs={{0,2},{1,3},{2,0},{3,1},{4,6},{5,7},{6,4},{7,5},{8,10},{9,11},{10,... | collective-permute-start | bytes 319496 | tf_op jit(solution)/shard_map/ppermute | solution.py:372
  25.5 0.2 collective-permute-start.22
  25.7 1.2 %shard_map.114.refs_3_ = bf16[104,512]{1,0:T(8,128)(2,1)S(1)} custom-call(bf16[104,3072]{1,0:T(8,128)(2,1)S(1)} %get-tuple-element.25.x_ref.refs_2_, bf16[3072,2048]{1,0:T(8,128)(2,1)S(1)} %bitcast.5, bf16[3072,2048]{1,0:T(8,128)(2,1)S(1)} %bitcast.7), custom_call_target="tpu_custom_call" | custom-call | flops 1000000000 | tf_op jit(solution)/shard_map/pallas_call | solution.py:138
  26.9 1.1 %collective-permute-start.18 = (bf16[104,512]{1,0:T(8,128)(2,1)S(1)}, bf16[104,512]{1,0:T(8,128)(2,1)S(1)}, u32[]{:S(2)}, u32[]{:S(2)}) collective-permute-start(bf16[104,512]{1,0:T(8,128)(2,1)S(1)} %shard_map.114.refs_3_), channel_id=1, source_target_pairs={{0,2},{1,3},{2,0},{3,1},{4,6},{5,7},{6,4},{7,5},{8,10},{9,11},{10,... | collective-permute-start | bytes 319496 | tf_op jit(solution)/shard_map/ppermute | solution.py:372
  28.1 1.2 %shard_map.113.refs_4_ = bf16[104,512]{1,0:T(8,128)(2,1)S(1)} custom-call(bf16[104,3072]{1,0:T(8,128)(2,1)S(1)} %get-tuple-element.25.x_ref.refs_2_, bf16[3072,2048]{1,0:T(8,128)(2,1)S(1)} %bitcast.5, bf16[3072,2048]{1,0:T(8,128)(2,1)S(1)} %bitcast.7), custom_call_target="tpu_custom_call" | custom-call | flops 1000000000 | tf_op jit(solution)/shard_map/pallas_call | solution.py:138
  29.3 1.0 %collective-permute-start.15 = (bf16[104,512]{1,0:T(8,128)(2,1)S(1)}, bf16[104,512]{1,0:T(8,128)(2,1)S(1)}, u32[]{:S(2)}, u32[]{:S(2)}) collective-permute-start(bf16[104,512]{1,0:T(8,128)(2,1)S(1)} %shard_map.113.refs_4_), channel_id=1, source_target_pairs={{0,2},{1,3},{2,0},{3,1},{4,6},{5,7},{6,4},{7,5},{8,10},{9,11},{10,... | collective-permute-start | bytes 319496 | tf_op jit(solution)/shard_map/ppermute | solution.py:372
  30.3 0.2 collective-permute-start.23
  30.5 0.7 %shard_map.119 = (bf16[128,128]{1,0:T(8,128)(2,1)S(1)}, f32[104,128]{1,0:T(8,128)S(1)}) custom-call(bf16[64,128]{1,0:T(8,128)(2,1)S(1)} %get-tuple-element.27.refs_0_, bf16[64,128]{1,0:T(8,128)(2,1)S(1)} %get-tuple-element.28.refs_1_, bf16[104,3072]{1,0:T(8,128)(2,1)S(1)} %get-tuple-element.25.x_ref.refs_2_, bf16[4,3072]{1,0:T(4,128)(2,1)S(1)} %bitcast.8), custom_call_target="tpu_custom_call" | custom-call | flops 1000000000 | tf_op jit(solution)/shard_map/pallas_call | solution.py:138
  31.2 1.0 %collective-permute-done.18.refs_0_ = bf16[104,512]{1,0:T(8,128)(2,1)S(1)} collective-permute-done((bf16[104,512]{1,0:T(8,128)(2,1)S(1)}, bf16[104,512]{1,0:T(8,128)(2,1)S(1)}, u32[]{:S(2)}, u32[]{:S(2)}) %collective-permute-start.18) | collective-permute-done | bytes 106528 | tf_op jit(solution)/shard_map/ppermute | solution.py:372
  32.2 0.5 collective-permute-start.20
  32.7 0.6 %shard_map.116.refs_5_ = f32[104,768]{1,0:T(8,128)S(1)} custom-call(bf16[104,512]{1,0:T(8,128)(2,1)S(1)} %collective-permute-done.24.refs_0_, bf16[104,512]{1,0:T(8,128)(2,1)S(1)} %collective-permute-done.25.refs_1_, bf16[104,512]{1,0:T(8,128)(2,1)S(1)} %collective-permute-done.26.refs_2_, bf16[104,512]{1,0:T(8,128)(2,1)S(1)} %get-tuple-element.26.refs_3_, ...), custom_call_target="tpu_custom_call" | custom-call | flops 1000000000 | tf_op jit(solution)/shard_map/pallas_call | solution.py:138
  33.4 1.2 %collective-permute-done.15.refs_0_ = bf16[104,512]{1,0:T(8,128)(2,1)S(1)} collective-permute-done((bf16[104,512]{1,0:T(8,128)(2,1)S(1)}, bf16[104,512]{1,0:T(8,128)(2,1)S(1)}, u32[]{:S(2)}, u32[]{:S(2)}) %collective-permute-start.15) | collective-permute-done | bytes 106528 | tf_op jit(solution)/shard_map/ppermute | solution.py:372
  34.7 0.6 %shard_map.117.refs_6_ = f32[104,768]{1,0:T(8,128)S(1)} custom-call(bf16[104,512]{1,0:T(8,128)(2,1)S(1)} %collective-permute-done.21.refs_0_, bf16[104,512]{1,0:T(8,128)(2,1)S(1)} %collective-permute-done.22.refs_1_, bf16[104,512]{1,0:T(8,128)(2,1)S(1)} %collective-permute-done.23.refs_2_, bf16[104,512]{1,0:T(8,128)(2,1)S(1)} %shard_map.115.refs_3_, ...), custom_call_target="tpu_custom_call" | custom-call | flops 1000000000 | tf_op jit(solution)/shard_map/pallas_call | solution.py:138
  35.3 0.7 %shard_map.118.refs_4_ = f32[104,768]{1,0:T(8,128)S(1)} custom-call(bf16[104,512]{1,0:T(8,128)(2,1)S(1)} %collective-permute-done.18.refs_0_, bf16[104,512]{1,0:T(8,128)(2,1)S(1)} %collective-permute-done.19.refs_1_, bf16[104,512]{1,0:T(8,128)(2,1)S(1)} %collective-permute-done.20.refs_2_, bf16[104,512]{1,0:T(8,128)(2,1)S(1)} %shard_map.114.refs_3_, ...), custom_call_target="tpu_custom_call" | custom-call | flops 1000000000 | tf_op jit(solution)/shard_map/pallas_call | solution.py:138
  36.0 0.7 %shard_map.120 = (bf16[32,768]{1,0:T(8,128)(2,1)S(1)}, bf16[32,768]{1,0:T(8,128)(2,1)S(1)}, bf16[32,768]{1,0:T(8,128)(2,1)S(1)}, bf16[32,768]{1,0:T(8,128)(2,1)S(1)}) custom-call(bf16[104,512]{1,0:T(8,128)(2,1)S(1)} %collective-permute-done.15.refs_0_, bf16[104,512]{1,0:T(8,128)(2,1)S(1)} %collective-permute-done.16.refs_1_, ...), custom_call_target="tpu_custom_call" | custom-call | flops 1000000000 | tf_op jit(solution)/shard_map/pallas_call | solution.py:138
  36.8 2.3 %collective-permute-start.27 = (bf16[32,768]{1,0:T(8,128)(2,1)S(1)}, bf16[32,768]{1,0:T(8,128)(2,1)S(1)}, u32[]{:S(2)}, u32[]{:S(2)}) collective-permute-start(bf16[32,768]{1,0:T(8,128)(2,1)S(1)} %get-tuple-element.32), channel_id=1, source_target_pairs={{0,12},{4,8},{8,4},{12,0},{1,13},{5,9},{9,5},{13,1},{2,14},{6,10},... | collective-permute-start | bytes 147464 | tf_op jit(solution)/shard_map/ppermute | solution.py:372
  39.1 2.1 %collective-permute-start.29 = (bf16[32,768]{1,0:T(8,128)(2,1)S(1)}, bf16[32,768]{1,0:T(8,128)(2,1)S(1)}, u32[]{:S(2)}, u32[]{:S(2)}) collective-permute-start(bf16[32,768]{1,0:T(8,128)(2,1)S(1)} %get-tuple-element.34), channel_id=1, source_target_pairs={{0,4},{4,0},{8,12},{12,8},{1,5},{5,1},{9,13},{13,9},{2,6},{6,2},{1... | collective-permute-start | bytes 147464 | tf_op jit(solution)/shard_map/ppermute | solution.py:372
  41.2 1.8 %collective-permute-done.27.refs_1_ = bf16[32,768]{1,0:T(8,128)(2,1)S(1)} collective-permute-done((bf16[32,768]{1,0:T(8,128)(2,1)S(1)}, bf16[32,768]{1,0:T(8,128)(2,1)S(1)}, u32[]{:S(2)}, u32[]{:S(2)}) %collective-permute-start.27) | collective-permute-done | bytes 49184 | tf_op jit(solution)/shard_map/ppermute | solution.py:372
  43.0 1.8 %collective-permute-done.28.refs_2_ = bf16[32,768]{1,0:T(8,128)(2,1)S(1)} collective-permute-done((bf16[32,768]{1,0:T(8,128)(2,1)S(1)}, bf16[32,768]{1,0:T(8,128)(2,1)S(1)}, u32[]{:S(2)}, u32[]{:S(2)}) %collective-permute-start.28) | collective-permute-done | bytes 49184 | tf_op jit(solution)/shard_map/ppermute | solution.py:372
  45.0 0.5 collective-permute-start.30
  45.5 1.0 %collective-permute-start.31 = (bf16[8,768]{1,0:T(8,128)(2,1)S(1)}, bf16[8,768]{1,0:T(8,128)(2,1)S(1)}, u32[]{:S(2)}, u32[]{:S(2)}) collective-permute-start(bf16[8,768]{1,0:T(8,128)(2,1)S(1)} %get-tuple-element.37), channel_id=1, source_target_pairs={{0,2},{1,3},{2,0},{3,1},{4,6},{5,7},{6,4},{7,5},{8,10},{9,11},{10,... | collective-permute-start | bytes 36872 | tf_op jit(solution)/shard_map/ppermute | solution.py:372
  46.5 1.0 %collective-permute-start.33 = (bf16[8,768]{1,0:T(8,128)(2,1)S(1)}, bf16[8,768]{1,0:T(8,128)(2,1)S(1)}, u32[]{:S(2)}, u32[]{:S(2)}) collective-permute-start(bf16[8,768]{1,0:T(8,128)(2,1)S(1)} %collective-permute-done.32), channel_id=1, source_target_pairs={{0,2},{1,3},{2,0},{3,1},{4,6},{5,7},{6,4},{7,5},{8,10},{9,11},{10,... | collective-permute-start | bytes 36872 | tf_op jit(solution)/shard_map/ppermute | solution.py:372
  47.5 1.7 %collective-permute-done.31.refs_2_ = bf16[8,768]{1,0:T(8,128)(2,1)S(1)} collective-permute-done((bf16[8,768]{1,0:T(8,128)(2,1)S(1)}, bf16[8,768]{1,0:T(8,128)(2,1)S(1)}, u32[]{:S(2)}, u32[]{:S(2)}) %collective-permute-start.31) | collective-permute-done | bytes 12320 | tf_op jit(solution)/shard_map/ppermute | solution.py:372
  49.2 1.0 %collective-permute-done.33.refs_3_ = bf16[8,768]{1,0:T(8,128)(2,1)S(1)} collective-permute-done((bf16[8,768]{1,0:T(8,128)(2,1)S(1)}, bf16[8,768]{1,0:T(8,128)(2,1)S(1)}, u32[]{:S(2)}, u32[]{:S(2)}) %collective-permute-start.33) | collective-permute-done | bytes 12320 | tf_op jit(solution)/shard_map/ppermute | solution.py:372
  50.2 0.6 %shard_map.122 = bf16[8,3072]{1,0:T(8,128)(2,1)} custom-call(bf16[8,3072]{1,0:T(8,128)(2,1)S(1)} %get-tuple-element.22.resid_ref, f32[8,768]{1,0:T(8,128)S(1)} %get-tuple-element.35.refs_0_, bf16[8,768]{1,0:T(8,128)(2,1)S(1)} %collective-permute-done.30.refs_1_, bf16[8,768]{1,0:T(8,128)(2,1)S(1)} %collective-permute-done.31.refs_2_, ...), custom_call_target="tpu_custom_call" | custom-call | flops 1000000 | tf_op jit(solution)/shard_map/pallas_call | solution.py:138
  (71 shorter events, 0.8 us)
Async XLA Ops:
  0.0 1.3 %copy-start = (bf16[8,128,512]{2,1,0:T(8,128)(2,1)S(1)}, bf16[8,128,512]{2,1,0:T(8,128)(2,1)}, u32[]{:S(2)}) copy-start(bf16[8,128,512]{2,1,0:T(8,128)(2,1)} %keys_ref.1) | copy-start | bytes 3145732
  0.0 1.6 %copy-start.1 = (bf16[8,128,512]{2,1,0:T(8,128)(2,1)S(1)}, bf16[8,128,512]{2,1,0:T(8,128)(2,1)}, u32[]{:S(2)}) copy-start(bf16[8,128,512]{2,1,0:T(8,128)(2,1)} %values_ref.1) | copy-start | bytes 3145732
  0.0 1.6 %copy-start.7 = (s32[8]{0:T(128)S(1)}, s32[8]{0:T(128)}, u32[]{:S(2)}) copy-start(s32[8]{0:T(128)} %lengths_ref.1) | copy-start | bytes 100
  0.0 1.6 %copy-start.5 = (bf16[3072]{0:T(1024)(128)(2,1)S(1)}, bf16[3072]{0:T(1024)(128)(2,1)}, u32[]{:S(2)}) copy-start(bf16[3072]{0:T(1024)(128)(2,1)} %gain_ref.1) | copy-start | bytes 18436
  0.0 20.5 %slice-start.3 = ((s8[12582912]{0:T(1024)(128)(4,1)}), s8[4194304]{0:T(1024)(128)(4,1)S(1)}, s32[]{:S(2)}) async-start(s8[12582912]{0:T(1024)(128)(4,1)} %bitcast.4), calls=%async_computation.3 | async-start | bytes 8388608
  0.0 20.5 %slice-start.6 = ((s8[12582912]{0:T(1024)(128)(4,1)}), s8[4194304]{0:T(1024)(128)(4,1)S(1)}, s32[]{:S(2)}) async-start(s8[12582912]{0:T(1024)(128)(4,1)} %bitcast.6), calls=%async_computation.6 | async-start | bytes 8388608
  1.6 18.9 %slice-start.4 = ((s8[12582912]{0:T(1024)(128)(4,1)}), s8[4194304]{0:T(1024)(128)(4,1)S(1)}, s32[]{:S(2)}) async-start(s8[12582912]{0:T(1024)(128)(4,1)} %bitcast.4), calls=%async_computation.4 | async-start | bytes 8388608
  1.6 18.9 %slice-start.5 = ((s8[12582912]{0:T(1024)(128)(4,1)}), s8[4194304]{0:T(1024)(128)(4,1)S(1)}, s32[]{:S(2)}) async-start(s8[12582912]{0:T(1024)(128)(4,1)} %bitcast.4), calls=%async_computation.5 | async-start | bytes 8388608
  1.6 18.9 %slice-start.7 = ((s8[12582912]{0:T(1024)(128)(4,1)}), s8[4194304]{0:T(1024)(128)(4,1)S(1)}, s32[]{:S(2)}) async-start(s8[12582912]{0:T(1024)(128)(4,1)} %bitcast.6), calls=%async_computation.7 | async-start | bytes 8388608
  1.6 18.9 %slice-start.8 = ((s8[12582912]{0:T(1024)(128)(4,1)}), s8[4194304]{0:T(1024)(128)(4,1)S(1)}, s32[]{:S(2)}) async-start(s8[12582912]{0:T(1024)(128)(4,1)} %bitcast.6), calls=%async_computation.8 | async-start | bytes 8388608
  3.3 7.2 %collective-permute-start.7 = (bf16[8,3200]{1,0:T(8,128)(2,1)S(1)}, bf16[8,3200]{1,0:T(8,128)(2,1)S(1)}, u32[]{:S(2)}, u32[]{:S(2)}) collective-permute-start(bf16[8,3200]{1,0:T(8,128)(2,1)S(1)} %get-tuple-element.23.refs_0_), channel_id=1, source_target_pairs={{0,4},{4,0},{8,12},{12,8},{1,5},{5,1},{9,13},{13,9},{2,6},{6,2},{1... | collective-permute-start | bytes 153608 | tf_op jit(solution)/shard_map/ppermute | solution.py:372
  6.4 6.6 %collective-permute-start.11 = (bf16[8,3200]{1,0:T(8,128)(2,1)S(1)}, bf16[8,3200]{1,0:T(8,128)(2,1)S(1)}, u32[]{:S(2)}, u32[]{:S(2)}) collective-permute-start(bf16[8,3200]{1,0:T(8,128)(2,1)S(1)} %get-tuple-element.23.refs_0_), channel_id=1, source_target_pairs={{0,12},{4,8},{8,4},{12,0},{1,13},{5,9},{9,5},{13,1},{2,14},{6,10},... | collective-permute-start | bytes 153608 | tf_op jit(solution)/shard_map/ppermute | solution.py:372
  8.9 5.6 %collective-permute-start.3 = (bf16[8,3200]{1,0:T(8,128)(2,1)S(1)}, bf16[8,3200]{1,0:T(8,128)(2,1)S(1)}, u32[]{:S(2)}, u32[]{:S(2)}) collective-permute-start(bf16[8,3200]{1,0:T(8,128)(2,1)S(1)} %get-tuple-element.23.refs_0_), channel_id=1, source_target_pairs={{0,8},{4,12},{8,0},{12,4},{1,9},{5,13},{9,1},{13,5},{2,10},{6,14},... | collective-permute-start | bytes 153608 | tf_op jit(solution)/shard_map/ppermute | solution.py:372
  9.0 6.0 %collective-permute-start.1 = (bf16[8,3200]{1,0:T(8,128)(2,1)S(1)}, bf16[8,3200]{1,0:T(8,128)(2,1)S(1)}, u32[]{:S(2)}, u32[]{:S(2)}) collective-permute-start(bf16[8,3200]{1,0:T(8,128)(2,1)S(1)} %get-tuple-element.23.refs_0_), channel_id=1, source_target_pairs={{0,2},{1,3},{2,0},{3,1},{4,6},{5,7},{6,4},{7,5},{8,10},{9,11},{10,... | collective-permute-start | bytes 153608 | tf_op jit(solution)/shard_map/ppermute | solution.py:372
  10.5 5.4 %collective-permute-start.9 = (bf16[8,3200]{1,0:T(8,128)(2,1)S(1)}, bf16[8,3200]{1,0:T(8,128)(2,1)S(1)}, u32[]{:S(2)}, u32[]{:S(2)}) collective-permute-start(bf16[8,3200]{1,0:T(8,128)(2,1)S(1)} %collective-permute-done.7.refs_0_), channel_id=1, source_target_pairs={{0,2},{1,3},{2,0},{3,1},{4,6},{5,7},{6,4},{7,5},{8,10},{9,11},{10,... | collective-permute-start | bytes 153608 | tf_op jit(solution)/shard_map/ppermute | solution.py:372
  13.0 4.1 %collective-permute-start.13 = (bf16[8,3200]{1,0:T(8,128)(2,1)S(1)}, bf16[8,3200]{1,0:T(8,128)(2,1)S(1)}, u32[]{:S(2)}, u32[]{:S(2)}) collective-permute-start(bf16[8,3200]{1,0:T(8,128)(2,1)S(1)} %collective-permute-done.11.refs_4_), channel_id=1, source_target_pairs={{0,2},{1,3},{2,0},{3,1},{4,6},{5,7},{6,4},{7,5},{8,10},{9,11},{10,... | collective-permute-start | bytes 153608 | tf_op jit(solution)/shard_map/ppermute | solution.py:372
  14.5 2.6 %collective-permute-start.12 = (bf16[8,3200]{1,0:T(8,128)(2,1)S(1)}, bf16[8,3200]{1,0:T(8,128)(2,1)S(1)}, u32[]{:S(2)}, u32[]{:S(2)}) collective-permute-start(bf16[8,3200]{1,0:T(8,128)(2,1)S(1)} %collective-permute-done.11.refs_4_), channel_id=1, source_target_pairs={{0,1},{1,0},{2,3},{3,2},{4,5},{5,4},{6,7},{7,6},{8,9},{9,8},{10,11... | collective-permute-start | bytes 153608 | tf_op jit(solution)/shard_map/ppermute | solution.py:372
  14.5 3.1 %collective-permute-start.8 = (bf16[8,3200]{1,0:T(8,128)(2,1)S(1)}, bf16[8,3200]{1,0:T(8,128)(2,1)S(1)}, u32[]{:S(2)}, u32[]{:S(2)}) collective-permute-start(bf16[8,3200]{1,0:T(8,128)(2,1)S(1)} %collective-permute-done.7.refs_0_), channel_id=1, source_target_pairs={{0,1},{1,0},{2,3},{3,2},{4,5},{5,4},{6,7},{7,6},{8,9},{9,8},{10,11... | collective-permute-start | bytes 153608 | tf_op jit(solution)/shard_map/ppermute | solution.py:372
  15.0 4.1 %collective-permute-start.5 = (bf16[8,3200]{1,0:T(8,128)(2,1)S(1)}, bf16[8,3200]{1,0:T(8,128)(2,1)S(1)}, u32[]{:S(2)}, u32[]{:S(2)}) collective-permute-start(bf16[8,3200]{1,0:T(8,128)(2,1)S(1)} %collective-permute-done.3.refs_4_), channel_id=1, source_target_pairs={{0,2},{1,3},{2,0},{3,1},{4,6},{5,7},{6,4},{7,5},{8,10},{9,11},{10,... | collective-permute-start | bytes 153608 | tf_op jit(solution)/shard_map/ppermute | solution.py:372
  16.0 3.1 %collective-permute-start.10 = (bf16[8,3200]{1,0:T(8,128)(2,1)S(1)}, bf16[8,3200]{1,0:T(8,128)(2,1)S(1)}, u32[]{:S(2)}, u32[]{:S(2)}) collective-permute-start(bf16[8,3200]{1,0:T(8,128)(2,1)S(1)} %collective-permute-done.9.refs_2_), channel_id=1, source_target_pairs={{0,1},{1,0},{2,3},{3,2},{4,5},{5,4},{6,7},{7,6},{8,9},{9,8},{10,11... | collective-permute-start | bytes 153608 | tf_op jit(solution)/shard_map/ppermute | solution.py:372
  17.1 2.5 %collective-permute-start.14 = (bf16[8,3200]{1,0:T(8,128)(2,1)S(1)}, bf16[8,3200]{1,0:T(8,128)(2,1)S(1)}, u32[]{:S(2)}, u32[]{:S(2)}) collective-permute-start(bf16[8,3200]{1,0:T(8,128)(2,1)S(1)} %collective-permute-done.13.refs_6_), channel_id=1, source_target_pairs={{0,1},{1,0},{2,3},{3,2},{4,5},{5,4},{6,7},{7,6},{8,9},{9,8},{10,11... | collective-permute-start | bytes 153608 | tf_op jit(solution)/shard_map/ppermute | solution.py:372
  17.1 3.1 %collective-permute-start = (bf16[8,3200]{1,0:T(8,128)(2,1)S(1)}, bf16[8,3200]{1,0:T(8,128)(2,1)S(1)}, u32[]{:S(2)}, u32[]{:S(2)}) collective-permute-start(bf16[8,3200]{1,0:T(8,128)(2,1)S(1)} %get-tuple-element.23.refs_0_), channel_id=1, source_target_pairs={{0,1},{1,0},{2,3},{3,2},{4,5},{5,4},{6,7},{7,6},{8,9},{9,8},{10,11... | collective-permute-start | bytes 153608 | tf_op jit(solution)/shard_map/ppermute | solution.py:372
  17.6 2.6 %collective-permute-start.4 = (bf16[8,3200]{1,0:T(8,128)(2,1)S(1)}, bf16[8,3200]{1,0:T(8,128)(2,1)S(1)}, u32[]{:S(2)}, u32[]{:S(2)}) collective-permute-start(bf16[8,3200]{1,0:T(8,128)(2,1)S(1)} %collective-permute-done.3.refs_4_), channel_id=1, source_target_pairs={{0,1},{1,0},{2,3},{3,2},{4,5},{5,4},{6,7},{7,6},{8,9},{9,8},{10,11... | collective-permute-start | bytes 153608 | tf_op jit(solution)/shard_map/ppermute | solution.py:372
  19.1 1.2 %collective-permute-start.2 = (bf16[8,3200]{1,0:T(8,128)(2,1)S(1)}, bf16[8,3200]{1,0:T(8,128)(2,1)S(1)}, u32[]{:S(2)}, u32[]{:S(2)}) collective-permute-start(bf16[8,3200]{1,0:T(8,128)(2,1)S(1)} %collective-permute-done.1.refs_2_), channel_id=1, source_target_pairs={{0,1},{1,0},{2,3},{3,2},{4,5},{5,4},{6,7},{7,6},{8,9},{9,8},{10,11... | collective-permute-start | bytes 153608 | tf_op jit(solution)/shard_map/ppermute | solution.py:372
  19.1 1.4 %collective-permute-start.6 = (bf16[8,3200]{1,0:T(8,128)(2,1)S(1)}, bf16[8,3200]{1,0:T(8,128)(2,1)S(1)}, u32[]{:S(2)}, u32[]{:S(2)}) collective-permute-start(bf16[8,3200]{1,0:T(8,128)(2,1)S(1)} %collective-permute-done.5.refs_6_), channel_id=1, source_target_pairs={{0,1},{1,0},{2,3},{3,2},{4,5},{5,4},{6,7},{7,6},{8,9},{9,8},{10,11... | collective-permute-start | bytes 153608 | tf_op jit(solution)/shard_map/ppermute | solution.py:372
  22.1 5.9 %collective-permute-start.24 = (bf16[104,512]{1,0:T(8,128)(2,1)S(1)}, bf16[104,512]{1,0:T(8,128)(2,1)S(1)}, u32[]{:S(2)}, u32[]{:S(2)}) collective-permute-start(bf16[104,512]{1,0:T(8,128)(2,1)S(1)} %get-tuple-element.26.refs_3_), channel_id=1, source_target_pairs={{0,2},{1,3},{2,0},{3,1},{4,6},{5,7},{6,4},{7,5},{8,10},{9,11},{10,... | collective-permute-start | bytes 319496 | tf_op jit(solution)/shard_map/ppermute | solution.py:372
  23.3 6.0 %collective-permute-start.25 = (bf16[104,512]{1,0:T(8,128)(2,1)S(1)}, bf16[104,512]{1,0:T(8,128)(2,1)S(1)}, u32[]{:S(2)}, u32[]{:S(2)}) collective-permute-start(bf16[104,512]{1,0:T(8,128)(2,1)S(1)} %get-tuple-element.26.refs_3_), channel_id=1, source_target_pairs={{0,1},{1,0},{2,3},{3,2},{4,5},{5,4},{6,7},{7,6},{8,9},{9,8},{10,11... | collective-permute-start | bytes 319496 | tf_op jit(solution)/shard_map/ppermute | solution.py:372
  24.5 5.8 %collective-permute-start.21 = (bf16[104,512]{1,0:T(8,128)(2,1)S(1)}, bf16[104,512]{1,0:T(8,128)(2,1)S(1)}, u32[]{:S(2)}, u32[]{:S(2)}) collective-permute-start(bf16[104,512]{1,0:T(8,128)(2,1)S(1)} %shard_map.115.refs_3_), channel_id=1, source_target_pairs={{0,2},{1,3},{2,0},{3,1},{4,6},{5,7},{6,4},{7,5},{8,10},{9,11},{10,... | collective-permute-start | bytes 319496 | tf_op jit(solution)/shard_map/ppermute | solution.py:372
  25.5 7.8 %collective-permute-start.22 = (bf16[104,512]{1,0:T(8,128)(2,1)S(1)}, bf16[104,512]{1,0:T(8,128)(2,1)S(1)}, u32[]{:S(2)}, u32[]{:S(2)}) collective-permute-start(bf16[104,512]{1,0:T(8,128)(2,1)S(1)} %shard_map.115.refs_3_), channel_id=1, source_target_pairs={{0,1},{1,0},{2,3},{3,2},{4,5},{5,4},{6,7},{7,6},{8,9},{9,8},{10,11... | collective-permute-start | bytes 319496 | tf_op jit(solution)/shard_map/ppermute | solution.py:372
  25.7 7.0 %slice-start = ((s8[12582912]{0:T(1024)(128)(4,1)}), s8[4194304]{0:T(1024)(128)(4,1)S(1)}, s32[]{:S(2)}) async-start(s8[12582912]{0:T(1024)(128)(4,1)} %bitcast.2), calls=%async_computation | async-start | bytes 8388608
  25.7 7.0 %slice-start.1 = ((s8[12582912]{0:T(1024)(128)(4,1)}), s8[4194304]{0:T(1024)(128)(4,1)S(1)}, s32[]{:S(2)}) async-start(s8[12582912]{0:T(1024)(128)(4,1)} %bitcast.2), calls=%async_computation.1 | async-start | bytes 8388608
  26.9 3.6 %copy-start.4 = (bf16[3072,4]{0,1:T(4,128)(2,1)S(1)}, bf16[3072,4]{0,1:T(4,128)(2,1)}, u32[]{:S(2)}) copy-start(bf16[3072,4]{0,1:T(4,128)(2,1)} %param.17) | copy-start | bytes 73732
  26.9 5.8 %slice-start.2 = ((s8[12582912]{0:T(1024)(128)(4,1)}), s8[4194304]{0:T(1024)(128)(4,1)S(1)}, s32[]{:S(2)}) async-start(s8[12582912]{0:T(1024)(128)(4,1)} %bitcast.2), calls=%async_computation.2 | async-start | bytes 8388608
  26.9 5.3 %collective-permute-start.18 = (bf16[104,512]{1,0:T(8,128)(2,1)S(1)}, bf16[104,512]{1,0:T(8,128)(2,1)S(1)}, u32[]{:S(2)}, u32[]{:S(2)}) collective-permute-start(bf16[104,512]{1,0:T(8,128)(2,1)S(1)} %shard_map.114.refs_3_), channel_id=1, source_target_pairs={{0,2},{1,3},{2,0},{3,1},{4,6},{5,7},{6,4},{7,5},{8,10},{9,11},{10,... | collective-permute-start | bytes 319496 | tf_op jit(solution)/shard_map/ppermute | solution.py:372
  28.0 4.2 %collective-permute-start.26 = (bf16[104,512]{1,0:T(8,128)(2,1)S(1)}, bf16[104,512]{1,0:T(8,128)(2,1)S(1)}, u32[]{:S(2)}, u32[]{:S(2)}) collective-permute-start(bf16[104,512]{1,0:T(8,128)(2,1)S(1)} %collective-permute-done.24.refs_0_), channel_id=1, source_target_pairs={{0,1},{1,0},{2,3},{3,2},{4,5},{5,4},{6,7},{7,6},{8,9},{9,8},{10,11... | collective-permute-start | bytes 319496 | tf_op jit(solution)/shard_map/ppermute | solution.py:372
  29.3 5.4 %collective-permute-start.15 = (bf16[104,512]{1,0:T(8,128)(2,1)S(1)}, bf16[104,512]{1,0:T(8,128)(2,1)S(1)}, u32[]{:S(2)}, u32[]{:S(2)}) collective-permute-start(bf16[104,512]{1,0:T(8,128)(2,1)S(1)} %shard_map.113.refs_4_), channel_id=1, source_target_pairs={{0,2},{1,3},{2,0},{3,1},{4,6},{5,7},{6,4},{7,5},{8,10},{9,11},{10,... | collective-permute-start | bytes 319496 | tf_op jit(solution)/shard_map/ppermute | solution.py:372
  30.3 4.3 %collective-permute-start.23 = (bf16[104,512]{1,0:T(8,128)(2,1)S(1)}, bf16[104,512]{1,0:T(8,128)(2,1)S(1)}, u32[]{:S(2)}, u32[]{:S(2)}) collective-permute-start(bf16[104,512]{1,0:T(8,128)(2,1)S(1)} %collective-permute-done.21.refs_0_), channel_id=1, source_target_pairs={{0,1},{1,0},{2,3},{3,2},{4,5},{5,4},{6,7},{7,6},{8,9},{9,8},{10,11... | collective-permute-start | bytes 319496 | tf_op jit(solution)/shard_map/ppermute | solution.py:372
  32.2 3.1 %collective-permute-start.19 = (bf16[104,512]{1,0:T(8,128)(2,1)S(1)}, bf16[104,512]{1,0:T(8,128)(2,1)S(1)}, u32[]{:S(2)}, u32[]{:S(2)}) collective-permute-start(bf16[104,512]{1,0:T(8,128)(2,1)S(1)} %shard_map.114.refs_3_), channel_id=1, source_target_pairs={{0,1},{1,0},{2,3},{3,2},{4,5},{5,4},{6,7},{7,6},{8,9},{9,8},{10,11... | collective-permute-start | bytes 319496 | tf_op jit(solution)/shard_map/ppermute | solution.py:372
  32.2 3.1 %collective-permute-start.20 = (bf16[104,512]{1,0:T(8,128)(2,1)S(1)}, bf16[104,512]{1,0:T(8,128)(2,1)S(1)}, u32[]{:S(2)}, u32[]{:S(2)}) collective-permute-start(bf16[104,512]{1,0:T(8,128)(2,1)S(1)} %collective-permute-done.18.refs_0_), channel_id=1, source_target_pairs={{0,1},{1,0},{2,3},{3,2},{4,5},{5,4},{6,7},{7,6},{8,9},{9,8},{10,11... | collective-permute-start | bytes 319496 | tf_op jit(solution)/shard_map/ppermute | solution.py:372
  33.3 2.7 %collective-permute-start.16 = (bf16[104,512]{1,0:T(8,128)(2,1)S(1)}, bf16[104,512]{1,0:T(8,128)(2,1)S(1)}, u32[]{:S(2)}, u32[]{:S(2)}) collective-permute-start(bf16[104,512]{1,0:T(8,128)(2,1)S(1)} %shard_map.113.refs_4_), channel_id=1, source_target_pairs={{0,1},{1,0},{2,3},{3,2},{4,5},{5,4},{6,7},{7,6},{8,9},{9,8},{10,11... | collective-permute-start | bytes 319496 | tf_op jit(solution)/shard_map/ppermute | solution.py:372
  34.7 1.4 %collective-permute-start.17 = (bf16[104,512]{1,0:T(8,128)(2,1)S(1)}, bf16[104,512]{1,0:T(8,128)(2,1)S(1)}, u32[]{:S(2)}, u32[]{:S(2)}) collective-permute-start(bf16[104,512]{1,0:T(8,128)(2,1)S(1)} %collective-permute-done.15.refs_0_), channel_id=1, source_target_pairs={{0,1},{1,0},{2,3},{3,2},{4,5},{5,4},{6,7},{7,6},{8,9},{9,8},{10,11... | collective-permute-start | bytes 319496 | tf_op jit(solution)/shard_map/ppermute | solution.py:372
  36.8 6.3 %collective-permute-start.27 = (bf16[32,768]{1,0:T(8,128)(2,1)S(1)}, bf16[32,768]{1,0:T(8,128)(2,1)S(1)}, u32[]{:S(2)}, u32[]{:S(2)}) collective-permute-start(bf16[32,768]{1,0:T(8,128)(2,1)S(1)} %get-tuple-element.32), channel_id=1, source_target_pairs={{0,12},{4,8},{8,4},{12,0},{1,13},{5,9},{9,5},{13,1},{2,14},{6,10},... | collective-permute-start | bytes 147464 | tf_op jit(solution)/shard_map/ppermute | solution.py:372
  39.1 5.8 %collective-permute-start.28 = (bf16[32,768]{1,0:T(8,128)(2,1)S(1)}, bf16[32,768]{1,0:T(8,128)(2,1)S(1)}, u32[]{:S(2)}, u32[]{:S(2)}) collective-permute-start(bf16[32,768]{1,0:T(8,128)(2,1)S(1)} %get-tuple-element.33), channel_id=1, source_target_pairs={{0,8},{4,12},{8,0},{12,4},{1,9},{5,13},{9,1},{13,5},{2,10},{6,14},... | collective-permute-start | bytes 147464 | tf_op jit(solution)/shard_map/ppermute | solution.py:372
  39.1 5.8 %collective-permute-start.29 = (bf16[32,768]{1,0:T(8,128)(2,1)S(1)}, bf16[32,768]{1,0:T(8,128)(2,1)S(1)}, u32[]{:S(2)}, u32[]{:S(2)}) collective-permute-start(bf16[32,768]{1,0:T(8,128)(2,1)S(1)} %get-tuple-element.34), channel_id=1, source_target_pairs={{0,4},{4,0},{8,12},{12,8},{1,5},{5,1},{9,13},{13,9},{2,6},{6,2},{1... | collective-permute-start | bytes 147464 | tf_op jit(solution)/shard_map/ppermute | solution.py:372
  44.9 1.6 %collective-permute-start.32 = (bf16[8,768]{1,0:T(8,128)(2,1)S(1)}, bf16[8,768]{1,0:T(8,128)(2,1)S(1)}, u32[]{:S(2)}, u32[]{:S(2)}) collective-permute-start(bf16[8,768]{1,0:T(8,128)(2,1)S(1)} %get-tuple-element.38), channel_id=1, source_target_pairs={{0,1},{1,0},{2,3},{3,2},{4,5},{5,4},{6,7},{7,6},{8,9},{9,8},{10,11... | collective-permute-start | bytes 36872 | tf_op jit(solution)/shard_map/ppermute | solution.py:372
  45.0 2.5 %collective-permute-start.30 = (bf16[8,768]{1,0:T(8,128)(2,1)S(1)}, bf16[8,768]{1,0:T(8,128)(2,1)S(1)}, u32[]{:S(2)}, u32[]{:S(2)}) collective-permute-start(bf16[8,768]{1,0:T(8,128)(2,1)S(1)} %get-tuple-element.36), channel_id=1, source_target_pairs={{0,1},{1,0},{2,3},{3,2},{4,5},{5,4},{6,7},{7,6},{8,9},{9,8},{10,11... | collective-permute-start | bytes 36872 | tf_op jit(solution)/shard_map/ppermute | solution.py:372
  45.5 3.7 %collective-permute-start.31 = (bf16[8,768]{1,0:T(8,128)(2,1)S(1)}, bf16[8,768]{1,0:T(8,128)(2,1)S(1)}, u32[]{:S(2)}, u32[]{:S(2)}) collective-permute-start(bf16[8,768]{1,0:T(8,128)(2,1)S(1)} %get-tuple-element.37), channel_id=1, source_target_pairs={{0,2},{1,3},{2,0},{3,1},{4,6},{5,7},{6,4},{7,5},{8,10},{9,11},{10,... | collective-permute-start | bytes 36872 | tf_op jit(solution)/shard_map/ppermute | solution.py:372
  46.5 3.7 %collective-permute-start.33 = (bf16[8,768]{1,0:T(8,128)(2,1)S(1)}, bf16[8,768]{1,0:T(8,128)(2,1)S(1)}, u32[]{:S(2)}, u32[]{:S(2)}) collective-permute-start(bf16[8,768]{1,0:T(8,128)(2,1)S(1)} %collective-permute-done.32), channel_id=1, source_target_pairs={{0,2},{1,3},{2,0},{3,1},{4,6},{5,7},{6,4},{7,5},{8,10},{9,11},{10,... | collective-permute-start | bytes 36872 | tf_op jit(solution)/shard_map/ppermute | solution.py:372
  (3 other events, 2.3 us)

commit v5 on v4

--- a/solution.py
+++ b/solution.py
@@ -538,9 +538,9 @@
         flops=10**6,
         vmem=4 * MIB,
     )
-    from_across = flip(flip(to_across, "sub", 1), "sub", 2)
     from_near = flip(to_near, "sub", 1)
     from_far = flip(to_far, "sub", 2)
+    from_across = flip(to_across, "sub", 3)
     return call(
         finish_kernel,
         jax.ShapeDtypeStruct((rows, width), bf16),

time: 51 us -> 50 us (0.980)
  starting transfers between devices: 24.4 us -> 23.8 us
    ppermute x34 -> x33, starting transfers between devices: 24.4 us -> 23.8 us  [flip(): lax.ppermute(x, axis, [(i, i ^ bits) for i in range(lax.axis_size(axis))])]
    ppermute x34 -> x33, waiting for transfers between devices: 13.1 us -> 12.8 us  [flip(): lax.ppermute(x, axis, [(i, i ^ bits) for i in range(lax.axis_size(axis))])]
  transfers between devices with their start and end apart: 34 -> 33, of which waited for: 11 -> 11; matrix products, arithmetic and copies ran while one was open for 0% -> 0% of each run, Pallas kernels for 13% -> 13%
where the time goes in v5:
time: 50 us; the launch traced here: 49.8 us
  starting transfers between devices  23.8 us (48%)
  waiting for transfers between devices  12.8 us (26%)
  Pallas kernels  11.3 us (23%)
  local copies, waits for them, and re-layouts  1.61 us (3%)
    ppermute x33, starting transfers between devices, flip(): lax.ppermute(x, axis, [(i, i ^ bits) for i in range(lax.axis_size(axis))])  23.8 us
    ppermute x33, waiting for transfers between devices, flip(): lax.ppermute(x, axis, [(i, i ^ bits) for i in range(lax.axis_size(axis))])  12.8 us
    pallas_call x14, Pallas kernels, call(): pl.pallas_call(body, out_shape=out_shapes, in_specs=specs, out_specs=jax....  11.3 us
    unnamed x34, local copies, waits for them, and re-layouts  1.61 us
  transfers between devices with their start and end apart: 33, of which 11 were waited for; matrix products, arithmetic and copies ran while one was open for 0% of the time, Pallas kernels for 13%

profile of v5, /device:TPU:0, one launch (start us, length us, event | category | flops | bytes accessed | tf_op | source)
XLA Modules:
  0.0 49.8 jit_solution(11501404862074639730)
XLA Ops:
  0.1 0.6 %copy-done.6 = s32[32,2]{0,1:T(2,128)S(1)} copy-done((s32[32,2]{0,1:T(2,128)S(1)}, s32[32,2]{0,1:T(2,128)}, u32[]{:S(2)}) %copy-start.6) | copy-done | bytes 280
  0.7 0.1 copy-done.3
  0.8 0.5 copy-done
  1.3 0.3 copy-done.1
  1.7 1.7 %shard_map.110 = (bf16[8,3200]{1,0:T(8,128)(2,1)S(1)}, bf16[8,3072]{1,0:T(8,128)(2,1)S(1)}) custom-call(f32[8,128]{1,0:T(8,128)S(1)} %shard_map.109._, s32[8]{0:T(128)S(1)} %copy-done.7, s32[2,32]{1,0:T(2,128)S(1)} %bitcast.9, bf16[8,3072]{1,0:T(8,128)(2,1)S(1)} %copy-done.2, bf16[8,128,512]{2,1,0:T(8,128)(2,1)S(1)} %copy-done, ...), custom_call_target="tpu_custom_call" | custom-call | flops 30000001024 | bytes 104857600 | tf_op jit(solution)/shard_map/pallas_call | solution.py:138
  3.3 3.1 %collective-permute-start.7 = (bf16[8,3200]{1,0:T(8,128)(2,1)S(1)}, bf16[8,3200]{1,0:T(8,128)(2,1)S(1)}, u32[]{:S(2)}, u32[]{:S(2)}) collective-permute-start(bf16[8,3200]{1,0:T(8,128)(2,1)S(1)} %get-tuple-element.23.refs_0_), channel_id=1, source_target_pairs={{0,4},{4,0},{8,12},{12,8},{1,5},{5,1},{9,13},{13,9},{2,6},{6,2},{1... | collective-permute-start | bytes 153608 | tf_op jit(solution)/shard_map/ppermute | solution.py:372
  6.4 2.5 %collective-permute-start.11 = (bf16[8,3200]{1,0:T(8,128)(2,1)S(1)}, bf16[8,3200]{1,0:T(8,128)(2,1)S(1)}, u32[]{:S(2)}, u32[]{:S(2)}) collective-permute-start(bf16[8,3200]{1,0:T(8,128)(2,1)S(1)} %get-tuple-element.23.refs_0_), channel_id=1, source_target_pairs={{0,12},{4,8},{8,4},{12,0},{1,13},{5,9},{9,5},{13,1},{2,14},{6,10},... | collective-permute-start | bytes 153608 | tf_op jit(solution)/shard_map/ppermute | solution.py:372
  8.9 0.1 collective-permute-start.3
  9.0 1.5 %collective-permute-start.1 = (bf16[8,3200]{1,0:T(8,128)(2,1)S(1)}, bf16[8,3200]{1,0:T(8,128)(2,1)S(1)}, u32[]{:S(2)}, u32[]{:S(2)}) collective-permute-start(bf16[8,3200]{1,0:T(8,128)(2,1)S(1)} %get-tuple-element.23.refs_0_), channel_id=1, source_target_pairs={{0,2},{1,3},{2,0},{3,1},{4,6},{5,7},{6,4},{7,5},{8,10},{9,11},{10,... | collective-permute-start | bytes 153608 | tf_op jit(solution)/shard_map/ppermute | solution.py:372
  10.5 0.5 %collective-permute-start.9 = (bf16[8,3200]{1,0:T(8,128)(2,1)S(1)}, bf16[8,3200]{1,0:T(8,128)(2,1)S(1)}, u32[]{:S(2)}, u32[]{:S(2)}) collective-permute-start(bf16[8,3200]{1,0:T(8,128)(2,1)S(1)} %collective-permute-done.7.refs_0_), channel_id=1, source_target_pairs={{0,2},{1,3},{2,0},{3,1},{4,6},{5,7},{6,4},{7,5},{8,10},{9,11},{10,... | collective-permute-start | bytes 153608 | tf_op jit(solution)/shard_map/ppermute | solution.py:372
  11.1 1.9 %collective-permute-done.11.refs_4_ = bf16[8,3200]{1,0:T(8,128)(2,1)S(1)} collective-permute-done((bf16[8,3200]{1,0:T(8,128)(2,1)S(1)}, bf16[8,3200]{1,0:T(8,128)(2,1)S(1)}, u32[]{:S(2)}, u32[]{:S(2)}) %collective-permute-start.11) | collective-permute-done | bytes 51232 | tf_op jit(solution)/shard_map/ppermute | solution.py:372
  13.0 1.5 %collective-permute-start.13 = (bf16[8,3200]{1,0:T(8,128)(2,1)S(1)}, bf16[8,3200]{1,0:T(8,128)(2,1)S(1)}, u32[]{:S(2)}, u32[]{:S(2)}) collective-permute-start(bf16[8,3200]{1,0:T(8,128)(2,1)S(1)} %collective-permute-done.11.refs_4_), channel_id=1, source_target_pairs={{0,2},{1,3},{2,0},{3,1},{4,6},{5,7},{6,4},{7,5},{8,10},{9,11},{10,... | collective-permute-start | bytes 153608 | tf_op jit(solution)/shard_map/ppermute | solution.py:372
  14.5 0.5 %collective-permute-start.8 = (bf16[8,3200]{1,0:T(8,128)(2,1)S(1)}, bf16[8,3200]{1,0:T(8,128)(2,1)S(1)}, u32[]{:S(2)}, u32[]{:S(2)}) collective-permute-start(bf16[8,3200]{1,0:T(8,128)(2,1)S(1)} %collective-permute-done.7.refs_0_), channel_id=1, source_target_pairs={{0,1},{1,0},{2,3},{3,2},{4,5},{5,4},{6,7},{7,6},{8,9},{9,8},{10,11... | collective-permute-start | bytes 153608 | tf_op jit(solution)/shard_map/ppermute | solution.py:372
  15.0 1.0 %collective-permute-start.5 = (bf16[8,3200]{1,0:T(8,128)(2,1)S(1)}, bf16[8,3200]{1,0:T(8,128)(2,1)S(1)}, u32[]{:S(2)}, u32[]{:S(2)}) collective-permute-start(bf16[8,3200]{1,0:T(8,128)(2,1)S(1)} %collective-permute-done.3.refs_4_), channel_id=1, source_target_pairs={{0,2},{1,3},{2,0},{3,1},{4,6},{5,7},{6,4},{7,5},{8,10},{9,11},{10,... | collective-permute-start | bytes 153608 | tf_op jit(solution)/shard_map/ppermute | solution.py:372
  16.0 0.2 collective-permute-start.10
  16.2 0.9 %collective-permute-done.13.refs_6_ = bf16[8,3200]{1,0:T(8,128)(2,1)S(1)} collective-permute-done((bf16[8,3200]{1,0:T(8,128)(2,1)S(1)}, bf16[8,3200]{1,0:T(8,128)(2,1)S(1)}, u32[]{:S(2)}, u32[]{:S(2)}) %collective-permute-start.13) | collective-permute-done | bytes 51232 | tf_op jit(solution)/shard_map/ppermute | solution.py:372
  17.1 0.5 %collective-permute-start = (bf16[8,3200]{1,0:T(8,128)(2,1)S(1)}, bf16[8,3200]{1,0:T(8,128)(2,1)S(1)}, u32[]{:S(2)}, u32[]{:S(2)}) collective-permute-start(bf16[8,3200]{1,0:T(8,128)(2,1)S(1)} %get-tuple-element.23.refs_0_), channel_id=1, source_target_pairs={{0,1},{1,0},{2,3},{3,2},{4,5},{5,4},{6,7},{7,6},{8,9},{9,8},{10,11... | collective-permute-start | bytes 153608 | tf_op jit(solution)/shard_map/ppermute | solution.py:372
  17.7 1.4 %collective-permute-done.5.refs_6_ = bf16[8,3200]{1,0:T(8,128)(2,1)S(1)} collective-permute-done((bf16[8,3200]{1,0:T(8,128)(2,1)S(1)}, bf16[8,3200]{1,0:T(8,128)(2,1)S(1)}, u32[]{:S(2)}, u32[]{:S(2)}) %collective-permute-start.5) | collective-permute-done | bytes 51232 | tf_op jit(solution)/shard_map/ppermute | solution.py:372
  19.1 0.5 %collective-permute-start.6 = (bf16[8,3200]{1,0:T(8,128)(2,1)S(1)}, bf16[8,3200]{1,0:T(8,128)(2,1)S(1)}, u32[]{:S(2)}, u32[]{:S(2)}) collective-permute-start(bf16[8,3200]{1,0:T(8,128)(2,1)S(1)} %collective-permute-done.5.refs_6_), channel_id=1, source_target_pairs={{0,1},{1,0},{2,3},{3,2},{4,5},{5,4},{6,7},{7,6},{8,9},{9,8},{10,11... | collective-permute-start | bytes 153608 | tf_op jit(solution)/shard_map/ppermute | solution.py:372
  19.6 0.6 %shard_map.111 = (bf16[104,3072]{1,0:T(8,128)(2,1)S(1)}, bf16[64,128]{1,0:T(8,128)(2,1)S(1)}) custom-call(bf16[8,3200]{1,0:T(8,128)(2,1)S(1)} %collective-permute-done.7.refs_0_, bf16[8,3200]{1,0:T(8,128)(2,1)S(1)} %collective-permute-done.8.refs_1_, bf16[8,3200]{1,0:T(8,128)(2,1)S(1)} %collective-permute-done.9.refs_2_, ...), custom_call_target="tpu_custom_call" | custom-call | flops 100000000 | tf_op jit(solution)/shard_map/pallas_call | solution.py:138
  20.3 0.2 collective-permute-done.6.refs_7_
  20.6 1.6 %shard_map.112 = (bf16[104,3072]{1,0:T(8,128)(2,1)S(1)}, bf16[64,128]{1,0:T(8,128)(2,1)S(1)}, bf16[104,512]{1,0:T(8,128)(2,1)S(1)}) custom-call(bf16[8,3200]{1,0:T(8,128)(2,1)S(1)} %get-tuple-element.23.refs_0_, bf16[8,3200]{1,0:T(8,128)(2,1)S(1)} %collective-permute-done.refs_1_, bf16[8,3200]{1,0:T(8,128)(2,1)S(1)} %collective-permute-done.1.refs_2_, ...), custom_call_target="tpu_custom_call" | custom-call | flops 1000000000 | tf_op jit(solution)/shard_map/pallas_call | solution.py:138
  22.1 1.1 %collective-permute-start.24 = (bf16[104,512]{1,0:T(8,128)(2,1)S(1)}, bf16[104,512]{1,0:T(8,128)(2,1)S(1)}, u32[]{:S(2)}, u32[]{:S(2)}) collective-permute-start(bf16[104,512]{1,0:T(8,128)(2,1)S(1)} %get-tuple-element.26.refs_3_), channel_id=1, source_target_pairs={{0,2},{1,3},{2,0},{3,1},{4,6},{5,7},{6,4},{7,5},{8,10},{9,11},{10,... | collective-permute-start | bytes 319496 | tf_op jit(solution)/shard_map/ppermute | solution.py:372
  23.3 1.2 %shard_map.115.refs_3_ = bf16[104,512]{1,0:T(8,128)(2,1)S(1)} custom-call(bf16[104,3072]{1,0:T(8,128)(2,1)S(1)} %get-tuple-element.25.x_ref.refs_2_, bf16[3072,2048]{1,0:T(8,128)(2,1)S(1)} %bitcast.5, bf16[3072,2048]{1,0:T(8,128)(2,1)S(1)} %bitcast.7), custom_call_target="tpu_custom_call" | custom-call | flops 1000000000 | tf_op jit(solution)/shard_map/pallas_call | solution.py:138
  24.5 1.0 %collective-permute-start.21 = (bf16[104,512]{1,0:T(8,128)(2,1)S(1)}, bf16[104,512]{1,0:T(8,128)(2,1)S(1)}, u32[]{:S(2)}, u32[]{:S(2)}) collective-permute-start(bf16[104,512]{1,0:T(8,128)(2,1)S(1)} %shard_map.115.refs_3_), channel_id=1, source_target_pairs={{0,2},{1,3},{2,0},{3,1},{4,6},{5,7},{6,4},{7,5},{8,10},{9,11},{10,... | collective-permute-start | bytes 319496 | tf_op jit(solution)/shard_map/ppermute | solution.py:372
  25.5 0.2 collective-permute-start.22
  25.7 1.2 %shard_map.114.refs_3_ = bf16[104,512]{1,0:T(8,128)(2,1)S(1)} custom-call(bf16[104,3072]{1,0:T(8,128)(2,1)S(1)} %get-tuple-element.25.x_ref.refs_2_, bf16[3072,2048]{1,0:T(8,128)(2,1)S(1)} %bitcast.5, bf16[3072,2048]{1,0:T(8,128)(2,1)S(1)} %bitcast.7), custom_call_target="tpu_custom_call" | custom-call | flops 1000000000 | tf_op jit(solution)/shard_map/pallas_call | solution.py:138
  26.9 1.1 %collective-permute-start.18 = (bf16[104,512]{1,0:T(8,128)(2,1)S(1)}, bf16[104,512]{1,0:T(8,128)(2,1)S(1)}, u32[]{:S(2)}, u32[]{:S(2)}) collective-permute-start(bf16[104,512]{1,0:T(8,128)(2,1)S(1)} %shard_map.114.refs_3_), channel_id=1, source_target_pairs={{0,2},{1,3},{2,0},{3,1},{4,6},{5,7},{6,4},{7,5},{8,10},{9,11},{10,... | collective-permute-start | bytes 319496 | tf_op jit(solution)/shard_map/ppermute | solution.py:372
  28.1 1.2 %shard_map.113.refs_4_ = bf16[104,512]{1,0:T(8,128)(2,1)S(1)} custom-call(bf16[104,3072]{1,0:T(8,128)(2,1)S(1)} %get-tuple-element.25.x_ref.refs_2_, bf16[3072,2048]{1,0:T(8,128)(2,1)S(1)} %bitcast.5, bf16[3072,2048]{1,0:T(8,128)(2,1)S(1)} %bitcast.7), custom_call_target="tpu_custom_call" | custom-call | flops 1000000000 | tf_op jit(solution)/shard_map/pallas_call | solution.py:138
  29.3 1.0 %collective-permute-start.15 = (bf16[104,512]{1,0:T(8,128)(2,1)S(1)}, bf16[104,512]{1,0:T(8,128)(2,1)S(1)}, u32[]{:S(2)}, u32[]{:S(2)}) collective-permute-start(bf16[104,512]{1,0:T(8,128)(2,1)S(1)} %shard_map.113.refs_4_), channel_id=1, source_target_pairs={{0,2},{1,3},{2,0},{3,1},{4,6},{5,7},{6,4},{7,5},{8,10},{9,11},{10,... | collective-permute-start | bytes 319496 | tf_op jit(solution)/shard_map/ppermute | solution.py:372
  30.3 0.2 collective-permute-start.23
  30.5 0.7 %shard_map.119 = (bf16[128,128]{1,0:T(8,128)(2,1)S(1)}, f32[104,128]{1,0:T(8,128)S(1)}) custom-call(bf16[64,128]{1,0:T(8,128)(2,1)S(1)} %get-tuple-element.27.refs_0_, bf16[64,128]{1,0:T(8,128)(2,1)S(1)} %get-tuple-element.28.refs_1_, bf16[104,3072]{1,0:T(8,128)(2,1)S(1)} %get-tuple-element.25.x_ref.refs_2_, bf16[4,3072]{1,0:T(4,128)(2,1)S(1)} %bitcast.8), custom_call_target="tpu_custom_call" | custom-call | flops 1000000000 | tf_op jit(solution)/shard_map/pallas_call | solution.py:138
  31.2 1.0 %collective-permute-done.18.refs_0_ = bf16[104,512]{1,0:T(8,128)(2,1)S(1)} collective-permute-done((bf16[104,512]{1,0:T(8,128)(2,1)S(1)}, bf16[104,512]{1,0:T(8,128)(2,1)S(1)}, u32[]{:S(2)}, u32[]{:S(2)}) %collective-permute-start.18) | collective-permute-done | bytes 106528 | tf_op jit(solution)/shard_map/ppermute | solution.py:372
  32.2 0.5 %collective-permute-start.20 = (bf16[104,512]{1,0:T(8,128)(2,1)S(1)}, bf16[104,512]{1,0:T(8,128)(2,1)S(1)}, u32[]{:S(2)}, u32[]{:S(2)}) collective-permute-start(bf16[104,512]{1,0:T(8,128)(2,1)S(1)} %collective-permute-done.18.refs_0_), channel_id=1, source_target_pairs={{0,1},{1,0},{2,3},{3,2},{4,5},{5,4},{6,7},{7,6},{8,9},{9,8},{10,11... | collective-permute-start | bytes 319496 | tf_op jit(solution)/shard_map/ppermute | solution.py:372
  32.7 0.6 %shard_map.116.refs_5_ = f32[104,768]{1,0:T(8,128)S(1)} custom-call(bf16[104,512]{1,0:T(8,128)(2,1)S(1)} %collective-permute-done.24.refs_0_, bf16[104,512]{1,0:T(8,128)(2,1)S(1)} %collective-permute-done.25.refs_1_, bf16[104,512]{1,0:T(8,128)(2,1)S(1)} %collective-permute-done.26.refs_2_, bf16[104,512]{1,0:T(8,128)(2,1)S(1)} %get-tuple-element.26.refs_3_, ...), custom_call_target="tpu_custom_call" | custom-call | flops 1000000000 | tf_op jit(solution)/shard_map/pallas_call | solution.py:138
  33.4 1.2 %collective-permute-done.15.refs_0_ = bf16[104,512]{1,0:T(8,128)(2,1)S(1)} collective-permute-done((bf16[104,512]{1,0:T(8,128)(2,1)S(1)}, bf16[104,512]{1,0:T(8,128)(2,1)S(1)}, u32[]{:S(2)}, u32[]{:S(2)}) %collective-permute-start.15) | collective-permute-done | bytes 106528 | tf_op jit(solution)/shard_map/ppermute | solution.py:372
  34.7 0.6 %shard_map.117.refs_6_ = f32[104,768]{1,0:T(8,128)S(1)} custom-call(bf16[104,512]{1,0:T(8,128)(2,1)S(1)} %collective-permute-done.21.refs_0_, bf16[104,512]{1,0:T(8,128)(2,1)S(1)} %collective-permute-done.22.refs_1_, bf16[104,512]{1,0:T(8,128)(2,1)S(1)} %collective-permute-done.23.refs_2_, bf16[104,512]{1,0:T(8,128)(2,1)S(1)} %shard_map.115.refs_3_, ...), custom_call_target="tpu_custom_call" | custom-call | flops 1000000000 | tf_op jit(solution)/shard_map/pallas_call | solution.py:138
  35.3 0.7 %shard_map.118.refs_4_ = f32[104,768]{1,0:T(8,128)S(1)} custom-call(bf16[104,512]{1,0:T(8,128)(2,1)S(1)} %collective-permute-done.18.refs_0_, bf16[104,512]{1,0:T(8,128)(2,1)S(1)} %collective-permute-done.19.refs_1_, bf16[104,512]{1,0:T(8,128)(2,1)S(1)} %collective-permute-done.20.refs_2_, bf16[104,512]{1,0:T(8,128)(2,1)S(1)} %shard_map.114.refs_3_, ...), custom_call_target="tpu_custom_call" | custom-call | flops 1000000000 | tf_op jit(solution)/shard_map/pallas_call | solution.py:138
  36.0 0.7 %shard_map.120 = (bf16[32,768]{1,0:T(8,128)(2,1)S(1)}, bf16[32,768]{1,0:T(8,128)(2,1)S(1)}, bf16[32,768]{1,0:T(8,128)(2,1)S(1)}, bf16[32,768]{1,0:T(8,128)(2,1)S(1)}) custom-call(bf16[104,512]{1,0:T(8,128)(2,1)S(1)} %collective-permute-done.15.refs_0_, bf16[104,512]{1,0:T(8,128)(2,1)S(1)} %collective-permute-done.16.refs_1_, ...), custom_call_target="tpu_custom_call" | custom-call | flops 1000000000 | tf_op jit(solution)/shard_map/pallas_call | solution.py:138
  36.8 2.3 %collective-permute-start.27 = (bf16[32,768]{1,0:T(8,128)(2,1)S(1)}, bf16[32,768]{1,0:T(8,128)(2,1)S(1)}, u32[]{:S(2)}, u32[]{:S(2)}) collective-permute-start(bf16[32,768]{1,0:T(8,128)(2,1)S(1)} %get-tuple-element.32), channel_id=1, source_target_pairs={{0,12},{4,8},{8,4},{12,0},{1,13},{5,9},{9,5},{13,1},{2,14},{6,10},... | collective-permute-start | bytes 147464 | tf_op jit(solution)/shard_map/ppermute | solution.py:372
  39.1 2.1 %collective-permute-start.29 = (bf16[32,768]{1,0:T(8,128)(2,1)S(1)}, bf16[32,768]{1,0:T(8,128)(2,1)S(1)}, u32[]{:S(2)}, u32[]{:S(2)}) collective-permute-start(bf16[32,768]{1,0:T(8,128)(2,1)S(1)} %get-tuple-element.34), channel_id=1, source_target_pairs={{0,4},{4,0},{8,12},{12,8},{1,5},{5,1},{9,13},{13,9},{2,6},{6,2},{1... | collective-permute-start | bytes 147464 | tf_op jit(solution)/shard_map/ppermute | solution.py:372
  41.2 1.8 %collective-permute-done.27.refs_1_ = bf16[32,768]{1,0:T(8,128)(2,1)S(1)} collective-permute-done((bf16[32,768]{1,0:T(8,128)(2,1)S(1)}, bf16[32,768]{1,0:T(8,128)(2,1)S(1)}, u32[]{:S(2)}, u32[]{:S(2)}) %collective-permute-start.27) | collective-permute-done | bytes 49184 | tf_op jit(solution)/shard_map/ppermute | solution.py:372
  43.0 1.8 %collective-permute-done.28.refs_2_ = bf16[32,768]{1,0:T(8,128)(2,1)S(1)} collective-permute-done((bf16[32,768]{1,0:T(8,128)(2,1)S(1)}, bf16[32,768]{1,0:T(8,128)(2,1)S(1)}, u32[]{:S(2)}, u32[]{:S(2)}) %collective-permute-start.28) | collective-permute-done | bytes 49184 | tf_op jit(solution)/shard_map/ppermute | solution.py:372
  45.0 1.0 %collective-permute-start.31 = (bf16[8,768]{1,0:T(8,128)(2,1)S(1)}, bf16[8,768]{1,0:T(8,128)(2,1)S(1)}, u32[]{:S(2)}, u32[]{:S(2)}) collective-permute-start(bf16[8,768]{1,0:T(8,128)(2,1)S(1)} %get-tuple-element.37), channel_id=1, source_target_pairs={{0,2},{1,3},{2,0},{3,1},{4,6},{5,7},{6,4},{7,5},{8,10},{9,11},{10,... | collective-permute-start | bytes 36872 | tf_op jit(solution)/shard_map/ppermute | solution.py:372
  46.0 0.8 %collective-permute-start.32 = (bf16[8,768]{1,0:T(8,128)(2,1)S(1)}, bf16[8,768]{1,0:T(8,128)(2,1)S(1)}, u32[]{:S(2)}, u32[]{:S(2)}) collective-permute-start(bf16[8,768]{1,0:T(8,128)(2,1)S(1)} %get-tuple-element.38), channel_id=1, source_target_pairs={{0,3},{1,2},{2,1},{3,0},{4,7},{5,6},{6,5},{7,4},{8,11},{9,10},{10,... | collective-permute-start | bytes 36872 | tf_op jit(solution)/shard_map/ppermute | solution.py:372
  46.9 1.9 %collective-permute-done.31.refs_2_ = bf16[8,768]{1,0:T(8,128)(2,1)S(1)} collective-permute-done((bf16[8,768]{1,0:T(8,128)(2,1)S(1)}, bf16[8,768]{1,0:T(8,128)(2,1)S(1)}, u32[]{:S(2)}, u32[]{:S(2)}) %collective-permute-start.31) | collective-permute-done | bytes 12320 | tf_op jit(solution)/shard_map/ppermute | solution.py:372
  48.8 0.4 collective-permute-done.32.refs_3_
  49.2 0.6 %shard_map.122 = bf16[8,3072]{1,0:T(8,128)(2,1)} custom-call(bf16[8,3072]{1,0:T(8,128)(2,1)S(1)} %get-tuple-element.22.resid_ref, f32[8,768]{1,0:T(8,128)S(1)} %get-tuple-element.35.refs_0_, bf16[8,768]{1,0:T(8,128)(2,1)S(1)} %collective-permute-done.30.refs_1_, bf16[8,768]{1,0:T(8,128)(2,1)S(1)} %collective-permute-done.31.refs_2_, ...), custom_call_target="tpu_custom_call" | custom-call | flops 1000000 | tf_op jit(solution)/shard_map/pallas_call | solution.py:138
  (69 shorter events, 0.7 us)
Async XLA Ops:
  0.0 0.8 %copy-start.2 = (bf16[8,3072]{1,0:T(8,128)(2,1)S(1)}, bf16[8,3072]{1,0:T(8,128)(2,1)}, u32[]{:S(2)}) copy-start(bf16[8,3072]{1,0:T(8,128)(2,1)} %queries_ref.1) | copy-start | bytes 147460
  0.0 1.3 %copy-start = (bf16[8,128,512]{2,1,0:T(8,128)(2,1)S(1)}, bf16[8,128,512]{2,1,0:T(8,128)(2,1)}, u32[]{:S(2)}) copy-start(bf16[8,128,512]{2,1,0:T(8,128)(2,1)} %keys_ref.1) | copy-start | bytes 3145732
  0.0 1.6 %copy-start.1 = (bf16[8,128,512]{2,1,0:T(8,128)(2,1)S(1)}, bf16[8,128,512]{2,1,0:T(8,128)(2,1)}, u32[]{:S(2)}) copy-start(bf16[8,128,512]{2,1,0:T(8,128)(2,1)} %values_ref.1) | copy-start | bytes 3145732
  0.0 1.6 %copy-start.7 = (s32[8]{0:T(128)S(1)}, s32[8]{0:T(128)}, u32[]{:S(2)}) copy-start(s32[8]{0:T(128)} %lengths_ref.1) | copy-start | bytes 100
  0.0 1.6 %copy-start.5 = (bf16[3072]{0:T(1024)(128)(2,1)S(1)}, bf16[3072]{0:T(1024)(128)(2,1)}, u32[]{:S(2)}) copy-start(bf16[3072]{0:T(1024)(128)(2,1)} %gain_ref.1) | copy-start | bytes 18436
  0.0 20.5 %slice-start.3 = ((s8[12582912]{0:T(1024)(128)(4,1)}), s8[4194304]{0:T(1024)(128)(4,1)S(1)}, s32[]{:S(2)}) async-start(s8[12582912]{0:T(1024)(128)(4,1)} %bitcast.4), calls=%async_computation.3 | async-start | bytes 8388608
  0.0 20.5 %slice-start.6 = ((s8[12582912]{0:T(1024)(128)(4,1)}), s8[4194304]{0:T(1024)(128)(4,1)S(1)}, s32[]{:S(2)}) async-start(s8[12582912]{0:T(1024)(128)(4,1)} %bitcast.6), calls=%async_computation.6 | async-start | bytes 8388608
  1.6 18.9 %slice-start.4 = ((s8[12582912]{0:T(1024)(128)(4,1)}), s8[4194304]{0:T(1024)(128)(4,1)S(1)}, s32[]{:S(2)}) async-start(s8[12582912]{0:T(1024)(128)(4,1)} %bitcast.4), calls=%async_computation.4 | async-start | bytes 8388608
  1.6 18.9 %slice-start.5 = ((s8[12582912]{0:T(1024)(128)(4,1)}), s8[4194304]{0:T(1024)(128)(4,1)S(1)}, s32[]{:S(2)}) async-start(s8[12582912]{0:T(1024)(128)(4,1)} %bitcast.4), calls=%async_computation.5 | async-start | bytes 8388608
  1.6 18.9 %slice-start.7 = ((s8[12582912]{0:T(1024)(128)(4,1)}), s8[4194304]{0:T(1024)(128)(4,1)S(1)}, s32[]{:S(2)}) async-start(s8[12582912]{0:T(1024)(128)(4,1)} %bitcast.6), calls=%async_computation.7 | async-start | bytes 8388608
  1.6 18.9 %slice-start.8 = ((s8[12582912]{0:T(1024)(128)(4,1)}), s8[4194304]{0:T(1024)(128)(4,1)S(1)}, s32[]{:S(2)}) async-start(s8[12582912]{0:T(1024)(128)(4,1)} %bitcast.6), calls=%async_computation.8 | async-start | bytes 8388608
  3.3 7.2 %collective-permute-start.7 = (bf16[8,3200]{1,0:T(8,128)(2,1)S(1)}, bf16[8,3200]{1,0:T(8,128)(2,1)S(1)}, u32[]{:S(2)}, u32[]{:S(2)}) collective-permute-start(bf16[8,3200]{1,0:T(8,128)(2,1)S(1)} %get-tuple-element.23.refs_0_), channel_id=1, source_target_pairs={{0,4},{4,0},{8,12},{12,8},{1,5},{5,1},{9,13},{13,9},{2,6},{6,2},{1... | collective-permute-start | bytes 153608 | tf_op jit(solution)/shard_map/ppermute | solution.py:372
  6.4 6.6 %collective-permute-start.11 = (bf16[8,3200]{1,0:T(8,128)(2,1)S(1)}, bf16[8,3200]{1,0:T(8,128)(2,1)S(1)}, u32[]{:S(2)}, u32[]{:S(2)}) collective-permute-start(bf16[8,3200]{1,0:T(8,128)(2,1)S(1)} %get-tuple-element.23.refs_0_), channel_id=1, source_target_pairs={{0,12},{4,8},{8,4},{12,0},{1,13},{5,9},{9,5},{13,1},{2,14},{6,10},... | collective-permute-start | bytes 153608 | tf_op jit(solution)/shard_map/ppermute | solution.py:372
  8.9 5.6 %collective-permute-start.3 = (bf16[8,3200]{1,0:T(8,128)(2,1)S(1)}, bf16[8,3200]{1,0:T(8,128)(2,1)S(1)}, u32[]{:S(2)}, u32[]{:S(2)}) collective-permute-start(bf16[8,3200]{1,0:T(8,128)(2,1)S(1)} %get-tuple-element.23.refs_0_), channel_id=1, source_target_pairs={{0,8},{4,12},{8,0},{12,4},{1,9},{5,13},{9,1},{13,5},{2,10},{6,14},... | collective-permute-start | bytes 153608 | tf_op jit(solution)/shard_map/ppermute | solution.py:372
  9.0 6.0 %collective-permute-start.1 = (bf16[8,3200]{1,0:T(8,128)(2,1)S(1)}, bf16[8,3200]{1,0:T(8,128)(2,1)S(1)}, u32[]{:S(2)}, u32[]{:S(2)}) collective-permute-start(bf16[8,3200]{1,0:T(8,128)(2,1)S(1)} %get-tuple-element.23.refs_0_), channel_id=1, source_target_pairs={{0,2},{1,3},{2,0},{3,1},{4,6},{5,7},{6,4},{7,5},{8,10},{9,11},{10,... | collective-permute-start | bytes 153608 | tf_op jit(solution)/shard_map/ppermute | solution.py:372
  10.5 5.4 %collective-permute-start.9 = (bf16[8,3200]{1,0:T(8,128)(2,1)S(1)}, bf16[8,3200]{1,0:T(8,128)(2,1)S(1)}, u32[]{:S(2)}, u32[]{:S(2)}) collective-permute-start(bf16[8,3200]{1,0:T(8,128)(2,1)S(1)} %collective-permute-done.7.refs_0_), channel_id=1, source_target_pairs={{0,2},{1,3},{2,0},{3,1},{4,6},{5,7},{6,4},{7,5},{8,10},{9,11},{10,... | collective-permute-start | bytes 153608 | tf_op jit(solution)/shard_map/ppermute | solution.py:372
  13.0 4.1 %collective-permute-start.13 = (bf16[8,3200]{1,0:T(8,128)(2,1)S(1)}, bf16[8,3200]{1,0:T(8,128)(2,1)S(1)}, u32[]{:S(2)}, u32[]{:S(2)}) collective-permute-start(bf16[8,3200]{1,0:T(8,128)(2,1)S(1)} %collective-permute-done.11.refs_4_), channel_id=1, source_target_pairs={{0,2},{1,3},{2,0},{3,1},{4,6},{5,7},{6,4},{7,5},{8,10},{9,11},{10,... | collective-permute-start | bytes 153608 | tf_op jit(solution)/shard_map/ppermute | solution.py:372
  14.5 2.6 %collective-permute-start.12 = (bf16[8,3200]{1,0:T(8,128)(2,1)S(1)}, bf16[8,3200]{1,0:T(8,128)(2,1)S(1)}, u32[]{:S(2)}, u32[]{:S(2)}) collective-permute-start(bf16[8,3200]{1,0:T(8,128)(2,1)S(1)} %collective-permute-done.11.refs_4_), channel_id=1, source_target_pairs={{0,1},{1,0},{2,3},{3,2},{4,5},{5,4},{6,7},{7,6},{8,9},{9,8},{10,11... | collective-permute-start | bytes 153608 | tf_op jit(solution)/shard_map/ppermute | solution.py:372
  14.5 3.1 %collective-permute-start.8 = (bf16[8,3200]{1,0:T(8,128)(2,1)S(1)}, bf16[8,3200]{1,0:T(8,128)(2,1)S(1)}, u32[]{:S(2)}, u32[]{:S(2)}) collective-permute-start(bf16[8,3200]{1,0:T(8,128)(2,1)S(1)} %collective-permute-done.7.refs_0_), channel_id=1, source_target_pairs={{0,1},{1,0},{2,3},{3,2},{4,5},{5,4},{6,7},{7,6},{8,9},{9,8},{10,11... | collective-permute-start | bytes 153608 | tf_op jit(solution)/shard_map/ppermute | solution.py:372
  15.0 4.1 %collective-permute-start.5 = (bf16[8,3200]{1,0:T(8,128)(2,1)S(1)}, bf16[8,3200]{1,0:T(8,128)(2,1)S(1)}, u32[]{:S(2)}, u32[]{:S(2)}) collective-permute-start(bf16[8,3200]{1,0:T(8,128)(2,1)S(1)} %collective-permute-done.3.refs_4_), channel_id=1, source_target_pairs={{0,2},{1,3},{2,0},{3,1},{4,6},{5,7},{6,4},{7,5},{8,10},{9,11},{10,... | collective-permute-start | bytes 153608 | tf_op jit(solution)/shard_map/ppermute | solution.py:372
  16.0 3.1 %collective-permute-start.10 = (bf16[8,3200]{1,0:T(8,128)(2,1)S(1)}, bf16[8,3200]{1,0:T(8,128)(2,1)S(1)}, u32[]{:S(2)}, u32[]{:S(2)}) collective-permute-start(bf16[8,3200]{1,0:T(8,128)(2,1)S(1)} %collective-permute-done.9.refs_2_), channel_id=1, source_target_pairs={{0,1},{1,0},{2,3},{3,2},{4,5},{5,4},{6,7},{7,6},{8,9},{9,8},{10,11... | collective-permute-start | bytes 153608 | tf_op jit(solution)/shard_map/ppermute | solution.py:372
  17.1 2.5 %collective-permute-start.14 = (bf16[8,3200]{1,0:T(8,128)(2,1)S(1)}, bf16[8,3200]{1,0:T(8,128)(2,1)S(1)}, u32[]{:S(2)}, u32[]{:S(2)}) collective-permute-start(bf16[8,3200]{1,0:T(8,128)(2,1)S(1)} %collective-permute-done.13.refs_6_), channel_id=1, source_target_pairs={{0,1},{1,0},{2,3},{3,2},{4,5},{5,4},{6,7},{7,6},{8,9},{9,8},{10,11... | collective-permute-start | bytes 153608 | tf_op jit(solution)/shard_map/ppermute | solution.py:372
  17.1 3.1 %collective-permute-start = (bf16[8,3200]{1,0:T(8,128)(2,1)S(1)}, bf16[8,3200]{1,0:T(8,128)(2,1)S(1)}, u32[]{:S(2)}, u32[]{:S(2)}) collective-permute-start(bf16[8,3200]{1,0:T(8,128)(2,1)S(1)} %get-tuple-element.23.refs_0_), channel_id=1, source_target_pairs={{0,1},{1,0},{2,3},{3,2},{4,5},{5,4},{6,7},{7,6},{8,9},{9,8},{10,11... | collective-permute-start | bytes 153608 | tf_op jit(solution)/shard_map/ppermute | solution.py:372
  17.6 2.6 %collective-permute-start.4 = (bf16[8,3200]{1,0:T(8,128)(2,1)S(1)}, bf16[8,3200]{1,0:T(8,128)(2,1)S(1)}, u32[]{:S(2)}, u32[]{:S(2)}) collective-permute-start(bf16[8,3200]{1,0:T(8,128)(2,1)S(1)} %collective-permute-done.3.refs_4_), channel_id=1, source_target_pairs={{0,1},{1,0},{2,3},{3,2},{4,5},{5,4},{6,7},{7,6},{8,9},{9,8},{10,11... | collective-permute-start | bytes 153608 | tf_op jit(solution)/shard_map/ppermute | solution.py:372
  19.1 1.2 %collective-permute-start.2 = (bf16[8,3200]{1,0:T(8,128)(2,1)S(1)}, bf16[8,3200]{1,0:T(8,128)(2,1)S(1)}, u32[]{:S(2)}, u32[]{:S(2)}) collective-permute-start(bf16[8,3200]{1,0:T(8,128)(2,1)S(1)} %collective-permute-done.1.refs_2_), channel_id=1, source_target_pairs={{0,1},{1,0},{2,3},{3,2},{4,5},{5,4},{6,7},{7,6},{8,9},{9,8},{10,11... | collective-permute-start | bytes 153608 | tf_op jit(solution)/shard_map/ppermute | solution.py:372
  19.1 1.4 %collective-permute-start.6 = (bf16[8,3200]{1,0:T(8,128)(2,1)S(1)}, bf16[8,3200]{1,0:T(8,128)(2,1)S(1)}, u32[]{:S(2)}, u32[]{:S(2)}) collective-permute-start(bf16[8,3200]{1,0:T(8,128)(2,1)S(1)} %collective-permute-done.5.refs_6_), channel_id=1, source_target_pairs={{0,1},{1,0},{2,3},{3,2},{4,5},{5,4},{6,7},{7,6},{8,9},{9,8},{10,11... | collective-permute-start | bytes 153608 | tf_op jit(solution)/shard_map/ppermute | solution.py:372
  22.1 5.9 %collective-permute-start.24 = (bf16[104,512]{1,0:T(8,128)(2,1)S(1)}, bf16[104,512]{1,0:T(8,128)(2,1)S(1)}, u32[]{:S(2)}, u32[]{:S(2)}) collective-permute-start(bf16[104,512]{1,0:T(8,128)(2,1)S(1)} %get-tuple-element.26.refs_3_), channel_id=1, source_target_pairs={{0,2},{1,3},{2,0},{3,1},{4,6},{5,7},{6,4},{7,5},{8,10},{9,11},{10,... | collective-permute-start | bytes 319496 | tf_op jit(solution)/shard_map/ppermute | solution.py:372
  23.3 6.0 %collective-permute-start.25 = (bf16[104,512]{1,0:T(8,128)(2,1)S(1)}, bf16[104,512]{1,0:T(8,128)(2,1)S(1)}, u32[]{:S(2)}, u32[]{:S(2)}) collective-permute-start(bf16[104,512]{1,0:T(8,128)(2,1)S(1)} %get-tuple-element.26.refs_3_), channel_id=1, source_target_pairs={{0,1},{1,0},{2,3},{3,2},{4,5},{5,4},{6,7},{7,6},{8,9},{9,8},{10,11... | collective-permute-start | bytes 319496 | tf_op jit(solution)/shard_map/ppermute | solution.py:372
  24.5 5.8 %collective-permute-start.21 = (bf16[104,512]{1,0:T(8,128)(2,1)S(1)}, bf16[104,512]{1,0:T(8,128)(2,1)S(1)}, u32[]{:S(2)}, u32[]{:S(2)}) collective-permute-start(bf16[104,512]{1,0:T(8,128)(2,1)S(1)} %shard_map.115.refs_3_), channel_id=1, source_target_pairs={{0,2},{1,3},{2,0},{3,1},{4,6},{5,7},{6,4},{7,5},{8,10},{9,11},{10,... | collective-permute-start | bytes 319496 | tf_op jit(solution)/shard_map/ppermute | solution.py:372
  25.5 7.8 %collective-permute-start.22 = (bf16[104,512]{1,0:T(8,128)(2,1)S(1)}, bf16[104,512]{1,0:T(8,128)(2,1)S(1)}, u32[]{:S(2)}, u32[]{:S(2)}) collective-permute-start(bf16[104,512]{1,0:T(8,128)(2,1)S(1)} %shard_map.115.refs_3_), channel_id=1, source_target_pairs={{0,1},{1,0},{2,3},{3,2},{4,5},{5,4},{6,7},{7,6},{8,9},{9,8},{10,11... | collective-permute-start | bytes 319496 | tf_op jit(solution)/shard_map/ppermute | solution.py:372
  25.7 7.0 %slice-start = ((s8[12582912]{0:T(1024)(128)(4,1)}), s8[4194304]{0:T(1024)(128)(4,1)S(1)}, s32[]{:S(2)}) async-start(s8[12582912]{0:T(1024)(128)(4,1)} %bitcast.2), calls=%async_computation | async-start | bytes 8388608
  25.7 7.0 %slice-start.1 = ((s8[12582912]{0:T(1024)(128)(4,1)}), s8[4194304]{0:T(1024)(128)(4,1)S(1)}, s32[]{:S(2)}) async-start(s8[12582912]{0:T(1024)(128)(4,1)} %bitcast.2), calls=%async_computation.1 | async-start | bytes 8388608
  26.9 3.6 %copy-start.4 = (bf16[3072,4]{0,1:T(4,128)(2,1)S(1)}, bf16[3072,4]{0,1:T(4,128)(2,1)}, u32[]{:S(2)}) copy-start(bf16[3072,4]{0,1:T(4,128)(2,1)} %param.17) | copy-start | bytes 73732
  26.9 5.8 %slice-start.2 = ((s8[12582912]{0:T(1024)(128)(4,1)}), s8[4194304]{0:T(1024)(128)(4,1)S(1)}, s32[]{:S(2)}) async-start(s8[12582912]{0:T(1024)(128)(4,1)} %bitcast.2), calls=%async_computation.2 | async-start | bytes 8388608
  26.9 5.3 %collective-permute-start.18 = (bf16[104,512]{1,0:T(8,128)(2,1)S(1)}, bf16[104,512]{1,0:T(8,128)(2,1)S(1)}, u32[]{:S(2)}, u32[]{:S(2)}) collective-permute-start(bf16[104,512]{1,0:T(8,128)(2,1)S(1)} %shard_map.114.refs_3_), channel_id=1, source_target_pairs={{0,2},{1,3},{2,0},{3,1},{4,6},{5,7},{6,4},{7,5},{8,10},{9,11},{10,... | collective-permute-start | bytes 319496 | tf_op jit(solution)/shard_map/ppermute | solution.py:372
  28.0 4.2 %collective-permute-start.26 = (bf16[104,512]{1,0:T(8,128)(2,1)S(1)}, bf16[104,512]{1,0:T(8,128)(2,1)S(1)}, u32[]{:S(2)}, u32[]{:S(2)}) collective-permute-start(bf16[104,512]{1,0:T(8,128)(2,1)S(1)} %collective-permute-done.24.refs_0_), channel_id=1, source_target_pairs={{0,1},{1,0},{2,3},{3,2},{4,5},{5,4},{6,7},{7,6},{8,9},{9,8},{10,11... | collective-permute-start | bytes 319496 | tf_op jit(solution)/shard_map/ppermute | solution.py:372
  29.3 5.4 %collective-permute-start.15 = (bf16[104,512]{1,0:T(8,128)(2,1)S(1)}, bf16[104,512]{1,0:T(8,128)(2,1)S(1)}, u32[]{:S(2)}, u32[]{:S(2)}) collective-permute-start(bf16[104,512]{1,0:T(8,128)(2,1)S(1)} %shard_map.113.refs_4_), channel_id=1, source_target_pairs={{0,2},{1,3},{2,0},{3,1},{4,6},{5,7},{6,4},{7,5},{8,10},{9,11},{10,... | collective-permute-start | bytes 319496 | tf_op jit(solution)/shard_map/ppermute | solution.py:372
  30.3 4.3 %collective-permute-start.23 = (bf16[104,512]{1,0:T(8,128)(2,1)S(1)}, bf16[104,512]{1,0:T(8,128)(2,1)S(1)}, u32[]{:S(2)}, u32[]{:S(2)}) collective-permute-start(bf16[104,512]{1,0:T(8,128)(2,1)S(1)} %collective-permute-done.21.refs_0_), channel_id=1, source_target_pairs={{0,1},{1,0},{2,3},{3,2},{4,5},{5,4},{6,7},{7,6},{8,9},{9,8},{10,11... | collective-permute-start | bytes 319496 | tf_op jit(solution)/shard_map/ppermute | solution.py:372
  32.2 3.1 %collective-permute-start.19 = (bf16[104,512]{1,0:T(8,128)(2,1)S(1)}, bf16[104,512]{1,0:T(8,128)(2,1)S(1)}, u32[]{:S(2)}, u32[]{:S(2)}) collective-permute-start(bf16[104,512]{1,0:T(8,128)(2,1)S(1)} %shard_map.114.refs_3_), channel_id=1, source_target_pairs={{0,1},{1,0},{2,3},{3,2},{4,5},{5,4},{6,7},{7,6},{8,9},{9,8},{10,11... | collective-permute-start | bytes 319496 | tf_op jit(solution)/shard_map/ppermute | solution.py:372
  32.2 3.1 %collective-permute-start.20 = (bf16[104,512]{1,0:T(8,128)(2,1)S(1)}, bf16[104,512]{1,0:T(8,128)(2,1)S(1)}, u32[]{:S(2)}, u32[]{:S(2)}) collective-permute-start(bf16[104,512]{1,0:T(8,128)(2,1)S(1)} %collective-permute-done.18.refs_0_), channel_id=1, source_target_pairs={{0,1},{1,0},{2,3},{3,2},{4,5},{5,4},{6,7},{7,6},{8,9},{9,8},{10,11... | collective-permute-start | bytes 319496 | tf_op jit(solution)/shard_map/ppermute | solution.py:372
  33.3 2.7 %collective-permute-start.16 = (bf16[104,512]{1,0:T(8,128)(2,1)S(1)}, bf16[104,512]{1,0:T(8,128)(2,1)S(1)}, u32[]{:S(2)}, u32[]{:S(2)}) collective-permute-start(bf16[104,512]{1,0:T(8,128)(2,1)S(1)} %shard_map.113.refs_4_), channel_id=1, source_target_pairs={{0,1},{1,0},{2,3},{3,2},{4,5},{5,4},{6,7},{7,6},{8,9},{9,8},{10,11... | collective-permute-start | bytes 319496 | tf_op jit(solution)/shard_map/ppermute | solution.py:372
  34.7 1.4 %collective-permute-start.17 = (bf16[104,512]{1,0:T(8,128)(2,1)S(1)}, bf16[104,512]{1,0:T(8,128)(2,1)S(1)}, u32[]{:S(2)}, u32[]{:S(2)}) collective-permute-start(bf16[104,512]{1,0:T(8,128)(2,1)S(1)} %collective-permute-done.15.refs_0_), channel_id=1, source_target_pairs={{0,1},{1,0},{2,3},{3,2},{4,5},{5,4},{6,7},{7,6},{8,9},{9,8},{10,11... | collective-permute-start | bytes 319496 | tf_op jit(solution)/shard_map/ppermute | solution.py:372
  36.8 6.3 %collective-permute-start.27 = (bf16[32,768]{1,0:T(8,128)(2,1)S(1)}, bf16[32,768]{1,0:T(8,128)(2,1)S(1)}, u32[]{:S(2)}, u32[]{:S(2)}) collective-permute-start(bf16[32,768]{1,0:T(8,128)(2,1)S(1)} %get-tuple-element.32), channel_id=1, source_target_pairs={{0,12},{4,8},{8,4},{12,0},{1,13},{5,9},{9,5},{13,1},{2,14},{6,10},... | collective-permute-start | bytes 147464 | tf_op jit(solution)/shard_map/ppermute | solution.py:372
  39.1 5.8 %collective-permute-start.28 = (bf16[32,768]{1,0:T(8,128)(2,1)S(1)}, bf16[32,768]{1,0:T(8,128)(2,1)S(1)}, u32[]{:S(2)}, u32[]{:S(2)}) collective-permute-start(bf16[32,768]{1,0:T(8,128)(2,1)S(1)} %get-tuple-element.33), channel_id=1, source_target_pairs={{0,8},{4,12},{8,0},{12,4},{1,9},{5,13},{9,1},{13,5},{2,10},{6,14},... | collective-permute-start | bytes 147464 | tf_op jit(solution)/shard_map/ppermute | solution.py:372
  39.1 5.8 %collective-permute-start.29 = (bf16[32,768]{1,0:T(8,128)(2,1)S(1)}, bf16[32,768]{1,0:T(8,128)(2,1)S(1)}, u32[]{:S(2)}, u32[]{:S(2)}) collective-permute-start(bf16[32,768]{1,0:T(8,128)(2,1)S(1)} %get-tuple-element.34), channel_id=1, source_target_pairs={{0,4},{4,0},{8,12},{12,8},{1,5},{5,1},{9,13},{13,9},{2,6},{6,2},{1... | collective-permute-start | bytes 147464 | tf_op jit(solution)/shard_map/ppermute | solution.py:372
  44.9 1.9 %collective-permute-start.30 = (bf16[8,768]{1,0:T(8,128)(2,1)S(1)}, bf16[8,768]{1,0:T(8,128)(2,1)S(1)}, u32[]{:S(2)}, u32[]{:S(2)}) collective-permute-start(bf16[8,768]{1,0:T(8,128)(2,1)S(1)} %get-tuple-element.36), channel_id=1, source_target_pairs={{0,1},{1,0},{2,3},{3,2},{4,5},{5,4},{6,7},{7,6},{8,9},{9,8},{10,11... | collective-permute-start | bytes 36872 | tf_op jit(solution)/shard_map/ppermute | solution.py:372
  45.0 3.7 %collective-permute-start.31 = (bf16[8,768]{1,0:T(8,128)(2,1)S(1)}, bf16[8,768]{1,0:T(8,128)(2,1)S(1)}, u32[]{:S(2)}, u32[]{:S(2)}) collective-permute-start(bf16[8,768]{1,0:T(8,128)(2,1)S(1)} %get-tuple-element.37), channel_id=1, source_target_pairs={{0,2},{1,3},{2,0},{3,1},{4,6},{5,7},{6,4},{7,5},{8,10},{9,11},{10,... | collective-permute-start | bytes 36872 | tf_op jit(solution)/shard_map/ppermute | solution.py:372
  46.0 3.1 %collective-permute-start.32 = (bf16[8,768]{1,0:T(8,128)(2,1)S(1)}, bf16[8,768]{1,0:T(8,128)(2,1)S(1)}, u32[]{:S(2)}, u32[]{:S(2)}) collective-permute-start(bf16[8,768]{1,0:T(8,128)(2,1)S(1)} %get-tuple-element.38), channel_id=1, source_target_pairs={{0,3},{1,2},{2,1},{3,0},{4,7},{5,6},{6,5},{7,4},{8,11},{9,10},{10,... | collective-permute-start | bytes 36872 | tf_op jit(solution)/shard_map/ppermute | solution.py:372
  (2 other events, 1.5 us)

commit v6 on v5

--- a/solution.py
+++ b/solution.py
@@ -124,8 +124,7 @@
 CHUNKS = (4, 4, 4, 4)
 Z_ORDER = (3, 2, 1)
 EARLY, LATE = (1, 3), (0, 2)
-PAIRED = 0
-LAST_FLOPS = 10**9
+DOWN_GROUPS = ((0,), (1,), (2,), (3,))
 PACK_FLOPS = 10**8
 OPENING_FLOPS = 6 * 10**9
 ATTENTION_FLOPS = 30 * 10**9
@@ -252,7 +251,7 @@
 
 
 def hidden_columns(x, gate_ref, up_ref, out_ref, begin):
-    step = min(256, out_ref.shape[1])
+    step = min(512, out_ref.shape[1])
     end = out_ref.shape[1]
     for j in range(0, end, step):
         columns = slice(begin + j, begin + min(j + step, end))
@@ -296,12 +295,6 @@
 
 def next_hidden_kernel(begin, x_ref, gate_ref, up_ref, hidden_ref):
     hidden_columns(x_ref[...], gate_ref, up_ref, hidden_ref, begin)
-
-
-def pair_kernel(first_ref, second_ref, out_ref):
-    width = first_ref.shape[1]
-    out_ref[:, :width] = first_ref[...]
-    out_ref[:, width:] = second_ref[...]
 
 
 def down_part(refs, sources, down_ref, own_width):
@@ -487,35 +480,23 @@
     )
     total_shape = jax.ShapeDtypeStruct((slots, out_width), jnp.float32)
     total = None
-    for i in range(chunks):
-        wide = widths[i]
-        if i < PAIRED:
-            both = call(
-                pair_kernel,
-                jax.ShapeDtypeStruct((slots, 2 * wide), bf16),
-                (own[i], far[i]),
-                [VMEM_SPEC] * 2,
-                flops=10**6,
-                vmem=4 * MIB,
-            )
-            taken = [both, flip(both, "sub", 1)]
-            sources = [(0, wide, wide, 2, begins[i]), (1, 0, wide, 1, begins[i]),
-                       (1, wide, wide, 3, begins[i])]
-        else:
-            taken = [far[i], flip(own[i], "sub", 1), flip(far[i], "sub", 1)]
-            sources = [(n, 0, wide, bits, begins[i]) for n, bits in enumerate((2, 1, 3))]
-        mine = [i] if i < chunks - 2 else [i, i + 1] if i == chunks - 2 else []
-        for n in mine:
-            sources.append((len(taken), 0, widths[n], 0, begins[n]))
-            taken.append(own[n])
+    for group in DOWN_GROUPS:
+        taken, sources = [], []
+        for i in group:
+            for bits, array in ((2, far[i]), (1, flip(own[i], "sub", 1)), (3, flip(far[i], "sub", 1))):
+                sources.append((len(taken), 0, widths[i], bits, begins[i]))
+                taken.append(array)
+            for n in [i] if i < chunks - 2 else [i, i + 1] if i == chunks - 2 else []:
+                sources.append((len(taken), 0, widths[n], 0, begins[n]))
+                taken.append(own[n])
         before = () if total is None else (total,)
-        if i < chunks - 1:
+        if group[-1] < chunks - 1:
             total = call(
-                functools.partial(down_kernel, sources, own_hidden, i > 0),
+                functools.partial(down_kernel, sources, own_hidden, total is not None),
                 total_shape,
                 (*taken, down_weight, *before),
                 [VMEM_SPEC] * (len(taken) + 1 + len(before)),
-                flops=LAST_FLOPS if i == chunks - 2 else DOWN_FLOPS,
+                flops=DOWN_FLOPS * len(group),
                 vmem=4 * MIB,
             )
         else:

time: 50 us -> 49.8 us (level)
  no operation moved by 1% of the time
where the time goes in v6:
time: 49.8 us; the launch traced here: 49.7 us
  starting transfers between devices  23.8 us (48%)
  waiting for transfers between devices  12.8 us (26%)
  Pallas kernels  11.2 us (22%)
  local copies, waits for them, and re-layouts  1.61 us (3%)
    ppermute x33, starting transfers between devices, flip(): lax.ppermute(x, axis, [(i, i ^ bits) for i in range(lax.axis_size(axis))])  23.8 us
    ppermute x33, waiting for transfers between devices, flip(): lax.ppermute(x, axis, [(i, i ^ bits) for i in range(lax.axis_size(axis))])  12.8 us
    pallas_call x14, Pallas kernels, call(): pl.pallas_call(body, out_shape=out_shapes, in_specs=specs, out_specs=jax....  11.2 us
    unnamed x34, local copies, waits for them, and re-layouts  1.61 us
  transfers between devices with their start and end apart: 33, of which 11 were waited for; matrix products, arithmetic and copies ran while one was open for 0% of the time, Pallas kernels for 13%

profile of v6, /device:TPU:0, one launch (start us, length us, event | category | flops | bytes accessed | tf_op | source)
XLA Modules:
  0.0 49.7 jit_solution(6325761939256422235)
XLA Ops:
  0.1 0.6 %copy-done.6 = s32[32,2]{0,1:T(2,128)S(1)} copy-done((s32[32,2]{0,1:T(2,128)S(1)}, s32[32,2]{0,1:T(2,128)}, u32[]{:S(2)}) %copy-start.6) | copy-done | bytes 280
  0.7 0.1 copy-done.3
  0.8 0.5 copy-done
  1.3 0.3 copy-done.1
  1.7 1.7 %shard_map.110 = (bf16[8,3200]{1,0:T(8,128)(2,1)S(1)}, bf16[8,3072]{1,0:T(8,128)(2,1)S(1)}) custom-call(f32[8,128]{1,0:T(8,128)S(1)} %shard_map.109._, s32[8]{0:T(128)S(1)} %copy-done.7, s32[2,32]{1,0:T(2,128)S(1)} %bitcast.9, bf16[8,3072]{1,0:T(8,128)(2,1)S(1)} %copy-done.2, bf16[8,128,512]{2,1,0:T(8,128)(2,1)S(1)} %copy-done, ...), custom_call_target="tpu_custom_call" | custom-call | flops 30000001024 | bytes 104857600 | tf_op jit(solution)/shard_map/pallas_call | solution.py:137
  3.3 3.1 %collective-permute-start.7 = (bf16[8,3200]{1,0:T(8,128)(2,1)S(1)}, bf16[8,3200]{1,0:T(8,128)(2,1)S(1)}, u32[]{:S(2)}, u32[]{:S(2)}) collective-permute-start(bf16[8,3200]{1,0:T(8,128)(2,1)S(1)} %get-tuple-element.23.refs_0_), channel_id=1, source_target_pairs={{0,4},{4,0},{8,12},{12,8},{1,5},{5,1},{9,13},{13,9},{2,6},{6,2},{1... | collective-permute-start | bytes 153608 | tf_op jit(solution)/shard_map/ppermute | solution.py:365
  6.4 2.5 %collective-permute-start.11 = (bf16[8,3200]{1,0:T(8,128)(2,1)S(1)}, bf16[8,3200]{1,0:T(8,128)(2,1)S(1)}, u32[]{:S(2)}, u32[]{:S(2)}) collective-permute-start(bf16[8,3200]{1,0:T(8,128)(2,1)S(1)} %get-tuple-element.23.refs_0_), channel_id=1, source_target_pairs={{0,12},{4,8},{8,4},{12,0},{1,13},{5,9},{9,5},{13,1},{2,14},{6,10},... | collective-permute-start | bytes 153608 | tf_op jit(solution)/shard_map/ppermute | solution.py:365
  8.9 0.1 collective-permute-start.3
  9.0 1.5 %collective-permute-start.1 = (bf16[8,3200]{1,0:T(8,128)(2,1)S(1)}, bf16[8,3200]{1,0:T(8,128)(2,1)S(1)}, u32[]{:S(2)}, u32[]{:S(2)}) collective-permute-start(bf16[8,3200]{1,0:T(8,128)(2,1)S(1)} %get-tuple-element.23.refs_0_), channel_id=1, source_target_pairs={{0,2},{1,3},{2,0},{3,1},{4,6},{5,7},{6,4},{7,5},{8,10},{9,11},{10,... | collective-permute-start | bytes 153608 | tf_op jit(solution)/shard_map/ppermute | solution.py:365
  10.5 0.5 %collective-permute-start.9 = (bf16[8,3200]{1,0:T(8,128)(2,1)S(1)}, bf16[8,3200]{1,0:T(8,128)(2,1)S(1)}, u32[]{:S(2)}, u32[]{:S(2)}) collective-permute-start(bf16[8,3200]{1,0:T(8,128)(2,1)S(1)} %collective-permute-done.7.refs_0_), channel_id=1, source_target_pairs={{0,2},{1,3},{2,0},{3,1},{4,6},{5,7},{6,4},{7,5},{8,10},{9,11},{10,... | collective-permute-start | bytes 153608 | tf_op jit(solution)/shard_map/ppermute | solution.py:365
  11.1 1.9 %collective-permute-done.11.refs_4_ = bf16[8,3200]{1,0:T(8,128)(2,1)S(1)} collective-permute-done((bf16[8,3200]{1,0:T(8,128)(2,1)S(1)}, bf16[8,3200]{1,0:T(8,128)(2,1)S(1)}, u32[]{:S(2)}, u32[]{:S(2)}) %collective-permute-start.11) | collective-permute-done | bytes 51232 | tf_op jit(solution)/shard_map/ppermute | solution.py:365
  13.0 1.5 %collective-permute-start.13 = (bf16[8,3200]{1,0:T(8,128)(2,1)S(1)}, bf16[8,3200]{1,0:T(8,128)(2,1)S(1)}, u32[]{:S(2)}, u32[]{:S(2)}) collective-permute-start(bf16[8,3200]{1,0:T(8,128)(2,1)S(1)} %collective-permute-done.11.refs_4_), channel_id=1, source_target_pairs={{0,2},{1,3},{2,0},{3,1},{4,6},{5,7},{6,4},{7,5},{8,10},{9,11},{10,... | collective-permute-start | bytes 153608 | tf_op jit(solution)/shard_map/ppermute | solution.py:365
  14.5 0.5 %collective-permute-start.8 = (bf16[8,3200]{1,0:T(8,128)(2,1)S(1)}, bf16[8,3200]{1,0:T(8,128)(2,1)S(1)}, u32[]{:S(2)}, u32[]{:S(2)}) collective-permute-start(bf16[8,3200]{1,0:T(8,128)(2,1)S(1)} %collective-permute-done.7.refs_0_), channel_id=1, source_target_pairs={{0,1},{1,0},{2,3},{3,2},{4,5},{5,4},{6,7},{7,6},{8,9},{9,8},{10,11... | collective-permute-start | bytes 153608 | tf_op jit(solution)/shard_map/ppermute | solution.py:365
  15.0 1.0 %collective-permute-start.5 = (bf16[8,3200]{1,0:T(8,128)(2,1)S(1)}, bf16[8,3200]{1,0:T(8,128)(2,1)S(1)}, u32[]{:S(2)}, u32[]{:S(2)}) collective-permute-start(bf16[8,3200]{1,0:T(8,128)(2,1)S(1)} %collective-permute-done.3.refs_4_), channel_id=1, source_target_pairs={{0,2},{1,3},{2,0},{3,1},{4,6},{5,7},{6,4},{7,5},{8,10},{9,11},{10,... | collective-permute-start | bytes 153608 | tf_op jit(solution)/shard_map/ppermute | solution.py:365
  16.0 0.2 collective-permute-start.10
  16.2 0.9 %collective-permute-done.13.refs_6_ = bf16[8,3200]{1,0:T(8,128)(2,1)S(1)} collective-permute-done((bf16[8,3200]{1,0:T(8,128)(2,1)S(1)}, bf16[8,3200]{1,0:T(8,128)(2,1)S(1)}, u32[]{:S(2)}, u32[]{:S(2)}) %collective-permute-start.13) | collective-permute-done | bytes 51232 | tf_op jit(solution)/shard_map/ppermute | solution.py:365
  17.1 0.5 %collective-permute-start = (bf16[8,3200]{1,0:T(8,128)(2,1)S(1)}, bf16[8,3200]{1,0:T(8,128)(2,1)S(1)}, u32[]{:S(2)}, u32[]{:S(2)}) collective-permute-start(bf16[8,3200]{1,0:T(8,128)(2,1)S(1)} %get-tuple-element.23.refs_0_), channel_id=1, source_target_pairs={{0,1},{1,0},{2,3},{3,2},{4,5},{5,4},{6,7},{7,6},{8,9},{9,8},{10,11... | collective-permute-start | bytes 153608 | tf_op jit(solution)/shard_map/ppermute | solution.py:365
  17.7 1.4 %collective-permute-done.5.refs_6_ = bf16[8,3200]{1,0:T(8,128)(2,1)S(1)} collective-permute-done((bf16[8,3200]{1,0:T(8,128)(2,1)S(1)}, bf16[8,3200]{1,0:T(8,128)(2,1)S(1)}, u32[]{:S(2)}, u32[]{:S(2)}) %collective-permute-start.5) | collective-permute-done | bytes 51232 | tf_op jit(solution)/shard_map/ppermute | solution.py:365
  19.1 0.5 %collective-permute-start.6 = (bf16[8,3200]{1,0:T(8,128)(2,1)S(1)}, bf16[8,3200]{1,0:T(8,128)(2,1)S(1)}, u32[]{:S(2)}, u32[]{:S(2)}) collective-permute-start(bf16[8,3200]{1,0:T(8,128)(2,1)S(1)} %collective-permute-done.5.refs_6_), channel_id=1, source_target_pairs={{0,1},{1,0},{2,3},{3,2},{4,5},{5,4},{6,7},{7,6},{8,9},{9,8},{10,11... | collective-permute-start | bytes 153608 | tf_op jit(solution)/shard_map/ppermute | solution.py:365
  19.6 0.6 %shard_map.111 = (bf16[104,3072]{1,0:T(8,128)(2,1)S(1)}, bf16[64,128]{1,0:T(8,128)(2,1)S(1)}) custom-call(bf16[8,3200]{1,0:T(8,128)(2,1)S(1)} %collective-permute-done.7.refs_0_, bf16[8,3200]{1,0:T(8,128)(2,1)S(1)} %collective-permute-done.8.refs_1_, bf16[8,3200]{1,0:T(8,128)(2,1)S(1)} %collective-permute-done.9.refs_2_, ...), custom_call_target="tpu_custom_call" | custom-call | flops 100000000 | tf_op jit(solution)/shard_map/pallas_call | solution.py:137
  20.3 0.2 collective-permute-done.6.refs_7_
  20.6 1.6 %shard_map.112 = (bf16[104,3072]{1,0:T(8,128)(2,1)S(1)}, bf16[64,128]{1,0:T(8,128)(2,1)S(1)}, bf16[104,512]{1,0:T(8,128)(2,1)S(1)}) custom-call(bf16[8,3200]{1,0:T(8,128)(2,1)S(1)} %get-tuple-element.23.refs_0_, bf16[8,3200]{1,0:T(8,128)(2,1)S(1)} %collective-permute-done.refs_1_, bf16[8,3200]{1,0:T(8,128)(2,1)S(1)} %collective-permute-done.1.refs_2_, ...), custom_call_target="tpu_custom_call" | custom-call | flops 1000000000 | tf_op jit(solution)/shard_map/pallas_call | solution.py:137
  22.1 1.1 %collective-permute-start.24 = (bf16[104,512]{1,0:T(8,128)(2,1)S(1)}, bf16[104,512]{1,0:T(8,128)(2,1)S(1)}, u32[]{:S(2)}, u32[]{:S(2)}) collective-permute-start(bf16[104,512]{1,0:T(8,128)(2,1)S(1)} %get-tuple-element.26.refs_3_), channel_id=1, source_target_pairs={{0,2},{1,3},{2,0},{3,1},{4,6},{5,7},{6,4},{7,5},{8,10},{9,11},{10,... | collective-permute-start | bytes 319496 | tf_op jit(solution)/shard_map/ppermute | solution.py:365
  23.3 1.1 %shard_map.115.refs_3_ = bf16[104,512]{1,0:T(8,128)(2,1)S(1)} custom-call(bf16[104,3072]{1,0:T(8,128)(2,1)S(1)} %get-tuple-element.25.x_ref.refs_2_, bf16[3072,2048]{1,0:T(8,128)(2,1)S(1)} %bitcast.5, bf16[3072,2048]{1,0:T(8,128)(2,1)S(1)} %bitcast.7), custom_call_target="tpu_custom_call" | custom-call | flops 1000000000 | tf_op jit(solution)/shard_map/pallas_call | solution.py:137
  24.4 1.0 %collective-permute-start.21 = (bf16[104,512]{1,0:T(8,128)(2,1)S(1)}, bf16[104,512]{1,0:T(8,128)(2,1)S(1)}, u32[]{:S(2)}, u32[]{:S(2)}) collective-permute-start(bf16[104,512]{1,0:T(8,128)(2,1)S(1)} %shard_map.115.refs_3_), channel_id=1, source_target_pairs={{0,2},{1,3},{2,0},{3,1},{4,6},{5,7},{6,4},{7,5},{8,10},{9,11},{10,... | collective-permute-start | bytes 319496 | tf_op jit(solution)/shard_map/ppermute | solution.py:365
  25.5 0.2 collective-permute-start.22
  25.7 1.1 %shard_map.114.refs_3_ = bf16[104,512]{1,0:T(8,128)(2,1)S(1)} custom-call(bf16[104,3072]{1,0:T(8,128)(2,1)S(1)} %get-tuple-element.25.x_ref.refs_2_, bf16[3072,2048]{1,0:T(8,128)(2,1)S(1)} %bitcast.5, bf16[3072,2048]{1,0:T(8,128)(2,1)S(1)} %bitcast.7), custom_call_target="tpu_custom_call" | custom-call | flops 1000000000 | tf_op jit(solution)/shard_map/pallas_call | solution.py:137
  26.8 1.1 %collective-permute-start.18 = (bf16[104,512]{1,0:T(8,128)(2,1)S(1)}, bf16[104,512]{1,0:T(8,128)(2,1)S(1)}, u32[]{:S(2)}, u32[]{:S(2)}) collective-permute-start(bf16[104,512]{1,0:T(8,128)(2,1)S(1)} %shard_map.114.refs_3_), channel_id=1, source_target_pairs={{0,2},{1,3},{2,0},{3,1},{4,6},{5,7},{6,4},{7,5},{8,10},{9,11},{10,... | collective-permute-start | bytes 319496 | tf_op jit(solution)/shard_map/ppermute | solution.py:365
  28.0 1.1 %shard_map.113.refs_4_ = bf16[104,512]{1,0:T(8,128)(2,1)S(1)} custom-call(bf16[104,3072]{1,0:T(8,128)(2,1)S(1)} %get-tuple-element.25.x_ref.refs_2_, bf16[3072,2048]{1,0:T(8,128)(2,1)S(1)} %bitcast.5, bf16[3072,2048]{1,0:T(8,128)(2,1)S(1)} %bitcast.7), custom_call_target="tpu_custom_call" | custom-call | flops 1000000000 | tf_op jit(solution)/shard_map/pallas_call | solution.py:137
  29.1 1.0 %collective-permute-start.15 = (bf16[104,512]{1,0:T(8,128)(2,1)S(1)}, bf16[104,512]{1,0:T(8,128)(2,1)S(1)}, u32[]{:S(2)}, u32[]{:S(2)}) collective-permute-start(bf16[104,512]{1,0:T(8,128)(2,1)S(1)} %shard_map.113.refs_4_), channel_id=1, source_target_pairs={{0,2},{1,3},{2,0},{3,1},{4,6},{5,7},{6,4},{7,5},{8,10},{9,11},{10,... | collective-permute-start | bytes 319496 | tf_op jit(solution)/shard_map/ppermute | solution.py:365
  30.2 0.2 collective-permute-start.23
  30.4 0.7 %shard_map.119 = (bf16[128,128]{1,0:T(8,128)(2,1)S(1)}, f32[104,128]{1,0:T(8,128)S(1)}) custom-call(bf16[64,128]{1,0:T(8,128)(2,1)S(1)} %get-tuple-element.27.refs_0_, bf16[64,128]{1,0:T(8,128)(2,1)S(1)} %get-tuple-element.28.refs_1_, bf16[104,3072]{1,0:T(8,128)(2,1)S(1)} %get-tuple-element.25.x_ref.refs_2_, bf16[4,3072]{1,0:T(4,128)(2,1)S(1)} %bitcast.8), custom_call_target="tpu_custom_call" | custom-call | flops 1000000000 | tf_op jit(solution)/shard_map/pallas_call | solution.py:137
  31.1 1.0 %collective-permute-done.18.refs_0_ = bf16[104,512]{1,0:T(8,128)(2,1)S(1)} collective-permute-done((bf16[104,512]{1,0:T(8,128)(2,1)S(1)}, bf16[104,512]{1,0:T(8,128)(2,1)S(1)}, u32[]{:S(2)}, u32[]{:S(2)}) %collective-permute-start.18) | collective-permute-done | bytes 106528 | tf_op jit(solution)/shard_map/ppermute | solution.py:365
  32.1 0.5 %collective-permute-start.20 = (bf16[104,512]{1,0:T(8,128)(2,1)S(1)}, bf16[104,512]{1,0:T(8,128)(2,1)S(1)}, u32[]{:S(2)}, u32[]{:S(2)}) collective-permute-start(bf16[104,512]{1,0:T(8,128)(2,1)S(1)} %collective-permute-done.18.refs_0_), channel_id=1, source_target_pairs={{0,1},{1,0},{2,3},{3,2},{4,5},{5,4},{6,7},{7,6},{8,9},{9,8},{10,11... | collective-permute-start | bytes 319496 | tf_op jit(solution)/shard_map/ppermute | solution.py:365
  32.6 0.6 %shard_map.116.refs_5_ = f32[104,768]{1,0:T(8,128)S(1)} custom-call(bf16[104,512]{1,0:T(8,128)(2,1)S(1)} %collective-permute-done.24.refs_0_, bf16[104,512]{1,0:T(8,128)(2,1)S(1)} %collective-permute-done.25.refs_1_, bf16[104,512]{1,0:T(8,128)(2,1)S(1)} %collective-permute-done.26.refs_2_, bf16[104,512]{1,0:T(8,128)(2,1)S(1)} %get-tuple-element.26.refs_3_, ...), custom_call_target="tpu_custom_call" | custom-call | flops 1000000000 | tf_op jit(solution)/shard_map/pallas_call | solution.py:137
  33.4 1.2 %collective-permute-done.15.refs_0_ = bf16[104,512]{1,0:T(8,128)(2,1)S(1)} collective-permute-done((bf16[104,512]{1,0:T(8,128)(2,1)S(1)}, bf16[104,512]{1,0:T(8,128)(2,1)S(1)}, u32[]{:S(2)}, u32[]{:S(2)}) %collective-permute-start.15) | collective-permute-done | bytes 106528 | tf_op jit(solution)/shard_map/ppermute | solution.py:365
  34.5 0.6 %shard_map.117.refs_6_ = f32[104,768]{1,0:T(8,128)S(1)} custom-call(bf16[104,512]{1,0:T(8,128)(2,1)S(1)} %collective-permute-done.21.refs_0_, bf16[104,512]{1,0:T(8,128)(2,1)S(1)} %collective-permute-done.22.refs_1_, bf16[104,512]{1,0:T(8,128)(2,1)S(1)} %collective-permute-done.23.refs_2_, bf16[104,512]{1,0:T(8,128)(2,1)S(1)} %shard_map.115.refs_3_, ...), custom_call_target="tpu_custom_call" | custom-call | flops 1000000000 | tf_op jit(solution)/shard_map/pallas_call | solution.py:137
  35.2 0.7 %shard_map.118.refs_4_ = f32[104,768]{1,0:T(8,128)S(1)} custom-call(bf16[104,512]{1,0:T(8,128)(2,1)S(1)} %collective-permute-done.18.refs_0_, bf16[104,512]{1,0:T(8,128)(2,1)S(1)} %collective-permute-done.19.refs_1_, bf16[104,512]{1,0:T(8,128)(2,1)S(1)} %collective-permute-done.20.refs_2_, bf16[104,512]{1,0:T(8,128)(2,1)S(1)} %shard_map.114.refs_3_, ...), custom_call_target="tpu_custom_call" | custom-call | flops 1000000000 | tf_op jit(solution)/shard_map/pallas_call | solution.py:137
  35.9 0.7 %shard_map.120 = (bf16[32,768]{1,0:T(8,128)(2,1)S(1)}, bf16[32,768]{1,0:T(8,128)(2,1)S(1)}, bf16[32,768]{1,0:T(8,128)(2,1)S(1)}, bf16[32,768]{1,0:T(8,128)(2,1)S(1)}) custom-call(bf16[104,512]{1,0:T(8,128)(2,1)S(1)} %collective-permute-done.15.refs_0_, bf16[104,512]{1,0:T(8,128)(2,1)S(1)} %collective-permute-done.16.refs_1_, ...), custom_call_target="tpu_custom_call" | custom-call | flops 1000000000 | tf_op jit(solution)/shard_map/pallas_call | solution.py:137
  36.6 2.3 %collective-permute-start.27 = (bf16[32,768]{1,0:T(8,128)(2,1)S(1)}, bf16[32,768]{1,0:T(8,128)(2,1)S(1)}, u32[]{:S(2)}, u32[]{:S(2)}) collective-permute-start(bf16[32,768]{1,0:T(8,128)(2,1)S(1)} %get-tuple-element.32), channel_id=1, source_target_pairs={{0,12},{4,8},{8,4},{12,0},{1,13},{5,9},{9,5},{13,1},{2,14},{6,10},... | collective-permute-start | bytes 147464 | tf_op jit(solution)/shard_map/ppermute | solution.py:365
  38.9 2.2 %collective-permute-start.29 = (bf16[32,768]{1,0:T(8,128)(2,1)S(1)}, bf16[32,768]{1,0:T(8,128)(2,1)S(1)}, u32[]{:S(2)}, u32[]{:S(2)}) collective-permute-start(bf16[32,768]{1,0:T(8,128)(2,1)S(1)} %get-tuple-element.34), channel_id=1, source_target_pairs={{0,4},{4,0},{8,12},{12,8},{1,5},{5,1},{9,13},{13,9},{2,6},{6,2},{1... | collective-permute-start | bytes 147464 | tf_op jit(solution)/shard_map/ppermute | solution.py:365
  41.1 1.8 %collective-permute-done.27.refs_1_ = bf16[32,768]{1,0:T(8,128)(2,1)S(1)} collective-permute-done((bf16[32,768]{1,0:T(8,128)(2,1)S(1)}, bf16[32,768]{1,0:T(8,128)(2,1)S(1)}, u32[]{:S(2)}, u32[]{:S(2)}) %collective-permute-start.27) | collective-permute-done | bytes 49184 | tf_op jit(solution)/shard_map/ppermute | solution.py:365
  42.9 1.9 %collective-permute-done.28.refs_2_ = bf16[32,768]{1,0:T(8,128)(2,1)S(1)} collective-permute-done((bf16[32,768]{1,0:T(8,128)(2,1)S(1)}, bf16[32,768]{1,0:T(8,128)(2,1)S(1)}, u32[]{:S(2)}, u32[]{:S(2)}) %collective-permute-start.28) | collective-permute-done | bytes 49184 | tf_op jit(solution)/shard_map/ppermute | solution.py:365
  44.9 1.1 %collective-permute-start.31 = (bf16[8,768]{1,0:T(8,128)(2,1)S(1)}, bf16[8,768]{1,0:T(8,128)(2,1)S(1)}, u32[]{:S(2)}, u32[]{:S(2)}) collective-permute-start(bf16[8,768]{1,0:T(8,128)(2,1)S(1)} %get-tuple-element.37), channel_id=1, source_target_pairs={{0,2},{1,3},{2,0},{3,1},{4,6},{5,7},{6,4},{7,5},{8,10},{9,11},{10,... | collective-permute-start | bytes 36872 | tf_op jit(solution)/shard_map/ppermute | solution.py:365
  45.9 0.8 %collective-permute-start.32 = (bf16[8,768]{1,0:T(8,128)(2,1)S(1)}, bf16[8,768]{1,0:T(8,128)(2,1)S(1)}, u32[]{:S(2)}, u32[]{:S(2)}) collective-permute-start(bf16[8,768]{1,0:T(8,128)(2,1)S(1)} %get-tuple-element.38), channel_id=1, source_target_pairs={{0,3},{1,2},{2,1},{3,0},{4,7},{5,6},{6,5},{7,4},{8,11},{9,10},{10,... | collective-permute-start | bytes 36872 | tf_op jit(solution)/shard_map/ppermute | solution.py:365
  46.7 1.9 %collective-permute-done.31.refs_2_ = bf16[8,768]{1,0:T(8,128)(2,1)S(1)} collective-permute-done((bf16[8,768]{1,0:T(8,128)(2,1)S(1)}, bf16[8,768]{1,0:T(8,128)(2,1)S(1)}, u32[]{:S(2)}, u32[]{:S(2)}) %collective-permute-start.31) | collective-permute-done | bytes 12320 | tf_op jit(solution)/shard_map/ppermute | solution.py:365
  48.6 0.4 collective-permute-done.32.refs_3_
  49.1 0.6 %shard_map.122 = bf16[8,3072]{1,0:T(8,128)(2,1)} custom-call(bf16[8,3072]{1,0:T(8,128)(2,1)S(1)} %get-tuple-element.22.resid_ref, f32[8,768]{1,0:T(8,128)S(1)} %get-tuple-element.35.refs_0_, bf16[8,768]{1,0:T(8,128)(2,1)S(1)} %collective-permute-done.30.refs_1_, bf16[8,768]{1,0:T(8,128)(2,1)S(1)} %collective-permute-done.31.refs_2_, ...), custom_call_target="tpu_custom_call" | custom-call | flops 1000000 | tf_op jit(solution)/shard_map/pallas_call | solution.py:137
  (69 shorter events, 0.7 us)
Async XLA Ops:
  0.0 0.8 %copy-start.2 = (bf16[8,3072]{1,0:T(8,128)(2,1)S(1)}, bf16[8,3072]{1,0:T(8,128)(2,1)}, u32[]{:S(2)}) copy-start(bf16[8,3072]{1,0:T(8,128)(2,1)} %queries_ref.1) | copy-start | bytes 147460
  0.0 1.3 %copy-start = (bf16[8,128,512]{2,1,0:T(8,128)(2,1)S(1)}, bf16[8,128,512]{2,1,0:T(8,128)(2,1)}, u32[]{:S(2)}) copy-start(bf16[8,128,512]{2,1,0:T(8,128)(2,1)} %keys_ref.1) | copy-start | bytes 3145732
  0.0 1.6 %copy-start.1 = (bf16[8,128,512]{2,1,0:T(8,128)(2,1)S(1)}, bf16[8,128,512]{2,1,0:T(8,128)(2,1)}, u32[]{:S(2)}) copy-start(bf16[8,128,512]{2,1,0:T(8,128)(2,1)} %values_ref.1) | copy-start | bytes 3145732
  0.0 1.6 %copy-start.7 = (s32[8]{0:T(128)S(1)}, s32[8]{0:T(128)}, u32[]{:S(2)}) copy-start(s32[8]{0:T(128)} %lengths_ref.1) | copy-start | bytes 100
  0.0 1.6 %copy-start.5 = (bf16[3072]{0:T(1024)(128)(2,1)S(1)}, bf16[3072]{0:T(1024)(128)(2,1)}, u32[]{:S(2)}) copy-start(bf16[3072]{0:T(1024)(128)(2,1)} %gain_ref.1) | copy-start | bytes 18436
  0.0 20.5 %slice-start.3 = ((s8[12582912]{0:T(1024)(128)(4,1)}), s8[4194304]{0:T(1024)(128)(4,1)S(1)}, s32[]{:S(2)}) async-start(s8[12582912]{0:T(1024)(128)(4,1)} %bitcast.4), calls=%async_computation.3 | async-start | bytes 8388608
  0.0 20.5 %slice-start.6 = ((s8[12582912]{0:T(1024)(128)(4,1)}), s8[4194304]{0:T(1024)(128)(4,1)S(1)}, s32[]{:S(2)}) async-start(s8[12582912]{0:T(1024)(128)(4,1)} %bitcast.6), calls=%async_computation.6 | async-start | bytes 8388608
  1.6 18.9 %slice-start.4 = ((s8[12582912]{0:T(1024)(128)(4,1)}), s8[4194304]{0:T(1024)(128)(4,1)S(1)}, s32[]{:S(2)}) async-start(s8[12582912]{0:T(1024)(128)(4,1)} %bitcast.4), calls=%async_computation.4 | async-start | bytes 8388608
  1.6 18.9 %slice-start.5 = ((s8[12582912]{0:T(1024)(128)(4,1)}), s8[4194304]{0:T(1024)(128)(4,1)S(1)}, s32[]{:S(2)}) async-start(s8[12582912]{0:T(1024)(128)(4,1)} %bitcast.4), calls=%async_computation.5 | async-start | bytes 8388608
  1.6 18.9 %slice-start.7 = ((s8[12582912]{0:T(1024)(128)(4,1)}), s8[4194304]{0:T(1024)(128)(4,1)S(1)}, s32[]{:S(2)}) async-start(s8[12582912]{0:T(1024)(128)(4,1)} %bitcast.6), calls=%async_computation.7 | async-start | bytes 8388608
  1.6 18.9 %slice-start.8 = ((s8[12582912]{0:T(1024)(128)(4,1)}), s8[4194304]{0:T(1024)(128)(4,1)S(1)}, s32[]{:S(2)}) async-start(s8[12582912]{0:T(1024)(128)(4,1)} %bitcast.6), calls=%async_computation.8 | async-start | bytes 8388608
  3.3 7.2 %collective-permute-start.7 = (bf16[8,3200]{1,0:T(8,128)(2,1)S(1)}, bf16[8,3200]{1,0:T(8,128)(2,1)S(1)}, u32[]{:S(2)}, u32[]{:S(2)}) collective-permute-start(bf16[8,3200]{1,0:T(8,128)(2,1)S(1)} %get-tuple-element.23.refs_0_), channel_id=1, source_target_pairs={{0,4},{4,0},{8,12},{12,8},{1,5},{5,1},{9,13},{13,9},{2,6},{6,2},{1... | collective-permute-start | bytes 153608 | tf_op jit(solution)/shard_map/ppermute | solution.py:365
  6.4 6.6 %collective-permute-start.11 = (bf16[8,3200]{1,0:T(8,128)(2,1)S(1)}, bf16[8,3200]{1,0:T(8,128)(2,1)S(1)}, u32[]{:S(2)}, u32[]{:S(2)}) collective-permute-start(bf16[8,3200]{1,0:T(8,128)(2,1)S(1)} %get-tuple-element.23.refs_0_), channel_id=1, source_target_pairs={{0,12},{4,8},{8,4},{12,0},{1,13},{5,9},{9,5},{13,1},{2,14},{6,10},... | collective-permute-start | bytes 153608 | tf_op jit(solution)/shard_map/ppermute | solution.py:365
  8.9 5.6 %collective-permute-start.3 = (bf16[8,3200]{1,0:T(8,128)(2,1)S(1)}, bf16[8,3200]{1,0:T(8,128)(2,1)S(1)}, u32[]{:S(2)}, u32[]{:S(2)}) collective-permute-start(bf16[8,3200]{1,0:T(8,128)(2,1)S(1)} %get-tuple-element.23.refs_0_), channel_id=1, source_target_pairs={{0,8},{4,12},{8,0},{12,4},{1,9},{5,13},{9,1},{13,5},{2,10},{6,14},... | collective-permute-start | bytes 153608 | tf_op jit(solution)/shard_map/ppermute | solution.py:365
  9.0 6.0 %collective-permute-start.1 = (bf16[8,3200]{1,0:T(8,128)(2,1)S(1)}, bf16[8,3200]{1,0:T(8,128)(2,1)S(1)}, u32[]{:S(2)}, u32[]{:S(2)}) collective-permute-start(bf16[8,3200]{1,0:T(8,128)(2,1)S(1)} %get-tuple-element.23.refs_0_), channel_id=1, source_target_pairs={{0,2},{1,3},{2,0},{3,1},{4,6},{5,7},{6,4},{7,5},{8,10},{9,11},{10,... | collective-permute-start | bytes 153608 | tf_op jit(solution)/shard_map/ppermute | solution.py:365
  10.5 5.4 %collective-permute-start.9 = (bf16[8,3200]{1,0:T(8,128)(2,1)S(1)}, bf16[8,3200]{1,0:T(8,128)(2,1)S(1)}, u32[]{:S(2)}, u32[]{:S(2)}) collective-permute-start(bf16[8,3200]{1,0:T(8,128)(2,1)S(1)} %collective-permute-done.7.refs_0_), channel_id=1, source_target_pairs={{0,2},{1,3},{2,0},{3,1},{4,6},{5,7},{6,4},{7,5},{8,10},{9,11},{10,... | collective-permute-start | bytes 153608 | tf_op jit(solution)/shard_map/ppermute | solution.py:365
  13.0 4.1 %collective-permute-start.13 = (bf16[8,3200]{1,0:T(8,128)(2,1)S(1)}, bf16[8,3200]{1,0:T(8,128)(2,1)S(1)}, u32[]{:S(2)}, u32[]{:S(2)}) collective-permute-start(bf16[8,3200]{1,0:T(8,128)(2,1)S(1)} %collective-permute-done.11.refs_4_), channel_id=1, source_target_pairs={{0,2},{1,3},{2,0},{3,1},{4,6},{5,7},{6,4},{7,5},{8,10},{9,11},{10,... | collective-permute-start | bytes 153608 | tf_op jit(solution)/shard_map/ppermute | solution.py:365
  14.5 2.6 %collective-permute-start.12 = (bf16[8,3200]{1,0:T(8,128)(2,1)S(1)}, bf16[8,3200]{1,0:T(8,128)(2,1)S(1)}, u32[]{:S(2)}, u32[]{:S(2)}) collective-permute-start(bf16[8,3200]{1,0:T(8,128)(2,1)S(1)} %collective-permute-done.11.refs_4_), channel_id=1, source_target_pairs={{0,1},{1,0},{2,3},{3,2},{4,5},{5,4},{6,7},{7,6},{8,9},{9,8},{10,11... | collective-permute-start | bytes 153608 | tf_op jit(solution)/shard_map/ppermute | solution.py:365
  14.5 3.1 %collective-permute-start.8 = (bf16[8,3200]{1,0:T(8,128)(2,1)S(1)}, bf16[8,3200]{1,0:T(8,128)(2,1)S(1)}, u32[]{:S(2)}, u32[]{:S(2)}) collective-permute-start(bf16[8,3200]{1,0:T(8,128)(2,1)S(1)} %collective-permute-done.7.refs_0_), channel_id=1, source_target_pairs={{0,1},{1,0},{2,3},{3,2},{4,5},{5,4},{6,7},{7,6},{8,9},{9,8},{10,11... | collective-permute-start | bytes 153608 | tf_op jit(solution)/shard_map/ppermute | solution.py:365
  15.0 4.1 %collective-permute-start.5 = (bf16[8,3200]{1,0:T(8,128)(2,1)S(1)}, bf16[8,3200]{1,0:T(8,128)(2,1)S(1)}, u32[]{:S(2)}, u32[]{:S(2)}) collective-permute-start(bf16[8,3200]{1,0:T(8,128)(2,1)S(1)} %collective-permute-done.3.refs_4_), channel_id=1, source_target_pairs={{0,2},{1,3},{2,0},{3,1},{4,6},{5,7},{6,4},{7,5},{8,10},{9,11},{10,... | collective-permute-start | bytes 153608 | tf_op jit(solution)/shard_map/ppermute | solution.py:365
  16.0 3.1 %collective-permute-start.10 = (bf16[8,3200]{1,0:T(8,128)(2,1)S(1)}, bf16[8,3200]{1,0:T(8,128)(2,1)S(1)}, u32[]{:S(2)}, u32[]{:S(2)}) collective-permute-start(bf16[8,3200]{1,0:T(8,128)(2,1)S(1)} %collective-permute-done.9.refs_2_), channel_id=1, source_target_pairs={{0,1},{1,0},{2,3},{3,2},{4,5},{5,4},{6,7},{7,6},{8,9},{9,8},{10,11... | collective-permute-start | bytes 153608 | tf_op jit(solution)/shard_map/ppermute | solution.py:365
  17.1 2.5 %collective-permute-start.14 = (bf16[8,3200]{1,0:T(8,128)(2,1)S(1)}, bf16[8,3200]{1,0:T(8,128)(2,1)S(1)}, u32[]{:S(2)}, u32[]{:S(2)}) collective-permute-start(bf16[8,3200]{1,0:T(8,128)(2,1)S(1)} %collective-permute-done.13.refs_6_), channel_id=1, source_target_pairs={{0,1},{1,0},{2,3},{3,2},{4,5},{5,4},{6,7},{7,6},{8,9},{9,8},{10,11... | collective-permute-start | bytes 153608 | tf_op jit(solution)/shard_map/ppermute | solution.py:365
  17.1 3.1 %collective-permute-start = (bf16[8,3200]{1,0:T(8,128)(2,1)S(1)}, bf16[8,3200]{1,0:T(8,128)(2,1)S(1)}, u32[]{:S(2)}, u32[]{:S(2)}) collective-permute-start(bf16[8,3200]{1,0:T(8,128)(2,1)S(1)} %get-tuple-element.23.refs_0_), channel_id=1, source_target_pairs={{0,1},{1,0},{2,3},{3,2},{4,5},{5,4},{6,7},{7,6},{8,9},{9,8},{10,11... | collective-permute-start | bytes 153608 | tf_op jit(solution)/shard_map/ppermute | solution.py:365
  17.6 2.6 %collective-permute-start.4 = (bf16[8,3200]{1,0:T(8,128)(2,1)S(1)}, bf16[8,3200]{1,0:T(8,128)(2,1)S(1)}, u32[]{:S(2)}, u32[]{:S(2)}) collective-permute-start(bf16[8,3200]{1,0:T(8,128)(2,1)S(1)} %collective-permute-done.3.refs_4_), channel_id=1, source_target_pairs={{0,1},{1,0},{2,3},{3,2},{4,5},{5,4},{6,7},{7,6},{8,9},{9,8},{10,11... | collective-permute-start | bytes 153608 | tf_op jit(solution)/shard_map/ppermute | solution.py:365
  19.1 1.2 %collective-permute-start.2 = (bf16[8,3200]{1,0:T(8,128)(2,1)S(1)}, bf16[8,3200]{1,0:T(8,128)(2,1)S(1)}, u32[]{:S(2)}, u32[]{:S(2)}) collective-permute-start(bf16[8,3200]{1,0:T(8,128)(2,1)S(1)} %collective-permute-done.1.refs_2_), channel_id=1, source_target_pairs={{0,1},{1,0},{2,3},{3,2},{4,5},{5,4},{6,7},{7,6},{8,9},{9,8},{10,11... | collective-permute-start | bytes 153608 | tf_op jit(solution)/shard_map/ppermute | solution.py:365
  19.1 1.4 %collective-permute-start.6 = (bf16[8,3200]{1,0:T(8,128)(2,1)S(1)}, bf16[8,3200]{1,0:T(8,128)(2,1)S(1)}, u32[]{:S(2)}, u32[]{:S(2)}) collective-permute-start(bf16[8,3200]{1,0:T(8,128)(2,1)S(1)} %collective-permute-done.5.refs_6_), channel_id=1, source_target_pairs={{0,1},{1,0},{2,3},{3,2},{4,5},{5,4},{6,7},{7,6},{8,9},{9,8},{10,11... | collective-permute-start | bytes 153608 | tf_op jit(solution)/shard_map/ppermute | solution.py:365
  22.1 5.8 %collective-permute-start.24 = (bf16[104,512]{1,0:T(8,128)(2,1)S(1)}, bf16[104,512]{1,0:T(8,128)(2,1)S(1)}, u32[]{:S(2)}, u32[]{:S(2)}) collective-permute-start(bf16[104,512]{1,0:T(8,128)(2,1)S(1)} %get-tuple-element.26.refs_3_), channel_id=1, source_target_pairs={{0,2},{1,3},{2,0},{3,1},{4,6},{5,7},{6,4},{7,5},{8,10},{9,11},{10,... | collective-permute-start | bytes 319496 | tf_op jit(solution)/shard_map/ppermute | solution.py:365
  23.2 5.9 %collective-permute-start.25 = (bf16[104,512]{1,0:T(8,128)(2,1)S(1)}, bf16[104,512]{1,0:T(8,128)(2,1)S(1)}, u32[]{:S(2)}, u32[]{:S(2)}) collective-permute-start(bf16[104,512]{1,0:T(8,128)(2,1)S(1)} %get-tuple-element.26.refs_3_), channel_id=1, source_target_pairs={{0,1},{1,0},{2,3},{3,2},{4,5},{5,4},{6,7},{7,6},{8,9},{9,8},{10,11... | collective-permute-start | bytes 319496 | tf_op jit(solution)/shard_map/ppermute | solution.py:365
  24.4 5.7 %collective-permute-start.21 = (bf16[104,512]{1,0:T(8,128)(2,1)S(1)}, bf16[104,512]{1,0:T(8,128)(2,1)S(1)}, u32[]{:S(2)}, u32[]{:S(2)}) collective-permute-start(bf16[104,512]{1,0:T(8,128)(2,1)S(1)} %shard_map.115.refs_3_), channel_id=1, source_target_pairs={{0,2},{1,3},{2,0},{3,1},{4,6},{5,7},{6,4},{7,5},{8,10},{9,11},{10,... | collective-permute-start | bytes 319496 | tf_op jit(solution)/shard_map/ppermute | solution.py:365
  25.5 7.8 %collective-permute-start.22 = (bf16[104,512]{1,0:T(8,128)(2,1)S(1)}, bf16[104,512]{1,0:T(8,128)(2,1)S(1)}, u32[]{:S(2)}, u32[]{:S(2)}) collective-permute-start(bf16[104,512]{1,0:T(8,128)(2,1)S(1)} %shard_map.115.refs_3_), channel_id=1, source_target_pairs={{0,1},{1,0},{2,3},{3,2},{4,5},{5,4},{6,7},{7,6},{8,9},{9,8},{10,11... | collective-permute-start | bytes 319496 | tf_op jit(solution)/shard_map/ppermute | solution.py:365
  25.7 7.0 %slice-start = ((s8[12582912]{0:T(1024)(128)(4,1)}), s8[4194304]{0:T(1024)(128)(4,1)S(1)}, s32[]{:S(2)}) async-start(s8[12582912]{0:T(1024)(128)(4,1)} %bitcast.2), calls=%async_computation | async-start | bytes 8388608
  25.7 7.0 %slice-start.1 = ((s8[12582912]{0:T(1024)(128)(4,1)}), s8[4194304]{0:T(1024)(128)(4,1)S(1)}, s32[]{:S(2)}) async-start(s8[12582912]{0:T(1024)(128)(4,1)} %bitcast.2), calls=%async_computation.1 | async-start | bytes 8388608
  26.8 3.6 %copy-start.4 = (bf16[3072,4]{0,1:T(4,128)(2,1)S(1)}, bf16[3072,4]{0,1:T(4,128)(2,1)}, u32[]{:S(2)}) copy-start(bf16[3072,4]{0,1:T(4,128)(2,1)} %param.17) | copy-start | bytes 73732
  26.8 5.8 %slice-start.2 = ((s8[12582912]{0:T(1024)(128)(4,1)}), s8[4194304]{0:T(1024)(128)(4,1)S(1)}, s32[]{:S(2)}) async-start(s8[12582912]{0:T(1024)(128)(4,1)} %bitcast.2), calls=%async_computation.2 | async-start | bytes 8388608
  26.8 5.3 %collective-permute-start.18 = (bf16[104,512]{1,0:T(8,128)(2,1)S(1)}, bf16[104,512]{1,0:T(8,128)(2,1)S(1)}, u32[]{:S(2)}, u32[]{:S(2)}) collective-permute-start(bf16[104,512]{1,0:T(8,128)(2,1)S(1)} %shard_map.114.refs_3_), channel_id=1, source_target_pairs={{0,2},{1,3},{2,0},{3,1},{4,6},{5,7},{6,4},{7,5},{8,10},{9,11},{10,... | collective-permute-start | bytes 319496 | tf_op jit(solution)/shard_map/ppermute | solution.py:365
  27.9 4.2 %collective-permute-start.26 = (bf16[104,512]{1,0:T(8,128)(2,1)S(1)}, bf16[104,512]{1,0:T(8,128)(2,1)S(1)}, u32[]{:S(2)}, u32[]{:S(2)}) collective-permute-start(bf16[104,512]{1,0:T(8,128)(2,1)S(1)} %collective-permute-done.24.refs_0_), channel_id=1, source_target_pairs={{0,1},{1,0},{2,3},{3,2},{4,5},{5,4},{6,7},{7,6},{8,9},{9,8},{10,11... | collective-permute-start | bytes 319496 | tf_op jit(solution)/shard_map/ppermute | solution.py:365
  29.1 5.4 %collective-permute-start.15 = (bf16[104,512]{1,0:T(8,128)(2,1)S(1)}, bf16[104,512]{1,0:T(8,128)(2,1)S(1)}, u32[]{:S(2)}, u32[]{:S(2)}) collective-permute-start(bf16[104,512]{1,0:T(8,128)(2,1)S(1)} %shard_map.113.refs_4_), channel_id=1, source_target_pairs={{0,2},{1,3},{2,0},{3,1},{4,6},{5,7},{6,4},{7,5},{8,10},{9,11},{10,... | collective-permute-start | bytes 319496 | tf_op jit(solution)/shard_map/ppermute | solution.py:365
  30.2 4.4 %collective-permute-start.23 = (bf16[104,512]{1,0:T(8,128)(2,1)S(1)}, bf16[104,512]{1,0:T(8,128)(2,1)S(1)}, u32[]{:S(2)}, u32[]{:S(2)}) collective-permute-start(bf16[104,512]{1,0:T(8,128)(2,1)S(1)} %collective-permute-done.21.refs_0_), channel_id=1, source_target_pairs={{0,1},{1,0},{2,3},{3,2},{4,5},{5,4},{6,7},{7,6},{8,9},{9,8},{10,11... | collective-permute-start | bytes 319496 | tf_op jit(solution)/shard_map/ppermute | solution.py:365
  32.1 3.0 %collective-permute-start.19 = (bf16[104,512]{1,0:T(8,128)(2,1)S(1)}, bf16[104,512]{1,0:T(8,128)(2,1)S(1)}, u32[]{:S(2)}, u32[]{:S(2)}) collective-permute-start(bf16[104,512]{1,0:T(8,128)(2,1)S(1)} %shard_map.114.refs_3_), channel_id=1, source_target_pairs={{0,1},{1,0},{2,3},{3,2},{4,5},{5,4},{6,7},{7,6},{8,9},{9,8},{10,11... | collective-permute-start | bytes 319496 | tf_op jit(solution)/shard_map/ppermute | solution.py:365
  32.1 3.0 %collective-permute-start.20 = (bf16[104,512]{1,0:T(8,128)(2,1)S(1)}, bf16[104,512]{1,0:T(8,128)(2,1)S(1)}, u32[]{:S(2)}, u32[]{:S(2)}) collective-permute-start(bf16[104,512]{1,0:T(8,128)(2,1)S(1)} %collective-permute-done.18.refs_0_), channel_id=1, source_target_pairs={{0,1},{1,0},{2,3},{3,2},{4,5},{5,4},{6,7},{7,6},{8,9},{9,8},{10,11... | collective-permute-start | bytes 319496 | tf_op jit(solution)/shard_map/ppermute | solution.py:365
  33.3 2.6 %collective-permute-start.16 = (bf16[104,512]{1,0:T(8,128)(2,1)S(1)}, bf16[104,512]{1,0:T(8,128)(2,1)S(1)}, u32[]{:S(2)}, u32[]{:S(2)}) collective-permute-start(bf16[104,512]{1,0:T(8,128)(2,1)S(1)} %shard_map.113.refs_4_), channel_id=1, source_target_pairs={{0,1},{1,0},{2,3},{3,2},{4,5},{5,4},{6,7},{7,6},{8,9},{9,8},{10,11... | collective-permute-start | bytes 319496 | tf_op jit(solution)/shard_map/ppermute | solution.py:365
  34.5 1.4 %collective-permute-start.17 = (bf16[104,512]{1,0:T(8,128)(2,1)S(1)}, bf16[104,512]{1,0:T(8,128)(2,1)S(1)}, u32[]{:S(2)}, u32[]{:S(2)}) collective-permute-start(bf16[104,512]{1,0:T(8,128)(2,1)S(1)} %collective-permute-done.15.refs_0_), channel_id=1, source_target_pairs={{0,1},{1,0},{2,3},{3,2},{4,5},{5,4},{6,7},{7,6},{8,9},{9,8},{10,11... | collective-permute-start | bytes 319496 | tf_op jit(solution)/shard_map/ppermute | solution.py:365
  36.6 6.2 %collective-permute-start.27 = (bf16[32,768]{1,0:T(8,128)(2,1)S(1)}, bf16[32,768]{1,0:T(8,128)(2,1)S(1)}, u32[]{:S(2)}, u32[]{:S(2)}) collective-permute-start(bf16[32,768]{1,0:T(8,128)(2,1)S(1)} %get-tuple-element.32), channel_id=1, source_target_pairs={{0,12},{4,8},{8,4},{12,0},{1,13},{5,9},{9,5},{13,1},{2,14},{6,10},... | collective-permute-start | bytes 147464 | tf_op jit(solution)/shard_map/ppermute | solution.py:365
  38.9 5.8 %collective-permute-start.28 = (bf16[32,768]{1,0:T(8,128)(2,1)S(1)}, bf16[32,768]{1,0:T(8,128)(2,1)S(1)}, u32[]{:S(2)}, u32[]{:S(2)}) collective-permute-start(bf16[32,768]{1,0:T(8,128)(2,1)S(1)} %get-tuple-element.33), channel_id=1, source_target_pairs={{0,8},{4,12},{8,0},{12,4},{1,9},{5,13},{9,1},{13,5},{2,10},{6,14},... | collective-permute-start | bytes 147464 | tf_op jit(solution)/shard_map/ppermute | solution.py:365
  38.9 5.8 %collective-permute-start.29 = (bf16[32,768]{1,0:T(8,128)(2,1)S(1)}, bf16[32,768]{1,0:T(8,128)(2,1)S(1)}, u32[]{:S(2)}, u32[]{:S(2)}) collective-permute-start(bf16[32,768]{1,0:T(8,128)(2,1)S(1)} %get-tuple-element.34), channel_id=1, source_target_pairs={{0,4},{4,0},{8,12},{12,8},{1,5},{5,1},{9,13},{13,9},{2,6},{6,2},{1... | collective-permute-start | bytes 147464 | tf_op jit(solution)/shard_map/ppermute | solution.py:365
  44.8 1.9 %collective-permute-start.30 = (bf16[8,768]{1,0:T(8,128)(2,1)S(1)}, bf16[8,768]{1,0:T(8,128)(2,1)S(1)}, u32[]{:S(2)}, u32[]{:S(2)}) collective-permute-start(bf16[8,768]{1,0:T(8,128)(2,1)S(1)} %get-tuple-element.36), channel_id=1, source_target_pairs={{0,1},{1,0},{2,3},{3,2},{4,5},{5,4},{6,7},{7,6},{8,9},{9,8},{10,11... | collective-permute-start | bytes 36872 | tf_op jit(solution)/shard_map/ppermute | solution.py:365
  44.9 3.8 %collective-permute-start.31 = (bf16[8,768]{1,0:T(8,128)(2,1)S(1)}, bf16[8,768]{1,0:T(8,128)(2,1)S(1)}, u32[]{:S(2)}, u32[]{:S(2)}) collective-permute-start(bf16[8,768]{1,0:T(8,128)(2,1)S(1)} %get-tuple-element.37), channel_id=1, source_target_pairs={{0,2},{1,3},{2,0},{3,1},{4,6},{5,7},{6,4},{7,5},{8,10},{9,11},{10,... | collective-permute-start | bytes 36872 | tf_op jit(solution)/shard_map/ppermute | solution.py:365
  45.9 3.1 %collective-permute-start.32 = (bf16[8,768]{1,0:T(8,128)(2,1)S(1)}, bf16[8,768]{1,0:T(8,128)(2,1)S(1)}, u32[]{:S(2)}, u32[]{:S(2)}) collective-permute-start(bf16[8,768]{1,0:T(8,128)(2,1)S(1)} %get-tuple-element.38), channel_id=1, source_target_pairs={{0,3},{1,2},{2,1},{3,0},{4,7},{5,6},{6,5},{7,4},{8,11},{9,10},{10,... | collective-permute-start | bytes 36872 | tf_op jit(solution)/shard_map/ppermute | solution.py:365
  (2 other events, 1.5 us)

commit v7 on v6

--- a/solution.py
+++ b/solution.py
@@ -208,8 +208,8 @@
         scores = dot_nt(query, key).reshape(pair * group, rows, rows * cache) * scale + bias
         exp_scores = jnp.exp(scores - jnp.max(scores, axis=2, keepdims=True))
         total = jnp.sum(exp_scores, axis=2, keepdims=True)
-        probs = (exp_scores * (1.0 / total)).reshape(pair * group * rows, rows * cache)
-        attended = dot(probs.astype(jnp.bfloat16), value)
+        weights = exp_scores.reshape(pair * group * rows, rows * cache).astype(jnp.bfloat16)
+        attended = dot(weights, value) * (1.0 / total).reshape(pair * group * rows, 1)
         for n in range(pair * group):
             h = kv * group + n
             one = n // group

time: 49.8 us -> 49.7 us (level)
  no operation moved by 1% of the time
where the time goes in v7:
time: 49.7 us; the launch traced here: 49.6 us
  starting transfers between devices  23.8 us (48%)
  waiting for transfers between devices  12.8 us (26%)
  Pallas kernels  11.1 us (22%)
  local copies, waits for them, and re-layouts  1.61 us (3%)
    ppermute x33, starting transfers between devices, flip(): lax.ppermute(x, axis, [(i, i ^ bits) for i in range(lax.axis_size(axis))])  23.8 us
    ppermute x33, waiting for transfers between devices, flip(): lax.ppermute(x, axis, [(i, i ^ bits) for i in range(lax.axis_size(axis))])  12.8 us
    pallas_call x14, Pallas kernels, call(): pl.pallas_call(body, out_shape=out_shapes, in_specs=specs, out_specs=jax....  11.1 us
    unnamed x34, local copies, waits for them, and re-layouts  1.61 us
  transfers between devices with their start and end apart: 33, of which 11 were waited for; matrix products, arithmetic and copies ran while one was open for 0% of the time, Pallas kernels for 13%

profile of v7, /device:TPU:0, one launch (start us, length us, event | category | flops | bytes accessed | tf_op | source)
XLA Modules:
  0.0 49.6 jit_solution(8730744132740502297)
XLA Ops:
  0.1 0.6 %copy-done.6 = s32[32,2]{0,1:T(2,128)S(1)} copy-done((s32[32,2]{0,1:T(2,128)S(1)}, s32[32,2]{0,1:T(2,128)}, u32[]{:S(2)}) %copy-start.6) | copy-done | bytes 280
  0.7 0.1 copy-done.3
  0.8 0.5 copy-done
  1.3 0.3 copy-done.1
  1.7 1.6 %shard_map.110 = (bf16[8,3200]{1,0:T(8,128)(2,1)S(1)}, bf16[8,3072]{1,0:T(8,128)(2,1)S(1)}) custom-call(f32[8,128]{1,0:T(8,128)S(1)} %shard_map.109._, s32[8]{0:T(128)S(1)} %copy-done.7, s32[2,32]{1,0:T(2,128)S(1)} %bitcast.9, bf16[8,3072]{1,0:T(8,128)(2,1)S(1)} %copy-done.2, bf16[8,128,512]{2,1,0:T(8,128)(2,1)S(1)} %copy-done, ...), custom_call_target="tpu_custom_call" | custom-call | flops 30000001024 | bytes 104857600 | tf_op jit(solution)/shard_map/pallas_call | solution.py:137
  3.2 3.1 %collective-permute-start.7 = (bf16[8,3200]{1,0:T(8,128)(2,1)S(1)}, bf16[8,3200]{1,0:T(8,128)(2,1)S(1)}, u32[]{:S(2)}, u32[]{:S(2)}) collective-permute-start(bf16[8,3200]{1,0:T(8,128)(2,1)S(1)} %get-tuple-element.23.refs_0_), channel_id=1, source_target_pairs={{0,4},{4,0},{8,12},{12,8},{1,5},{5,1},{9,13},{13,9},{2,6},{6,2},{1... | collective-permute-start | bytes 153608 | tf_op jit(solution)/shard_map/ppermute | solution.py:365
  6.3 2.5 %collective-permute-start.11 = (bf16[8,3200]{1,0:T(8,128)(2,1)S(1)}, bf16[8,3200]{1,0:T(8,128)(2,1)S(1)}, u32[]{:S(2)}, u32[]{:S(2)}) collective-permute-start(bf16[8,3200]{1,0:T(8,128)(2,1)S(1)} %get-tuple-element.23.refs_0_), channel_id=1, source_target_pairs={{0,12},{4,8},{8,4},{12,0},{1,13},{5,9},{9,5},{13,1},{2,14},{6,10},... | collective-permute-start | bytes 153608 | tf_op jit(solution)/shard_map/ppermute | solution.py:365
  8.8 0.1 collective-permute-start.3
  8.9 1.5 %collective-permute-start.1 = (bf16[8,3200]{1,0:T(8,128)(2,1)S(1)}, bf16[8,3200]{1,0:T(8,128)(2,1)S(1)}, u32[]{:S(2)}, u32[]{:S(2)}) collective-permute-start(bf16[8,3200]{1,0:T(8,128)(2,1)S(1)} %get-tuple-element.23.refs_0_), channel_id=1, source_target_pairs={{0,2},{1,3},{2,0},{3,1},{4,6},{5,7},{6,4},{7,5},{8,10},{9,11},{10,... | collective-permute-start | bytes 153608 | tf_op jit(solution)/shard_map/ppermute | solution.py:365
  10.4 0.5 %collective-permute-start.9 = (bf16[8,3200]{1,0:T(8,128)(2,1)S(1)}, bf16[8,3200]{1,0:T(8,128)(2,1)S(1)}, u32[]{:S(2)}, u32[]{:S(2)}) collective-permute-start(bf16[8,3200]{1,0:T(8,128)(2,1)S(1)} %collective-permute-done.7.refs_0_), channel_id=1, source_target_pairs={{0,2},{1,3},{2,0},{3,1},{4,6},{5,7},{6,4},{7,5},{8,10},{9,11},{10,... | collective-permute-start | bytes 153608 | tf_op jit(solution)/shard_map/ppermute | solution.py:365
  11.0 1.9 %collective-permute-done.11.refs_4_ = bf16[8,3200]{1,0:T(8,128)(2,1)S(1)} collective-permute-done((bf16[8,3200]{1,0:T(8,128)(2,1)S(1)}, bf16[8,3200]{1,0:T(8,128)(2,1)S(1)}, u32[]{:S(2)}, u32[]{:S(2)}) %collective-permute-start.11) | collective-permute-done | bytes 51232 | tf_op jit(solution)/shard_map/ppermute | solution.py:365
  12.9 1.5 %collective-permute-start.13 = (bf16[8,3200]{1,0:T(8,128)(2,1)S(1)}, bf16[8,3200]{1,0:T(8,128)(2,1)S(1)}, u32[]{:S(2)}, u32[]{:S(2)}) collective-permute-start(bf16[8,3200]{1,0:T(8,128)(2,1)S(1)} %collective-permute-done.11.refs_4_), channel_id=1, source_target_pairs={{0,2},{1,3},{2,0},{3,1},{4,6},{5,7},{6,4},{7,5},{8,10},{9,11},{10,... | collective-permute-start | bytes 153608 | tf_op jit(solution)/shard_map/ppermute | solution.py:365
  14.4 0.5 %collective-permute-start.8 = (bf16[8,3200]{1,0:T(8,128)(2,1)S(1)}, bf16[8,3200]{1,0:T(8,128)(2,1)S(1)}, u32[]{:S(2)}, u32[]{:S(2)}) collective-permute-start(bf16[8,3200]{1,0:T(8,128)(2,1)S(1)} %collective-permute-done.7.refs_0_), channel_id=1, source_target_pairs={{0,1},{1,0},{2,3},{3,2},{4,5},{5,4},{6,7},{7,6},{8,9},{9,8},{10,11... | collective-permute-start | bytes 153608 | tf_op jit(solution)/shard_map/ppermute | solution.py:365
  14.9 1.0 %collective-permute-start.5 = (bf16[8,3200]{1,0:T(8,128)(2,1)S(1)}, bf16[8,3200]{1,0:T(8,128)(2,1)S(1)}, u32[]{:S(2)}, u32[]{:S(2)}) collective-permute-start(bf16[8,3200]{1,0:T(8,128)(2,1)S(1)} %collective-permute-done.3.refs_4_), channel_id=1, source_target_pairs={{0,2},{1,3},{2,0},{3,1},{4,6},{5,7},{6,4},{7,5},{8,10},{9,11},{10,... | collective-permute-start | bytes 153608 | tf_op jit(solution)/shard_map/ppermute | solution.py:365
  15.9 0.2 collective-permute-start.10
  16.1 0.9 %collective-permute-done.13.refs_6_ = bf16[8,3200]{1,0:T(8,128)(2,1)S(1)} collective-permute-done((bf16[8,3200]{1,0:T(8,128)(2,1)S(1)}, bf16[8,3200]{1,0:T(8,128)(2,1)S(1)}, u32[]{:S(2)}, u32[]{:S(2)}) %collective-permute-start.13) | collective-permute-done | bytes 51232 | tf_op jit(solution)/shard_map/ppermute | solution.py:365
  17.0 0.5 %collective-permute-start = (bf16[8,3200]{1,0:T(8,128)(2,1)S(1)}, bf16[8,3200]{1,0:T(8,128)(2,1)S(1)}, u32[]{:S(2)}, u32[]{:S(2)}) collective-permute-start(bf16[8,3200]{1,0:T(8,128)(2,1)S(1)} %get-tuple-element.23.refs_0_), channel_id=1, source_target_pairs={{0,1},{1,0},{2,3},{3,2},{4,5},{5,4},{6,7},{7,6},{8,9},{9,8},{10,11... | collective-permute-start | bytes 153608 | tf_op jit(solution)/shard_map/ppermute | solution.py:365
  17.6 1.4 %collective-permute-done.5.refs_6_ = bf16[8,3200]{1,0:T(8,128)(2,1)S(1)} collective-permute-done((bf16[8,3200]{1,0:T(8,128)(2,1)S(1)}, bf16[8,3200]{1,0:T(8,128)(2,1)S(1)}, u32[]{:S(2)}, u32[]{:S(2)}) %collective-permute-start.5) | collective-permute-done | bytes 51232 | tf_op jit(solution)/shard_map/ppermute | solution.py:365
  19.0 0.5 %collective-permute-start.6 = (bf16[8,3200]{1,0:T(8,128)(2,1)S(1)}, bf16[8,3200]{1,0:T(8,128)(2,1)S(1)}, u32[]{:S(2)}, u32[]{:S(2)}) collective-permute-start(bf16[8,3200]{1,0:T(8,128)(2,1)S(1)} %collective-permute-done.5.refs_6_), channel_id=1, source_target_pairs={{0,1},{1,0},{2,3},{3,2},{4,5},{5,4},{6,7},{7,6},{8,9},{9,8},{10,11... | collective-permute-start | bytes 153608 | tf_op jit(solution)/shard_map/ppermute | solution.py:365
  19.5 0.6 %shard_map.111 = (bf16[104,3072]{1,0:T(8,128)(2,1)S(1)}, bf16[64,128]{1,0:T(8,128)(2,1)S(1)}) custom-call(bf16[8,3200]{1,0:T(8,128)(2,1)S(1)} %collective-permute-done.7.refs_0_, bf16[8,3200]{1,0:T(8,128)(2,1)S(1)} %collective-permute-done.8.refs_1_, bf16[8,3200]{1,0:T(8,128)(2,1)S(1)} %collective-permute-done.9.refs_2_, ...), custom_call_target="tpu_custom_call" | custom-call | flops 100000000 | tf_op jit(solution)/shard_map/pallas_call | solution.py:137
  20.3 0.2 collective-permute-done.6.refs_7_
  20.5 1.6 %shard_map.112 = (bf16[104,3072]{1,0:T(8,128)(2,1)S(1)}, bf16[64,128]{1,0:T(8,128)(2,1)S(1)}, bf16[104,512]{1,0:T(8,128)(2,1)S(1)}) custom-call(bf16[8,3200]{1,0:T(8,128)(2,1)S(1)} %get-tuple-element.23.refs_0_, bf16[8,3200]{1,0:T(8,128)(2,1)S(1)} %collective-permute-done.refs_1_, bf16[8,3200]{1,0:T(8,128)(2,1)S(1)} %collective-permute-done.1.refs_2_, ...), custom_call_target="tpu_custom_call" | custom-call | flops 1000000000 | tf_op jit(solution)/shard_map/pallas_call | solution.py:137
  22.0 1.1 %collective-permute-start.24 = (bf16[104,512]{1,0:T(8,128)(2,1)S(1)}, bf16[104,512]{1,0:T(8,128)(2,1)S(1)}, u32[]{:S(2)}, u32[]{:S(2)}) collective-permute-start(bf16[104,512]{1,0:T(8,128)(2,1)S(1)} %get-tuple-element.26.refs_3_), channel_id=1, source_target_pairs={{0,2},{1,3},{2,0},{3,1},{4,6},{5,7},{6,4},{7,5},{8,10},{9,11},{10,... | collective-permute-start | bytes 319496 | tf_op jit(solution)/shard_map/ppermute | solution.py:365
  23.2 1.1 %shard_map.115.refs_3_ = bf16[104,512]{1,0:T(8,128)(2,1)S(1)} custom-call(bf16[104,3072]{1,0:T(8,128)(2,1)S(1)} %get-tuple-element.25.x_ref.refs_2_, bf16[3072,2048]{1,0:T(8,128)(2,1)S(1)} %bitcast.5, bf16[3072,2048]{1,0:T(8,128)(2,1)S(1)} %bitcast.7), custom_call_target="tpu_custom_call" | custom-call | flops 1000000000 | tf_op jit(solution)/shard_map/pallas_call | solution.py:137
  24.4 1.0 %collective-permute-start.21 = (bf16[104,512]{1,0:T(8,128)(2,1)S(1)}, bf16[104,512]{1,0:T(8,128)(2,1)S(1)}, u32[]{:S(2)}, u32[]{:S(2)}) collective-permute-start(bf16[104,512]{1,0:T(8,128)(2,1)S(1)} %shard_map.115.refs_3_), channel_id=1, source_target_pairs={{0,2},{1,3},{2,0},{3,1},{4,6},{5,7},{6,4},{7,5},{8,10},{9,11},{10,... | collective-permute-start | bytes 319496 | tf_op jit(solution)/shard_map/ppermute | solution.py:365
  25.4 0.2 collective-permute-start.22
  25.6 1.1 %shard_map.114.refs_3_ = bf16[104,512]{1,0:T(8,128)(2,1)S(1)} custom-call(bf16[104,3072]{1,0:T(8,128)(2,1)S(1)} %get-tuple-element.25.x_ref.refs_2_, bf16[3072,2048]{1,0:T(8,128)(2,1)S(1)} %bitcast.5, bf16[3072,2048]{1,0:T(8,128)(2,1)S(1)} %bitcast.7), custom_call_target="tpu_custom_call" | custom-call | flops 1000000000 | tf_op jit(solution)/shard_map/pallas_call | solution.py:137
  26.7 1.1 %collective-permute-start.18 = (bf16[104,512]{1,0:T(8,128)(2,1)S(1)}, bf16[104,512]{1,0:T(8,128)(2,1)S(1)}, u32[]{:S(2)}, u32[]{:S(2)}) collective-permute-start(bf16[104,512]{1,0:T(8,128)(2,1)S(1)} %shard_map.114.refs_3_), channel_id=1, source_target_pairs={{0,2},{1,3},{2,0},{3,1},{4,6},{5,7},{6,4},{7,5},{8,10},{9,11},{10,... | collective-permute-start | bytes 319496 | tf_op jit(solution)/shard_map/ppermute | solution.py:365
  27.9 1.1 %shard_map.113.refs_4_ = bf16[104,512]{1,0:T(8,128)(2,1)S(1)} custom-call(bf16[104,3072]{1,0:T(8,128)(2,1)S(1)} %get-tuple-element.25.x_ref.refs_2_, bf16[3072,2048]{1,0:T(8,128)(2,1)S(1)} %bitcast.5, bf16[3072,2048]{1,0:T(8,128)(2,1)S(1)} %bitcast.7), custom_call_target="tpu_custom_call" | custom-call | flops 1000000000 | tf_op jit(solution)/shard_map/pallas_call | solution.py:137
  29.1 1.0 %collective-permute-start.15 = (bf16[104,512]{1,0:T(8,128)(2,1)S(1)}, bf16[104,512]{1,0:T(8,128)(2,1)S(1)}, u32[]{:S(2)}, u32[]{:S(2)}) collective-permute-start(bf16[104,512]{1,0:T(8,128)(2,1)S(1)} %shard_map.113.refs_4_), channel_id=1, source_target_pairs={{0,2},{1,3},{2,0},{3,1},{4,6},{5,7},{6,4},{7,5},{8,10},{9,11},{10,... | collective-permute-start | bytes 319496 | tf_op jit(solution)/shard_map/ppermute | solution.py:365
  30.1 0.2 collective-permute-start.23
  30.3 0.7 %shard_map.119 = (bf16[128,128]{1,0:T(8,128)(2,1)S(1)}, f32[104,128]{1,0:T(8,128)S(1)}) custom-call(bf16[64,128]{1,0:T(8,128)(2,1)S(1)} %get-tuple-element.27.refs_0_, bf16[64,128]{1,0:T(8,128)(2,1)S(1)} %get-tuple-element.28.refs_1_, bf16[104,3072]{1,0:T(8,128)(2,1)S(1)} %get-tuple-element.25.x_ref.refs_2_, bf16[4,3072]{1,0:T(4,128)(2,1)S(1)} %bitcast.8), custom_call_target="tpu_custom_call" | custom-call | flops 1000000000 | tf_op jit(solution)/shard_map/pallas_call | solution.py:137
  31.0 1.1 %collective-permute-done.18.refs_0_ = bf16[104,512]{1,0:T(8,128)(2,1)S(1)} collective-permute-done((bf16[104,512]{1,0:T(8,128)(2,1)S(1)}, bf16[104,512]{1,0:T(8,128)(2,1)S(1)}, u32[]{:S(2)}, u32[]{:S(2)}) %collective-permute-start.18) | collective-permute-done | bytes 106528 | tf_op jit(solution)/shard_map/ppermute | solution.py:365
  32.0 0.5 %collective-permute-start.20 = (bf16[104,512]{1,0:T(8,128)(2,1)S(1)}, bf16[104,512]{1,0:T(8,128)(2,1)S(1)}, u32[]{:S(2)}, u32[]{:S(2)}) collective-permute-start(bf16[104,512]{1,0:T(8,128)(2,1)S(1)} %collective-permute-done.18.refs_0_), channel_id=1, source_target_pairs={{0,1},{1,0},{2,3},{3,2},{4,5},{5,4},{6,7},{7,6},{8,9},{9,8},{10,11... | collective-permute-start | bytes 319496 | tf_op jit(solution)/shard_map/ppermute | solution.py:365
  32.6 0.6 %shard_map.116.refs_5_ = f32[104,768]{1,0:T(8,128)S(1)} custom-call(bf16[104,512]{1,0:T(8,128)(2,1)S(1)} %collective-permute-done.24.refs_0_, bf16[104,512]{1,0:T(8,128)(2,1)S(1)} %collective-permute-done.25.refs_1_, bf16[104,512]{1,0:T(8,128)(2,1)S(1)} %collective-permute-done.26.refs_2_, bf16[104,512]{1,0:T(8,128)(2,1)S(1)} %get-tuple-element.26.refs_3_, ...), custom_call_target="tpu_custom_call" | custom-call | flops 1000000000 | tf_op jit(solution)/shard_map/pallas_call | solution.py:137
  33.3 1.2 %collective-permute-done.15.refs_0_ = bf16[104,512]{1,0:T(8,128)(2,1)S(1)} collective-permute-done((bf16[104,512]{1,0:T(8,128)(2,1)S(1)}, bf16[104,512]{1,0:T(8,128)(2,1)S(1)}, u32[]{:S(2)}, u32[]{:S(2)}) %collective-permute-start.15) | collective-permute-done | bytes 106528 | tf_op jit(solution)/shard_map/ppermute | solution.py:365
  34.4 0.6 %shard_map.117.refs_6_ = f32[104,768]{1,0:T(8,128)S(1)} custom-call(bf16[104,512]{1,0:T(8,128)(2,1)S(1)} %collective-permute-done.21.refs_0_, bf16[104,512]{1,0:T(8,128)(2,1)S(1)} %collective-permute-done.22.refs_1_, bf16[104,512]{1,0:T(8,128)(2,1)S(1)} %collective-permute-done.23.refs_2_, bf16[104,512]{1,0:T(8,128)(2,1)S(1)} %shard_map.115.refs_3_, ...), custom_call_target="tpu_custom_call" | custom-call | flops 1000000000 | tf_op jit(solution)/shard_map/pallas_call | solution.py:137
  35.1 0.7 %shard_map.118.refs_4_ = f32[104,768]{1,0:T(8,128)S(1)} custom-call(bf16[104,512]{1,0:T(8,128)(2,1)S(1)} %collective-permute-done.18.refs_0_, bf16[104,512]{1,0:T(8,128)(2,1)S(1)} %collective-permute-done.19.refs_1_, bf16[104,512]{1,0:T(8,128)(2,1)S(1)} %collective-permute-done.20.refs_2_, bf16[104,512]{1,0:T(8,128)(2,1)S(1)} %shard_map.114.refs_3_, ...), custom_call_target="tpu_custom_call" | custom-call | flops 1000000000 | tf_op jit(solution)/shard_map/pallas_call | solution.py:137
  35.8 0.7 %shard_map.120 = (bf16[32,768]{1,0:T(8,128)(2,1)S(1)}, bf16[32,768]{1,0:T(8,128)(2,1)S(1)}, bf16[32,768]{1,0:T(8,128)(2,1)S(1)}, bf16[32,768]{1,0:T(8,128)(2,1)S(1)}) custom-call(bf16[104,512]{1,0:T(8,128)(2,1)S(1)} %collective-permute-done.15.refs_0_, bf16[104,512]{1,0:T(8,128)(2,1)S(1)} %collective-permute-done.16.refs_1_, ...), custom_call_target="tpu_custom_call" | custom-call | flops 1000000000 | tf_op jit(solution)/shard_map/pallas_call | solution.py:137
  36.5 2.3 %collective-permute-start.27 = (bf16[32,768]{1,0:T(8,128)(2,1)S(1)}, bf16[32,768]{1,0:T(8,128)(2,1)S(1)}, u32[]{:S(2)}, u32[]{:S(2)}) collective-permute-start(bf16[32,768]{1,0:T(8,128)(2,1)S(1)} %get-tuple-element.32), channel_id=1, source_target_pairs={{0,12},{4,8},{8,4},{12,0},{1,13},{5,9},{9,5},{13,1},{2,14},{6,10},... | collective-permute-start | bytes 147464 | tf_op jit(solution)/shard_map/ppermute | solution.py:365
  38.9 2.2 %collective-permute-start.29 = (bf16[32,768]{1,0:T(8,128)(2,1)S(1)}, bf16[32,768]{1,0:T(8,128)(2,1)S(1)}, u32[]{:S(2)}, u32[]{:S(2)}) collective-permute-start(bf16[32,768]{1,0:T(8,128)(2,1)S(1)} %get-tuple-element.34), channel_id=1, source_target_pairs={{0,4},{4,0},{8,12},{12,8},{1,5},{5,1},{9,13},{13,9},{2,6},{6,2},{1... | collective-permute-start | bytes 147464 | tf_op jit(solution)/shard_map/ppermute | solution.py:365
  41.0 1.8 %collective-permute-done.27.refs_1_ = bf16[32,768]{1,0:T(8,128)(2,1)S(1)} collective-permute-done((bf16[32,768]{1,0:T(8,128)(2,1)S(1)}, bf16[32,768]{1,0:T(8,128)(2,1)S(1)}, u32[]{:S(2)}, u32[]{:S(2)}) %collective-permute-start.27) | collective-permute-done | bytes 49184 | tf_op jit(solution)/shard_map/ppermute | solution.py:365
  42.8 1.9 %collective-permute-done.28.refs_2_ = bf16[32,768]{1,0:T(8,128)(2,1)S(1)} collective-permute-done((bf16[32,768]{1,0:T(8,128)(2,1)S(1)}, bf16[32,768]{1,0:T(8,128)(2,1)S(1)}, u32[]{:S(2)}, u32[]{:S(2)}) %collective-permute-start.28) | collective-permute-done | bytes 49184 | tf_op jit(solution)/shard_map/ppermute | solution.py:365
  44.8 1.1 %collective-permute-start.31 = (bf16[8,768]{1,0:T(8,128)(2,1)S(1)}, bf16[8,768]{1,0:T(8,128)(2,1)S(1)}, u32[]{:S(2)}, u32[]{:S(2)}) collective-permute-start(bf16[8,768]{1,0:T(8,128)(2,1)S(1)} %get-tuple-element.37), channel_id=1, source_target_pairs={{0,2},{1,3},{2,0},{3,1},{4,6},{5,7},{6,4},{7,5},{8,10},{9,11},{10,... | collective-permute-start | bytes 36872 | tf_op jit(solution)/shard_map/ppermute | solution.py:365
  45.8 0.8 %collective-permute-start.32 = (bf16[8,768]{1,0:T(8,128)(2,1)S(1)}, bf16[8,768]{1,0:T(8,128)(2,1)S(1)}, u32[]{:S(2)}, u32[]{:S(2)}) collective-permute-start(bf16[8,768]{1,0:T(8,128)(2,1)S(1)} %get-tuple-element.38), channel_id=1, source_target_pairs={{0,3},{1,2},{2,1},{3,0},{4,7},{5,6},{6,5},{7,4},{8,11},{9,10},{10,... | collective-permute-start | bytes 36872 | tf_op jit(solution)/shard_map/ppermute | solution.py:365
  46.6 1.9 %collective-permute-done.31.refs_2_ = bf16[8,768]{1,0:T(8,128)(2,1)S(1)} collective-permute-done((bf16[8,768]{1,0:T(8,128)(2,1)S(1)}, bf16[8,768]{1,0:T(8,128)(2,1)S(1)}, u32[]{:S(2)}, u32[]{:S(2)}) %collective-permute-start.31) | collective-permute-done | bytes 12320 | tf_op jit(solution)/shard_map/ppermute | solution.py:365
  48.5 0.4 collective-permute-done.32.refs_3_
  49.0 0.6 %shard_map.122 = bf16[8,3072]{1,0:T(8,128)(2,1)} custom-call(bf16[8,3072]{1,0:T(8,128)(2,1)S(1)} %get-tuple-element.22.resid_ref, f32[8,768]{1,0:T(8,128)S(1)} %get-tuple-element.35.refs_0_, bf16[8,768]{1,0:T(8,128)(2,1)S(1)} %collective-permute-done.30.refs_1_, bf16[8,768]{1,0:T(8,128)(2,1)S(1)} %collective-permute-done.31.refs_2_, ...), custom_call_target="tpu_custom_call" | custom-call | flops 1000000 | tf_op jit(solution)/shard_map/pallas_call | solution.py:137
  (69 shorter events, 0.7 us)
Async XLA Ops:
  0.0 0.8 %copy-start.2 = (bf16[8,3072]{1,0:T(8,128)(2,1)S(1)}, bf16[8,3072]{1,0:T(8,128)(2,1)}, u32[]{:S(2)}) copy-start(bf16[8,3072]{1,0:T(8,128)(2,1)} %queries_ref.1) | copy-start | bytes 147460
  0.0 1.3 %copy-start = (bf16[8,128,512]{2,1,0:T(8,128)(2,1)S(1)}, bf16[8,128,512]{2,1,0:T(8,128)(2,1)}, u32[]{:S(2)}) copy-start(bf16[8,128,512]{2,1,0:T(8,128)(2,1)} %keys_ref.1) | copy-start | bytes 3145732
  0.0 1.6 %copy-start.1 = (bf16[8,128,512]{2,1,0:T(8,128)(2,1)S(1)}, bf16[8,128,512]{2,1,0:T(8,128)(2,1)}, u32[]{:S(2)}) copy-start(bf16[8,128,512]{2,1,0:T(8,128)(2,1)} %values_ref.1) | copy-start | bytes 3145732
  0.0 1.6 %copy-start.7 = (s32[8]{0:T(128)S(1)}, s32[8]{0:T(128)}, u32[]{:S(2)}) copy-start(s32[8]{0:T(128)} %lengths_ref.1) | copy-start | bytes 100
  0.0 1.6 %copy-start.5 = (bf16[3072]{0:T(1024)(128)(2,1)S(1)}, bf16[3072]{0:T(1024)(128)(2,1)}, u32[]{:S(2)}) copy-start(bf16[3072]{0:T(1024)(128)(2,1)} %gain_ref.1) | copy-start | bytes 18436
  0.0 20.4 %slice-start.3 = ((s8[12582912]{0:T(1024)(128)(4,1)}), s8[4194304]{0:T(1024)(128)(4,1)S(1)}, s32[]{:S(2)}) async-start(s8[12582912]{0:T(1024)(128)(4,1)} %bitcast.4), calls=%async_computation.3 | async-start | bytes 8388608
  0.0 20.4 %slice-start.6 = ((s8[12582912]{0:T(1024)(128)(4,1)}), s8[4194304]{0:T(1024)(128)(4,1)S(1)}, s32[]{:S(2)}) async-start(s8[12582912]{0:T(1024)(128)(4,1)} %bitcast.6), calls=%async_computation.6 | async-start | bytes 8388608
  1.6 18.8 %slice-start.4 = ((s8[12582912]{0:T(1024)(128)(4,1)}), s8[4194304]{0:T(1024)(128)(4,1)S(1)}, s32[]{:S(2)}) async-start(s8[12582912]{0:T(1024)(128)(4,1)} %bitcast.4), calls=%async_computation.4 | async-start | bytes 8388608
  1.6 18.8 %slice-start.5 = ((s8[12582912]{0:T(1024)(128)(4,1)}), s8[4194304]{0:T(1024)(128)(4,1)S(1)}, s32[]{:S(2)}) async-start(s8[12582912]{0:T(1024)(128)(4,1)} %bitcast.4), calls=%async_computation.5 | async-start | bytes 8388608
  1.6 18.8 %slice-start.7 = ((s8[12582912]{0:T(1024)(128)(4,1)}), s8[4194304]{0:T(1024)(128)(4,1)S(1)}, s32[]{:S(2)}) async-start(s8[12582912]{0:T(1024)(128)(4,1)} %bitcast.6), calls=%async_computation.7 | async-start | bytes 8388608
  1.6 18.8 %slice-start.8 = ((s8[12582912]{0:T(1024)(128)(4,1)}), s8[4194304]{0:T(1024)(128)(4,1)S(1)}, s32[]{:S(2)}) async-start(s8[12582912]{0:T(1024)(128)(4,1)} %bitcast.6), calls=%async_computation.8 | async-start | bytes 8388608
  3.2 7.2 %collective-permute-start.7 = (bf16[8,3200]{1,0:T(8,128)(2,1)S(1)}, bf16[8,3200]{1,0:T(8,128)(2,1)S(1)}, u32[]{:S(2)}, u32[]{:S(2)}) collective-permute-start(bf16[8,3200]{1,0:T(8,128)(2,1)S(1)} %get-tuple-element.23.refs_0_), channel_id=1, source_target_pairs={{0,4},{4,0},{8,12},{12,8},{1,5},{5,1},{9,13},{13,9},{2,6},{6,2},{1... | collective-permute-start | bytes 153608 | tf_op jit(solution)/shard_map/ppermute | solution.py:365
  6.3 6.6 %collective-permute-start.11 = (bf16[8,3200]{1,0:T(8,128)(2,1)S(1)}, bf16[8,3200]{1,0:T(8,128)(2,1)S(1)}, u32[]{:S(2)}, u32[]{:S(2)}) collective-permute-start(bf16[8,3200]{1,0:T(8,128)(2,1)S(1)} %get-tuple-element.23.refs_0_), channel_id=1, source_target_pairs={{0,12},{4,8},{8,4},{12,0},{1,13},{5,9},{9,5},{13,1},{2,14},{6,10},... | collective-permute-start | bytes 153608 | tf_op jit(solution)/shard_map/ppermute | solution.py:365
  8.8 5.6 %collective-permute-start.3 = (bf16[8,3200]{1,0:T(8,128)(2,1)S(1)}, bf16[8,3200]{1,0:T(8,128)(2,1)S(1)}, u32[]{:S(2)}, u32[]{:S(2)}) collective-permute-start(bf16[8,3200]{1,0:T(8,128)(2,1)S(1)} %get-tuple-element.23.refs_0_), channel_id=1, source_target_pairs={{0,8},{4,12},{8,0},{12,4},{1,9},{5,13},{9,1},{13,5},{2,10},{6,14},... | collective-permute-start | bytes 153608 | tf_op jit(solution)/shard_map/ppermute | solution.py:365
  8.9 6.0 %collective-permute-start.1 = (bf16[8,3200]{1,0:T(8,128)(2,1)S(1)}, bf16[8,3200]{1,0:T(8,128)(2,1)S(1)}, u32[]{:S(2)}, u32[]{:S(2)}) collective-permute-start(bf16[8,3200]{1,0:T(8,128)(2,1)S(1)} %get-tuple-element.23.refs_0_), channel_id=1, source_target_pairs={{0,2},{1,3},{2,0},{3,1},{4,6},{5,7},{6,4},{7,5},{8,10},{9,11},{10,... | collective-permute-start | bytes 153608 | tf_op jit(solution)/shard_map/ppermute | solution.py:365
  10.4 5.4 %collective-permute-start.9 = (bf16[8,3200]{1,0:T(8,128)(2,1)S(1)}, bf16[8,3200]{1,0:T(8,128)(2,1)S(1)}, u32[]{:S(2)}, u32[]{:S(2)}) collective-permute-start(bf16[8,3200]{1,0:T(8,128)(2,1)S(1)} %collective-permute-done.7.refs_0_), channel_id=1, source_target_pairs={{0,2},{1,3},{2,0},{3,1},{4,6},{5,7},{6,4},{7,5},{8,10},{9,11},{10,... | collective-permute-start | bytes 153608 | tf_op jit(solution)/shard_map/ppermute | solution.py:365
  12.9 4.1 %collective-permute-start.13 = (bf16[8,3200]{1,0:T(8,128)(2,1)S(1)}, bf16[8,3200]{1,0:T(8,128)(2,1)S(1)}, u32[]{:S(2)}, u32[]{:S(2)}) collective-permute-start(bf16[8,3200]{1,0:T(8,128)(2,1)S(1)} %collective-permute-done.11.refs_4_), channel_id=1, source_target_pairs={{0,2},{1,3},{2,0},{3,1},{4,6},{5,7},{6,4},{7,5},{8,10},{9,11},{10,... | collective-permute-start | bytes 153608 | tf_op jit(solution)/shard_map/ppermute | solution.py:365
  14.4 2.6 %collective-permute-start.12 = (bf16[8,3200]{1,0:T(8,128)(2,1)S(1)}, bf16[8,3200]{1,0:T(8,128)(2,1)S(1)}, u32[]{:S(2)}, u32[]{:S(2)}) collective-permute-start(bf16[8,3200]{1,0:T(8,128)(2,1)S(1)} %collective-permute-done.11.refs_4_), channel_id=1, source_target_pairs={{0,1},{1,0},{2,3},{3,2},{4,5},{5,4},{6,7},{7,6},{8,9},{9,8},{10,11... | collective-permute-start | bytes 153608 | tf_op jit(solution)/shard_map/ppermute | solution.py:365
  14.4 3.1 %collective-permute-start.8 = (bf16[8,3200]{1,0:T(8,128)(2,1)S(1)}, bf16[8,3200]{1,0:T(8,128)(2,1)S(1)}, u32[]{:S(2)}, u32[]{:S(2)}) collective-permute-start(bf16[8,3200]{1,0:T(8,128)(2,1)S(1)} %collective-permute-done.7.refs_0_), channel_id=1, source_target_pairs={{0,1},{1,0},{2,3},{3,2},{4,5},{5,4},{6,7},{7,6},{8,9},{9,8},{10,11... | collective-permute-start | bytes 153608 | tf_op jit(solution)/shard_map/ppermute | solution.py:365
  14.9 4.1 %collective-permute-start.5 = (bf16[8,3200]{1,0:T(8,128)(2,1)S(1)}, bf16[8,3200]{1,0:T(8,128)(2,1)S(1)}, u32[]{:S(2)}, u32[]{:S(2)}) collective-permute-start(bf16[8,3200]{1,0:T(8,128)(2,1)S(1)} %collective-permute-done.3.refs_4_), channel_id=1, source_target_pairs={{0,2},{1,3},{2,0},{3,1},{4,6},{5,7},{6,4},{7,5},{8,10},{9,11},{10,... | collective-permute-start | bytes 153608 | tf_op jit(solution)/shard_map/ppermute | solution.py:365
  15.9 3.2 %collective-permute-start.10 = (bf16[8,3200]{1,0:T(8,128)(2,1)S(1)}, bf16[8,3200]{1,0:T(8,128)(2,1)S(1)}, u32[]{:S(2)}, u32[]{:S(2)}) collective-permute-start(bf16[8,3200]{1,0:T(8,128)(2,1)S(1)} %collective-permute-done.9.refs_2_), channel_id=1, source_target_pairs={{0,1},{1,0},{2,3},{3,2},{4,5},{5,4},{6,7},{7,6},{8,9},{9,8},{10,11... | collective-permute-start | bytes 153608 | tf_op jit(solution)/shard_map/ppermute | solution.py:365
  17.0 2.5 %collective-permute-start.14 = (bf16[8,3200]{1,0:T(8,128)(2,1)S(1)}, bf16[8,3200]{1,0:T(8,128)(2,1)S(1)}, u32[]{:S(2)}, u32[]{:S(2)}) collective-permute-start(bf16[8,3200]{1,0:T(8,128)(2,1)S(1)} %collective-permute-done.13.refs_6_), channel_id=1, source_target_pairs={{0,1},{1,0},{2,3},{3,2},{4,5},{5,4},{6,7},{7,6},{8,9},{9,8},{10,11... | collective-permute-start | bytes 153608 | tf_op jit(solution)/shard_map/ppermute | solution.py:365
  17.0 3.1 %collective-permute-start = (bf16[8,3200]{1,0:T(8,128)(2,1)S(1)}, bf16[8,3200]{1,0:T(8,128)(2,1)S(1)}, u32[]{:S(2)}, u32[]{:S(2)}) collective-permute-start(bf16[8,3200]{1,0:T(8,128)(2,1)S(1)} %get-tuple-element.23.refs_0_), channel_id=1, source_target_pairs={{0,1},{1,0},{2,3},{3,2},{4,5},{5,4},{6,7},{7,6},{8,9},{9,8},{10,11... | collective-permute-start | bytes 153608 | tf_op jit(solution)/shard_map/ppermute | solution.py:365
  17.5 2.6 %collective-permute-start.4 = (bf16[8,3200]{1,0:T(8,128)(2,1)S(1)}, bf16[8,3200]{1,0:T(8,128)(2,1)S(1)}, u32[]{:S(2)}, u32[]{:S(2)}) collective-permute-start(bf16[8,3200]{1,0:T(8,128)(2,1)S(1)} %collective-permute-done.3.refs_4_), channel_id=1, source_target_pairs={{0,1},{1,0},{2,3},{3,2},{4,5},{5,4},{6,7},{7,6},{8,9},{9,8},{10,11... | collective-permute-start | bytes 153608 | tf_op jit(solution)/shard_map/ppermute | solution.py:365
  19.0 1.2 %collective-permute-start.2 = (bf16[8,3200]{1,0:T(8,128)(2,1)S(1)}, bf16[8,3200]{1,0:T(8,128)(2,1)S(1)}, u32[]{:S(2)}, u32[]{:S(2)}) collective-permute-start(bf16[8,3200]{1,0:T(8,128)(2,1)S(1)} %collective-permute-done.1.refs_2_), channel_id=1, source_target_pairs={{0,1},{1,0},{2,3},{3,2},{4,5},{5,4},{6,7},{7,6},{8,9},{9,8},{10,11... | collective-permute-start | bytes 153608 | tf_op jit(solution)/shard_map/ppermute | solution.py:365
  19.0 1.4 %collective-permute-start.6 = (bf16[8,3200]{1,0:T(8,128)(2,1)S(1)}, bf16[8,3200]{1,0:T(8,128)(2,1)S(1)}, u32[]{:S(2)}, u32[]{:S(2)}) collective-permute-start(bf16[8,3200]{1,0:T(8,128)(2,1)S(1)} %collective-permute-done.5.refs_6_), channel_id=1, source_target_pairs={{0,1},{1,0},{2,3},{3,2},{4,5},{5,4},{6,7},{7,6},{8,9},{9,8},{10,11... | collective-permute-start | bytes 153608 | tf_op jit(solution)/shard_map/ppermute | solution.py:365
  22.0 5.8 %collective-permute-start.24 = (bf16[104,512]{1,0:T(8,128)(2,1)S(1)}, bf16[104,512]{1,0:T(8,128)(2,1)S(1)}, u32[]{:S(2)}, u32[]{:S(2)}) collective-permute-start(bf16[104,512]{1,0:T(8,128)(2,1)S(1)} %get-tuple-element.26.refs_3_), channel_id=1, source_target_pairs={{0,2},{1,3},{2,0},{3,1},{4,6},{5,7},{6,4},{7,5},{8,10},{9,11},{10,... | collective-permute-start | bytes 319496 | tf_op jit(solution)/shard_map/ppermute | solution.py:365
  23.2 5.9 %collective-permute-start.25 = (bf16[104,512]{1,0:T(8,128)(2,1)S(1)}, bf16[104,512]{1,0:T(8,128)(2,1)S(1)}, u32[]{:S(2)}, u32[]{:S(2)}) collective-permute-start(bf16[104,512]{1,0:T(8,128)(2,1)S(1)} %get-tuple-element.26.refs_3_), channel_id=1, source_target_pairs={{0,1},{1,0},{2,3},{3,2},{4,5},{5,4},{6,7},{7,6},{8,9},{9,8},{10,11... | collective-permute-start | bytes 319496 | tf_op jit(solution)/shard_map/ppermute | solution.py:365
  24.4 5.7 %collective-permute-start.21 = (bf16[104,512]{1,0:T(8,128)(2,1)S(1)}, bf16[104,512]{1,0:T(8,128)(2,1)S(1)}, u32[]{:S(2)}, u32[]{:S(2)}) collective-permute-start(bf16[104,512]{1,0:T(8,128)(2,1)S(1)} %shard_map.115.refs_3_), channel_id=1, source_target_pairs={{0,2},{1,3},{2,0},{3,1},{4,6},{5,7},{6,4},{7,5},{8,10},{9,11},{10,... | collective-permute-start | bytes 319496 | tf_op jit(solution)/shard_map/ppermute | solution.py:365
  25.4 7.8 %collective-permute-start.22 = (bf16[104,512]{1,0:T(8,128)(2,1)S(1)}, bf16[104,512]{1,0:T(8,128)(2,1)S(1)}, u32[]{:S(2)}, u32[]{:S(2)}) collective-permute-start(bf16[104,512]{1,0:T(8,128)(2,1)S(1)} %shard_map.115.refs_3_), channel_id=1, source_target_pairs={{0,1},{1,0},{2,3},{3,2},{4,5},{5,4},{6,7},{7,6},{8,9},{9,8},{10,11... | collective-permute-start | bytes 319496 | tf_op jit(solution)/shard_map/ppermute | solution.py:365
  25.6 7.0 %slice-start = ((s8[12582912]{0:T(1024)(128)(4,1)}), s8[4194304]{0:T(1024)(128)(4,1)S(1)}, s32[]{:S(2)}) async-start(s8[12582912]{0:T(1024)(128)(4,1)} %bitcast.2), calls=%async_computation | async-start | bytes 8388608
  25.6 7.0 %slice-start.1 = ((s8[12582912]{0:T(1024)(128)(4,1)}), s8[4194304]{0:T(1024)(128)(4,1)S(1)}, s32[]{:S(2)}) async-start(s8[12582912]{0:T(1024)(128)(4,1)} %bitcast.2), calls=%async_computation.1 | async-start | bytes 8388608
  26.7 3.6 %copy-start.4 = (bf16[3072,4]{0,1:T(4,128)(2,1)S(1)}, bf16[3072,4]{0,1:T(4,128)(2,1)}, u32[]{:S(2)}) copy-start(bf16[3072,4]{0,1:T(4,128)(2,1)} %param.17) | copy-start | bytes 73732
  26.7 5.8 %slice-start.2 = ((s8[12582912]{0:T(1024)(128)(4,1)}), s8[4194304]{0:T(1024)(128)(4,1)S(1)}, s32[]{:S(2)}) async-start(s8[12582912]{0:T(1024)(128)(4,1)} %bitcast.2), calls=%async_computation.2 | async-start | bytes 8388608
  26.7 5.3 %collective-permute-start.18 = (bf16[104,512]{1,0:T(8,128)(2,1)S(1)}, bf16[104,512]{1,0:T(8,128)(2,1)S(1)}, u32[]{:S(2)}, u32[]{:S(2)}) collective-permute-start(bf16[104,512]{1,0:T(8,128)(2,1)S(1)} %shard_map.114.refs_3_), channel_id=1, source_target_pairs={{0,2},{1,3},{2,0},{3,1},{4,6},{5,7},{6,4},{7,5},{8,10},{9,11},{10,... | collective-permute-start | bytes 319496 | tf_op jit(solution)/shard_map/ppermute | solution.py:365
  27.8 4.2 %collective-permute-start.26 = (bf16[104,512]{1,0:T(8,128)(2,1)S(1)}, bf16[104,512]{1,0:T(8,128)(2,1)S(1)}, u32[]{:S(2)}, u32[]{:S(2)}) collective-permute-start(bf16[104,512]{1,0:T(8,128)(2,1)S(1)} %collective-permute-done.24.refs_0_), channel_id=1, source_target_pairs={{0,1},{1,0},{2,3},{3,2},{4,5},{5,4},{6,7},{7,6},{8,9},{9,8},{10,11... | collective-permute-start | bytes 319496 | tf_op jit(solution)/shard_map/ppermute | solution.py:365
  29.1 5.4 %collective-permute-start.15 = (bf16[104,512]{1,0:T(8,128)(2,1)S(1)}, bf16[104,512]{1,0:T(8,128)(2,1)S(1)}, u32[]{:S(2)}, u32[]{:S(2)}) collective-permute-start(bf16[104,512]{1,0:T(8,128)(2,1)S(1)} %shard_map.113.refs_4_), channel_id=1, source_target_pairs={{0,2},{1,3},{2,0},{3,1},{4,6},{5,7},{6,4},{7,5},{8,10},{9,11},{10,... | collective-permute-start | bytes 319496 | tf_op jit(solution)/shard_map/ppermute | solution.py:365
  30.1 4.4 %collective-permute-start.23 = (bf16[104,512]{1,0:T(8,128)(2,1)S(1)}, bf16[104,512]{1,0:T(8,128)(2,1)S(1)}, u32[]{:S(2)}, u32[]{:S(2)}) collective-permute-start(bf16[104,512]{1,0:T(8,128)(2,1)S(1)} %collective-permute-done.21.refs_0_), channel_id=1, source_target_pairs={{0,1},{1,0},{2,3},{3,2},{4,5},{5,4},{6,7},{7,6},{8,9},{9,8},{10,11... | collective-permute-start | bytes 319496 | tf_op jit(solution)/shard_map/ppermute | solution.py:365
  32.0 3.0 %collective-permute-start.19 = (bf16[104,512]{1,0:T(8,128)(2,1)S(1)}, bf16[104,512]{1,0:T(8,128)(2,1)S(1)}, u32[]{:S(2)}, u32[]{:S(2)}) collective-permute-start(bf16[104,512]{1,0:T(8,128)(2,1)S(1)} %shard_map.114.refs_3_), channel_id=1, source_target_pairs={{0,1},{1,0},{2,3},{3,2},{4,5},{5,4},{6,7},{7,6},{8,9},{9,8},{10,11... | collective-permute-start | bytes 319496 | tf_op jit(solution)/shard_map/ppermute | solution.py:365
  32.0 3.0 %collective-permute-start.20 = (bf16[104,512]{1,0:T(8,128)(2,1)S(1)}, bf16[104,512]{1,0:T(8,128)(2,1)S(1)}, u32[]{:S(2)}, u32[]{:S(2)}) collective-permute-start(bf16[104,512]{1,0:T(8,128)(2,1)S(1)} %collective-permute-done.18.refs_0_), channel_id=1, source_target_pairs={{0,1},{1,0},{2,3},{3,2},{4,5},{5,4},{6,7},{7,6},{8,9},{9,8},{10,11... | collective-permute-start | bytes 319496 | tf_op jit(solution)/shard_map/ppermute | solution.py:365
  33.2 2.6 %collective-permute-start.16 = (bf16[104,512]{1,0:T(8,128)(2,1)S(1)}, bf16[104,512]{1,0:T(8,128)(2,1)S(1)}, u32[]{:S(2)}, u32[]{:S(2)}) collective-permute-start(bf16[104,512]{1,0:T(8,128)(2,1)S(1)} %shard_map.113.refs_4_), channel_id=1, source_target_pairs={{0,1},{1,0},{2,3},{3,2},{4,5},{5,4},{6,7},{7,6},{8,9},{9,8},{10,11... | collective-permute-start | bytes 319496 | tf_op jit(solution)/shard_map/ppermute | solution.py:365
  34.4 1.4 %collective-permute-start.17 = (bf16[104,512]{1,0:T(8,128)(2,1)S(1)}, bf16[104,512]{1,0:T(8,128)(2,1)S(1)}, u32[]{:S(2)}, u32[]{:S(2)}) collective-permute-start(bf16[104,512]{1,0:T(8,128)(2,1)S(1)} %collective-permute-done.15.refs_0_), channel_id=1, source_target_pairs={{0,1},{1,0},{2,3},{3,2},{4,5},{5,4},{6,7},{7,6},{8,9},{9,8},{10,11... | collective-permute-start | bytes 319496 | tf_op jit(solution)/shard_map/ppermute | solution.py:365
  36.5 6.2 %collective-permute-start.27 = (bf16[32,768]{1,0:T(8,128)(2,1)S(1)}, bf16[32,768]{1,0:T(8,128)(2,1)S(1)}, u32[]{:S(2)}, u32[]{:S(2)}) collective-permute-start(bf16[32,768]{1,0:T(8,128)(2,1)S(1)} %get-tuple-element.32), channel_id=1, source_target_pairs={{0,12},{4,8},{8,4},{12,0},{1,13},{5,9},{9,5},{13,1},{2,14},{6,10},... | collective-permute-start | bytes 147464 | tf_op jit(solution)/shard_map/ppermute | solution.py:365
  38.8 5.8 %collective-permute-start.28 = (bf16[32,768]{1,0:T(8,128)(2,1)S(1)}, bf16[32,768]{1,0:T(8,128)(2,1)S(1)}, u32[]{:S(2)}, u32[]{:S(2)}) collective-permute-start(bf16[32,768]{1,0:T(8,128)(2,1)S(1)} %get-tuple-element.33), channel_id=1, source_target_pairs={{0,8},{4,12},{8,0},{12,4},{1,9},{5,13},{9,1},{13,5},{2,10},{6,14},... | collective-permute-start | bytes 147464 | tf_op jit(solution)/shard_map/ppermute | solution.py:365
  38.9 5.8 %collective-permute-start.29 = (bf16[32,768]{1,0:T(8,128)(2,1)S(1)}, bf16[32,768]{1,0:T(8,128)(2,1)S(1)}, u32[]{:S(2)}, u32[]{:S(2)}) collective-permute-start(bf16[32,768]{1,0:T(8,128)(2,1)S(1)} %get-tuple-element.34), channel_id=1, source_target_pairs={{0,4},{4,0},{8,12},{12,8},{1,5},{5,1},{9,13},{13,9},{2,6},{6,2},{1... | collective-permute-start | bytes 147464 | tf_op jit(solution)/shard_map/ppermute | solution.py:365
  44.7 1.9 %collective-permute-start.30 = (bf16[8,768]{1,0:T(8,128)(2,1)S(1)}, bf16[8,768]{1,0:T(8,128)(2,1)S(1)}, u32[]{:S(2)}, u32[]{:S(2)}) collective-permute-start(bf16[8,768]{1,0:T(8,128)(2,1)S(1)} %get-tuple-element.36), channel_id=1, source_target_pairs={{0,1},{1,0},{2,3},{3,2},{4,5},{5,4},{6,7},{7,6},{8,9},{9,8},{10,11... | collective-permute-start | bytes 36872 | tf_op jit(solution)/shard_map/ppermute | solution.py:365
  44.8 3.8 %collective-permute-start.31 = (bf16[8,768]{1,0:T(8,128)(2,1)S(1)}, bf16[8,768]{1,0:T(8,128)(2,1)S(1)}, u32[]{:S(2)}, u32[]{:S(2)}) collective-permute-start(bf16[8,768]{1,0:T(8,128)(2,1)S(1)} %get-tuple-element.37), channel_id=1, source_target_pairs={{0,2},{1,3},{2,0},{3,1},{4,6},{5,7},{6,4},{7,5},{8,10},{9,11},{10,... | collective-permute-start | bytes 36872 | tf_op jit(solution)/shard_map/ppermute | solution.py:365
  45.8 3.1 %collective-permute-start.32 = (bf16[8,768]{1,0:T(8,128)(2,1)S(1)}, bf16[8,768]{1,0:T(8,128)(2,1)S(1)}, u32[]{:S(2)}, u32[]{:S(2)}) collective-permute-start(bf16[8,768]{1,0:T(8,128)(2,1)S(1)} %get-tuple-element.38), channel_id=1, source_target_pairs={{0,3},{1,2},{2,1},{3,0},{4,7},{5,6},{6,5},{7,4},{8,11},{9,10},{10,... | collective-permute-start | bytes 36872 | tf_op jit(solution)/shard_map/ppermute | solution.py:365
  (2 other events, 1.5 us)
